TPU v7x, 32 devices: a whole 2x2x4 slice. The times are simulated.
32 devices in a mesh: seq: 16 (over z, x, core), head: 2 (over y).
Axes of the slice: x: 2, y: 2, z: 4, core: 2. Of those that a mesh axis runs over, the one named last changes fastest.
Arguments:
- query_rows: bfloat16 [2048, 3072], P(('seq', 'head')), may hold values from -5 to 5
- key_rows: bfloat16 [2048, 3072], P(('seq', 'head')), may hold values from -5 to 5
- value_rows: bfloat16 [2048, 3072], P(('seq', 'head')), may hold values from -6 to 6
- out_grad: bfloat16 [2048, 3072], P(('seq', 'head')), may hold values from -6 to 6
- block_mask: int32 [2, 4, 4], replicated, may hold values 0 or 1
Outputs:
- attended: bfloat16 [2048, 3072], P(('seq', 'head'))
- grad_query: bfloat16 [2048, 3072], P(('seq', 'head'))
- grad_keys: bfloat16 [2048, 3072], P(('seq', 'head'))
- grad_values: bfloat16 [2048, 3072], P(('seq', 'head'))
All inputs are finite; a program needn't handle non-finite values.
Results may differ from a plain program's by a relative error of at most 0.024.
Values may be sent and summed in bfloat16 or wider, within the bound.
No kernel may reach another device: no remote copies, remote signals or barrier semaphores. Data moves between devices by JAX's collectives and lax.ppermute only.
A program may use at most 64 MiB of HBM per device.

v0:
```python
import math

import jax
import jax.numpy as jnp
from jax import lax
from jax.sharding import PartitionSpec as P

HD = 128
BLOCK = 128
GROUP = 4


def partner_2(shard, axis, distance):
    return lax.ppermute(shard, axis, [(i, i ^ 1 << distance) for i in range(lax.axis_size(axis))])


def passed_along(shard, axis, by):
    peers = lax.axis_size(axis)
    pairs = [(i, i + by) for i in range(peers) if 0 <= i + by < peers]
    return lax.ppermute(shard, axis, pairs)


def widen_mask(bits):
    blocks = bits.shape[0]
    grid = jnp.broadcast_to((bits > 0)[:, None, :, None], (blocks, BLOCK, blocks, BLOCK))
    return grid.reshape(blocks * BLOCK, blocks * BLOCK)


def place_pair(mine, other, is_low, dim):
    return lax.cond(
        is_low,
        lambda pair: jnp.concatenate([pair[0], pair[1]], dim),
        lambda pair: jnp.concatenate([pair[1], pair[0]], dim),
        (mine, other),
    )


def per_device(query_rows, key_rows, value_rows, out_grad, block_mask):
    queries, keys_local, values_local, grads_output = (
        lax.all_to_all(query_rows, "head", split_axis=1, concat_axis=0, tiled=True),
        lax.all_to_all(key_rows, "head", split_axis=1, concat_axis=0, tiled=True),
        lax.all_to_all(value_rows, "head", split_axis=1, concat_axis=0, tiled=True),
        lax.all_to_all(out_grad, "head", split_axis=1, concat_axis=0, tiled=True),
    )
    seq_index = lax.axis_index("seq")
    group_bits = GROUP.bit_length() - 1
    rank = seq_index % GROUP
    frame_index = seq_index // GROUP
    frame_count = lax.axis_size("seq") // GROUP
    level_count = block_mask.shape[0]
    block_rows = queries.shape[0]
    frame_tokens = block_rows * GROUP
    head_count = queries.shape[1] // HD
    score_scale = 1.0 / math.sqrt(HD)
    own_pair = jnp.stack([keys_local, values_local])

    def low_bit(bit):
        return seq_index >> bit & 1 == 0

    whole_pair = own_pair
    for bit in range(group_bits):
        other = partner_2(whole_pair, "seq", bit)
        whole_pair = place_pair(whole_pair, other, low_bit(bit), 1)
    partner_list = []
    for level_index in range(level_count):
        for orient in (1, -1):
            partner_list.append(
                passed_along(whole_pair, "seq", orient * GROUP * (1 << level_index))
            )
    every_pair = jnp.concatenate([whole_pair] + partner_list, axis=1)
    keys_all, values_all = (every_pair[0], every_pair[1])
    allowed_list = [jnp.ones((block_rows, frame_tokens), bool)]
    for level_index in range(level_count):
        for orient in (1, -1):
            partner = frame_index - orient * (1 << level_index)
            inside = (partner >= 0) & (partner < frame_count)
            allowed_list.append(
                lax.dynamic_slice_in_dim(
                    widen_mask(block_mask[level_index]), rank * block_rows, block_rows, 0
                )
                & inside
            )
    allowed = jnp.concatenate(allowed_list, axis=1)

    def head_scores(query_head, keys_head):
        scores = (
            jnp.einsum("qd,kd->qk", query_head, keys_head, preferred_element_type=jnp.float32)
            * score_scale
        )
        return jnp.where(allowed, scores, -jnp.inf)

    outputs = []
    logsums = []
    for head_index in range(head_count):
        columns = slice(head_index * HD, (head_index + 1) * HD)
        scores = head_scores(queries[:, columns], keys_all[:, columns])
        peak = jnp.max(scores, axis=1, keepdims=True)
        logsum = peak + jnp.log(jnp.sum(jnp.exp(scores - peak), axis=1, keepdims=True))
        weights = jnp.exp(scores - logsum).astype(jnp.bfloat16)
        outputs.append(
            jnp.dot(weights, values_all[:, columns], preferred_element_type=jnp.float32).astype(
                jnp.bfloat16
            )
        )
        logsums.append(logsum)
    attended = jnp.concatenate(outputs, axis=1)
    query_grads = []
    key_grads = []
    value_grads = []
    for head_index in range(head_count):
        columns = slice(head_index * HD, (head_index + 1) * HD)
        query_head = queries[:, columns]
        grad_head = grads_output[:, columns]
        scores = head_scores(query_head, keys_all[:, columns])
        probability = jnp.exp(scores - logsums[head_index])
        weights = probability.astype(jnp.bfloat16)
        grad_weights = jnp.einsum(
            "qd,kd->qk", grad_head, values_all[:, columns], preferred_element_type=jnp.float32
        )
        delta_row = jnp.sum(
            grad_head.astype(jnp.float32) * attended[:, columns].astype(jnp.float32),
            axis=1,
            keepdims=True,
        )
        grad_scores = (probability * (grad_weights - delta_row) * score_scale).astype(jnp.bfloat16)
        query_grads.append(
            jnp.dot(grad_scores, keys_all[:, columns], preferred_element_type=jnp.float32).astype(
                jnp.bfloat16
            )
        )
        key_grads.append(
            jnp.einsum(
                "qk,qd->kd", grad_scores, query_head, preferred_element_type=jnp.float32
            ).astype(jnp.bfloat16)
        )
        value_grads.append(
            jnp.einsum("qk,qd->kd", weights, grad_head, preferred_element_type=jnp.float32).astype(
                jnp.bfloat16
            )
        )
    grad_query = jnp.concatenate(query_grads, axis=1)
    grad_pair = jnp.stack(
        [jnp.concatenate(key_grads, axis=1), jnp.concatenate(value_grads, axis=1)]
    )
    total = grad_pair[:, :frame_tokens].astype(jnp.float32)
    piece_index = 1
    for level_index in range(level_count):
        for orient in (1, -1):
            piece = grad_pair[:, piece_index * frame_tokens : (piece_index + 1) * frame_tokens]
            returned = passed_along(piece, "seq", -orient * GROUP * (1 << level_index))
            total = total + returned.astype(jnp.float32)
            piece_index += 1
    for bit in reversed(range(group_bits)):
        half = total.shape[1] // 2
        first_half = total[:, :half]
        second_half = total[:, half:]
        is_low = low_bit(bit)
        outgoing = jnp.where(is_low, second_half, first_half)
        staying = jnp.where(is_low, first_half, second_half)
        total = staying + partner_2(outgoing, "seq", bit)
    grad_keys = total[0].astype(jnp.bfloat16)
    grad_values = total[1].astype(jnp.bfloat16)
    return (
        lax.all_to_all(attended, "head", split_axis=0, concat_axis=1, tiled=True),
        lax.all_to_all(grad_query, "head", split_axis=0, concat_axis=1, tiled=True),
        lax.all_to_all(grad_keys, "head", split_axis=0, concat_axis=1, tiled=True),
        lax.all_to_all(grad_values, "head", split_axis=0, concat_axis=1, tiled=True),
    )


def solution(mesh):
    placed = (
        P(("seq", "head"), None),
        P(("seq", "head"), None),
        P(("seq", "head"), None),
        P(("seq", "head"), None),
        P(),
    )
    return jax.shard_map(
        per_device,
        mesh=mesh,
        in_specs=placed,
        out_specs=(
            P(("seq", "head"), None),
            P(("seq", "head"), None),
            P(("seq", "head"), None),
            P(("seq", "head"), None),
        ),
        check_vma=False,
    )
```

profile of v0, /device:TPU:10, one launch (start us, length us, event | category | flops | bytes accessed | tf_op | source)
XLA Modules:
  0.0 668.3 jit_solution(17430742267840205656)
XLA Ops:
  0.6 1.8 copy.122
  2.5 3.5 all-to-all-start.1
  6.0 6.8 %all-to-all-done.1 = bf16[64,2,1536]{2,0,1:T(8,128)(2,1)S(1)} async-done(((bf16[64,2,1536]{2,0,1:T(8,128)(2,1)}), bf16[64,2,1536]{2,0,1:T(8,128)(2,1)S(1)}, u32[]{:S(2)}, u32[]{:S(2)}) %all-to-all-start.1) | async-done | bytes 393248 | tf_op jit(solution)/shard_map/all_to_all | solution.py:42
  12.8 8.4 %all_to_all.140 = bf16[64,2,1536]{2,0,1:T(8,128)(2,1)S(1)} all-to-all(bf16[64,2,1536]{2,0,1:T(8,128)(2,1)S(1)} %bitcast.276), channel_id=1, replica_groups=mesh['seq'=16,'head'=2] {'head'}, dimensions={1} | all-to-all | bytes 786432 | tf_op jit(solution)/shard_map/all_to_all | solution.py:41
  21.3 2.3 collective-permute-done
  24.3 35.9 %collective-permute-done.1 = bf16[2,256,1536]{2,1,0:T(8,128)(2,1)S(1)} collective-permute-done((bf16[2,256,1536]{2,1,0:T(8,128)(2,1)S(1)}, bf16[2,256,1536]{2,1,0:T(8,128)(2,1)S(1)}, u32[]{:S(2)}, u32[]{:S(2)}) %collective-permute-start.1) | collective-permute-done | bytes 1572896 | tf_op jit(solution)/shard_map/ppermute | solution.py:14
  60.2 1.9 conditional.3
  60.2 1.9 pad_maximum_fusion.2
  62.1 3.6 collective-permute-start.2
  65.7 4.0 collective-permute-start.3
  69.7 6.1 collective-permute-start.4
  77.9 3.5 all-to-all-start.4
  83.8 1.9 copy.121
  86.4 1.5 and_dynamic-update-slice_fusion.3
  87.9 1.5 and_dynamic-update-slice_fusion.2
  89.4 1.5 and_dynamic-update-slice_fusion.1
  90.9 1.5 and_dynamic-update-slice_fusion
  92.4 4.2 all-to-all-start.2
  101.7 1.5 copy.93
  115.1 86.8 %collective-permute-done.2 = bf16[2,512,1536]{2,1,0:T(8,128)(2,1)} collective-permute-done((bf16[2,512,1536]{2,1,0:T(8,128)(2,1)}, bf16[2,512,1536]{2,1,0:T(8,128)(2,1)}, u32[]{:S(2)}, u32[]{:S(2)}) %collective-permute-start.2) | collective-permute-done | bytes 3145760 | tf_op jit(solution)/shard_map/ppermute | solution.py:20
  201.9 2.1 constant_dynamic-update-slice_fusion.3
  204.0 2.3 collective-permute-done.3
  206.3 2.1 constant_dynamic-update-slice_fusion.2
  208.4 59.2 %collective-permute-done.4 = bf16[2,512,1536]{2,1,0:T(8,128)(2,1)} collective-permute-done((bf16[2,512,1536]{2,1,0:T(8,128)(2,1)}, bf16[2,512,1536]{2,1,0:T(8,128)(2,1)}, u32[]{:S(2)}, u32[]{:S(2)}) %collective-permute-start.4) | collective-permute-done | bytes 3145760 | tf_op jit(solution)/shard_map/ppermute | solution.py:20
  267.6 2.1 constant_dynamic-update-slice_fusion.1
  269.7 2.1 constant_dynamic-update-slice_fusion
  271.8 6.3 slice_bitcast_fusion.1
  278.1 1.9 fusion.248
  280.0 2.1 fusion.249
  282.2 1.7 fusion.250
  283.9 1.5 fusion.251
  285.4 1.5 fusion.252
  286.9 1.5 fusion.253
  288.4 1.5 fusion.254
  289.9 1.7 fusion.255
  291.6 1.5 fusion.256
  293.1 1.5 fusion.257
  294.6 1.7 fusion.258
  296.3 1.5 fusion.259
  336.2 2.6 fusion.98
  338.8 5.5 collective-permute-start.9
  345.6 3.8 collective-permute-start.7
  349.4 2.2 collective-permute-start.6
  351.6 125.1 %collective-permute-done.9 = bf16[2,512,1536]{1,2,0:T(8,128)(2,1)S(1)} collective-permute-done((bf16[2,512,1536]{1,2,0:T(8,128)(2,1)}, bf16[2,512,1536]{1,2,0:T(8,128)(2,1)S(1)}, u32[]{:S(2)}, u32[]{:S(2)}) %collective-permute-start.9) | collective-permute-done | bytes 3145760 | tf_op jit(solution)/shard_map/ppermute | solution.py:20
  476.7 67.2 %collective-permute-done.7 = bf16[2,512,1536]{1,2,0:T(8,128)(2,1)S(1)} collective-permute-done((bf16[2,512,1536]{1,2,0:T(8,128)(2,1)S(1)}, bf16[2,512,1536]{1,2,0:T(8,128)(2,1)S(1)}, u32[]{:S(2)}, u32[]{:S(2)}) %collective-permute-start.7) | collective-permute-done | bytes 3145760 | tf_op jit(solution)/shard_map/ppermute | solution.py:20
  544.0 4.1 collective-permute-done.6
  548.1 2.1 convert_add_fusion
  550.6 2.3 copy-done
  554.4 3.7 all-to-all-start.3
  558.1 2.4 fusion.123
  560.6 2.3 fusion.122
  562.8 2.3 fusion.121
  565.1 2.4 fusion.120
  567.6 2.3 fusion.119
  569.8 51.2 %collective-permute-done.10 = f32[2,256,1536]{1,2,0:T(8,128)} collective-permute-done((f32[2,256,1536]{1,2,0:T(8,128)S(1)}, f32[2,256,1536]{1,2,0:T(8,128)}, u32[]{:S(2)}, u32[]{:S(2)}) %collective-permute-start.10) | collective-permute-done | bytes 3145760 | tf_op jit(solution)/shard_map/ppermute | solution.py:14
  621.0 2.8 select_add_fusion
  632.3 1.9 copy.84
  634.2 2.5 add_convert_fusion
  636.7 3.6 all-to-all-start.5
  641.3 6.5 all-to-all-done.5
  647.8 3.5 all-to-all-start.6
  652.2 5.8 all-to-all-done.6
  657.9 3.5 all-to-all-start.7
  663.7 3.5 all-to-all-done.7
  (226 shorter events, 77.5 us)
Async XLA Ops:
  0.6 5.3 copy-start.24
  2.5 10.3 %all-to-all-start.1 = ((bf16[64,2,1536]{2,0,1:T(8,128)(2,1)}), bf16[64,2,1536]{2,0,1:T(8,128)(2,1)S(1)}, u32[]{:S(2)}, u32[]{:S(2)}) async-start(bf16[64,2,1536]{2,0,1:T(8,128)(2,1)} %bitcast.234), calls=%async_computation.1 | async-start | bytes 786432 | tf_op jit(solution)/shard_map/all_to_all | solution.py:42
  21.2 2.4 collective-permute-start
  23.7 36.5 %collective-permute-start.1 = (bf16[2,256,1536]{2,1,0:T(8,128)(2,1)S(1)}, bf16[2,256,1536]{2,1,0:T(8,128)(2,1)S(1)}, u32[]{:S(2)}, u32[]{:S(2)}) collective-permute-start(bf16[2,256,1536]{2,1,0:T(8,128)(2,1)S(1)} %get-tuple-element.104), channel_id=1, source_target_pairs={{0,4},{2,6},{4,0},{6,2},{8,12},{10,14},{12,8},{14,10},{16,20},{18,... | collective-permute-start | bytes 4718600 | tf_op jit(solution)/shard_map/ppermute | solution.py:14
  60.2 17.0 %copy-start.25 = (bf16[64,3072]{1,0:T(8,128)(2,1)S(1)}, bf16[64,3072]{1,0:T(8,128)(2,1)}, u32[]{:S(2)}) copy-start(bf16[64,3072]{1,0:T(8,128)(2,1)} %param.12) | copy-start | bytes 1179652
  62.1 19.4 %copy-start.38 = (s32[2,4,4]{2,1,0:T(4,128)S(1)}, s32[2,4,4]{2,1,0:T(4,128)}, u32[]{:S(2)}) copy-start(s32[2,4,4]{2,1,0:T(4,128)} %param.13) | copy-start | bytes 388
  62.1 139.9 %collective-permute-start.2 = (bf16[2,512,1536]{2,1,0:T(8,128)(2,1)}, bf16[2,512,1536]{2,1,0:T(8,128)(2,1)}, u32[]{:S(2)}, u32[]{:S(2)}) collective-permute-start(bf16[2,512,1536]{2,1,0:T(8,128)(2,1)} %get-tuple-element.105), channel_id=1, source_target_pairs={{0,8},{2,10},{4,12},{6,14},{8,16},{10,18},{12,20},{14,22},{16,24},... | collective-permute-start | bytes 9437192 | tf_op jit(solution)/shard_map/ppermute | solution.py:20
  65.7 140.7 %collective-permute-start.3 = (bf16[2,512,1536]{2,1,0:T(8,128)(2,1)}, bf16[2,512,1536]{2,1,0:T(8,128)(2,1)}, u32[]{:S(2)}, u32[]{:S(2)}) collective-permute-start(bf16[2,512,1536]{2,1,0:T(8,128)(2,1)} %get-tuple-element.105), channel_id=1, source_target_pairs={{8,0},{10,2},{12,4},{14,6},{16,8},{18,10},{20,12},{22,14},{24,16},... | collective-permute-start | bytes 9437192 | tf_op jit(solution)/shard_map/ppermute | solution.py:20
  69.7 197.9 %collective-permute-start.4 = (bf16[2,512,1536]{2,1,0:T(8,128)(2,1)}, bf16[2,512,1536]{2,1,0:T(8,128)(2,1)}, u32[]{:S(2)}, u32[]{:S(2)}) collective-permute-start(bf16[2,512,1536]{2,1,0:T(8,128)(2,1)} %get-tuple-element.105), channel_id=1, source_target_pairs={{0,16},{2,18},{4,20},{6,22},{8,24},{10,26},{12,28},{14,30},{1,17},... | collective-permute-start | bytes 9437192 | tf_op jit(solution)/shard_map/ppermute | solution.py:20
  75.9 193.9 %collective-permute-start.5 = (bf16[2,512,1536]{2,1,0:T(8,128)(2,1)}, bf16[2,512,1536]{2,1,0:T(8,128)(2,1)}, u32[]{:S(2)}, u32[]{:S(2)}) collective-permute-start(bf16[2,512,1536]{2,1,0:T(8,128)(2,1)} %get-tuple-element.105), channel_id=1, source_target_pairs={{16,0},{18,2},{20,4},{22,6},{24,8},{26,10},{28,12},{30,14},{17,1},... | collective-permute-start | bytes 9437192 | tf_op jit(solution)/shard_map/ppermute | solution.py:20
  77.9 14.4 %all-to-all-start.4 = ((bf16[64,2,1536]{2,0,1:T(8,128)(2,1)}), bf16[64,2,1536]{2,0,1:T(8,128)(2,1)S(1)}, u32[]{:S(2)}, u32[]{:S(2)}) async-start(bf16[64,2,1536]{2,0,1:T(8,128)(2,1)} %bitcast.232), calls=%async_computation.4 | async-start | bytes 786432 | tf_op jit(solution)/shard_map/all_to_all | solution.py:43
  83.8 31.1 %copy-start.2 = (bf16[2,512,1536]{2,1,0:T(8,128)(2,1)S(1)}, bf16[2,512,1536]{2,1,0:T(8,128)(2,1)}, u32[]{:S(2)}) copy-start(bf16[2,512,1536]{2,1,0:T(8,128)(2,1)} %get-tuple-element.105) | copy-start | bytes 9437188
  92.4 185.7 %all-to-all-start.2 = ((bf16[64,2,1536]{2,0,1:T(8,128)(2,1)}), bf16[64,2,1536]{2,0,1:T(8,128)(2,1)}, u32[]{:S(2)}, u32[]{:S(2)}) async-start(bf16[64,2,1536]{2,0,1:T(8,128)(2,1)} %bitcast.269), calls=%async_computation.2 | async-start | bytes 786432 | tf_op jit(solution)/shard_map/all_to_all | solution.py:40
  278.1 5.8 copy-start.3
  289.9 8.6 %slice-start = ((s8[7864320]{0:T(1024)(128)(4,1)}), s8[4194304]{0:T(1024)(128)(4,1)S(1)}, s32[]{:S(2)}) async-start(s8[7864320]{0:T(1024)(128)(4,1)} %bitcast.236), calls=%async_computation.8 | async-start | bytes 8388608
  294.6 3.9 slice-start.1
  302.4 0.8 copy-start.37
  303.7 14.3 %copy-start.5 = (bf16[128,2560]{0,1:T(8,128)(2,1)}, bf16[128,2560]{0,1:T(8,128)(2,1)S(1)}, u32[]{:S(2)}) copy-start(bf16[128,2560]{0,1:T(8,128)(2,1)S(1)} %fusion.71) | copy-start | bytes 1966084
  303.7 0.8 copy-start.36
  304.9 18.4 %copy-start.6 = (bf16[128,2560]{0,1:T(8,128)(2,1)}, bf16[128,2560]{0,1:T(8,128)(2,1)S(1)}, u32[]{:S(2)}) copy-start(bf16[128,2560]{0,1:T(8,128)(2,1)S(1)} %fusion.70) | copy-start | bytes 1966084
  305.0 0.8 copy-start.35
  306.4 18.3 %copy-start.7 = (bf16[128,2560]{0,1:T(8,128)(2,1)}, bf16[128,2560]{0,1:T(8,128)(2,1)S(1)}, u32[]{:S(2)}) copy-start(bf16[128,2560]{0,1:T(8,128)(2,1)S(1)} %fusion.69) | copy-start | bytes 1966084
  306.4 0.8 copy-start.34
  307.7 18.2 %copy-start.8 = (bf16[128,2560]{0,1:T(8,128)(2,1)}, bf16[128,2560]{0,1:T(8,128)(2,1)S(1)}, u32[]{:S(2)}) copy-start(bf16[128,2560]{0,1:T(8,128)(2,1)S(1)} %fusion.68) | copy-start | bytes 1966084
  307.7 0.8 copy-start.33
  309.0 18.1 %copy-start.11 = (bf16[128,2560]{0,1:T(8,128)(2,1)}, bf16[128,2560]{0,1:T(8,128)(2,1)S(1)}, u32[]{:S(2)}) copy-start(bf16[128,2560]{0,1:T(8,128)(2,1)S(1)} %fusion.67) | copy-start | bytes 1966084
  309.0 0.8 copy-start.32
  310.2 17.9 %copy-start.9 = (bf16[128,2560]{0,1:T(8,128)(2,1)}, bf16[128,2560]{0,1:T(8,128)(2,1)S(1)}, u32[]{:S(2)}) copy-start(bf16[128,2560]{0,1:T(8,128)(2,1)S(1)} %fusion.66) | copy-start | bytes 1966084
  310.2 0.8 copy-start.31
  311.5 17.8 %copy-start.12 = (bf16[128,2560]{0,1:T(8,128)(2,1)}, bf16[128,2560]{0,1:T(8,128)(2,1)S(1)}, u32[]{:S(2)}) copy-start(bf16[128,2560]{0,1:T(8,128)(2,1)S(1)} %fusion.65) | copy-start | bytes 1966084
  311.5 0.8 copy-start.30
  312.8 17.7 %copy-start.14 = (bf16[128,2560]{0,1:T(8,128)(2,1)}, bf16[128,2560]{0,1:T(8,128)(2,1)S(1)}, u32[]{:S(2)}) copy-start(bf16[128,2560]{0,1:T(8,128)(2,1)S(1)} %fusion.64) | copy-start | bytes 1966084
  312.8 0.8 copy-start.29
  314.1 17.5 %copy-start.16 = (bf16[128,2560]{0,1:T(8,128)(2,1)}, bf16[128,2560]{0,1:T(8,128)(2,1)S(1)}, u32[]{:S(2)}) copy-start(bf16[128,2560]{0,1:T(8,128)(2,1)S(1)} %fusion.63) | copy-start | bytes 1966084
  314.1 0.8 copy-start.28
  315.4 17.4 %copy-start.18 = (bf16[128,2560]{0,1:T(8,128)(2,1)}, bf16[128,2560]{0,1:T(8,128)(2,1)S(1)}, u32[]{:S(2)}) copy-start(bf16[128,2560]{0,1:T(8,128)(2,1)S(1)} %fusion.62) | copy-start | bytes 1966084
  315.4 0.8 copy-start.27
  316.6 17.3 %copy-start.20 = (bf16[128,2560]{0,1:T(8,128)(2,1)}, bf16[128,2560]{0,1:T(8,128)(2,1)S(1)}, u32[]{:S(2)}) copy-start(bf16[128,2560]{0,1:T(8,128)(2,1)S(1)} %fusion.61) | copy-start | bytes 1966084
  316.7 0.8 copy-start.26
  317.9 17.1 %copy-start.22 = (bf16[128,2560]{0,1:T(8,128)(2,1)}, bf16[128,2560]{0,1:T(8,128)(2,1)S(1)}, u32[]{:S(2)}) copy-start(bf16[128,2560]{0,1:T(8,128)(2,1)S(1)} %fusion.60) | copy-start | bytes 1966084
  338.8 138.0 %collective-permute-start.9 = (bf16[2,512,1536]{1,2,0:T(8,128)(2,1)}, bf16[2,512,1536]{1,2,0:T(8,128)(2,1)S(1)}, u32[]{:S(2)}, u32[]{:S(2)}) collective-permute-start(bf16[2,512,1536]{1,2,0:T(8,128)(2,1)} %get-tuple-element.36), channel_id=1, source_target_pairs={{0,16},{2,18},{4,20},{6,22},{8,24},{10,26},{12,28},{14,30},{1,17},... | collective-permute-start | bytes 9437192 | tf_op jit(solution)/shard_map/ppermute | solution.py:20
  344.3 132.5 %collective-permute-start.8 = (bf16[2,512,1536]{1,2,0:T(8,128)(2,1)S(1)}, bf16[2,512,1536]{1,2,0:T(8,128)(2,1)S(1)}, u32[]{:S(2)}, u32[]{:S(2)}) collective-permute-start(bf16[2,512,1536]{1,2,0:T(8,128)(2,1)S(1)} %get-tuple-element.37), channel_id=1, source_target_pairs={{16,0},{18,2},{20,4},{22,6},{24,8},{26,10},{28,12},{30,14},{17,1},... | collective-permute-start | bytes 9437192 | tf_op jit(solution)/shard_map/ppermute | solution.py:20
  345.6 198.4 %collective-permute-start.7 = (bf16[2,512,1536]{1,2,0:T(8,128)(2,1)S(1)}, bf16[2,512,1536]{1,2,0:T(8,128)(2,1)S(1)}, u32[]{:S(2)}, u32[]{:S(2)}) collective-permute-start(bf16[2,512,1536]{1,2,0:T(8,128)(2,1)S(1)} %get-tuple-element.35), channel_id=1, source_target_pairs={{0,8},{2,10},{4,12},{6,14},{8,16},{10,18},{12,20},{14,22},{16,24},... | collective-permute-start | bytes 9437192 | tf_op jit(solution)/shard_map/ppermute | solution.py:20
  349.4 198.7 %collective-permute-start.6 = (bf16[2,512,1536]{1,2,0:T(8,128)(2,1)S(1)}, bf16[2,512,1536]{1,2,0:T(8,128)(2,1)S(1)}, u32[]{:S(2)}, u32[]{:S(2)}) collective-permute-start(bf16[2,512,1536]{1,2,0:T(8,128)(2,1)S(1)} %get-tuple-element.34), channel_id=1, source_target_pairs={{8,0},{10,2},{12,4},{14,6},{16,8},{18,10},{20,12},{22,14},{24,16},... | collective-permute-start | bytes 9437192 | tf_op jit(solution)/shard_map/ppermute | solution.py:20
  550.2 2.7 copy-start
  552.9 68.1 %collective-permute-start.10 = (f32[2,256,1536]{1,2,0:T(8,128)S(1)}, f32[2,256,1536]{1,2,0:T(8,128)}, u32[]{:S(2)}, u32[]{:S(2)}) collective-permute-start(f32[2,256,1536]{1,2,0:T(8,128)S(1)} %slice_select_fusion), channel_id=1, source_target_pairs={{0,4},{2,6},{4,0},{6,2},{8,12},{10,14},{12,8},{14,10},{16,20},{18,... | collective-permute-start | bytes 9437192 | tf_op jit(solution)/shard_map/ppermute | solution.py:14
  554.4 82.3 %all-to-all-start.3 = ((bf16[2,64,1536]{2,1,0:T(8,128)(2,1)}), bf16[2,64,1536]{2,1,0:T(8,128)(2,1)S(1)}, u32[]{:S(2)}, u32[]{:S(2)}) async-start(bf16[2,64,1536]{2,1,0:T(8,128)(2,1)} %bitcast.271), calls=%async_computation.3 | async-start | bytes 786432 | tf_op jit(solution)/shard_map/all_to_all | solution.py:164
  558.1 62.9 %copy-start.1 = (f32[2,512,1536]{1,2,0:T(8,128)S(1)}, f32[2,512,1536]{1,2,0:T(8,128)}, u32[]{:S(2)}) copy-start(f32[2,512,1536]{1,2,0:T(8,128)} %copy-done) | copy-start | bytes 18874372
  565.1 60.0 %slice-start.2 = ((s8[7864320]{0:T(1024)(128)(4,1)}), s8[4194304]{0:T(1024)(128)(4,1)S(1)}, s32[]{:S(2)}) async-start(s8[7864320]{0:T(1024)(128)(4,1)} %bitcast.242), calls=%async_computation.10 | async-start | bytes 8388608
  569.8 55.3 %slice-start.3 = ((s8[7864320]{0:T(1024)(128)(4,1)}), s8[3670016]{0:T(1024)(128)(4,1)S(1)}, s32[]{:S(2)}) async-start(s8[7864320]{0:T(1024)(128)(4,1)} %bitcast.242), calls=%async_computation.11 | async-start | bytes 7340032
  623.8 1.4 copy-start.10
  625.2 1.1 copy-start.13
  625.2 2.1 copy-start.15
  625.2 9.1 %collective-permute-start.11 = (f32[2,128,1536]{1,2,0:T(8,128)}, f32[2,128,1536]{1,2,0:T(8,128)}, u32[]{:S(2)}, u32[]{:S(2)}) collective-permute-start(f32[2,128,1536]{1,2,0:T(8,128)} %slice_select_fusion.1), channel_id=1, source_target_pairs={{0,2},{2,0},{4,6},{6,4},{8,10},{10,8},{12,14},{14,12},{16,18},{18,... | collective-permute-start | bytes 4718600 | tf_op jit(solution)/shard_map/ppermute | solution.py:14
  626.2 2.0 copy-start.17
  627.3 2.0 copy-start.19
  628.3 2.0 copy-start.21
  629.3 2.0 copy-start.23
  636.7 3.6 copy-start.4
  636.7 11.1 %all-to-all-start.5 = ((bf16[2,64,1536]{2,1,0:T(8,128)(2,1)}), bf16[2,64,1536]{2,1,0:T(8,128)(2,1)S(1)}, u32[]{:S(2)}, u32[]{:S(2)}) async-start(bf16[2,64,1536]{2,1,0:T(8,128)(2,1)} %bitcast.273), calls=%async_computation.5 | async-start | bytes 786432 | tf_op jit(solution)/shard_map/all_to_all | solution.py:165
  647.8 10.2 %all-to-all-start.6 = ((bf16[2,64,1536]{2,1,0:T(8,128)(2,1)}), bf16[2,64,1536]{2,1,0:T(8,128)(2,1)S(1)}, u32[]{:S(2)}, u32[]{:S(2)}) async-start(bf16[2,64,1536]{2,1,0:T(8,128)(2,1)} %bitcast.44), calls=%async_computation.6 | async-start | bytes 786432 | tf_op jit(solution)/shard_map/all_to_all | solution.py:166
  657.9 9.3 %all-to-all-start.7 = ((bf16[2,64,1536]{2,1,0:T(8,128)(2,1)}), bf16[2,64,1536]{2,1,0:T(8,128)(2,1)S(1)}, u32[]{:S(2)}, u32[]{:S(2)}) async-start(bf16[2,64,1536]{2,1,0:T(8,128)(2,1)} %bitcast.46), calls=%async_computation.7 | async-start | bytes 786432 | tf_op jit(solution)/shard_map/all_to_all | solution.py:167
where the time goes:
time: 676 us; the launch traced here: 668 us
  waiting for transfers between devices  457 us (68%)
  matrix products  68.1 us (10%)
  starting transfers between devices  54.4 us (8%)
  local copies, waits for them, and re-layouts  54.1 us (8%)
  other arithmetic  24.7 us (4%)
  blocking collectives  8.37 us (1%)
    ppermute x8, waiting for transfers between devices, passed_along(): return lax.ppermute(shard, axis, pairs)  345 us
    ppermute x4, waiting for transfers between devices, partner_2(): lax.ppermute(shard, axis, [(i, i ^ 1 << distance) for i in range(lax.axis...  89.3 us
    unnamed x106, local copies, waits for them, and re-layouts  32.7 us
    ppermute x8, starting transfers between devices, passed_along(): return lax.ppermute(shard, axis, pairs)  27.9 us
    dot_general x12, matrix products, head_scores(): jnp.einsum('qd,kd->qk', query_head, keys_head, preferred_element_type=jnp...  19.6 us
    dot_general x12, matrix products, per_device(): jnp.dot(grad_scores, keys_all[:, columns], preferred_element_type=jnp.flo...  18.7 us
    dot_general x12, matrix products, per_device(): jnp.einsum('qk,qd->kd', grad_scores, query_head, preferred_element_type=j...  13.8 us
  transfers between devices with their start and end apart: 19, of which 13 were waited for; matrix products, arithmetic and copies ran while one was open for 12% of the time, Pallas kernels for 0%

commit v1 on v0

--- a/solution.py
+++ b/solution.py
@@ -3,11 +3,18 @@
 import jax
 import jax.numpy as jnp
 from jax import lax
+from jax.experimental import pallas as pl
+from jax.experimental.pallas import tpu as pltpu
+from jax.sharding import Mesh
 from jax.sharding import PartitionSpec as P
 
 HD = 128
 BLOCK = 128
 GROUP = 4
+SCALE = 1.0 / math.sqrt(HD)
+SCALE_LOG2 = SCALE * math.log2(math.e)
+MASKED = -1e30
+VMEM_BYTES = 40 * 1024 * 1024
 
 
 def partner_2(shard, axis, distance):
@@ -35,7 +42,7 @@
     )
 
 
-def per_device(query_rows, key_rows, value_rows, out_grad, block_mask):
+def per_device_general(query_rows, key_rows, value_rows, out_grad, block_mask):
     queries, keys_local, values_local, grads_output = (
         lax.all_to_all(query_rows, "head", split_axis=1, concat_axis=0, tiled=True),
         lax.all_to_all(key_rows, "head", split_axis=1, concat_axis=0, tiled=True),
@@ -168,23 +175,289 @@
     )
 
 
+NT = (((1,), (1,)), ((), ()))
+F32 = jnp.float32
+BF16 = jnp.bfloat16
+
+
+def dot(a, b):
+    return jnp.dot(a, b, preferred_element_type=F32)
+
+
+def dot_nt(a, b):
+    return lax.dot_general(a, b, NT, preferred_element_type=F32)
+
+
+def rows_of(ref, which):
+    part = ref[:, which]
+    return part.reshape(part.shape[0] * part.shape[1], part.shape[2])
+
+
+def put_rows(ref, which, rows):
+    ref[:, which] = rows.reshape(ref.shape[0], ref.shape[2], ref.shape[3])
+
+
+def bias_rows(mask_ref, level, valid, blocks):
+    lane_block = lax.broadcasted_iota(jnp.int32, (1, blocks * BLOCK), 1) // BLOCK
+    rows = []
+    for key_block in range(blocks):
+        row = jnp.zeros((1, blocks * BLOCK), F32)
+        for query_block in range(blocks):
+            open_ = (mask_ref[level, query_block, key_block] > 0) & valid
+            value = jnp.where(open_, 0.0, MASKED).astype(F32)
+            row = jnp.where(lane_block == query_block, value, row)
+        rows.append(row)
+    return rows
+
+
+def masked_scores(keys, queries, bias):
+    scores = dot_nt(keys, queries) * SCALE_LOG2
+    if bias is None:
+        return scores
+    blocks = len(bias)
+    return jnp.concatenate(
+        [scores[j * BLOCK : (j + 1) * BLOCK] + bias[j] for j in range(blocks)], axis=0
+    )
+
+
+def near_forward_kernel(frame_ref, mask_ref, qg_ref, kv0_ref, kv1_ref, kv3_ref, e_ref, acc_ref, ml_ref):
+    tokens = e_ref.shape[2]
+    blocks = tokens // BLOCK
+    frame = frame_ref[0]
+    inner = (frame == 1) | (frame == 2)
+    queries = rows_of(qg_ref, 0)
+    slots = (
+        (kv0_ref, None),
+        (kv1_ref, bias_rows(mask_ref, 0, frame >= 0, blocks)),
+        (kv3_ref, bias_rows(mask_ref, 0, inner, blocks)),
+    )
+    scores = [masked_scores(rows_of(ref, 0), queries, bias) for ref, bias in slots]
+    peak = scores[0].max(axis=0, keepdims=True)
+    for score in scores[1:]:
+        peak = jnp.maximum(peak, score.max(axis=0, keepdims=True))
+    total = jnp.zeros((1, tokens), F32)
+    acc = jnp.zeros((HD, tokens), F32)
+    for index, (ref, _) in enumerate(slots):
+        e = jnp.exp2(scores[index] - peak)
+        total = total + e.sum(axis=0, keepdims=True)
+        e = e.astype(BF16)
+        e_ref[0, index * tokens : (index + 1) * tokens] = e
+        acc = acc + dot(rows_of(ref, 1).T, e)
+    acc_ref[0] = acc
+    ml_ref[0, 0:1] = peak
+    ml_ref[0, 1:2] = total
+
+
+def far_kernel(
+    frame_ref, mask_ref, qg_ref, kva_ref, kvb_ref, acc_ref, ml_ref,
+    dkv_ref, att_ref, wd_ref, dq_ref,
+):
+    tokens = acc_ref.shape[2]
+    blocks = tokens // BLOCK
+    frame = frame_ref[0]
+    inner = (frame == 1) | (frame == 2)
+    queries = rows_of(qg_ref, 0)
+    keys = jnp.where(inner, rows_of(kvb_ref, 0), rows_of(kva_ref, 0))
+    values = jnp.where(inner, rows_of(kvb_ref, 1), rows_of(kva_ref, 1))
+    scores = masked_scores(keys, queries, bias_rows(mask_ref, 1, frame >= 0, blocks))
+    peak2 = scores.max(axis=0, keepdims=True)
+    e = jnp.exp2(scores - peak2)
+    total2 = e.sum(axis=0, keepdims=True)
+    e = e.astype(BF16)
+    acc2 = dot(values.T, e)
+    peak1 = ml_ref[0, 0:1]
+    peak = jnp.maximum(peak1, peak2)
+    near = jnp.exp2(peak1 - peak)
+    far = jnp.exp2(peak2 - peak)
+    inv = 1.0 / (near * ml_ref[0, 1:2] + far * total2)
+    near = near * inv
+    far = far * inv
+    out = (acc_ref[0] * near + acc2 * far).astype(BF16)
+    att = out.T
+    att_ref[...] = att.reshape(att_ref.shape)
+    grads = rows_of(qg_ref, 1).T.astype(F32)
+    delta = (grads * out.astype(F32)).sum(axis=0, keepdims=True)
+    wd_ref[0, 0:1] = near
+    wd_ref[0, 1:2] = near * delta
+    scaled = (grads * far).astype(BF16)
+    ds = (e.astype(F32) * (dot(values, scaled) - far * delta)).astype(BF16)
+    put_rows(dkv_ref, 0, (dot(ds, queries) * SCALE).astype(BF16))
+    put_rows(dkv_ref, 1, dot_nt(e, scaled).astype(BF16))
+    dq_ref[0] = dot(keys.T, ds)
+
+
+def near_backward_kernel(
+    qg_ref, kv0_ref, kv1_ref, kv3_ref, e_ref, wd_ref, dq2_ref, att_ref,
+    dkv0_ref, dkv1_ref, dkv3_ref, out_ref,
+):
+    tokens = e_ref.shape[2]
+    queries = rows_of(qg_ref, 0)
+    grads = rows_of(qg_ref, 1).T.astype(F32)
+    near = wd_ref[0, 0:1]
+    delta = wd_ref[0, 1:2]
+    scaled = (grads * near).astype(BF16)
+    dq = dq2_ref[0]
+    for index, (kv_ref, dkv_ref) in enumerate(
+        ((kv0_ref, dkv0_ref), (kv1_ref, dkv1_ref), (kv3_ref, dkv3_ref))
+    ):
+        e = e_ref[0, index * tokens : (index + 1) * tokens]
+        keys = rows_of(kv_ref, 0)
+        ds = (e.astype(F32) * (dot(rows_of(kv_ref, 1), scaled) - delta)).astype(BF16)
+        put_rows(dkv_ref, 0, (dot(ds, queries) * SCALE).astype(BF16))
+        put_rows(dkv_ref, 1, dot_nt(e, scaled).astype(BF16))
+        dq = dq + dot(keys.T, ds)
+    put_rows(out_ref, 1, (dq * SCALE).astype(BF16).T)
+    out_ref[:, 0] = att_ref[...]
+
+
+def pack_kernel(a_ref, b_ref, out_ref):
+    width = out_ref.shape[3]
+    for peer in range(out_ref.shape[0]):
+        out_ref[peer, 0] = a_ref[:, peer * width : (peer + 1) * width]
+        out_ref[peer, 1] = b_ref[:, peer * width : (peer + 1) * width]
+
+
+def unpack_kernel(in_ref, a_ref, b_ref):
+    width = in_ref.shape[3]
+    for peer in range(in_ref.shape[0]):
+        a_ref[:, peer * width : (peer + 1) * width] = in_ref[peer, 0]
+        b_ref[:, peer * width : (peer + 1) * width] = in_ref[peer, 1]
+
+
+def params():
+    return pltpu.CompilerParams(vmem_limit_bytes=VMEM_BYTES)
+
+
+def cost(flops, data):
+    return pl.CostEstimate(flops=flops, bytes_accessed=data, transcendentals=0)
+
+
+def per_device_line(query_rows, key_rows, value_rows, out_grad, block_mask):
+    plane = ("rank", "head")
+    peers = lax.axis_size("rank") * lax.axis_size("head")
+    rows, columns = query_rows.shape
+    width = columns // peers
+    heads = width // HD
+    tokens = peers * rows
+    pair_shape = (peers, 2, rows, width)
+    pair_type = jax.ShapeDtypeStruct(pair_shape, BF16)
+    frame = lax.axis_index("frame").astype(jnp.int32).reshape(1)
+
+    def pack(a, b):
+        return pl.pallas_call(pack_kernel, out_shape=pair_type)(a, b)
+
+    def unpack(pair):
+        row_type = jax.ShapeDtypeStruct((rows, columns), BF16)
+        return pl.pallas_call(unpack_kernel, out_shape=(row_type, row_type))(pair)
+
+    def swap(pair):
+        return lax.all_to_all(pair, plane, 0, 0, tiled=True)
+
+    smem = pl.BlockSpec(memory_space=pltpu.SMEM)
+    pair_spec = pl.BlockSpec((peers, 2, rows, HD), lambda h: (0, 0, 0, h))
+    one_spec = pl.BlockSpec((peers, rows, HD), lambda h: (0, 0, h))
+
+    def head_spec(*shape):
+        return pl.BlockSpec((1,) + shape, lambda h: (h, 0, 0))
+
+    pair_flops = heads * 2 * tokens * tokens * HD
+
+    kv0 = swap(pack(key_rows, value_rows))
+    edge = [(0, 1), (1, 0), (2, 3), (3, 2)]
+    middle = [(1, 2), (2, 1)]
+    kv3 = lax.ppermute(kv0, "frame", middle)
+    kv1 = lax.ppermute(kv0, "frame", edge)
+    qg = swap(pack(query_rows, out_grad))
+    kv2b = lax.ppermute(kv1, "frame", middle)
+    kv2a = lax.ppermute(kv3, "frame", [(1, 0), (2, 3)])
+
+    e, acc, ml = pl.pallas_call(
+        near_forward_kernel,
+        grid=(heads,),
+        in_specs=[smem, smem, pair_spec, pair_spec, pair_spec, pair_spec],
+        out_specs=[head_spec(3 * tokens, tokens), head_spec(HD, tokens), head_spec(8, tokens)],
+        out_shape=[
+            jax.ShapeDtypeStruct((heads, 3 * tokens, tokens), BF16),
+            jax.ShapeDtypeStruct((heads, HD, tokens), F32),
+            jax.ShapeDtypeStruct((heads, 8, tokens), F32),
+        ],
+        compiler_params=params(),
+        cost_estimate=cost(20 * pair_flops, 8 << 20),
+    )(frame, block_mask, qg, kv0, kv1, kv3)
+
+    dkv2, att, wd, dq2 = pl.pallas_call(
+        far_kernel,
+        grid=(heads,),
+        in_specs=[
+            smem, smem, pair_spec, pair_spec, pair_spec,
+            head_spec(HD, tokens), head_spec(8, tokens),
+        ],
+        out_specs=[pair_spec, one_spec, head_spec(8, tokens), head_spec(HD, tokens)],
+        out_shape=[
+            pair_type,
+            jax.ShapeDtypeStruct((peers, rows, width), BF16),
+            jax.ShapeDtypeStruct((heads, 8, tokens), F32),
+            jax.ShapeDtypeStruct((heads, HD, tokens), F32),
+        ],
+        compiler_params=params(),
+        cost_estimate=cost(20 * pair_flops, 8 << 20),
+    )(frame, block_mask, qg, kv2a, kv2b, acc, ml)
+
+    back_edge = lax.ppermute(dkv2, "frame", [(0, 1), (3, 2)])
+    back_middle = lax.ppermute(dkv2, "frame", middle)
+
+    dkv0, dkv1, dkv3, att_dq = pl.pallas_call(
+        near_backward_kernel,
+        grid=(heads,),
+        in_specs=[
+            pair_spec, pair_spec, pair_spec, pair_spec,
+            head_spec(3 * tokens, tokens), head_spec(8, tokens), head_spec(HD, tokens), one_spec,
+        ],
+        out_specs=[pair_spec] * 4,
+        out_shape=[pair_type] * 4,
+        compiler_params=params(),
+        cost_estimate=cost(20 * pair_flops, 8 << 20),
+    )(qg, kv0, kv1, kv3, e, wd, dq2, att)
+
+    def added(*pairs):
+        total = pairs[0].astype(F32)
+        for pair in pairs[1:]:
+            total = total + pair.astype(F32)
+        return total.astype(BF16)
+
+    last_middle = lax.ppermute(added(dkv3, back_edge), "frame", middle)
+    last_edge = lax.ppermute(added(dkv1, back_middle), "frame", edge)
+    attended, grad_query = unpack(swap(att_dq))
+    grad_keys, grad_values = unpack(swap(added(dkv0, last_edge, last_middle)))
+    return attended, grad_query, grad_keys, grad_values
+
+
 def solution(mesh):
-    placed = (
-        P(("seq", "head"), None),
-        P(("seq", "head"), None),
-        P(("seq", "head"), None),
-        P(("seq", "head"), None),
-        P(),
-    )
-    return jax.shard_map(
-        per_device,
-        mesh=mesh,
-        in_specs=placed,
-        out_specs=(
-            P(("seq", "head"), None),
-            P(("seq", "head"), None),
-            P(("seq", "head"), None),
-            P(("seq", "head"), None),
-        ),
-        check_vma=False,
-    )
+    seq, head = mesh.shape["seq"], mesh.shape["head"]
+    frames = seq // GROUP
+    line = Mesh(mesh.devices.reshape(frames, GROUP, head), ("frame", "rank", "head"))
+
+    def run(query_rows, key_rows, value_rows, out_grad, block_mask):
+        heads = query_rows.shape[1] // HD
+        tokens = query_rows.shape[0] // frames
+        fits = (
+            frames == 4
+            and block_mask.shape[0] == 2
+            and heads % (GROUP * head) == 0
+            and tokens == block_mask.shape[1] * BLOCK
+            and tokens // (GROUP * head) % 16 == 0
+        )
+        if fits:
+            body, where, axes = per_device_line, line, ("frame", "rank", "head")
+        else:
+            body, where, axes = per_device_general, mesh, ("seq", "head")
+        row_spec = P(axes, None)
+        return jax.shard_map(
+            body,
+            mesh=where,
+            in_specs=(row_spec,) * 4 + (P(),),
+            out_specs=(row_spec,) * 4,
+            check_vma=False,
+        )(query_rows, key_rows, value_rows, out_grad, block_mask)
+
+    return run

time: 676 us -> 133 us (0.20)
  waiting for transfers between devices: 457 us -> 51.7 us
  matrix products: 68.1 us -> 0 us
  local copies, waits for them, and re-layouts: 54.1 us -> 0.9 us
  Pallas kernels: 0 us -> 26 us
  starting transfers between devices: 54.4 us -> 32.2 us
  other arithmetic: 24.7 us -> 3.8 us
    ppermute x12 -> x8, waiting for transfers between devices: 434 us -> 42.8 us  [the longest x1 11.5 us: per_device_line(): kv3 = lax.ppermute(kv0, 'frame', middle)]
    dot_general x72 -> x0, matrix products: 68.1 us -> none  [the longest x12 19.6 us: head_scores(): jnp.einsum('qd,kd->qk', query_head, keys_head, preferred_element_type=jnp...]
    unnamed x106 -> x10, local copies, waits for them, and re-layouts: 32.7 us -> 0.9 us
    pallas_call x0 -> x7, Pallas kernels: none -> 26 us  [the longest x1 7.04 us: per_device_line(): pl.pallas_call(near_backward_kernel, grid=(heads,), in_specs=[pair_spec,...]
    all_to_all x7 -> x3, waiting for transfers between devices: 22.6 us -> 8.95 us  [swap(): return lax.all_to_all(pair, plane, 0, 0, tiled=True)]
    ppermute x12 -> x8, starting transfers between devices: 29.1 us -> 17.6 us  [the longest x1 3.6 us: per_device_line(): kv3 = lax.ppermute(kv0, 'frame', middle)]
    all_to_all x7 -> x3, starting transfers between devices: 25.4 us -> 14.6 us  [swap(): return lax.all_to_all(pair, plane, 0, 0, tiled=True)]
    all_to_all x8 -> x0, local copies, waits for them, and re-layouts: 7.62 us -> none  [the longest x1 1.92 us: per_device(): lax.all_to_all(query_rows, 'head', split_axis=1, concat_axis=0, tiled=True)]
  transfers between devices with their start and end apart: 19 -> 11, of which waited for: 13 -> 7; matrix products, arithmetic and copies ran while one was open for 12% -> 3% of each run, Pallas kernels for 0% -> 13%
where the time goes in v1:
time: 133 us; the launch traced here: 130 us
  waiting for transfers between devices  51.7 us (39%)
  starting transfers between devices  32.2 us (24%)
  Pallas kernels  26 us (20%)
  blocking collectives  15.1 us (11%)
  other arithmetic  3.8 us (3%)
    all_to_all x1, blocking collectives, swap(): return lax.all_to_all(pair, plane, 0, 0, tiled=True)  15.1 us
    all_to_all x3, starting transfers between devices, swap(): return lax.all_to_all(pair, plane, 0, 0, tiled=True)  14.6 us
    ppermute x1, waiting for transfers between devices, per_device_line(): kv3 = lax.ppermute(kv0, 'frame', middle)  11.5 us
    ppermute x1, waiting for transfers between devices, per_device_line(): last_middle = lax.ppermute(added(dkv3, back_edge), 'frame', middle)  9.07 us
    all_to_all x3, waiting for transfers between devices, swap(): return lax.all_to_all(pair, plane, 0, 0, tiled=True)  8.95 us
    ppermute x1, waiting for transfers between devices, per_device_line(): back_edge = lax.ppermute(dkv2, 'frame', [(0, 1), (3, 2)])  7.85 us
    pallas_call x1, Pallas kernels, per_device_line(): pl.pallas_call(near_backward_kernel, grid=(heads,), in_specs=[pair_spec,...  7.04 us
    ppermute x1, waiting for transfers between devices, per_device_line(): kv2a = lax.ppermute(kv3, 'frame', [(1, 0), (2, 3)])  6.4 us
  transfers between devices with their start and end apart: 11, of which 7 were waited for; matrix products, arithmetic and copies ran while one was open for 3% of the time, Pallas kernels for 13%

profile of v1, /device:TPU:10, one launch (start us, length us, event | category | flops | bytes accessed | tf_op | source)
XLA Modules:
  0.0 130.5 jit_solution(6508106699890195272)
XLA Ops:
  0.6 2.1 %shard_map.85 = bf16[8,2,64,384]{3,2,1,0:T(8,128)(2,1)} custom-call(bf16[64,3072]{1,0:T(8,128)(2,1)} %a_ref.3, bf16[64,3072]{1,0:T(8,128)(2,1)} %b_ref.3), custom_call_target="tpu_custom_call" | custom-call | tf_op jit(solution)/shard_map/pallas_call | solution.py:347
  2.7 15.1 %all_to_all.20.kv0_ref = bf16[8,2,64,384]{3,2,1,0:T(8,128)(2,1)S(1)} all-to-all(bf16[8,2,64,384]{3,2,1,0:T(8,128)(2,1)} %shard_map.85), channel_id=1, replica_groups=mesh['frame'=4,'rank'=4,'head'=2] {'rank','head'}, dimensions={0} | all-to-all | bytes 1572864 | tf_op jit(solution)/shard_map/all_to_all | solution.py:354
  17.9 0.0 copy-start.2
  17.9 3.6 %collective-permute-start.1 = (bf16[8,2,64,384]{3,2,1,0:T(8,128)(2,1)S(1)}, bf16[8,2,64,384]{3,2,1,0:T(8,128)(2,1)S(1)}, u32[]{:S(2)}, u32[]{:S(2)}) collective-permute-start(bf16[8,2,64,384]{3,2,1,0:T(8,128)(2,1)S(1)} %all_to_all.20.kv0_ref), channel_id=1, source_target_pairs={{8,16},{16,8},{9,17},{17,9},{10,18},{18,10},{11,19},{19,11},{12,20... | collective-permute-start | bytes 2359304 | tf_op jit(solution)/shard_map/ppermute | solution.py:368
  21.5 0.1 collective-permute-start
  21.5 2.1 %shard_map.84 = bf16[8,2,64,384]{3,2,1,0:T(8,128)(2,1)} custom-call(bf16[64,3072]{1,0:T(8,128)(2,1)} %a_ref.2, bf16[64,3072]{1,0:T(8,128)(2,1)} %b_ref.2), custom_call_target="tpu_custom_call" | custom-call | tf_op jit(solution)/shard_map/pallas_call | solution.py:347
  23.7 4.2 %all-to-all-start = ((bf16[8,2,64,384]{3,2,1,0:T(8,128)(2,1)}), bf16[8,2,64,384]{3,2,1,0:T(8,128)(2,1)S(1)}, u32[]{:S(2)}, u32[]{:S(2)}) async-start(bf16[8,2,64,384]{3,2,1,0:T(8,128)(2,1)} %shard_map.84), calls=%async_computation | async-start | bytes 1572864 | tf_op jit(solution)/shard_map/all_to_all | solution.py:354
  27.9 11.5 %collective-permute-done.1.kv3_ref = bf16[8,2,64,384]{3,2,1,0:T(8,128)(2,1)S(1)} collective-permute-done((bf16[8,2,64,384]{3,2,1,0:T(8,128)(2,1)S(1)}, bf16[8,2,64,384]{3,2,1,0:T(8,128)(2,1)S(1)}, u32[]{:S(2)}, u32[]{:S(2)}) %collective-permute-start.1) | collective-permute-done | bytes 786464 | tf_op jit(solution)/shard_map/ppermute | solution.py:368
  39.4 2.2 %collective-permute-start.2 = (bf16[8,2,64,384]{3,2,1,0:T(8,128)(2,1)S(1)}, bf16[8,2,64,384]{3,2,1,0:T(8,128)(2,1)}, u32[]{:S(2)}, u32[]{:S(2)}) collective-permute-start(bf16[8,2,64,384]{3,2,1,0:T(8,128)(2,1)S(1)} %collective-permute-done.1.kv3_ref), channel_id=1, source_target_pairs={{8,0},{16,24},{9,1},{17,25},{10,2},{18,26},{11,3},{19,27},{12,4},{... | collective-permute-start | bytes 2359304 | tf_op jit(solution)/shard_map/ppermute | solution.py:372
  41.6 0.0 collective-permute-done.kv1_ref
  41.6 0.0 copy-start
  41.6 3.5 %collective-permute-start.3 = (bf16[8,2,64,384]{3,2,1,0:T(8,128)(2,1)S(1)}, bf16[8,2,64,384]{3,2,1,0:T(8,128)(2,1)}, u32[]{:S(2)}, u32[]{:S(2)}) collective-permute-start(bf16[8,2,64,384]{3,2,1,0:T(8,128)(2,1)S(1)} %collective-permute-done.kv1_ref), channel_id=1, source_target_pairs={{8,16},{16,8},{9,17},{17,9},{10,18},{18,10},{11,19},{19,11},{12,20... | collective-permute-start | bytes 2359304 | tf_op jit(solution)/shard_map/ppermute | solution.py:371
  45.1 0.0 all-to-all-done.qg_ref
  45.1 0.0 copy-done.2
  45.1 5.7 %shard_map.86 = (bf16[3,1536,512]{2,1,0:T(8,128)(2,1)S(1)}, f32[3,128,512]{2,1,0:T(8,128)S(1)}, f32[3,8,512]{2,1,0:T(8,128)S(1)}) custom-call(s32[1]{0:T(128)} %bitcast.frame_ref, s32[2,4,4]{2,1,0:T(4,128)S(1)} %copy-done.2, bf16[8,2,64,384]{3,2,1,0:T(8,128)(2,1)S(1)} %all-to-all-done.qg_ref, bf16[8,2,64,384]{3,2,1,0:T(8,128)(2,1)S(1)} %all_to_all.20.kv0_ref, ...), custom_call_target="tpu_custom_call" | custom-call | flops 4026531840 | bytes 8388608 | tf_op jit(solution)/shard_map/pallas_call | solution.py:374
  50.8 0.0 copy-done
  50.8 6.4 %collective-permute-done.2.kva_ref = bf16[8,2,64,384]{3,2,1,0:T(8,128)(2,1)} collective-permute-done((bf16[8,2,64,384]{3,2,1,0:T(8,128)(2,1)S(1)}, bf16[8,2,64,384]{3,2,1,0:T(8,128)(2,1)}, u32[]{:S(2)}, u32[]{:S(2)}) %collective-permute-start.2) | collective-permute-done | bytes 786464 | tf_op jit(solution)/shard_map/ppermute | solution.py:372
  57.2 5.1 %collective-permute-done.3.kvb_ref = bf16[8,2,64,384]{3,2,1,0:T(8,128)(2,1)} collective-permute-done((bf16[8,2,64,384]{3,2,1,0:T(8,128)(2,1)S(1)}, bf16[8,2,64,384]{3,2,1,0:T(8,128)(2,1)}, u32[]{:S(2)}, u32[]{:S(2)}) %collective-permute-start.3) | collective-permute-done | bytes 786464 | tf_op jit(solution)/shard_map/ppermute | solution.py:371
  62.3 0.0 copy-start.1
  62.3 4.9 %shard_map.87 = (bf16[8,2,64,384]{3,2,1,0:T(8,128)(2,1)S(1)}, bf16[8,64,384]{2,1,0:T(8,128)(2,1)S(1)}, f32[3,8,512]{2,1,0:T(8,128)S(1)}, f32[3,128,512]{2,1,0:T(8,128)S(1)}) custom-call(s32[1]{0:T(128)} %bitcast.frame_ref, s32[2,4,4]{2,1,0:T(4,128)S(1)} %copy-done.2, bf16[8,2,64,384]{3,2,1,0:T(8,128)(2,1)S(1)} %all-to-all-done.qg_ref, ...), custom_call_target="tpu_custom_call" | custom-call | flops 4026531840 | bytes 8388608 | tf_op jit(solution)/shard_map/pallas_call | solution.py:388
  67.3 1.3 collective-permute-start.6
  68.6 3.5 %collective-permute-start.4 = (bf16[8,2,64,384]{3,2,1,0:T(8,128)(2,1)S(1)}, bf16[8,2,64,384]{3,2,1,0:T(8,128)(2,1)S(1)}, u32[]{:S(2)}, u32[]{:S(2)}) collective-permute-start(bf16[8,2,64,384]{3,2,1,0:T(8,128)(2,1)S(1)} %get-tuple-element.30), channel_id=1, source_target_pairs={{8,16},{16,8},{9,17},{17,9},{10,18},{18,10},{11,19},{19,11},{12,20... | collective-permute-start | bytes 2359304 | tf_op jit(solution)/shard_map/ppermute | solution.py:407
  72.0 0.0 copy-done.1
  72.1 7.0 %shard_map.88 = (bf16[8,2,64,384]{3,2,1,0:T(8,128)(2,1)S(1)}, bf16[8,2,64,384]{3,2,1,0:T(8,128)(2,1)S(1)}, bf16[8,2,64,384]{3,2,1,0:T(8,128)(2,1)S(1)}, bf16[8,2,64,384]{3,2,1,0:T(8,128)(2,1)}) custom-call(bf16[8,2,64,384]{3,2,1,0:T(8,128)(2,1)S(1)} %all-to-all-done.qg_ref, bf16[8,2,64,384]{3,2,1,0:T(8,128)(2,1)S(1)} %all_to_all.20.kv0_ref, ...), custom_call_target="tpu_custom_call" | custom-call | flops 4026531840 | bytes 8388608 | tf_op jit(solution)/shard_map/pallas_call | solution.py:409
  79.1 7.9 %collective-permute-done.6 = bf16[8,2,64,384]{3,2,1,0:T(8,128)(2,1)S(1)} collective-permute-done((bf16[8,2,64,384]{3,2,1,0:T(8,128)(2,1)S(1)}, bf16[8,2,64,384]{3,2,1,0:T(8,128)(2,1)S(1)}, u32[]{:S(2)}, u32[]{:S(2)}) %collective-permute-start.6) | collective-permute-done | bytes 786464 | tf_op jit(solution)/shard_map/ppermute | solution.py:406
  86.9 0.2 add_convert_fusion.1
  87.2 3.5 %collective-permute-start.7 = (bf16[8,2,64,384]{3,2,1,0:T(8,128)(2,1)S(1)}, bf16[8,2,64,384]{3,2,1,0:T(8,128)(2,1)S(1)}, u32[]{:S(2)}, u32[]{:S(2)}) collective-permute-start(bf16[8,2,64,384]{3,2,1,0:T(8,128)(2,1)S(1)} %add_convert_fusion.1), channel_id=1, source_target_pairs={{8,16},{16,8},{9,17},{17,9},{10,18},{18,10},{11,19},{19,11},{12,20... | collective-permute-start | bytes 2359304 | tf_op jit(solution)/shard_map/ppermute | solution.py:428
  90.7 0.0 collective-permute-done.4
  90.7 1.2 add_convert_fusion.2
  91.8 0.0 collective-permute-start.5
  91.8 5.0 %all-to-all-start.2 = ((bf16[8,2,64,384]{3,2,1,0:T(8,128)(2,1)}), bf16[8,2,64,384]{3,2,1,0:T(8,128)(2,1)S(1)}, u32[]{:S(2)}, u32[]{:S(2)}) async-start(bf16[8,2,64,384]{3,2,1,0:T(8,128)(2,1)} %get-tuple-element.25), calls=%async_computation.2 | async-start | bytes 1572864 | tf_op jit(solution)/shard_map/all_to_all | solution.py:354
  96.9 9.1 %collective-permute-done.7 = bf16[8,2,64,384]{3,2,1,0:T(8,128)(2,1)S(1)} collective-permute-done((bf16[8,2,64,384]{3,2,1,0:T(8,128)(2,1)S(1)}, bf16[8,2,64,384]{3,2,1,0:T(8,128)(2,1)S(1)}, u32[]{:S(2)}, u32[]{:S(2)}) %collective-permute-start.7) | collective-permute-done | bytes 786464 | tf_op jit(solution)/shard_map/ppermute | solution.py:428
  105.9 2.8 %collective-permute-done.5 = bf16[8,2,64,384]{3,2,1,0:T(8,128)(2,1)} collective-permute-done((bf16[8,2,64,384]{3,2,1,0:T(8,128)(2,1)}, bf16[8,2,64,384]{3,2,1,0:T(8,128)(2,1)}, u32[]{:S(2)}, u32[]{:S(2)}) %collective-permute-start.5) | collective-permute-done | bytes 786464 | tf_op jit(solution)/shard_map/ppermute | solution.py:429
  108.7 2.4 %add_convert_fusion = bf16[8,2,64,384]{3,2,1,0:T(8,128)(2,1)} fusion(bf16[8,2,64,384]{3,2,1,0:T(8,128)(2,1)S(1)} %collective-permute-done.7, bf16[8,2,64,384]{3,2,1,0:T(8,128)(2,1)} %collective-permute-done.5, bf16[8,2,64,384]{3,2,1,0:T(8,128)(2,1)S(1)} %get-tuple-element.28), kind=kLoop, calls=%fused_computation | loop fusion | flops 2359296 | bytes 3145728 | tf_op jit(solution)/shard_map/convert_element_type | solution.py:426
  111.2 0.0 all-to-all-done.2.in_ref
  111.2 0.0 copy-start.3
  111.2 5.3 %all-to-all-start.3 = ((bf16[8,2,64,384]{3,2,1,0:T(8,128)(2,1)}), bf16[8,2,64,384]{3,2,1,0:T(8,128)(2,1)S(1)}, u32[]{:S(2)}, u32[]{:S(2)}) async-start(bf16[8,2,64,384]{3,2,1,0:T(8,128)(2,1)} %add_convert_fusion), calls=%async_computation.3 | async-start | bytes 1572864 | tf_op jit(solution)/shard_map/all_to_all | solution.py:354
  116.5 0.0 copy-done.3
  116.5 2.1 %shard_map.89 = (bf16[64,3072]{1,0:T(8,128)(2,1)}, bf16[64,3072]{1,0:T(8,128)(2,1)}) custom-call(bf16[8,2,64,384]{3,2,1,0:T(8,128)(2,1)} %copy-done.3), custom_call_target="tpu_custom_call" | custom-call | tf_op jit(solution)/shard_map/pallas_call | solution.py:351
  118.6 8.9 %all-to-all-done.3.in_ref = bf16[8,2,64,384]{3,2,1,0:T(8,128)(2,1)S(1)} async-done(((bf16[8,2,64,384]{3,2,1,0:T(8,128)(2,1)}), bf16[8,2,64,384]{3,2,1,0:T(8,128)(2,1)S(1)}, u32[]{:S(2)}, u32[]{:S(2)}) %all-to-all-start.3) | async-done | bytes 786464 | tf_op jit(solution)/shard_map/all_to_all | solution.py:354
  127.5 0.0 copy-start.4
  127.5 0.9 copy-done.4
  128.4 2.1 %shard_map.90 = (bf16[64,3072]{1,0:T(8,128)(2,1)}, bf16[64,3072]{1,0:T(8,128)(2,1)}) custom-call(bf16[8,2,64,384]{3,2,1,0:T(8,128)(2,1)} %copy-done.4), custom_call_target="tpu_custom_call" | custom-call | tf_op jit(solution)/shard_map/pallas_call | solution.py:351
Async XLA Ops:
  17.9 27.3 %copy-start.2 = (s32[2,4,4]{2,1,0:T(4,128)S(1)}, s32[2,4,4]{2,1,0:T(4,128)}, u32[]{:S(2)}) copy-start(s32[2,4,4]{2,1,0:T(4,128)} %mask_ref.3) | copy-start | bytes 388
  17.9 21.6 %collective-permute-start.1 = (bf16[8,2,64,384]{3,2,1,0:T(8,128)(2,1)S(1)}, bf16[8,2,64,384]{3,2,1,0:T(8,128)(2,1)S(1)}, u32[]{:S(2)}, u32[]{:S(2)}) collective-permute-start(bf16[8,2,64,384]{3,2,1,0:T(8,128)(2,1)S(1)} %all_to_all.20.kv0_ref), channel_id=1, source_target_pairs={{8,16},{16,8},{9,17},{17,9},{10,18},{18,10},{11,19},{19,11},{12,20... | collective-permute-start | bytes 2359304 | tf_op jit(solution)/shard_map/ppermute | solution.py:368
  21.5 20.1 %collective-permute-start = (bf16[8,2,64,384]{3,2,1,0:T(8,128)(2,1)S(1)}, bf16[8,2,64,384]{3,2,1,0:T(8,128)(2,1)S(1)}, u32[]{:S(2)}, u32[]{:S(2)}) collective-permute-start(bf16[8,2,64,384]{3,2,1,0:T(8,128)(2,1)S(1)} %all_to_all.20.kv0_ref), channel_id=1, source_target_pairs={{0,8},{8,0},{16,24},{24,16},{1,9},{9,1},{17,25},{25,17},{2,10},{10... | collective-permute-start | bytes 2359304 | tf_op jit(solution)/shard_map/ppermute | solution.py:369
  23.7 21.4 %all-to-all-start = ((bf16[8,2,64,384]{3,2,1,0:T(8,128)(2,1)}), bf16[8,2,64,384]{3,2,1,0:T(8,128)(2,1)S(1)}, u32[]{:S(2)}, u32[]{:S(2)}) async-start(bf16[8,2,64,384]{3,2,1,0:T(8,128)(2,1)} %shard_map.84), calls=%async_computation | async-start | bytes 1572864 | tf_op jit(solution)/shard_map/all_to_all | solution.py:354
  39.4 17.8 %collective-permute-start.2 = (bf16[8,2,64,384]{3,2,1,0:T(8,128)(2,1)S(1)}, bf16[8,2,64,384]{3,2,1,0:T(8,128)(2,1)}, u32[]{:S(2)}, u32[]{:S(2)}) collective-permute-start(bf16[8,2,64,384]{3,2,1,0:T(8,128)(2,1)S(1)} %collective-permute-done.1.kv3_ref), channel_id=1, source_target_pairs={{8,0},{16,24},{9,1},{17,25},{10,2},{18,26},{11,3},{19,27},{12,4},{... | collective-permute-start | bytes 2359304 | tf_op jit(solution)/shard_map/ppermute | solution.py:372
  41.6 9.2 %copy-start = (bf16[8,2,64,384]{3,2,1,0:T(8,128)(2,1)}, bf16[8,2,64,384]{3,2,1,0:T(8,128)(2,1)S(1)}, u32[]{:S(2)}) copy-start(bf16[8,2,64,384]{3,2,1,0:T(8,128)(2,1)S(1)} %collective-permute-done.kv1_ref) | copy-start | bytes 2359300
  41.6 20.7 %collective-permute-start.3 = (bf16[8,2,64,384]{3,2,1,0:T(8,128)(2,1)S(1)}, bf16[8,2,64,384]{3,2,1,0:T(8,128)(2,1)}, u32[]{:S(2)}, u32[]{:S(2)}) collective-permute-start(bf16[8,2,64,384]{3,2,1,0:T(8,128)(2,1)S(1)} %collective-permute-done.kv1_ref), channel_id=1, source_target_pairs={{8,16},{16,8},{9,17},{17,9},{10,18},{18,10},{11,19},{19,11},{12,20... | collective-permute-start | bytes 2359304 | tf_op jit(solution)/shard_map/ppermute | solution.py:371
  62.3 9.7 %copy-start.1 = (bf16[8,2,64,384]{3,2,1,0:T(8,128)(2,1)S(1)}, bf16[8,2,64,384]{3,2,1,0:T(8,128)(2,1)}, u32[]{:S(2)}) copy-start(bf16[8,2,64,384]{3,2,1,0:T(8,128)(2,1)} %copy-done) | copy-start | bytes 2359300
  67.3 19.7 %collective-permute-start.6 = (bf16[8,2,64,384]{3,2,1,0:T(8,128)(2,1)S(1)}, bf16[8,2,64,384]{3,2,1,0:T(8,128)(2,1)S(1)}, u32[]{:S(2)}, u32[]{:S(2)}) collective-permute-start(bf16[8,2,64,384]{3,2,1,0:T(8,128)(2,1)S(1)} %get-tuple-element.30), channel_id=1, source_target_pairs={{0,8},{24,16},{1,9},{25,17},{2,10},{26,18},{3,11},{27,19},{4,12},{... | collective-permute-start | bytes 2359304 | tf_op jit(solution)/shard_map/ppermute | solution.py:406
  68.6 22.1 %collective-permute-start.4 = (bf16[8,2,64,384]{3,2,1,0:T(8,128)(2,1)S(1)}, bf16[8,2,64,384]{3,2,1,0:T(8,128)(2,1)S(1)}, u32[]{:S(2)}, u32[]{:S(2)}) collective-permute-start(bf16[8,2,64,384]{3,2,1,0:T(8,128)(2,1)S(1)} %get-tuple-element.30), channel_id=1, source_target_pairs={{8,16},{16,8},{9,17},{17,9},{10,18},{18,10},{11,19},{19,11},{12,20... | collective-permute-start | bytes 2359304 | tf_op jit(solution)/shard_map/ppermute | solution.py:407
  87.2 18.8 %collective-permute-start.7 = (bf16[8,2,64,384]{3,2,1,0:T(8,128)(2,1)S(1)}, bf16[8,2,64,384]{3,2,1,0:T(8,128)(2,1)S(1)}, u32[]{:S(2)}, u32[]{:S(2)}) collective-permute-start(bf16[8,2,64,384]{3,2,1,0:T(8,128)(2,1)S(1)} %add_convert_fusion.1), channel_id=1, source_target_pairs={{8,16},{16,8},{9,17},{17,9},{10,18},{18,10},{11,19},{19,11},{12,20... | collective-permute-start | bytes 2359304 | tf_op jit(solution)/shard_map/ppermute | solution.py:428
  91.8 16.9 %collective-permute-start.5 = (bf16[8,2,64,384]{3,2,1,0:T(8,128)(2,1)}, bf16[8,2,64,384]{3,2,1,0:T(8,128)(2,1)}, u32[]{:S(2)}, u32[]{:S(2)}) collective-permute-start(bf16[8,2,64,384]{3,2,1,0:T(8,128)(2,1)} %add_convert_fusion.2), channel_id=1, source_target_pairs={{0,8},{8,0},{16,24},{24,16},{1,9},{9,1},{17,25},{25,17},{2,10},{10... | collective-permute-start | bytes 2359304 | tf_op jit(solution)/shard_map/ppermute | solution.py:429
  91.8 19.3 %all-to-all-start.2 = ((bf16[8,2,64,384]{3,2,1,0:T(8,128)(2,1)}), bf16[8,2,64,384]{3,2,1,0:T(8,128)(2,1)S(1)}, u32[]{:S(2)}, u32[]{:S(2)}) async-start(bf16[8,2,64,384]{3,2,1,0:T(8,128)(2,1)} %get-tuple-element.25), calls=%async_computation.2 | async-start | bytes 1572864 | tf_op jit(solution)/shard_map/all_to_all | solution.py:354
  111.2 5.3 %copy-start.3 = (bf16[8,2,64,384]{3,2,1,0:T(8,128)(2,1)}, bf16[8,2,64,384]{3,2,1,0:T(8,128)(2,1)S(1)}, u32[]{:S(2)}) copy-start(bf16[8,2,64,384]{3,2,1,0:T(8,128)(2,1)S(1)} %all-to-all-done.2.in_ref) | copy-start | bytes 2359300
  111.2 16.4 %all-to-all-start.3 = ((bf16[8,2,64,384]{3,2,1,0:T(8,128)(2,1)}), bf16[8,2,64,384]{3,2,1,0:T(8,128)(2,1)S(1)}, u32[]{:S(2)}, u32[]{:S(2)}) async-start(bf16[8,2,64,384]{3,2,1,0:T(8,128)(2,1)} %add_convert_fusion), calls=%async_computation.3 | async-start | bytes 1572864 | tf_op jit(solution)/shard_map/all_to_all | solution.py:354
  127.5 0.9 copy-start.4

commit v2 on v1

--- a/solution.py
+++ b/solution.py
@@ -193,6 +193,14 @@
     return part.reshape(part.shape[0] * part.shape[1], part.shape[2])
 
 
+def flat(ref):
+    return ref[...].reshape(ref.shape[0] * ref.shape[1], ref.shape[2])
+
+
+def put(ref, rows):
+    ref[...] = rows.reshape(ref.shape)
+
+
 def put_rows(ref, which, rows):
     ref[:, which] = rows.reshape(ref.shape[0], ref.shape[2], ref.shape[3])
 
@@ -220,108 +228,168 @@
     )
 
 
-def near_forward_kernel(frame_ref, mask_ref, qg_ref, kv0_ref, kv1_ref, kv3_ref, e_ref, acc_ref, ml_ref):
+def near_scores_kernel(frame_ref, mask_ref, qg_ref, k0_ref, k1_ref, k3_ref, e_ref, ml_ref):
     tokens = e_ref.shape[2]
     blocks = tokens // BLOCK
     frame = frame_ref[0]
     inner = (frame == 1) | (frame == 2)
     queries = rows_of(qg_ref, 0)
     slots = (
-        (kv0_ref, None),
-        (kv1_ref, bias_rows(mask_ref, 0, frame >= 0, blocks)),
-        (kv3_ref, bias_rows(mask_ref, 0, inner, blocks)),
+        (k0_ref, None),
+        (k1_ref, bias_rows(mask_ref, 0, frame >= 0, blocks)),
+        (k3_ref, bias_rows(mask_ref, 0, inner, blocks)),
     )
-    scores = [masked_scores(rows_of(ref, 0), queries, bias) for ref, bias in slots]
+    scores = [masked_scores(flat(ref), queries, bias) for ref, bias in slots]
     peak = scores[0].max(axis=0, keepdims=True)
     for score in scores[1:]:
         peak = jnp.maximum(peak, score.max(axis=0, keepdims=True))
     total = jnp.zeros((1, tokens), F32)
-    acc = jnp.zeros((HD, tokens), F32)
-    for index, (ref, _) in enumerate(slots):
-        e = jnp.exp2(scores[index] - peak)
+    for index, score in enumerate(scores):
+        e = jnp.exp2(score - peak)
         total = total + e.sum(axis=0, keepdims=True)
-        e = e.astype(BF16)
-        e_ref[0, index * tokens : (index + 1) * tokens] = e
-        acc = acc + dot(rows_of(ref, 1).T, e)
-    acc_ref[0] = acc
+        e_ref[0, index * tokens : (index + 1) * tokens] = e.astype(BF16)
     ml_ref[0, 0:1] = peak
     ml_ref[0, 1:2] = total
 
 
-def far_kernel(
-    frame_ref, mask_ref, qg_ref, kva_ref, kvb_ref, acc_ref, ml_ref,
-    dkv_ref, att_ref, wd_ref, dq_ref,
-):
-    tokens = acc_ref.shape[2]
+def far_scores_kernel(frame_ref, mask_ref, qg_ref, ka_ref, kb_ref, ml_ref, e_ref, w_ref, dv_ref):
+    tokens = e_ref.shape[2]
     blocks = tokens // BLOCK
     frame = frame_ref[0]
     inner = (frame == 1) | (frame == 2)
-    queries = rows_of(qg_ref, 0)
-    keys = jnp.where(inner, rows_of(kvb_ref, 0), rows_of(kva_ref, 0))
-    values = jnp.where(inner, rows_of(kvb_ref, 1), rows_of(kva_ref, 1))
-    scores = masked_scores(keys, queries, bias_rows(mask_ref, 1, frame >= 0, blocks))
+    keys = jnp.where(inner, flat(kb_ref), flat(ka_ref))
+    bias = bias_rows(mask_ref, 1, frame >= 0, blocks)
+    scores = masked_scores(keys, rows_of(qg_ref, 0), bias)
     peak2 = scores.max(axis=0, keepdims=True)
     e = jnp.exp2(scores - peak2)
     total2 = e.sum(axis=0, keepdims=True)
     e = e.astype(BF16)
-    acc2 = dot(values.T, e)
     peak1 = ml_ref[0, 0:1]
     peak = jnp.maximum(peak1, peak2)
     near = jnp.exp2(peak1 - peak)
     far = jnp.exp2(peak2 - peak)
     inv = 1.0 / (near * ml_ref[0, 1:2] + far * total2)
-    near = near * inv
     far = far * inv
-    out = (acc_ref[0] * near + acc2 * far).astype(BF16)
-    att = out.T
-    att_ref[...] = att.reshape(att_ref.shape)
+    scaled = (rows_of(qg_ref, 1).T.astype(F32) * far).astype(BF16)
+    put(dv_ref, dot_nt(e, scaled).astype(BF16))
+    e_ref[0] = e
+    w_ref[0, 0:1] = near * inv
+    w_ref[0, 1:2] = far
+
+
+def near_values_kernel(qg_ref, e_ref, w_ref, v0_ref, v1_ref, v3_ref, dv0_ref, dv1_ref, dv3_ref, acc_ref):
+    tokens = e_ref.shape[2]
+    scaled = (rows_of(qg_ref, 1).T.astype(F32) * w_ref[0, 0:1]).astype(BF16)
+    acc = jnp.zeros(acc_ref.shape[1:], F32)
+    for index, (v_ref, dv_ref) in enumerate(
+        ((v0_ref, dv0_ref), (v1_ref, dv1_ref), (v3_ref, dv3_ref))
+    ):
+        e = e_ref[0, index * tokens : (index + 1) * tokens]
+        put(dv_ref, dot_nt(e, scaled).astype(BF16))
+        acc = acc + dot(flat(v_ref).T, e)
+    acc_ref[0] = acc
+
+
+def far_values_kernel(
+    frame_ref, qg_ref, ka_ref, kb_ref, va_ref, vb_ref, e_ref, w_ref, acc_ref,
+    dk_ref, att_ref, delta_ref, dq_ref,
+):
+    frame = frame_ref[0]
+    inner = (frame == 1) | (frame == 2)
+    keys = jnp.where(inner, flat(kb_ref), flat(ka_ref))
+    values = jnp.where(inner, flat(vb_ref), flat(va_ref))
+    e = e_ref[0]
+    near = w_ref[0, 0:1]
+    far = w_ref[0, 1:2]
+    out = (acc_ref[0] * near + dot(values.T, e) * far).astype(BF16)
+    put(att_ref, out.T)
     grads = rows_of(qg_ref, 1).T.astype(F32)
     delta = (grads * out.astype(F32)).sum(axis=0, keepdims=True)
-    wd_ref[0, 0:1] = near
-    wd_ref[0, 1:2] = near * delta
+    delta_ref[0, 0:1] = near
+    delta_ref[0, 1:2] = near * delta
     scaled = (grads * far).astype(BF16)
     ds = (e.astype(F32) * (dot(values, scaled) - far * delta)).astype(BF16)
-    put_rows(dkv_ref, 0, (dot(ds, queries) * SCALE).astype(BF16))
-    put_rows(dkv_ref, 1, dot_nt(e, scaled).astype(BF16))
+    put(dk_ref, (dot(ds, rows_of(qg_ref, 0)) * SCALE).astype(BF16))
     dq_ref[0] = dot(keys.T, ds)
 
 
-def near_backward_kernel(
-    qg_ref, kv0_ref, kv1_ref, kv3_ref, e_ref, wd_ref, dq2_ref, att_ref,
-    dkv0_ref, dkv1_ref, dkv3_ref, out_ref,
+def near_keys_kernel(
+    qg_ref, k0_ref, k1_ref, k3_ref, v0_ref, v1_ref, v3_ref, e_ref, delta_ref, dq2_ref, att_ref,
+    dk0_ref, dk1_ref, dk3_ref, out_ref,
 ):
     tokens = e_ref.shape[2]
     queries = rows_of(qg_ref, 0)
-    grads = rows_of(qg_ref, 1).T.astype(F32)
-    near = wd_ref[0, 0:1]
-    delta = wd_ref[0, 1:2]
-    scaled = (grads * near).astype(BF16)
+    near = delta_ref[0, 0:1]
+    delta = delta_ref[0, 1:2]
+    scaled = (rows_of(qg_ref, 1).T.astype(F32) * near).astype(BF16)
     dq = dq2_ref[0]
-    for index, (kv_ref, dkv_ref) in enumerate(
-        ((kv0_ref, dkv0_ref), (kv1_ref, dkv1_ref), (kv3_ref, dkv3_ref))
+    for index, (k_ref, v_ref, dk_ref) in enumerate(
+        ((k0_ref, v0_ref, dk0_ref), (k1_ref, v1_ref, dk1_ref), (k3_ref, v3_ref, dk3_ref))
     ):
         e = e_ref[0, index * tokens : (index + 1) * tokens]
-        keys = rows_of(kv_ref, 0)
-        ds = (e.astype(F32) * (dot(rows_of(kv_ref, 1), scaled) - delta)).astype(BF16)
-        put_rows(dkv_ref, 0, (dot(ds, queries) * SCALE).astype(BF16))
-        put_rows(dkv_ref, 1, dot_nt(e, scaled).astype(BF16))
-        dq = dq + dot(keys.T, ds)
+        ds = (e.astype(F32) * (dot(flat(v_ref), scaled) - delta)).astype(BF16)
+        put(dk_ref, (dot(ds, queries) * SCALE).astype(BF16))
+        dq = dq + dot(flat(k_ref).T, ds)
     put_rows(out_ref, 1, (dq * SCALE).astype(BF16).T)
     out_ref[:, 0] = att_ref[...]
 
 
-def pack_kernel(a_ref, b_ref, out_ref):
-    width = out_ref.shape[3]
-    for peer in range(out_ref.shape[0]):
-        out_ref[peer, 0] = a_ref[:, peer * width : (peer + 1) * width]
-        out_ref[peer, 1] = b_ref[:, peer * width : (peer + 1) * width]
-
-
-def unpack_kernel(in_ref, a_ref, b_ref):
-    width = in_ref.shape[3]
-    for peer in range(in_ref.shape[0]):
-        a_ref[:, peer * width : (peer + 1) * width] = in_ref[peer, 0]
-        b_ref[:, peer * width : (peer + 1) * width] = in_ref[peer, 1]
+def pack_kernel(in_ref, out_ref, sems):
+    peers, _, width = out_ref.shape
+    copies = [
+        pltpu.make_async_copy(
+            in_ref.at[:, peer * width : (peer + 1) * width], out_ref.at[peer], sems.at[peer]
+        )
+        for peer in range(peers)
+    ]
+    for copy in copies:
+        copy.start()
+    for copy in copies:
+        copy.wait()
+
+
+def pack_pair_kernel(a_ref, b_ref, out_ref, sems):
+    peers, _, _, width = out_ref.shape
+    copies = [
+        pltpu.make_async_copy(
+            ref.at[:, peer * width : (peer + 1) * width], out_ref.at[peer, which], sems.at[peer, which]
+        )
+        for peer in range(peers)
+        for which, ref in enumerate((a_ref, b_ref))
+    ]
+    for copy in copies:
+        copy.start()
+    for copy in copies:
+        copy.wait()
+
+
+def unpack_kernel(in_ref, out_ref, sems):
+    peers, _, width = in_ref.shape
+    copies = [
+        pltpu.make_async_copy(
+            in_ref.at[peer], out_ref.at[:, peer * width : (peer + 1) * width], sems.at[peer]
+        )
+        for peer in range(peers)
+    ]
+    for copy in copies:
+        copy.start()
+    for copy in copies:
+        copy.wait()
+
+
+def unpack_pair_kernel(in_ref, a_ref, b_ref, sems):
+    peers, _, _, width = in_ref.shape
+    copies = [
+        pltpu.make_async_copy(
+            in_ref.at[peer, which], ref.at[:, peer * width : (peer + 1) * width], sems.at[peer, which]
+        )
+        for peer in range(peers)
+        for which, ref in enumerate((a_ref, b_ref))
+    ]
+    for copy in copies:
+        copy.start()
+    for copy in copies:
+        copy.wait()
 
 
 def params():
@@ -339,16 +407,33 @@
     width = columns // peers
     heads = width // HD
     tokens = peers * rows
-    pair_shape = (peers, 2, rows, width)
-    pair_type = jax.ShapeDtypeStruct(pair_shape, BF16)
+    pair_type = jax.ShapeDtypeStruct((peers, 2, rows, width), BF16)
+    one_type = jax.ShapeDtypeStruct((peers, rows, width), BF16)
+    row_type = jax.ShapeDtypeStruct((rows, columns), BF16)
     frame = lax.axis_index("frame").astype(jnp.int32).reshape(1)
-
-    def pack(a, b):
-        return pl.pallas_call(pack_kernel, out_shape=pair_type)(a, b)
-
-    def unpack(pair):
-        row_type = jax.ShapeDtypeStruct((rows, columns), BF16)
-        return pl.pallas_call(unpack_kernel, out_shape=(row_type, row_type))(pair)
+    anywhere = pl.BlockSpec(memory_space=pl.ANY)
+
+    def moved(kernel, out_shape, sems, *operands):
+        several = isinstance(out_shape, tuple)
+        return pl.pallas_call(
+            kernel,
+            in_specs=[anywhere] * len(operands),
+            out_specs=(anywhere,) * len(out_shape) if several else anywhere,
+            out_shape=out_shape,
+            scratch_shapes=[pltpu.SemaphoreType.DMA(sems)],
+        )(*operands)
+
+    def pack(rows_):
+        return moved(pack_kernel, one_type, (peers,), rows_)
+
+    def pack_pair(a, b):
+        return moved(pack_pair_kernel, pair_type, (peers, 2), a, b)
+
+    def unpack(one):
+        return moved(unpack_kernel, row_type, (peers,), one)
+
+    def unpack_pair(pair):
+        return moved(unpack_pair_kernel, (row_type, row_type), (peers, 2), pair)
 
     def swap(pair):
         return lax.all_to_all(pair, plane, 0, 0, tiled=True)
@@ -360,75 +445,89 @@
     def head_spec(*shape):
         return pl.BlockSpec((1,) + shape, lambda h: (h, 0, 0))
 
+    def head_type(dtype, *shape):
+        return jax.ShapeDtypeStruct((heads,) + shape, dtype)
+
+    near_spec, near_type = head_spec(3 * tokens, tokens), head_type(BF16, 3 * tokens, tokens)
+    far_spec, far_type = head_spec(tokens, tokens), head_type(BF16, tokens, tokens)
+    stat_spec, stat_type = head_spec(8, tokens), head_type(F32, 8, tokens)
+    acc_spec, acc_type = head_spec(HD, tokens), head_type(F32, HD, tokens)
     pair_flops = heads * 2 * tokens * tokens * HD
 
-    kv0 = swap(pack(key_rows, value_rows))
+    def by_head(kernel, in_specs, outs, work):
+        return pl.pallas_call(
+            kernel,
+            grid=(heads,),
+            in_specs=in_specs,
+            out_specs=[spec for spec, _ in outs],
+            out_shape=[kind for _, kind in outs],
+            compiler_params=params(),
+            cost_estimate=cost(work * pair_flops, 4 << 20),
+        )
+
     edge = [(0, 1), (1, 0), (2, 3), (3, 2)]
+    inward = [(0, 1), (3, 2)]
+    outward = [(1, 0), (2, 3)]
     middle = [(1, 2), (2, 1)]
-    kv3 = lax.ppermute(kv0, "frame", middle)
-    kv1 = lax.ppermute(kv0, "frame", edge)
-    qg = swap(pack(query_rows, out_grad))
-    kv2b = lax.ppermute(kv1, "frame", middle)
-    kv2a = lax.ppermute(kv3, "frame", [(1, 0), (2, 3)])
-
-    e, acc, ml = pl.pallas_call(
-        near_forward_kernel,
-        grid=(heads,),
-        in_specs=[smem, smem, pair_spec, pair_spec, pair_spec, pair_spec],
-        out_specs=[head_spec(3 * tokens, tokens), head_spec(HD, tokens), head_spec(8, tokens)],
-        out_shape=[
-            jax.ShapeDtypeStruct((heads, 3 * tokens, tokens), BF16),
-            jax.ShapeDtypeStruct((heads, HD, tokens), F32),
-            jax.ShapeDtypeStruct((heads, 8, tokens), F32),
-        ],
-        compiler_params=params(),
-        cost_estimate=cost(20 * pair_flops, 8 << 20),
-    )(frame, block_mask, qg, kv0, kv1, kv3)
-
-    dkv2, att, wd, dq2 = pl.pallas_call(
-        far_kernel,
-        grid=(heads,),
-        in_specs=[
-            smem, smem, pair_spec, pair_spec, pair_spec,
-            head_spec(HD, tokens), head_spec(8, tokens),
-        ],
-        out_specs=[pair_spec, one_spec, head_spec(8, tokens), head_spec(HD, tokens)],
-        out_shape=[
-            pair_type,
-            jax.ShapeDtypeStruct((peers, rows, width), BF16),
-            jax.ShapeDtypeStruct((heads, 8, tokens), F32),
-            jax.ShapeDtypeStruct((heads, HD, tokens), F32),
-        ],
-        compiler_params=params(),
-        cost_estimate=cost(20 * pair_flops, 8 << 20),
-    )(frame, block_mask, qg, kv2a, kv2b, acc, ml)
-
-    back_edge = lax.ppermute(dkv2, "frame", [(0, 1), (3, 2)])
-    back_middle = lax.ppermute(dkv2, "frame", middle)
-
-    dkv0, dkv1, dkv3, att_dq = pl.pallas_call(
-        near_backward_kernel,
-        grid=(heads,),
-        in_specs=[
-            pair_spec, pair_spec, pair_spec, pair_spec,
-            head_spec(3 * tokens, tokens), head_spec(8, tokens), head_spec(HD, tokens), one_spec,
-        ],
-        out_specs=[pair_spec] * 4,
-        out_shape=[pair_type] * 4,
-        compiler_params=params(),
-        cost_estimate=cost(20 * pair_flops, 8 << 20),
-    )(qg, kv0, kv1, kv3, e, wd, dq2, att)
-
-    def added(*pairs):
-        total = pairs[0].astype(F32)
-        for pair in pairs[1:]:
-            total = total + pair.astype(F32)
+
+    def send(array, pairs):
+        return lax.ppermute(array, "frame", pairs)
+
+    k0 = swap(pack(key_rows))
+    k1, k3 = send(k0, edge), send(k0, middle)
+    qg = swap(pack_pair(query_rows, out_grad))
+    v0 = swap(pack(value_rows))
+    v1, v3 = send(v0, edge), send(v0, middle)
+    k2a, k2b = send(k3, outward), send(k1, middle)
+
+    e_near, ml = by_head(
+        near_scores_kernel,
+        [smem, smem, pair_spec, one_spec, one_spec, one_spec],
+        [(near_spec, near_type), (stat_spec, stat_type)],
+        6,
+    )(frame, block_mask, qg, k0, k1, k3)
+    v2a, v2b = send(v3, outward), send(v1, middle)
+    e_far, w, dv2 = by_head(
+        far_scores_kernel,
+        [smem, smem, pair_spec, one_spec, one_spec, stat_spec],
+        [(far_spec, far_type), (stat_spec, stat_type), (one_spec, one_type)],
+        6,
+    )(frame, block_mask, qg, k2a, k2b, ml)
+    dv_edge, dv_middle = send(dv2, inward), send(dv2, middle)
+    dv0, dv1, dv3, acc = by_head(
+        near_values_kernel,
+        [pair_spec, near_spec, stat_spec, one_spec, one_spec, one_spec],
+        [(one_spec, one_type)] * 3 + [(acc_spec, acc_type)],
+        6,
+    )(qg, e_near, w, v0, v1, v3)
+    dk2, att, delta, dq2 = by_head(
+        far_values_kernel,
+        [smem, pair_spec] + [one_spec] * 4 + [far_spec, stat_spec, acc_spec],
+        [(one_spec, one_type), (one_spec, one_type), (stat_spec, stat_type), (acc_spec, acc_type)],
+        6,
+    )(frame, qg, k2a, k2b, v2a, v2b, e_far, w, acc)
+    dk_edge, dk_middle = send(dk2, inward), send(dk2, middle)
+    dk0, dk1, dk3, att_dq = by_head(
+        near_keys_kernel,
+        [pair_spec] + [one_spec] * 6 + [near_spec, stat_spec, acc_spec, one_spec],
+        [(one_spec, one_type)] * 3 + [(pair_spec, pair_type)],
+        9,
+    )(qg, k0, k1, k3, v0, v1, v3, e_near, delta, dq2, att)
+
+    def added(*parts):
+        total = parts[0].astype(F32)
+        for part in parts[1:]:
+            total = total + part.astype(F32)
         return total.astype(BF16)
 
-    last_middle = lax.ppermute(added(dkv3, back_edge), "frame", middle)
-    last_edge = lax.ppermute(added(dkv1, back_middle), "frame", edge)
-    attended, grad_query = unpack(swap(att_dq))
-    grad_keys, grad_values = unpack(swap(added(dkv0, last_edge, last_middle)))
+    def last_round(own, first, third, from_edge, from_middle):
+        over_middle = send(added(third, from_edge), middle)
+        over_edge = send(added(first, from_middle), edge)
+        return unpack(swap(added(own, over_edge, over_middle)))
+
+    grad_values = last_round(dv0, dv1, dv3, dv_edge, dv_middle)
+    attended, grad_query = unpack_pair(swap(att_dq))
+    grad_keys = last_round(dk0, dk1, dk3, dk_edge, dk_middle)
     return attended, grad_query, grad_keys, grad_values
 
 

time: 133 us -> 218 us (1.64)
  Pallas kernels: 26 us -> 125 us
  waiting for transfers between devices: 51.7 us -> 22.4 us
  starting transfers between devices: 32.2 us -> 59.2 us
  blocking collectives: 15.1 us -> 0 us
  other arithmetic: 3.8 us -> 7.27 us
    pallas_call x7 -> x11, Pallas kernels: 26 us -> 125 us  [the longest x6 102 us: moved(): pl.pallas_call(kernel, in_specs=[anywhere] * len(operands), out_specs=(an...]
    ppermute x8 -> x16, waiting for transfers between devices: 42.8 us -> 18.6 us  [send(): return lax.ppermute(array, 'frame', pairs)]
    ppermute x8 -> x16, starting transfers between devices: 17.6 us -> 34 us  [send(): return lax.ppermute(array, 'frame', pairs)]
    all_to_all x1 -> x0, blocking collectives: 15.1 us -> none  [swap(): return lax.all_to_all(pair, plane, 0, 0, tiled=True)]
    all_to_all x3 -> x6, starting transfers between devices: 14.6 us -> 25.2 us  [swap(): return lax.all_to_all(pair, plane, 0, 0, tiled=True)]
    all_to_all x3 -> x6, waiting for transfers between devices: 8.95 us -> 3.73 us  [swap(): return lax.all_to_all(pair, plane, 0, 0, tiled=True)]
    convert_element_type x3 -> x6, other arithmetic: 3.8 us -> 7.27 us  [added(): return total.astype(BF16)]
  transfers between devices with their start and end apart: 11 -> 22, of which waited for: 7 -> 6; matrix products, arithmetic and copies ran while one was open for 3% -> 3% of each run, Pallas kernels for 13% -> 46%
where the time goes in v2:
time: 218 us; the launch traced here: 217 us
  Pallas kernels  125 us (57%)
  starting transfers between devices  59.2 us (27%)
  waiting for transfers between devices  22.4 us (10%)
  other arithmetic  7.27 us (3%)
  local copies, waits for them, and re-layouts  2.26 us (1%)
    pallas_call x6, Pallas kernels, moved(): pl.pallas_call(kernel, in_specs=[anywhere] * len(operands), out_specs=(an...  102 us
    ppermute x16, starting transfers between devices, send(): return lax.ppermute(array, 'frame', pairs)  34 us
    all_to_all x6, starting transfers between devices, swap(): return lax.all_to_all(pair, plane, 0, 0, tiled=True)  25.2 us
    ppermute x16, waiting for transfers between devices, send(): return lax.ppermute(array, 'frame', pairs)  18.6 us
    convert_element_type x6, other arithmetic, added(): return total.astype(BF16)  7.27 us
    pallas_call x1, Pallas kernels, per_device_line(): by_head(near_keys_kernel, [pair_spec] + [one_spec] * 6 + [near_spec, stat...  5.55 us
    pallas_call x1, Pallas kernels, per_device_line(): by_head(far_scores_kernel, [smem, smem, pair_spec, one_spec, one_spec, st...  4.78 us
    pallas_call x1, Pallas kernels, per_device_line(): by_head(far_values_kernel, [smem, pair_spec] + [one_spec] * 4 + [far_spec...  4.67 us
  transfers between devices with their start and end apart: 22, of which 6 were waited for; matrix products, arithmetic and copies ran while one was open for 3% of the time, Pallas kernels for 46%

profile of v2, /device:TPU:10, one launch (start us, length us, event | category | flops | bytes accessed | tf_op | source)
XLA Modules:
  0.0 217.0 jit_solution(4197489691519723607)
XLA Ops:
  0.6 13.1 %shard_map.85 = bf16[8,64,384]{2,1,0:T(8,128)(2,1)} custom-call(bf16[64,3072]{1,0:T(8,128)(2,1)} %in_ref.2), custom_call_target="tpu_custom_call" | custom-call | tf_op jit(solution)/shard_map/pallas_call | solution.py:418
  13.7 4.3 %all-to-all-start.1 = ((bf16[8,64,384]{2,1,0:T(8,128)(2,1)}), bf16[8,64,384]{2,1,0:T(8,128)(2,1)S(1)}, u32[]{:S(2)}, u32[]{:S(2)}) async-start(bf16[8,64,384]{2,1,0:T(8,128)(2,1)} %shard_map.85), calls=%async_computation.1 | async-start | bytes 786432 | tf_op jit(solution)/shard_map/all_to_all | solution.py:439
  18.0 13.1 %shard_map.86 = bf16[8,64,384]{2,1,0:T(8,128)(2,1)} custom-call(bf16[64,3072]{1,0:T(8,128)(2,1)} %in_ref.3), custom_call_target="tpu_custom_call" | custom-call | tf_op jit(solution)/shard_map/pallas_call | solution.py:418
  31.1 0.0 all-to-all-done.1.k0_ref
  31.1 4.2 %all-to-all-start.2 = ((bf16[8,64,384]{2,1,0:T(8,128)(2,1)}), bf16[8,64,384]{2,1,0:T(8,128)(2,1)S(1)}, u32[]{:S(2)}, u32[]{:S(2)}) async-start(bf16[8,64,384]{2,1,0:T(8,128)(2,1)} %shard_map.86), calls=%async_computation.2 | async-start | bytes 786432 | tf_op jit(solution)/shard_map/all_to_all | solution.py:439
  35.3 25.1 %shard_map.84 = bf16[8,2,64,384]{3,2,1,0:T(8,128)(2,1)} custom-call(bf16[64,3072]{1,0:T(8,128)(2,1)} %a_ref.1, bf16[64,3072]{1,0:T(8,128)(2,1)} %b_ref.1), custom_call_target="tpu_custom_call" | custom-call | tf_op jit(solution)/shard_map/pallas_call | solution.py:418
  60.4 0.0 all-to-all-done.2.v0_ref
  60.4 4.2 %all-to-all-start = ((bf16[8,2,64,384]{3,2,1,0:T(8,128)(2,1)}), bf16[8,2,64,384]{3,2,1,0:T(8,128)(2,1)S(1)}, u32[]{:S(2)}, u32[]{:S(2)}) async-start(bf16[8,2,64,384]{3,2,1,0:T(8,128)(2,1)} %shard_map.84), calls=%async_computation | async-start | bytes 1572864 | tf_op jit(solution)/shard_map/all_to_all | solution.py:439
  64.6 3.5 %collective-permute-start.1 = (bf16[8,64,384]{2,1,0:T(8,128)(2,1)S(1)}, bf16[8,64,384]{2,1,0:T(8,128)(2,1)S(1)}, u32[]{:S(2)}, u32[]{:S(2)}) collective-permute-start(bf16[8,64,384]{2,1,0:T(8,128)(2,1)S(1)} %all-to-all-done.1.k0_ref), channel_id=1, source_target_pairs={{8,16},{16,8},{9,17},{17,9},{10,18},{18,10},{11,19},{19,11},{12,20... | collective-permute-start | bytes 1179656 | tf_op jit(solution)/shard_map/ppermute | solution.py:474
  68.1 0.1 collective-permute-start
  68.2 2.4 %collective-permute-start.3 = (bf16[8,64,384]{2,1,0:T(8,128)(2,1)S(1)}, bf16[8,64,384]{2,1,0:T(8,128)(2,1)S(1)}, u32[]{:S(2)}, u32[]{:S(2)}) collective-permute-start(bf16[8,64,384]{2,1,0:T(8,128)(2,1)S(1)} %all-to-all-done.2.v0_ref), channel_id=1, source_target_pairs={{8,16},{16,8},{9,17},{17,9},{10,18},{18,10},{11,19},{19,11},{12,20... | collective-permute-start | bytes 1179656 | tf_op jit(solution)/shard_map/ppermute | solution.py:474
  70.5 0.4 collective-permute-start.2
  70.9 7.5 %collective-permute-done.1.k3_ref = bf16[8,64,384]{2,1,0:T(8,128)(2,1)S(1)} collective-permute-done((bf16[8,64,384]{2,1,0:T(8,128)(2,1)S(1)}, bf16[8,64,384]{2,1,0:T(8,128)(2,1)S(1)}, u32[]{:S(2)}, u32[]{:S(2)}) %collective-permute-start.1) | collective-permute-done | bytes 393248 | tf_op jit(solution)/shard_map/ppermute | solution.py:474
  78.4 1.3 collective-permute-start.4
  79.8 0.4 collective-permute-done.k1_ref
  80.1 3.1 %collective-permute-start.5 = (bf16[8,64,384]{2,1,0:T(8,128)(2,1)S(1)}, bf16[8,64,384]{2,1,0:T(8,128)(2,1)}, u32[]{:S(2)}, u32[]{:S(2)}) collective-permute-start(bf16[8,64,384]{2,1,0:T(8,128)(2,1)S(1)} %collective-permute-done.k1_ref), channel_id=1, source_target_pairs={{8,16},{16,8},{9,17},{17,9},{10,18},{18,10},{11,19},{19,11},{12,20... | collective-permute-start | bytes 1179656 | tf_op jit(solution)/shard_map/ppermute | solution.py:474
  83.3 3.6 %collective-permute-done.3.v3_ref = bf16[8,64,384]{2,1,0:T(8,128)(2,1)S(1)} collective-permute-done((bf16[8,64,384]{2,1,0:T(8,128)(2,1)S(1)}, bf16[8,64,384]{2,1,0:T(8,128)(2,1)S(1)}, u32[]{:S(2)}, u32[]{:S(2)}) %collective-permute-start.3) | collective-permute-done | bytes 393248 | tf_op jit(solution)/shard_map/ppermute | solution.py:474
  86.9 2.1 collective-permute-start.6
  88.9 0.0 collective-permute-done.2.v1_ref
  88.9 3.5 %collective-permute-start.7 = (bf16[8,64,384]{2,1,0:T(8,128)(2,1)S(1)}, bf16[8,64,384]{2,1,0:T(8,128)(2,1)}, u32[]{:S(2)}, u32[]{:S(2)}) collective-permute-start(bf16[8,64,384]{2,1,0:T(8,128)(2,1)S(1)} %collective-permute-done.2.v1_ref), channel_id=1, source_target_pairs={{8,16},{16,8},{9,17},{17,9},{10,18},{18,10},{11,19},{19,11},{12,20... | collective-permute-start | bytes 1179656 | tf_op jit(solution)/shard_map/ppermute | solution.py:474
  92.4 0.0 all-to-all-done.qg_ref
  92.4 4.3 %shard_map.87 = (bf16[3,1536,512]{2,1,0:T(8,128)(2,1)S(1)}, f32[3,8,512]{2,1,0:T(8,128)S(1)}) custom-call(s32[1]{0:T(128)} %bitcast.frame_ref, s32[2,4,4]{2,1,0:T(4,128)S(1)} %copy-done.7, bf16[8,2,64,384]{3,2,1,0:T(8,128)(2,1)S(1)} %all-to-all-done.qg_ref, bf16[8,64,384]{2,1,0:T(8,128)(2,1)S(1)} %all-to-all-done.1.k0_ref, ...), custom_call_target="tpu_custom_call" | custom-call | flops 1207959552 | bytes 4194304 | tf_op jit(solution)/shard_map/pallas_call | solution.py:483
  96.8 0.0 collective-permute-done.4.ka_ref
  96.8 0.0 collective-permute-done.5.kb_ref
  96.8 4.8 %shard_map.88 = (bf16[3,512,512]{2,1,0:T(8,128)(2,1)S(1)}, f32[3,8,512]{2,1,0:T(8,128)S(1)}, bf16[8,64,384]{2,1,0:T(8,128)(2,1)}) custom-call(s32[1]{0:T(128)} %bitcast.frame_ref, s32[2,4,4]{2,1,0:T(4,128)S(1)} %copy-done.7, bf16[8,2,64,384]{3,2,1,0:T(8,128)(2,1)S(1)} %all-to-all-done.qg_ref, bf16[8,64,384]{2,1,0:T(8,128)(2,1)S(1)} %collective-permute-done.4.ka_ref, ...), custom_call_target="tpu_custom_call" | custom-call | flops 1207959552 | bytes 4194304 | tf_op jit(solution)/shard_map/pallas_call | solution.py:490
  101.6 2.3 %collective-permute-start.12 = (bf16[8,64,384]{2,1,0:T(8,128)(2,1)}, bf16[8,64,384]{2,1,0:T(8,128)(2,1)}, u32[]{:S(2)}, u32[]{:S(2)}) collective-permute-start(bf16[8,64,384]{2,1,0:T(8,128)(2,1)} %get-tuple-element.40), channel_id=1, source_target_pairs={{8,16},{16,8},{9,17},{17,9},{10,18},{18,10},{11,19},{19,11},{12,20... | collective-permute-start | bytes 1179656 | tf_op jit(solution)/shard_map/ppermute | solution.py:474
  103.9 1.3 collective-permute-start.14
  105.2 3.1 %shard_map.89 = (bf16[8,64,384]{2,1,0:T(8,128)(2,1)S(1)}, bf16[8,64,384]{2,1,0:T(8,128)(2,1)S(1)}, bf16[8,64,384]{2,1,0:T(8,128)(2,1)S(1)}, f32[3,128,512]{2,1,0:T(8,128)S(1)}) custom-call(bf16[8,2,64,384]{3,2,1,0:T(8,128)(2,1)S(1)} %all-to-all-done.qg_ref, bf16[3,1536,512]{2,1,0:T(8,128)(2,1)S(1)} %get-tuple-element.23.e_ref, ...), custom_call_target="tpu_custom_call" | custom-call | flops 1207959552 | bytes 4194304 | tf_op jit(solution)/shard_map/pallas_call | solution.py:497
  108.4 0.0 collective-permute-done.6.va_ref
  108.4 0.0 collective-permute-done.7.vb_ref
  108.4 4.7 %shard_map.90 = (bf16[8,64,384]{2,1,0:T(8,128)(2,1)}, bf16[8,64,384]{2,1,0:T(8,128)(2,1)S(1)}, f32[3,8,512]{2,1,0:T(8,128)S(1)}, f32[3,128,512]{2,1,0:T(8,128)S(1)}) custom-call(s32[1]{0:T(128)} %bitcast.frame_ref, bf16[8,2,64,384]{3,2,1,0:T(8,128)(2,1)S(1)} %all-to-all-done.qg_ref, bf16[8,64,384]{2,1,0:T(8,128)(2,1)S(1)} %collective-permute-done.4.ka_ref, ...), custom_call_target="tpu_custom_call" | custom-call | flops 1207959552 | bytes 4194304 | tf_op jit(solution)/shard_map/pallas_call | solution.py:503
  113.1 3.5 %collective-permute-start.8 = (bf16[8,64,384]{2,1,0:T(8,128)(2,1)}, bf16[8,64,384]{2,1,0:T(8,128)(2,1)}, u32[]{:S(2)}, u32[]{:S(2)}) collective-permute-start(bf16[8,64,384]{2,1,0:T(8,128)(2,1)} %get-tuple-element.36), channel_id=1, source_target_pairs={{8,16},{16,8},{9,17},{17,9},{10,18},{18,10},{11,19},{19,11},{12,20... | collective-permute-start | bytes 1179656 | tf_op jit(solution)/shard_map/ppermute | solution.py:474
  116.6 1.3 collective-permute-start.10
  117.9 5.6 %shard_map.91 = (bf16[8,64,384]{2,1,0:T(8,128)(2,1)S(1)}, bf16[8,64,384]{2,1,0:T(8,128)(2,1)S(1)}, bf16[8,64,384]{2,1,0:T(8,128)(2,1)S(1)}, bf16[8,2,64,384]{3,2,1,0:T(8,128)(2,1)}) custom-call(bf16[8,2,64,384]{3,2,1,0:T(8,128)(2,1)S(1)} %all-to-all-done.qg_ref, bf16[8,64,384]{2,1,0:T(8,128)(2,1)S(1)} %all-to-all-done.1.k0_ref, ...), custom_call_target="tpu_custom_call" | custom-call | flops 1811939328 | bytes 4194304 | tf_op jit(solution)/shard_map/pallas_call | solution.py:510
  123.4 0.7 copy-done.4
  124.2 0.7 copy-done.6
  124.9 4.3 %all-to-all-start.3 = ((bf16[8,2,64,384]{3,2,1,0:T(8,128)(2,1)}), bf16[8,2,64,384]{3,2,1,0:T(8,128)(2,1)S(1)}, u32[]{:S(2)}, u32[]{:S(2)}) async-start(bf16[8,2,64,384]{3,2,1,0:T(8,128)(2,1)} %get-tuple-element.31), calls=%async_computation.3 | async-start | bytes 1572864 | tf_op jit(solution)/shard_map/all_to_all | solution.py:439
  129.2 0.0 collective-permute-done.12
  129.2 1.2 add_convert_fusion.2
  130.5 3.4 %collective-permute-start.13 = (bf16[8,64,384]{2,1,0:T(8,128)(2,1)S(1)}, bf16[8,64,384]{2,1,0:T(8,128)(2,1)S(1)}, u32[]{:S(2)}, u32[]{:S(2)}) collective-permute-start(bf16[8,64,384]{2,1,0:T(8,128)(2,1)S(1)} %add_convert_fusion.2), channel_id=1, source_target_pairs={{0,8},{8,0},{16,24},{24,16},{1,9},{9,1},{17,25},{25,17},{2,10},{10... | collective-permute-start | bytes 1179656 | tf_op jit(solution)/shard_map/ppermute | solution.py:474
  133.9 0.0 collective-permute-done.14
  133.9 1.2 add_convert_fusion.1
  135.1 2.4 %collective-permute-start.15 = (bf16[8,64,384]{2,1,0:T(8,128)(2,1)S(1)}, bf16[8,64,384]{2,1,0:T(8,128)(2,1)S(1)}, u32[]{:S(2)}, u32[]{:S(2)}) collective-permute-start(bf16[8,64,384]{2,1,0:T(8,128)(2,1)S(1)} %add_convert_fusion.1), channel_id=1, source_target_pairs={{8,16},{16,8},{9,17},{17,9},{10,18},{18,10},{11,19},{19,11},{12,20... | collective-permute-start | bytes 1179656 | tf_op jit(solution)/shard_map/ppermute | solution.py:474
  137.5 0.0 collective-permute-done.8
  137.5 1.2 add_convert_fusion.5
  138.7 0.1 collective-permute-start.9
  138.8 0.0 collective-permute-done.10
  138.8 1.8 add_convert_fusion.4
  140.7 3.5 %collective-permute-start.11 = (bf16[8,64,384]{2,1,0:T(8,128)(2,1)}, bf16[8,64,384]{2,1,0:T(8,128)(2,1)S(1)}, u32[]{:S(2)}, u32[]{:S(2)}) collective-permute-start(bf16[8,64,384]{2,1,0:T(8,128)(2,1)} %add_convert_fusion.4), channel_id=1, source_target_pairs={{8,16},{16,8},{9,17},{17,9},{10,18},{18,10},{11,19},{19,11},{12,20... | collective-permute-start | bytes 1179656 | tf_op jit(solution)/shard_map/ppermute | solution.py:474
  144.1 0.0 collective-permute-done.13
  144.1 4.9 %collective-permute-done.15 = bf16[8,64,384]{2,1,0:T(8,128)(2,1)S(1)} collective-permute-done((bf16[8,64,384]{2,1,0:T(8,128)(2,1)S(1)}, bf16[8,64,384]{2,1,0:T(8,128)(2,1)S(1)}, u32[]{:S(2)}, u32[]{:S(2)}) %collective-permute-start.15) | collective-permute-done | bytes 393248 | tf_op jit(solution)/shard_map/ppermute | solution.py:474
  149.0 0.9 add_convert_fusion
  149.9 0.0 all-to-all-done.3.in_ref
  149.9 4.2 %all-to-all-start.5 = ((bf16[8,64,384]{2,1,0:T(8,128)(2,1)}), bf16[8,64,384]{2,1,0:T(8,128)(2,1)S(1)}, u32[]{:S(2)}, u32[]{:S(2)}) async-start(bf16[8,64,384]{2,1,0:T(8,128)(2,1)} %add_convert_fusion), calls=%async_computation.5 | async-start | bytes 786432 | tf_op jit(solution)/shard_map/all_to_all | solution.py:439
  154.1 0.0 collective-permute-done.9
  154.1 2.2 %collective-permute-done.11 = bf16[8,64,384]{2,1,0:T(8,128)(2,1)S(1)} collective-permute-done((bf16[8,64,384]{2,1,0:T(8,128)(2,1)}, bf16[8,64,384]{2,1,0:T(8,128)(2,1)S(1)}, u32[]{:S(2)}, u32[]{:S(2)}) %collective-permute-start.11) | collective-permute-done | bytes 393248 | tf_op jit(solution)/shard_map/ppermute | solution.py:474
  156.3 0.9 add_convert_fusion.3
  157.2 3.7 %all-to-all-done.5.in_ref = bf16[8,64,384]{2,1,0:T(8,128)(2,1)S(1)} async-done(((bf16[8,64,384]{2,1,0:T(8,128)(2,1)}), bf16[8,64,384]{2,1,0:T(8,128)(2,1)S(1)}, u32[]{:S(2)}, u32[]{:S(2)}) %all-to-all-start.5) | async-done | bytes 393248 | tf_op jit(solution)/shard_map/all_to_all | solution.py:439
  160.9 4.0 %all-to-all-start.4 = ((bf16[8,64,384]{2,1,0:T(8,128)(2,1)}), bf16[8,64,384]{2,1,0:T(8,128)(2,1)S(1)}, u32[]{:S(2)}, u32[]{:S(2)}) async-start(bf16[8,64,384]{2,1,0:T(8,128)(2,1)} %add_convert_fusion.3), calls=%async_computation.4 | async-start | bytes 786432 | tf_op jit(solution)/shard_map/all_to_all | solution.py:439
  164.9 25.1 %shard_map.92 = (bf16[64,3072]{1,0:T(8,128)(2,1)}, bf16[64,3072]{1,0:T(8,128)(2,1)}) custom-call(bf16[8,2,64,384]{3,2,1,0:T(8,128)(2,1)} %copy-done.8), custom_call_target="tpu_custom_call" | custom-call | tf_op jit(solution)/shard_map/pallas_call | solution.py:418
  190.0 13.1 %shard_map.94 = bf16[64,3072]{1,0:T(8,128)(2,1)} custom-call(bf16[8,64,384]{2,1,0:T(8,128)(2,1)} %copy-done.9), custom_call_target="tpu_custom_call" | custom-call | tf_op jit(solution)/shard_map/pallas_call | solution.py:418
  203.1 0.0 all-to-all-done.4.in_ref
  203.1 0.7 copy-done.10
  203.9 13.1 %shard_map.93 = bf16[64,3072]{1,0:T(8,128)(2,1)} custom-call(bf16[8,64,384]{2,1,0:T(8,128)(2,1)} %copy-done.10), custom_call_target="tpu_custom_call" | custom-call | tf_op jit(solution)/shard_map/pallas_call | solution.py:418
  (19 shorter events, 0.0 us)
Async XLA Ops:
  0.6 91.8 %copy-start.7 = (s32[2,4,4]{2,1,0:T(4,128)S(1)}, s32[2,4,4]{2,1,0:T(4,128)}, u32[]{:S(2)}) copy-start(s32[2,4,4]{2,1,0:T(4,128)} %mask_ref.3) | copy-start | bytes 388
  13.7 17.4 %all-to-all-start.1 = ((bf16[8,64,384]{2,1,0:T(8,128)(2,1)}), bf16[8,64,384]{2,1,0:T(8,128)(2,1)S(1)}, u32[]{:S(2)}, u32[]{:S(2)}) async-start(bf16[8,64,384]{2,1,0:T(8,128)(2,1)} %shard_map.85), calls=%async_computation.1 | async-start | bytes 786432 | tf_op jit(solution)/shard_map/all_to_all | solution.py:439
  31.1 29.3 %all-to-all-start.2 = ((bf16[8,64,384]{2,1,0:T(8,128)(2,1)}), bf16[8,64,384]{2,1,0:T(8,128)(2,1)S(1)}, u32[]{:S(2)}, u32[]{:S(2)}) async-start(bf16[8,64,384]{2,1,0:T(8,128)(2,1)} %shard_map.86), calls=%async_computation.2 | async-start | bytes 786432 | tf_op jit(solution)/shard_map/all_to_all | solution.py:439
  60.4 32.0 %all-to-all-start = ((bf16[8,2,64,384]{3,2,1,0:T(8,128)(2,1)}), bf16[8,2,64,384]{3,2,1,0:T(8,128)(2,1)S(1)}, u32[]{:S(2)}, u32[]{:S(2)}) async-start(bf16[8,2,64,384]{3,2,1,0:T(8,128)(2,1)} %shard_map.84), calls=%async_computation | async-start | bytes 1572864 | tf_op jit(solution)/shard_map/all_to_all | solution.py:439
  64.6 13.8 %collective-permute-start.1 = (bf16[8,64,384]{2,1,0:T(8,128)(2,1)S(1)}, bf16[8,64,384]{2,1,0:T(8,128)(2,1)S(1)}, u32[]{:S(2)}, u32[]{:S(2)}) collective-permute-start(bf16[8,64,384]{2,1,0:T(8,128)(2,1)S(1)} %all-to-all-done.1.k0_ref), channel_id=1, source_target_pairs={{8,16},{16,8},{9,17},{17,9},{10,18},{18,10},{11,19},{19,11},{12,20... | collective-permute-start | bytes 1179656 | tf_op jit(solution)/shard_map/ppermute | solution.py:474
  68.1 12.1 %collective-permute-start = (bf16[8,64,384]{2,1,0:T(8,128)(2,1)S(1)}, bf16[8,64,384]{2,1,0:T(8,128)(2,1)S(1)}, u32[]{:S(2)}, u32[]{:S(2)}) collective-permute-start(bf16[8,64,384]{2,1,0:T(8,128)(2,1)S(1)} %all-to-all-done.1.k0_ref), channel_id=1, source_target_pairs={{0,8},{8,0},{16,24},{24,16},{1,9},{9,1},{17,25},{25,17},{2,10},{10... | collective-permute-start | bytes 1179656 | tf_op jit(solution)/shard_map/ppermute | solution.py:474
  68.2 18.7 %collective-permute-start.3 = (bf16[8,64,384]{2,1,0:T(8,128)(2,1)S(1)}, bf16[8,64,384]{2,1,0:T(8,128)(2,1)S(1)}, u32[]{:S(2)}, u32[]{:S(2)}) collective-permute-start(bf16[8,64,384]{2,1,0:T(8,128)(2,1)S(1)} %all-to-all-done.2.v0_ref), channel_id=1, source_target_pairs={{8,16},{16,8},{9,17},{17,9},{10,18},{18,10},{11,19},{19,11},{12,20... | collective-permute-start | bytes 1179656 | tf_op jit(solution)/shard_map/ppermute | solution.py:474
  70.5 18.4 %collective-permute-start.2 = (bf16[8,64,384]{2,1,0:T(8,128)(2,1)S(1)}, bf16[8,64,384]{2,1,0:T(8,128)(2,1)S(1)}, u32[]{:S(2)}, u32[]{:S(2)}) collective-permute-start(bf16[8,64,384]{2,1,0:T(8,128)(2,1)S(1)} %all-to-all-done.2.v0_ref), channel_id=1, source_target_pairs={{0,8},{8,0},{16,24},{24,16},{1,9},{9,1},{17,25},{25,17},{2,10},{10... | collective-permute-start | bytes 1179656 | tf_op jit(solution)/shard_map/ppermute | solution.py:474
  78.4 18.3 %collective-permute-start.4 = (bf16[8,64,384]{2,1,0:T(8,128)(2,1)S(1)}, bf16[8,64,384]{2,1,0:T(8,128)(2,1)S(1)}, u32[]{:S(2)}, u32[]{:S(2)}) collective-permute-start(bf16[8,64,384]{2,1,0:T(8,128)(2,1)S(1)} %collective-permute-done.1.k3_ref), channel_id=1, source_target_pairs={{8,0},{16,24},{9,1},{17,25},{10,2},{18,26},{11,3},{19,27},{12,4},{... | collective-permute-start | bytes 1179656 | tf_op jit(solution)/shard_map/ppermute | solution.py:474
  80.1 16.6 %collective-permute-start.5 = (bf16[8,64,384]{2,1,0:T(8,128)(2,1)S(1)}, bf16[8,64,384]{2,1,0:T(8,128)(2,1)}, u32[]{:S(2)}, u32[]{:S(2)}) collective-permute-start(bf16[8,64,384]{2,1,0:T(8,128)(2,1)S(1)} %collective-permute-done.k1_ref), channel_id=1, source_target_pairs={{8,16},{16,8},{9,17},{17,9},{10,18},{18,10},{11,19},{19,11},{12,20... | collective-permute-start | bytes 1179656 | tf_op jit(solution)/shard_map/ppermute | solution.py:474
  86.9 21.5 %collective-permute-start.6 = (bf16[8,64,384]{2,1,0:T(8,128)(2,1)S(1)}, bf16[8,64,384]{2,1,0:T(8,128)(2,1)}, u32[]{:S(2)}, u32[]{:S(2)}) collective-permute-start(bf16[8,64,384]{2,1,0:T(8,128)(2,1)S(1)} %collective-permute-done.3.v3_ref), channel_id=1, source_target_pairs={{8,0},{16,24},{9,1},{17,25},{10,2},{18,26},{11,3},{19,27},{12,4},{... | collective-permute-start | bytes 1179656 | tf_op jit(solution)/shard_map/ppermute | solution.py:474
  88.9 19.5 %collective-permute-start.7 = (bf16[8,64,384]{2,1,0:T(8,128)(2,1)S(1)}, bf16[8,64,384]{2,1,0:T(8,128)(2,1)}, u32[]{:S(2)}, u32[]{:S(2)}) collective-permute-start(bf16[8,64,384]{2,1,0:T(8,128)(2,1)S(1)} %collective-permute-done.2.v1_ref), channel_id=1, source_target_pairs={{8,16},{16,8},{9,17},{17,9},{10,18},{18,10},{11,19},{19,11},{12,20... | collective-permute-start | bytes 1179656 | tf_op jit(solution)/shard_map/ppermute | solution.py:474
  101.6 27.7 %collective-permute-start.12 = (bf16[8,64,384]{2,1,0:T(8,128)(2,1)}, bf16[8,64,384]{2,1,0:T(8,128)(2,1)}, u32[]{:S(2)}, u32[]{:S(2)}) collective-permute-start(bf16[8,64,384]{2,1,0:T(8,128)(2,1)} %get-tuple-element.40), channel_id=1, source_target_pairs={{8,16},{16,8},{9,17},{17,9},{10,18},{18,10},{11,19},{19,11},{12,20... | collective-permute-start | bytes 1179656 | tf_op jit(solution)/shard_map/ppermute | solution.py:474
  103.9 30.0 %collective-permute-start.14 = (bf16[8,64,384]{2,1,0:T(8,128)(2,1)}, bf16[8,64,384]{2,1,0:T(8,128)(2,1)}, u32[]{:S(2)}, u32[]{:S(2)}) collective-permute-start(bf16[8,64,384]{2,1,0:T(8,128)(2,1)} %get-tuple-element.40), channel_id=1, source_target_pairs={{0,8},{24,16},{1,9},{25,17},{2,10},{26,18},{3,11},{27,19},{4,12},{... | collective-permute-start | bytes 1179656 | tf_op jit(solution)/shard_map/ppermute | solution.py:474
  108.3 4.7 %copy-start = (bf16[8,64,384]{2,1,0:T(8,128)(2,1)}, bf16[8,64,384]{2,1,0:T(8,128)(2,1)S(1)}, u32[]{:S(2)}) copy-start(bf16[8,64,384]{2,1,0:T(8,128)(2,1)S(1)} %get-tuple-element.38) | copy-start | bytes 1179652
  108.4 15.1 %copy-start.2 = (bf16[8,64,384]{2,1,0:T(8,128)(2,1)}, bf16[8,64,384]{2,1,0:T(8,128)(2,1)S(1)}, u32[]{:S(2)}) copy-start(bf16[8,64,384]{2,1,0:T(8,128)(2,1)S(1)} %get-tuple-element.41) | copy-start | bytes 1179652
  108.4 15.0 %copy-start.3 = (bf16[8,64,384]{2,1,0:T(8,128)(2,1)}, bf16[8,64,384]{2,1,0:T(8,128)(2,1)S(1)}, u32[]{:S(2)}) copy-start(bf16[8,64,384]{2,1,0:T(8,128)(2,1)S(1)} %get-tuple-element.39) | copy-start | bytes 1179652
  113.1 24.4 %collective-permute-start.8 = (bf16[8,64,384]{2,1,0:T(8,128)(2,1)}, bf16[8,64,384]{2,1,0:T(8,128)(2,1)}, u32[]{:S(2)}, u32[]{:S(2)}) collective-permute-start(bf16[8,64,384]{2,1,0:T(8,128)(2,1)} %get-tuple-element.36), channel_id=1, source_target_pairs={{8,16},{16,8},{9,17},{17,9},{10,18},{18,10},{11,19},{19,11},{12,20... | collective-permute-start | bytes 1179656 | tf_op jit(solution)/shard_map/ppermute | solution.py:474
  116.6 22.2 %collective-permute-start.10 = (bf16[8,64,384]{2,1,0:T(8,128)(2,1)}, bf16[8,64,384]{2,1,0:T(8,128)(2,1)}, u32[]{:S(2)}, u32[]{:S(2)}) collective-permute-start(bf16[8,64,384]{2,1,0:T(8,128)(2,1)} %get-tuple-element.36), channel_id=1, source_target_pairs={{0,8},{24,16},{1,9},{25,17},{2,10},{26,18},{3,11},{27,19},{4,12},{... | collective-permute-start | bytes 1179656 | tf_op jit(solution)/shard_map/ppermute | solution.py:474
  123.4 0.7 copy-start.4
  124.2 0.7 copy-start.6
  124.9 24.1 %copy-start.1 = (bf16[8,64,384]{2,1,0:T(8,128)(2,1)S(1)}, bf16[8,64,384]{2,1,0:T(8,128)(2,1)}, u32[]{:S(2)}) copy-start(bf16[8,64,384]{2,1,0:T(8,128)(2,1)} %copy-done) | copy-start | bytes 1179652
  124.9 13.9 %copy-start.5 = (bf16[8,64,384]{2,1,0:T(8,128)(2,1)S(1)}, bf16[8,64,384]{2,1,0:T(8,128)(2,1)}, u32[]{:S(2)}) copy-start(bf16[8,64,384]{2,1,0:T(8,128)(2,1)} %copy-done.4) | copy-start | bytes 1179652
  124.9 25.0 %all-to-all-start.3 = ((bf16[8,2,64,384]{3,2,1,0:T(8,128)(2,1)}), bf16[8,2,64,384]{3,2,1,0:T(8,128)(2,1)S(1)}, u32[]{:S(2)}, u32[]{:S(2)}) async-start(bf16[8,2,64,384]{3,2,1,0:T(8,128)(2,1)} %get-tuple-element.31), calls=%async_computation.3 | async-start | bytes 1572864 | tf_op jit(solution)/shard_map/all_to_all | solution.py:439
  130.5 13.7 %collective-permute-start.13 = (bf16[8,64,384]{2,1,0:T(8,128)(2,1)S(1)}, bf16[8,64,384]{2,1,0:T(8,128)(2,1)S(1)}, u32[]{:S(2)}, u32[]{:S(2)}) collective-permute-start(bf16[8,64,384]{2,1,0:T(8,128)(2,1)S(1)} %add_convert_fusion.2), channel_id=1, source_target_pairs={{0,8},{8,0},{16,24},{24,16},{1,9},{9,1},{17,25},{25,17},{2,10},{10... | collective-permute-start | bytes 1179656 | tf_op jit(solution)/shard_map/ppermute | solution.py:474
  135.1 13.9 %collective-permute-start.15 = (bf16[8,64,384]{2,1,0:T(8,128)(2,1)S(1)}, bf16[8,64,384]{2,1,0:T(8,128)(2,1)S(1)}, u32[]{:S(2)}, u32[]{:S(2)}) collective-permute-start(bf16[8,64,384]{2,1,0:T(8,128)(2,1)S(1)} %add_convert_fusion.1), channel_id=1, source_target_pairs={{8,16},{16,8},{9,17},{17,9},{10,18},{18,10},{11,19},{19,11},{12,20... | collective-permute-start | bytes 1179656 | tf_op jit(solution)/shard_map/ppermute | solution.py:474
  138.7 15.4 %collective-permute-start.9 = (bf16[8,64,384]{2,1,0:T(8,128)(2,1)S(1)}, bf16[8,64,384]{2,1,0:T(8,128)(2,1)S(1)}, u32[]{:S(2)}, u32[]{:S(2)}) collective-permute-start(bf16[8,64,384]{2,1,0:T(8,128)(2,1)S(1)} %add_convert_fusion.5), channel_id=1, source_target_pairs={{0,8},{8,0},{16,24},{24,16},{1,9},{9,1},{17,25},{25,17},{2,10},{10... | collective-permute-start | bytes 1179656 | tf_op jit(solution)/shard_map/ppermute | solution.py:474
  140.7 15.7 %collective-permute-start.11 = (bf16[8,64,384]{2,1,0:T(8,128)(2,1)}, bf16[8,64,384]{2,1,0:T(8,128)(2,1)S(1)}, u32[]{:S(2)}, u32[]{:S(2)}) collective-permute-start(bf16[8,64,384]{2,1,0:T(8,128)(2,1)} %add_convert_fusion.4), channel_id=1, source_target_pairs={{8,16},{16,8},{9,17},{17,9},{10,18},{18,10},{11,19},{19,11},{12,20... | collective-permute-start | bytes 1179656 | tf_op jit(solution)/shard_map/ppermute | solution.py:474
  149.9 15.0 %copy-start.8 = (bf16[8,2,64,384]{3,2,1,0:T(8,128)(2,1)}, bf16[8,2,64,384]{3,2,1,0:T(8,128)(2,1)S(1)}, u32[]{:S(2)}) copy-start(bf16[8,2,64,384]{3,2,1,0:T(8,128)(2,1)S(1)} %all-to-all-done.3.in_ref) | copy-start | bytes 2359300
  149.9 11.0 %all-to-all-start.5 = ((bf16[8,64,384]{2,1,0:T(8,128)(2,1)}), bf16[8,64,384]{2,1,0:T(8,128)(2,1)S(1)}, u32[]{:S(2)}, u32[]{:S(2)}) async-start(bf16[8,64,384]{2,1,0:T(8,128)(2,1)} %add_convert_fusion), calls=%async_computation.5 | async-start | bytes 786432 | tf_op jit(solution)/shard_map/all_to_all | solution.py:439
  160.9 29.1 %copy-start.9 = (bf16[8,64,384]{2,1,0:T(8,128)(2,1)}, bf16[8,64,384]{2,1,0:T(8,128)(2,1)S(1)}, u32[]{:S(2)}) copy-start(bf16[8,64,384]{2,1,0:T(8,128)(2,1)S(1)} %all-to-all-done.5.in_ref) | copy-start | bytes 1179652
  160.9 42.2 %all-to-all-start.4 = ((bf16[8,64,384]{2,1,0:T(8,128)(2,1)}), bf16[8,64,384]{2,1,0:T(8,128)(2,1)S(1)}, u32[]{:S(2)}, u32[]{:S(2)}) async-start(bf16[8,64,384]{2,1,0:T(8,128)(2,1)} %add_convert_fusion.3), calls=%async_computation.4 | async-start | bytes 786432 | tf_op jit(solution)/shard_map/all_to_all | solution.py:439
  203.1 0.7 copy-start.10

commit v3 on v0

--- a/solution.py
+++ b/solution.py
@@ -3,11 +3,18 @@
 import jax
 import jax.numpy as jnp
 from jax import lax
+from jax.experimental import pallas as pl
+from jax.experimental.pallas import tpu as pltpu
+from jax.sharding import Mesh
 from jax.sharding import PartitionSpec as P
 
 HD = 128
 BLOCK = 128
 GROUP = 4
+SCALE = 1.0 / math.sqrt(HD)
+SCALE_LOG2 = SCALE * math.log2(math.e)
+MASKED = -1e30
+VMEM_BYTES = 24 * 1024 * 1024
 
 
 def partner_2(shard, axis, distance):
@@ -35,7 +42,7 @@
     )
 
 
-def per_device(query_rows, key_rows, value_rows, out_grad, block_mask):
+def per_device_general(query_rows, key_rows, value_rows, out_grad, block_mask):
     queries, keys_local, values_local, grads_output = (
         lax.all_to_all(query_rows, "head", split_axis=1, concat_axis=0, tiled=True),
         lax.all_to_all(key_rows, "head", split_axis=1, concat_axis=0, tiled=True),
@@ -168,23 +175,354 @@
     )
 
 
+NT = (((1,), (1,)), ((), ()))
+F32 = jnp.float32
+BF16 = jnp.bfloat16
+
+
+def dot(a, b):
+    return jnp.dot(a, b, preferred_element_type=F32)
+
+
+def dot_nt(a, b):
+    return lax.dot_general(a, b, NT, preferred_element_type=F32)
+
+
+def head_columns(head):
+    return slice(head * HD, (head + 1) * HD)
+
+
+def flat(ref, head):
+    part = ref[:, :, head_columns(head)]
+    return part.reshape(part.shape[0] * part.shape[1], HD)
+
+
+def put(ref, head, rows):
+    ref[:, :, head_columns(head)] = rows.reshape(ref.shape[0], ref.shape[1], HD)
+
+
+def bias_rows(mask_ref, level, valid, blocks):
+    lane_block = lax.broadcasted_iota(jnp.int32, (1, blocks * BLOCK), 1) // BLOCK
+    rows = []
+    for key_block in range(blocks):
+        row = jnp.zeros((1, blocks * BLOCK), F32)
+        for query_block in range(blocks):
+            open_ = (mask_ref[level, query_block, key_block] > 0) & valid
+            value = jnp.where(open_, 0.0, MASKED).astype(F32)
+            row = jnp.where(lane_block == query_block, value, row)
+        rows.append(row)
+    return rows
+
+
+def masked_scores(keys, queries, bias):
+    scores = dot_nt(keys, queries) * SCALE_LOG2
+    if bias is None:
+        return scores
+    blocks = len(bias)
+    return jnp.concatenate(
+        [scores[j * BLOCK : (j + 1) * BLOCK] + bias[j] for j in range(blocks)], axis=0
+    )
+
+
+def near_scores_kernel(frame_ref, mask_ref, q_ref, k0_ref, k1_ref, k3_ref, e_ref, ml_ref):
+    heads, _, tokens = e_ref.shape
+    blocks = tokens // BLOCK
+    frame = frame_ref[0]
+    inner = (frame == 1) | (frame == 2)
+    bias1 = bias_rows(mask_ref, 0, frame >= 0, blocks)
+    bias3 = bias_rows(mask_ref, 0, inner, blocks)
+    for head in range(heads):
+        queries = flat(q_ref, head)
+        slots = ((k0_ref, None), (k1_ref, bias1), (k3_ref, bias3))
+        scores = [masked_scores(flat(ref, head), queries, bias) for ref, bias in slots]
+        peak = scores[0].max(axis=0, keepdims=True)
+        for score in scores[1:]:
+            peak = jnp.maximum(peak, score.max(axis=0, keepdims=True))
+        total = jnp.zeros((1, tokens), F32)
+        for index, score in enumerate(scores):
+            e = jnp.exp2(score - peak)
+            total = total + e.sum(axis=0, keepdims=True)
+            e_ref[head, index * tokens : (index + 1) * tokens] = e.astype(BF16)
+        ml_ref[head, 0:1] = peak
+        ml_ref[head, 1:2] = total
+
+
+def far_scores_kernel(frame_ref, mask_ref, q_ref, g_ref, ka_ref, kb_ref, ml_ref, e_ref, w_ref, dv_ref):
+    heads, _, tokens = e_ref.shape
+    blocks = tokens // BLOCK
+    frame = frame_ref[0]
+    inner = (frame == 1) | (frame == 2)
+    bias = bias_rows(mask_ref, 1, frame >= 0, blocks)
+    for head in range(heads):
+        keys = jnp.where(inner, flat(kb_ref, head), flat(ka_ref, head))
+        scores = masked_scores(keys, flat(q_ref, head), bias)
+        peak2 = scores.max(axis=0, keepdims=True)
+        e = jnp.exp2(scores - peak2)
+        total2 = e.sum(axis=0, keepdims=True)
+        e = e.astype(BF16)
+        peak1 = ml_ref[head, 0:1]
+        peak = jnp.maximum(peak1, peak2)
+        near = jnp.exp2(peak1 - peak)
+        far = jnp.exp2(peak2 - peak)
+        inv = 1.0 / (near * ml_ref[head, 1:2] + far * total2)
+        far = far * inv
+        scaled = (flat(g_ref, head).T.astype(F32) * far).astype(BF16)
+        put(dv_ref, head, dot_nt(e, scaled).astype(BF16))
+        e_ref[head] = e
+        w_ref[head, 0:1] = near * inv
+        w_ref[head, 1:2] = far
+
+
+def near_values_kernel(g_ref, e_ref, w_ref, v0_ref, v1_ref, v3_ref, dv0_ref, dv1_ref, dv3_ref, acc_ref):
+    heads, _, tokens = e_ref.shape
+    for head in range(heads):
+        scaled = (flat(g_ref, head).T.astype(F32) * w_ref[head, 0:1]).astype(BF16)
+        acc = jnp.zeros((HD, tokens), F32)
+        for index, (v_ref, dv_ref) in enumerate(
+            ((v0_ref, dv0_ref), (v1_ref, dv1_ref), (v3_ref, dv3_ref))
+        ):
+            e = e_ref[head, index * tokens : (index + 1) * tokens]
+            put(dv_ref, head, dot_nt(e, scaled).astype(BF16))
+            acc = acc + dot(flat(v_ref, head).T, e)
+        acc_ref[head] = acc
+
+
+def far_values_kernel(
+    frame_ref, q_ref, g_ref, ka_ref, kb_ref, va_ref, vb_ref, e_ref, w_ref, acc_ref,
+    dk_ref, att_ref, delta_ref, dq_ref,
+):
+    heads = e_ref.shape[0]
+    frame = frame_ref[0]
+    inner = (frame == 1) | (frame == 2)
+    for head in range(heads):
+        keys = jnp.where(inner, flat(kb_ref, head), flat(ka_ref, head))
+        values = jnp.where(inner, flat(vb_ref, head), flat(va_ref, head))
+        e = e_ref[head]
+        near = w_ref[head, 0:1]
+        far = w_ref[head, 1:2]
+        out = (acc_ref[head] * near + dot(values.T, e) * far).astype(BF16)
+        put(att_ref, head, out.T)
+        grads = flat(g_ref, head).T.astype(F32)
+        delta = (grads * out.astype(F32)).sum(axis=0, keepdims=True)
+        delta_ref[head, 0:1] = near
+        delta_ref[head, 1:2] = near * delta
+        scaled = (grads * far).astype(BF16)
+        ds = (e.astype(F32) * (dot(values, scaled) - far * delta)).astype(BF16)
+        put(dk_ref, head, (dot(ds, flat(q_ref, head)) * SCALE).astype(BF16))
+        dq_ref[head] = dot(keys.T, ds)
+
+
+def near_keys_kernel(
+    q_ref, g_ref, k0_ref, k1_ref, k3_ref, v0_ref, v1_ref, v3_ref, e_ref, delta_ref, dq2_ref,
+    dk0_ref, dk1_ref, dk3_ref, dq_ref,
+):
+    heads, _, tokens = e_ref.shape
+    for head in range(heads):
+        queries = flat(q_ref, head)
+        near = delta_ref[head, 0:1]
+        delta = delta_ref[head, 1:2]
+        scaled = (flat(g_ref, head).T.astype(F32) * near).astype(BF16)
+        dq = dq2_ref[head]
+        for index, (k_ref, v_ref, dk_ref) in enumerate(
+            ((k0_ref, v0_ref, dk0_ref), (k1_ref, v1_ref, dk1_ref), (k3_ref, v3_ref, dk3_ref))
+        ):
+            e = e_ref[head, index * tokens : (index + 1) * tokens]
+            ds = (e.astype(F32) * (dot(flat(v_ref, head), scaled) - delta)).astype(BF16)
+            put(dk_ref, head, (dot(ds, queries) * SCALE).astype(BF16))
+            dq = dq + dot(flat(k_ref, head).T, ds)
+        put(dq_ref, head, (dq * SCALE).astype(BF16).T)
+
+
+def add_kernel(frame_ref, own_ref, other_ref, out_ref):
+    out_ref[...] = (own_ref[...].astype(F32) + other_ref[...].astype(F32)).astype(BF16)
+
+
+def add_inner_kernel(frame_ref, own_ref, other_ref, out_ref):
+    inner = (frame_ref[0] == 1) | (frame_ref[0] == 2)
+
+    @pl.when(inner)
+    def _():
+        out_ref[...] = (own_ref[...].astype(F32) + other_ref[...].astype(F32)).astype(BF16)
+
+    @pl.when(jnp.logical_not(inner))
+    def _():
+        out_ref[...] = own_ref[...]
+
+
+def last_sum(frame_ref, own_ref, edge_ref, middle_ref):
+    inner = (frame_ref[0] == 1) | (frame_ref[0] == 2)
+    total = own_ref[...].astype(F32) + edge_ref[...].astype(F32)
+    return (total + jnp.where(inner, middle_ref[...].astype(F32), 0.0)).astype(BF16)
+
+
+def last_add_kernel(frame_ref, own_ref, edge_ref, middle_ref, out_ref):
+    out_ref[...] = last_sum(frame_ref, own_ref, edge_ref, middle_ref)
+
+
+def collect_kernel(frame_ref, own_ref, edge_ref, middle_ref, att_ref, dq_ref, out_ref):
+    out_ref[:, 0] = att_ref[...]
+    out_ref[:, 1] = dq_ref[...]
+    out_ref[:, 2] = last_sum(frame_ref, own_ref, edge_ref, middle_ref)
+
+
+def pack_kernel(in_ref, out_ref):
+    peers, _, width = out_ref.shape
+    for peer in range(peers):
+        out_ref[peer] = in_ref[:, peer * width : (peer + 1) * width]
+
+
+def unpack_kernel(in_ref, out_ref):
+    peers, _, width = in_ref.shape
+    for peer in range(peers):
+        out_ref[:, peer * width : (peer + 1) * width] = in_ref[peer]
+
+
+def unpack_three_kernel(in_ref, a_ref, b_ref, c_ref):
+    peers, _, _, width = in_ref.shape
+    for peer in range(peers):
+        for which, ref in enumerate((a_ref, b_ref, c_ref)):
+            ref[:, peer * width : (peer + 1) * width] = in_ref[peer, which]
+
+
+def params():
+    return pltpu.CompilerParams(vmem_limit_bytes=VMEM_BYTES)
+
+
+def cost(flops, data):
+    return pl.CostEstimate(flops=flops, bytes_accessed=data, transcendentals=0)
+
+
+def per_device_line(query_rows, key_rows, value_rows, out_grad, block_mask):
+    plane = ("rank", "head")
+    peers = lax.axis_size("rank") * lax.axis_size("head")
+    rows, columns = query_rows.shape
+    width = columns // peers
+    heads = width // HD
+    tokens = peers * rows
+    one = jax.ShapeDtypeStruct((peers, rows, width), BF16)
+    row_type = jax.ShapeDtypeStruct((rows, columns), BF16)
+    near_e = jax.ShapeDtypeStruct((heads, 3 * tokens, tokens), BF16)
+    far_e = jax.ShapeDtypeStruct((heads, tokens, tokens), BF16)
+    stat = jax.ShapeDtypeStruct((heads, 8, tokens), F32)
+    sums = jax.ShapeDtypeStruct((heads, HD, tokens), F32)
+    frame = lax.axis_index("frame").astype(jnp.int32).reshape(1)
+    smem = pl.BlockSpec(memory_space=pltpu.SMEM)
+    vmem = pl.BlockSpec(memory_space=pltpu.VMEM)
+    pair_flops = heads * 2 * tokens * tokens * HD
+
+    def call(kernel, outs, work, *operands):
+        several = isinstance(outs, tuple)
+        return pl.pallas_call(
+            kernel,
+            in_specs=[smem if x.dtype == jnp.int32 else vmem for x in operands],
+            out_specs=(vmem,) * len(outs) if several else vmem,
+            out_shape=outs,
+            compiler_params=params(),
+            cost_estimate=cost(work * pair_flops, 4 << 20),
+        )(*operands)
+
+    def swap(array):
+        return lax.all_to_all(array, plane, 0, 0, tiled=True)
+
+    def enter(rows_):
+        return swap(call(pack_kernel, one, 0, rows_))
+
+    def leave(array):
+        return call(unpack_kernel, row_type, 0, swap(array))
+
+    devices = ("frame", "rank", "head")
+    heads_axis = lax.axis_size("head")
+
+    def pairs_of(partner):
+        pairs = []
+        for frame_ in range(4):
+            for rank in range(GROUP):
+                for part in range(heads_axis):
+                    there = partner.get(frame_)
+                    place = (frame_, rank ^ 1) if there is None else (there, rank)
+                    pairs.append(
+                        (
+                            (frame_ * GROUP + rank) * heads_axis + part,
+                            (place[0] * GROUP + place[1]) * heads_axis + part,
+                        )
+                    )
+        return pairs
+
+    edge = pairs_of({0: 1, 1: 0, 2: 3, 3: 2})
+    middle = pairs_of({1: 2, 2: 1})
+
+    def send(array, pairs):
+        return lax.ppermute(array, devices, pairs)
+
+    k0 = enter(key_rows)
+    k1, k3 = send(k0, edge), send(k0, middle)
+    q = enter(query_rows)
+    v0 = enter(value_rows)
+    g = enter(out_grad)
+    k2a, k2b = send(k3, edge), send(k1, middle)
+    v1, v3 = send(v0, edge), send(v0, middle)
+    v2a, v2b = send(v3, edge), send(v1, middle)
+
+    e_near, ml = call(
+        near_scores_kernel, (near_e, stat), 6, frame, block_mask, q, k0, k1, k3
+    )
+    e_far, w, dv2 = call(
+        far_scores_kernel, (far_e, stat, one), 4, frame, block_mask, q, g, k2a, k2b, ml
+    )
+    dv_edge, dv_middle = send(dv2, edge), send(dv2, middle)
+    dv0, dv1, dv3, acc = call(
+        near_values_kernel, (one, one, one, sums), 6, g, e_near, w, v0, v1, v3
+    )
+    dk2, att, delta, dq2 = call(
+        far_values_kernel, (one, one, stat, sums), 4, frame, q, g, k2a, k2b, v2a, v2b, e_far, w, acc
+    )
+    dk_edge, dk_middle = send(dk2, edge), send(dk2, middle)
+    dk0, dk1, dk3, dq = call(
+        near_keys_kernel, (one, one, one, one), 9, q, g, k0, k1, k3, v0, v1, v3, e_near, delta, dq2
+    )
+
+    def last_round(first, third, from_edge, from_middle):
+        over_middle = send(call(add_kernel, one, 0, frame, third, from_edge), middle)
+        over_edge = send(call(add_inner_kernel, one, 0, frame, first, from_middle), edge)
+        return over_edge, over_middle
+
+    over = last_round(dv1, dv3, dv_edge, dv_middle)
+    three = jax.ShapeDtypeStruct((peers, 3, rows, width), BF16)
+    collected = swap(call(collect_kernel, three, 0, frame, dv0, *over, att, dq))
+    over = last_round(dk1, dk3, dk_edge, dk_middle)
+    attended, grad_query, grad_values = call(
+        unpack_three_kernel, (row_type, row_type, row_type), 0, collected
+    )
+    grad_keys = leave(call(last_add_kernel, one, 0, frame, dk0, *over))
+    return attended, grad_query, grad_keys, grad_values
+
+
 def solution(mesh):
-    placed = (
-        P(("seq", "head"), None),
-        P(("seq", "head"), None),
-        P(("seq", "head"), None),
-        P(("seq", "head"), None),
-        P(),
-    )
-    return jax.shard_map(
-        per_device,
-        mesh=mesh,
-        in_specs=placed,
-        out_specs=(
-            P(("seq", "head"), None),
-            P(("seq", "head"), None),
-            P(("seq", "head"), None),
-            P(("seq", "head"), None),
-        ),
-        check_vma=False,
-    )
+    seq, head = mesh.shape["seq"], mesh.shape["head"]
+    frames = seq // GROUP
+    line = Mesh(mesh.devices.reshape(frames, GROUP, head), ("frame", "rank", "head"))
+
+    def run(query_rows, key_rows, value_rows, out_grad, block_mask):
+        heads = query_rows.shape[1] // HD
+        tokens = query_rows.shape[0] // frames
+        fits = (
+            frames == 4
+            and block_mask.shape[0] == 2
+            and heads % (GROUP * head) == 0
+            and tokens == block_mask.shape[1] * BLOCK
+            and tokens // (GROUP * head) % 16 == 0
+        )
+        if fits:
+            body, where, axes = per_device_line, line, ("frame", "rank", "head")
+        else:
+            body, where, axes = per_device_general, mesh, ("seq", "head")
+        row_spec = P(axes, None)
+        return jax.shard_map(
+            body,
+            mesh=where,
+            in_specs=(row_spec,) * 4 + (P(),),
+            out_specs=(row_spec,) * 4,
+            check_vma=False,
+        )(query_rows, key_rows, value_rows, out_grad, block_mask)
+
+    return run

time: 676 us -> 126 us (0.19)
  waiting for transfers between devices: 457 us -> 56.5 us
  matrix products: 68.1 us -> 0 us
  local copies, waits for them, and re-layouts: 54.1 us -> 7.66 us
  other arithmetic: 24.7 us -> 0 us
  Pallas kernels: 0 us -> 22.6 us
  starting transfers between devices: 54.4 us -> 36.6 us
  blocking collectives: 8.37 us -> 0 us
    ppermute x12 -> x16, waiting for transfers between devices: 434 us -> 24.6 us  [send(): return lax.ppermute(array, devices, pairs)]
    dot_general x72 -> x0, matrix products: 68.1 us -> none  [the longest x12 19.6 us: head_scores(): jnp.einsum('qd,kd->qk', query_head, keys_head, preferred_element_type=jnp...]
    unnamed x106 -> x28, local copies, waits for them, and re-layouts: 32.7 us -> 7.66 us
    pallas_call x0 -> x17, Pallas kernels: none -> 22.6 us  [call(): pl.pallas_call(kernel, in_specs=[smem if x.dtype == jnp.int32 else vmem f...]
    ppermute x12 -> x16, starting transfers between devices: 29.1 us -> 12.1 us  [send(): return lax.ppermute(array, devices, pairs)]
    all_to_all x7 -> x6, waiting for transfers between devices: 22.6 us -> 31.9 us  [swap(): return lax.all_to_all(array, plane, 0, 0, tiled=True)]
    all_to_all x1 -> x0, blocking collectives: 8.37 us -> none  [per_device(): lax.all_to_all(key_rows, 'head', split_axis=1, concat_axis=0, tiled=True)]
    all_to_all x8 -> x0, local copies, waits for them, and re-layouts: 7.62 us -> none  [the longest x1 1.92 us: per_device(): lax.all_to_all(query_rows, 'head', split_axis=1, concat_axis=0, tiled=True)]
  transfers between devices with their start and end apart: 19 -> 22, of which waited for: 13 -> 14; matrix products, arithmetic and copies ran while one was open for 12% -> 0% of each run, Pallas kernels for 0% -> 14%
where the time goes in v3:
time: 126 us; the launch traced here: 124 us
  waiting for transfers between devices  56.5 us (45%)
  starting transfers between devices  36.6 us (29%)
  Pallas kernels  22.6 us (18%)
  local copies, waits for them, and re-layouts  7.66 us (6%)
    all_to_all x6, waiting for transfers between devices, swap(): return lax.all_to_all(array, plane, 0, 0, tiled=True)  31.9 us
    ppermute x16, waiting for transfers between devices, send(): return lax.ppermute(array, devices, pairs)  24.6 us
    all_to_all x6, starting transfers between devices, swap(): return lax.all_to_all(array, plane, 0, 0, tiled=True)  24.6 us
    pallas_call x17, Pallas kernels, call(): pl.pallas_call(kernel, in_specs=[smem if x.dtype == jnp.int32 else vmem f...  22.6 us
    ppermute x16, starting transfers between devices, send(): return lax.ppermute(array, devices, pairs)  12.1 us
    unnamed x28, local copies, waits for them, and re-layouts  7.66 us
  transfers between devices with their start and end apart: 22, of which 14 were waited for; matrix products, arithmetic and copies ran while one was open for 0% of the time, Pallas kernels for 14%

profile of v3, /device:TPU:10, one launch (start us, length us, event | category | flops | bytes accessed | tf_op | source)
XLA Modules:
  0.0 124.1 jit_solution(8097021214517474084)
XLA Ops:
  0.6 1.0 copy-done.3
  1.6 0.8 shard_map.86
  2.4 4.3 %all-to-all-start.2 = ((bf16[8,64,384]{2,1,0:T(8,128)(2,1)}), bf16[8,64,384]{2,1,0:T(8,128)(2,1)S(1)}, u32[]{:S(2)}, u32[]{:S(2)}) async-start(bf16[8,64,384]{2,1,0:T(8,128)(2,1)} %shard_map.86), calls=%async_computation.2 | async-start | bytes 786432 | tf_op jit(solution)/shard_map/all_to_all | solution.py:425
  6.7 0.8 shard_map.89
  7.5 6.0 %all-to-all-done.2.k0_ref = bf16[8,64,384]{2,1,0:T(8,128)(2,1)S(1)} async-done(((bf16[8,64,384]{2,1,0:T(8,128)(2,1)}), bf16[8,64,384]{2,1,0:T(8,128)(2,1)S(1)}, u32[]{:S(2)}, u32[]{:S(2)}) %all-to-all-start.2) | async-done | bytes 393248 | tf_op jit(solution)/shard_map/all_to_all | solution.py:425
  13.5 4.0 %all-to-all-start.3 = ((bf16[8,64,384]{2,1,0:T(8,128)(2,1)}), bf16[8,64,384]{2,1,0:T(8,128)(2,1)S(1)}, u32[]{:S(2)}, u32[]{:S(2)}) async-start(bf16[8,64,384]{2,1,0:T(8,128)(2,1)} %shard_map.89), calls=%async_computation.3 | async-start | bytes 786432 | tf_op jit(solution)/shard_map/all_to_all | solution.py:425
  17.5 1.6 %collective-permute-start.1 = (bf16[8,64,384]{2,1,0:T(8,128)(2,1)S(1)}, bf16[8,64,384]{2,1,0:T(8,128)(2,1)S(1)}, u32[]{:S(2)}, u32[]{:S(2)}) collective-permute-start(bf16[8,64,384]{2,1,0:T(8,128)(2,1)S(1)} %all-to-all-done.2.k0_ref), channel_id=1, source_target_pairs={{0,2},{1,3},{2,0},{3,1},{4,6},{5,7},{6,4},{7,5},{8,16},{9,17},{10,... | collective-permute-start | bytes 1179656 | tf_op jit(solution)/shard_map/ppermute | solution.py:455
  19.1 0.0 collective-permute-start
  19.1 0.8 shard_map.85
  19.9 4.4 %all-to-all-done.3.v0_ref = bf16[8,64,384]{2,1,0:T(8,128)(2,1)S(1)} async-done(((bf16[8,64,384]{2,1,0:T(8,128)(2,1)}), bf16[8,64,384]{2,1,0:T(8,128)(2,1)S(1)}, u32[]{:S(2)}, u32[]{:S(2)}) %all-to-all-start.3) | async-done | bytes 393248 | tf_op jit(solution)/shard_map/all_to_all | solution.py:425
  24.3 4.0 %all-to-all-start.1 = ((bf16[8,64,384]{2,1,0:T(8,128)(2,1)}), bf16[8,64,384]{2,1,0:T(8,128)(2,1)S(1)}, u32[]{:S(2)}, u32[]{:S(2)}) async-start(bf16[8,64,384]{2,1,0:T(8,128)(2,1)} %shard_map.85), calls=%async_computation.1 | async-start | bytes 786432 | tf_op jit(solution)/shard_map/all_to_all | solution.py:425
  28.3 1.6 %collective-permute-start.5 = (bf16[8,64,384]{2,1,0:T(8,128)(2,1)S(1)}, bf16[8,64,384]{2,1,0:T(8,128)(2,1)S(1)}, u32[]{:S(2)}, u32[]{:S(2)}) collective-permute-start(bf16[8,64,384]{2,1,0:T(8,128)(2,1)S(1)} %all-to-all-done.3.v0_ref), channel_id=1, source_target_pairs={{0,2},{1,3},{2,0},{3,1},{4,6},{5,7},{6,4},{7,5},{8,16},{9,17},{10,... | collective-permute-start | bytes 1179656 | tf_op jit(solution)/shard_map/ppermute | solution.py:455
  29.9 2.0 %collective-permute-start.2 = (bf16[8,64,384]{2,1,0:T(8,128)(2,1)S(1)}, bf16[8,64,384]{2,1,0:T(8,128)(2,1)S(1)}, u32[]{:S(2)}, u32[]{:S(2)}) collective-permute-start(bf16[8,64,384]{2,1,0:T(8,128)(2,1)S(1)} %collective-permute-done.1.k3_ref), channel_id=1, source_target_pairs={{0,8},{1,9},{2,10},{3,11},{4,12},{5,13},{6,14},{7,15},{8,0},{9,1},... | collective-permute-start | bytes 1179656 | tf_op jit(solution)/shard_map/ppermute | solution.py:455
  31.9 0.0 collective-permute-done.k1_ref
  31.9 0.5 collective-permute-start.3
  32.4 0.8 shard_map.84
  33.2 2.0 %all-to-all-done.1.q_ref = bf16[8,64,384]{2,1,0:T(8,128)(2,1)S(1)} async-done(((bf16[8,64,384]{2,1,0:T(8,128)(2,1)}), bf16[8,64,384]{2,1,0:T(8,128)(2,1)S(1)}, u32[]{:S(2)}, u32[]{:S(2)}) %all-to-all-start.1) | async-done | bytes 393248 | tf_op jit(solution)/shard_map/all_to_all | solution.py:425
  35.1 4.0 %all-to-all-start = ((bf16[8,64,384]{2,1,0:T(8,128)(2,1)}), bf16[8,64,384]{2,1,0:T(8,128)(2,1)S(1)}, u32[]{:S(2)}, u32[]{:S(2)}) async-start(bf16[8,64,384]{2,1,0:T(8,128)(2,1)} %shard_map.84), calls=%async_computation | async-start | bytes 786432 | tf_op jit(solution)/shard_map/all_to_all | solution.py:425
  39.1 1.1 collective-permute-done.5.v3_ref
  40.3 0.0 collective-permute-start.10
  40.3 1.6 %collective-permute-done.4.v1_ref = bf16[8,64,384]{2,1,0:T(8,128)(2,1)S(1)} collective-permute-done((bf16[8,64,384]{2,1,0:T(8,128)(2,1)S(1)}, bf16[8,64,384]{2,1,0:T(8,128)(2,1)S(1)}, u32[]{:S(2)}, u32[]{:S(2)}) %collective-permute-start.4) | collective-permute-done | bytes 393248 | tf_op jit(solution)/shard_map/ppermute | solution.py:455
  41.9 0.5 collective-permute-start.11
  42.3 3.5 %shard_map.87 = (bf16[3,1536,512]{2,1,0:T(8,128)(2,1)S(1)}, f32[3,8,512]{2,1,0:T(8,128)S(1)}) custom-call(s32[1]{0:T(128)} %bitcast.frame_ref, s32[2,4,4]{2,1,0:T(4,128)S(1)} %copy-done.11, bf16[8,64,384]{2,1,0:T(8,128)(2,1)S(1)} %all-to-all-done.1.q_ref, bf16[8,64,384]{2,1,0:T(8,128)(2,1)S(1)} %all-to-all-done.2.k0_ref, ...), custom_call_target="tpu_custom_call" | custom-call | flops 1207959552 | bytes 4194304 | tf_op jit(solution)/shard_map/pallas_call | solution.py:415
  45.9 2.1 %copy-done = bf16[3,1536,512]{2,1,0:T(8,128)(2,1)} copy-done((bf16[3,1536,512]{2,1,0:T(8,128)(2,1)}, bf16[3,1536,512]{2,1,0:T(8,128)(2,1)S(1)}, u32[]{:S(2)}) %copy-start) | copy-done | bytes 4718616
  48.0 0.6 copy-done.12
  48.6 0.0 all-to-all-done.g_ref
  48.6 1.7 %collective-permute-done.2.ka_ref = bf16[8,64,384]{2,1,0:T(8,128)(2,1)S(1)} collective-permute-done((bf16[8,64,384]{2,1,0:T(8,128)(2,1)S(1)}, bf16[8,64,384]{2,1,0:T(8,128)(2,1)S(1)}, u32[]{:S(2)}, u32[]{:S(2)}) %collective-permute-start.2) | collective-permute-done | bytes 393248 | tf_op jit(solution)/shard_map/ppermute | solution.py:455
  50.3 0.0 collective-permute-done.3.kb_ref
  50.3 0.8 copy-done.13
  51.1 2.8 %shard_map.88 = (bf16[3,512,512]{2,1,0:T(8,128)(2,1)S(1)}, f32[3,8,512]{2,1,0:T(8,128)S(1)}, bf16[8,64,384]{2,1,0:T(8,128)(2,1)S(1)}) custom-call(s32[1]{0:T(128)} %bitcast.frame_ref, s32[2,4,4]{2,1,0:T(4,128)S(1)} %copy-done.11, bf16[8,64,384]{2,1,0:T(8,128)(2,1)S(1)} %all-to-all-done.1.q_ref, bf16[8,64,384]{2,1,0:T(8,128)(2,1)S(1)} %all-to-all-done.g_ref, ...), custom_call_target="tpu_custom_call" | custom-call | flops 805306368 | bytes 4194304 | tf_op jit(solution)/shard_map/pallas_call | solution.py:415
  53.9 2.3 %copy-done.1 = bf16[3,1536,512]{2,1,0:T(8,128)(2,1)S(1)} copy-done((bf16[3,1536,512]{2,1,0:T(8,128)(2,1)S(1)}, bf16[3,1536,512]{2,1,0:T(8,128)(2,1)}, u32[]{:S(2)}) %copy-start.1) | copy-done | bytes 4718616
  56.2 2.1 %shard_map.90 = (bf16[8,64,384]{2,1,0:T(8,128)(2,1)S(1)}, bf16[8,64,384]{2,1,0:T(8,128)(2,1)S(1)}, bf16[8,64,384]{2,1,0:T(8,128)(2,1)S(1)}, f32[3,128,512]{2,1,0:T(8,128)S(1)}) custom-call(bf16[8,64,384]{2,1,0:T(8,128)(2,1)S(1)} %all-to-all-done.g_ref, bf16[3,1536,512]{2,1,0:T(8,128)(2,1)S(1)} %copy-done.1, f32[3,8,512]{2,1,0:T(8,128)S(1)} %get-tuple-element.26.w_ref, ...), custom_call_target="tpu_custom_call" | custom-call | flops 1207959552 | bytes 4194304 | tf_op jit(solution)/shard_map/pallas_call | solution.py:415
  58.3 0.0 copy-start.7
  58.3 0.7 copy-done.7
  59.0 0.0 collective-permute-done.10.va_ref
  59.1 0.0 collective-permute-done.11.vb_ref
  59.1 3.2 %shard_map.93 = (bf16[8,64,384]{2,1,0:T(8,128)(2,1)S(1)}, bf16[8,64,384]{2,1,0:T(8,128)(2,1)S(1)}, f32[3,8,512]{2,1,0:T(8,128)S(1)}, f32[3,128,512]{2,1,0:T(8,128)S(1)}) custom-call(s32[1]{0:T(128)} %bitcast.frame_ref, bf16[8,64,384]{2,1,0:T(8,128)(2,1)S(1)} %all-to-all-done.1.q_ref, bf16[8,64,384]{2,1,0:T(8,128)(2,1)S(1)} %all-to-all-done.g_ref, ...), custom_call_target="tpu_custom_call" | custom-call | flops 805306368 | bytes 4194304 | tf_op jit(solution)/shard_map/pallas_call | solution.py:415
  62.3 0.0 copy-start.9
  62.3 0.5 collective-permute-start.12
  62.8 1.6 %collective-permute-start.6 = (bf16[8,64,384]{2,1,0:T(8,128)(2,1)S(1)}, bf16[8,64,384]{2,1,0:T(8,128)(2,1)S(1)}, u32[]{:S(2)}, u32[]{:S(2)}) collective-permute-start(bf16[8,64,384]{2,1,0:T(8,128)(2,1)S(1)} %get-tuple-element.29), channel_id=1, source_target_pairs={{0,2},{1,3},{2,0},{3,1},{4,6},{5,7},{6,4},{7,5},{8,16},{9,17},{10,... | collective-permute-start | bytes 1179656 | tf_op jit(solution)/shard_map/ppermute | solution.py:455
  64.4 0.5 collective-permute-start.8
  64.9 3.4 %shard_map.94 = (bf16[8,64,384]{2,1,0:T(8,128)(2,1)S(1)}, bf16[8,64,384]{2,1,0:T(8,128)(2,1)S(1)}, bf16[8,64,384]{2,1,0:T(8,128)(2,1)S(1)}, bf16[8,64,384]{2,1,0:T(8,128)(2,1)S(1)}) custom-call(bf16[8,64,384]{2,1,0:T(8,128)(2,1)S(1)} %all-to-all-done.1.q_ref, bf16[8,64,384]{2,1,0:T(8,128)(2,1)S(1)} %all-to-all-done.g_ref, ...), custom_call_target="tpu_custom_call" | custom-call | flops 1811939328 | bytes 4194304 | tf_op jit(solution)/shard_map/pallas_call | solution.py:415
  68.3 6.2 %collective-permute-done.12.other_ref = bf16[8,64,384]{2,1,0:T(8,128)(2,1)S(1)} collective-permute-done((bf16[8,64,384]{2,1,0:T(8,128)(2,1)S(1)}, bf16[8,64,384]{2,1,0:T(8,128)(2,1)S(1)}, u32[]{:S(2)}, u32[]{:S(2)}) %collective-permute-start.12) | collective-permute-done | bytes 393248 | tf_op jit(solution)/shard_map/ppermute | solution.py:455
  74.4 0.1 shard_map.97
  74.5 0.1 collective-permute-start.13
  74.6 0.3 collective-permute-done.14.other_ref
  74.9 0.1 shard_map.98
  75.0 1.6 %collective-permute-start.15 = (bf16[8,64,384]{2,1,0:T(8,128)(2,1)S(1)}, bf16[8,64,384]{2,1,0:T(8,128)(2,1)S(1)}, u32[]{:S(2)}, u32[]{:S(2)}) collective-permute-start(bf16[8,64,384]{2,1,0:T(8,128)(2,1)S(1)} %shard_map.98), channel_id=1, source_target_pairs={{0,2},{1,3},{2,0},{3,1},{4,6},{5,7},{6,4},{7,5},{8,16},{9,17},{10,... | collective-permute-start | bytes 1179656 | tf_op jit(solution)/shard_map/ppermute | solution.py:455
  76.6 6.2 %collective-permute-done.6.other_ref = bf16[8,64,384]{2,1,0:T(8,128)(2,1)S(1)} collective-permute-done((bf16[8,64,384]{2,1,0:T(8,128)(2,1)S(1)}, bf16[8,64,384]{2,1,0:T(8,128)(2,1)S(1)}, u32[]{:S(2)}, u32[]{:S(2)}) %collective-permute-start.6) | collective-permute-done | bytes 393248 | tf_op jit(solution)/shard_map/ppermute | solution.py:455
  82.8 0.1 shard_map.91
  83.0 0.1 collective-permute-start.7
  83.0 0.3 collective-permute-done.8.other_ref
  83.3 0.1 shard_map.92
  83.4 1.6 %collective-permute-start.9 = (bf16[8,64,384]{2,1,0:T(8,128)(2,1)S(1)}, bf16[8,64,384]{2,1,0:T(8,128)(2,1)S(1)}, u32[]{:S(2)}, u32[]{:S(2)}) collective-permute-start(bf16[8,64,384]{2,1,0:T(8,128)(2,1)S(1)} %shard_map.92), channel_id=1, source_target_pairs={{0,2},{1,3},{2,0},{3,1},{4,6},{5,7},{6,4},{7,5},{8,16},{9,17},{10,... | collective-permute-start | bytes 1179656 | tf_op jit(solution)/shard_map/ppermute | solution.py:455
  85.1 6.7 %collective-permute-done.13.edge_ref = bf16[8,64,384]{2,1,0:T(8,128)(2,1)S(1)} collective-permute-done((bf16[8,64,384]{2,1,0:T(8,128)(2,1)S(1)}, bf16[8,64,384]{2,1,0:T(8,128)(2,1)S(1)}, u32[]{:S(2)}, u32[]{:S(2)}) %collective-permute-start.13) | collective-permute-done | bytes 393248 | tf_op jit(solution)/shard_map/ppermute | solution.py:455
  91.7 0.9 shard_map.99
  92.7 4.2 %all-to-all-start.5 = ((bf16[8,64,384]{2,1,0:T(8,128)(2,1)}), bf16[8,64,384]{2,1,0:T(8,128)(2,1)S(1)}, u32[]{:S(2)}, u32[]{:S(2)}) async-start(bf16[8,64,384]{2,1,0:T(8,128)(2,1)} %shard_map.99), calls=%async_computation.5 | async-start | bytes 786432 | tf_op jit(solution)/shard_map/all_to_all | solution.py:425
  96.9 0.6 collective-permute-done.7.edge_ref
  97.4 1.3 %shard_map.95 = bf16[8,3,64,384]{3,2,1,0:T(8,128)(2,1)} custom-call(s32[1]{0:T(128)} %bitcast.frame_ref, bf16[8,64,384]{2,1,0:T(8,128)(2,1)S(1)} %copy-done.8, bf16[8,64,384]{2,1,0:T(8,128)(2,1)S(1)} %collective-permute-done.7.edge_ref, bf16[8,64,384]{2,1,0:T(8,128)(2,1)S(1)} %collective-permute-done.9.middle_ref, bf16[8,64,384]{2,1,0:T(8,128)(2,1)S(1)} %copy-done.10, ...), custom_call_target="tpu_custom_call" | custom-call | bytes 4194304 | tf_op jit(solution)/shard_map/pallas_call | solution.py:415
  98.7 5.0 %all-to-all-done.5.in_ref = bf16[8,64,384]{2,1,0:T(8,128)(2,1)S(1)} async-done(((bf16[8,64,384]{2,1,0:T(8,128)(2,1)}), bf16[8,64,384]{2,1,0:T(8,128)(2,1)S(1)}, u32[]{:S(2)}, u32[]{:S(2)}) %all-to-all-start.5) | async-done | bytes 393248 | tf_op jit(solution)/shard_map/all_to_all | solution.py:425
  103.7 4.1 %all-to-all-start.4 = ((bf16[8,3,64,384]{3,2,1,0:T(8,128)(2,1)}), bf16[8,3,64,384]{3,2,1,0:T(8,128)(2,1)S(1)}, u32[]{:S(2)}, u32[]{:S(2)}) async-start(bf16[8,3,64,384]{3,2,1,0:T(8,128)(2,1)} %shard_map.95), calls=%async_computation.4 | async-start | bytes 2359296 | tf_op jit(solution)/shard_map/all_to_all | solution.py:425
  107.8 0.8 shard_map.100
  108.6 14.5 %all-to-all-done.4.in_ref = bf16[8,3,64,384]{3,2,1,0:T(8,128)(2,1)S(1)} async-done(((bf16[8,3,64,384]{3,2,1,0:T(8,128)(2,1)}), bf16[8,3,64,384]{3,2,1,0:T(8,128)(2,1)S(1)}, u32[]{:S(2)}, u32[]{:S(2)}) %all-to-all-start.4) | async-done | bytes 1179680 | tf_op jit(solution)/shard_map/all_to_all | solution.py:425
  123.0 1.1 shard_map.96
  (25 shorter events, 0.1 us)
Async XLA Ops:
  0.6 1.0 copy-start.3
  1.6 5.0 %copy-start.4 = (bf16[64,3072]{1,0:T(8,128)(2,1)S(1)}, bf16[64,3072]{1,0:T(8,128)(2,1)}, u32[]{:S(2)}) copy-start(bf16[64,3072]{1,0:T(8,128)(2,1)} %in_ref.7) | copy-start | bytes 1179652
  1.6 17.4 %copy-start.5 = (bf16[64,3072]{1,0:T(8,128)(2,1)S(1)}, bf16[64,3072]{1,0:T(8,128)(2,1)}, u32[]{:S(2)}) copy-start(bf16[64,3072]{1,0:T(8,128)(2,1)} %in_ref.5) | copy-start | bytes 1179652
  2.4 11.1 %all-to-all-start.2 = ((bf16[8,64,384]{2,1,0:T(8,128)(2,1)}), bf16[8,64,384]{2,1,0:T(8,128)(2,1)S(1)}, u32[]{:S(2)}, u32[]{:S(2)}) async-start(bf16[8,64,384]{2,1,0:T(8,128)(2,1)} %shard_map.86), calls=%async_computation.2 | async-start | bytes 786432 | tf_op jit(solution)/shard_map/all_to_all | solution.py:425
  7.5 24.9 %copy-start.6 = (bf16[64,3072]{1,0:T(8,128)(2,1)S(1)}, bf16[64,3072]{1,0:T(8,128)(2,1)}, u32[]{:S(2)}) copy-start(bf16[64,3072]{1,0:T(8,128)(2,1)} %in_ref.4) | copy-start | bytes 1179652
  13.5 10.8 %all-to-all-start.3 = ((bf16[8,64,384]{2,1,0:T(8,128)(2,1)}), bf16[8,64,384]{2,1,0:T(8,128)(2,1)S(1)}, u32[]{:S(2)}, u32[]{:S(2)}) async-start(bf16[8,64,384]{2,1,0:T(8,128)(2,1)} %shard_map.89), calls=%async_computation.3 | async-start | bytes 786432 | tf_op jit(solution)/shard_map/all_to_all | solution.py:425
  17.5 24.8 %copy-start.11 = (s32[2,4,4]{2,1,0:T(4,128)S(1)}, s32[2,4,4]{2,1,0:T(4,128)}, u32[]{:S(2)}) copy-start(s32[2,4,4]{2,1,0:T(4,128)} %mask_ref.3) | copy-start | bytes 388
  17.5 12.4 %collective-permute-start.1 = (bf16[8,64,384]{2,1,0:T(8,128)(2,1)S(1)}, bf16[8,64,384]{2,1,0:T(8,128)(2,1)S(1)}, u32[]{:S(2)}, u32[]{:S(2)}) collective-permute-start(bf16[8,64,384]{2,1,0:T(8,128)(2,1)S(1)} %all-to-all-done.2.k0_ref), channel_id=1, source_target_pairs={{0,2},{1,3},{2,0},{3,1},{4,6},{5,7},{6,4},{7,5},{8,16},{9,17},{10,... | collective-permute-start | bytes 1179656 | tf_op jit(solution)/shard_map/ppermute | solution.py:455
  19.1 12.9 %collective-permute-start = (bf16[8,64,384]{2,1,0:T(8,128)(2,1)S(1)}, bf16[8,64,384]{2,1,0:T(8,128)(2,1)S(1)}, u32[]{:S(2)}, u32[]{:S(2)}) collective-permute-start(bf16[8,64,384]{2,1,0:T(8,128)(2,1)S(1)} %all-to-all-done.2.k0_ref), channel_id=1, source_target_pairs={{0,8},{1,9},{2,10},{3,11},{4,12},{5,13},{6,14},{7,15},{8,0},{9,1},... | collective-permute-start | bytes 1179656 | tf_op jit(solution)/shard_map/ppermute | solution.py:455
  24.3 10.8 %all-to-all-start.1 = ((bf16[8,64,384]{2,1,0:T(8,128)(2,1)}), bf16[8,64,384]{2,1,0:T(8,128)(2,1)S(1)}, u32[]{:S(2)}, u32[]{:S(2)}) async-start(bf16[8,64,384]{2,1,0:T(8,128)(2,1)} %shard_map.85), calls=%async_computation.1 | async-start | bytes 786432 | tf_op jit(solution)/shard_map/all_to_all | solution.py:425
  28.3 12.0 %collective-permute-start.5 = (bf16[8,64,384]{2,1,0:T(8,128)(2,1)S(1)}, bf16[8,64,384]{2,1,0:T(8,128)(2,1)S(1)}, u32[]{:S(2)}, u32[]{:S(2)}) collective-permute-start(bf16[8,64,384]{2,1,0:T(8,128)(2,1)S(1)} %all-to-all-done.3.v0_ref), channel_id=1, source_target_pairs={{0,2},{1,3},{2,0},{3,1},{4,6},{5,7},{6,4},{7,5},{8,16},{9,17},{10,... | collective-permute-start | bytes 1179656 | tf_op jit(solution)/shard_map/ppermute | solution.py:455
  29.9 12.0 %collective-permute-start.4 = (bf16[8,64,384]{2,1,0:T(8,128)(2,1)S(1)}, bf16[8,64,384]{2,1,0:T(8,128)(2,1)S(1)}, u32[]{:S(2)}, u32[]{:S(2)}) collective-permute-start(bf16[8,64,384]{2,1,0:T(8,128)(2,1)S(1)} %all-to-all-done.3.v0_ref), channel_id=1, source_target_pairs={{0,8},{1,9},{2,10},{3,11},{4,12},{5,13},{6,14},{7,15},{8,0},{9,1},... | collective-permute-start | bytes 1179656 | tf_op jit(solution)/shard_map/ppermute | solution.py:455
  29.9 20.4 %collective-permute-start.2 = (bf16[8,64,384]{2,1,0:T(8,128)(2,1)S(1)}, bf16[8,64,384]{2,1,0:T(8,128)(2,1)S(1)}, u32[]{:S(2)}, u32[]{:S(2)}) collective-permute-start(bf16[8,64,384]{2,1,0:T(8,128)(2,1)S(1)} %collective-permute-done.1.k3_ref), channel_id=1, source_target_pairs={{0,8},{1,9},{2,10},{3,11},{4,12},{5,13},{6,14},{7,15},{8,0},{9,1},... | collective-permute-start | bytes 1179656 | tf_op jit(solution)/shard_map/ppermute | solution.py:455
  31.9 18.4 %collective-permute-start.3 = (bf16[8,64,384]{2,1,0:T(8,128)(2,1)S(1)}, bf16[8,64,384]{2,1,0:T(8,128)(2,1)}, u32[]{:S(2)}, u32[]{:S(2)}) collective-permute-start(bf16[8,64,384]{2,1,0:T(8,128)(2,1)S(1)} %collective-permute-done.k1_ref), channel_id=1, source_target_pairs={{0,2},{1,3},{2,0},{3,1},{4,6},{5,7},{6,4},{7,5},{8,16},{9,17},{10,... | collective-permute-start | bytes 1179656 | tf_op jit(solution)/shard_map/ppermute | solution.py:455
  35.1 13.5 %all-to-all-start = ((bf16[8,64,384]{2,1,0:T(8,128)(2,1)}), bf16[8,64,384]{2,1,0:T(8,128)(2,1)S(1)}, u32[]{:S(2)}, u32[]{:S(2)}) async-start(bf16[8,64,384]{2,1,0:T(8,128)(2,1)} %shard_map.84), calls=%async_computation | async-start | bytes 786432 | tf_op jit(solution)/shard_map/all_to_all | solution.py:425
  40.3 18.8 %collective-permute-start.10 = (bf16[8,64,384]{2,1,0:T(8,128)(2,1)S(1)}, bf16[8,64,384]{2,1,0:T(8,128)(2,1)}, u32[]{:S(2)}, u32[]{:S(2)}) collective-permute-start(bf16[8,64,384]{2,1,0:T(8,128)(2,1)S(1)} %collective-permute-done.5.v3_ref), channel_id=1, source_target_pairs={{0,8},{1,9},{2,10},{3,11},{4,12},{5,13},{6,14},{7,15},{8,0},{9,1},... | collective-permute-start | bytes 1179656 | tf_op jit(solution)/shard_map/ppermute | solution.py:455
  41.9 17.2 %collective-permute-start.11 = (bf16[8,64,384]{2,1,0:T(8,128)(2,1)S(1)}, bf16[8,64,384]{2,1,0:T(8,128)(2,1)}, u32[]{:S(2)}, u32[]{:S(2)}) collective-permute-start(bf16[8,64,384]{2,1,0:T(8,128)(2,1)S(1)} %collective-permute-done.4.v1_ref), channel_id=1, source_target_pairs={{0,2},{1,3},{2,0},{3,1},{4,6},{5,7},{6,4},{7,5},{8,16},{9,17},{10,... | collective-permute-start | bytes 1179656 | tf_op jit(solution)/shard_map/ppermute | solution.py:455
  45.9 2.2 %copy-start = (bf16[3,1536,512]{2,1,0:T(8,128)(2,1)}, bf16[3,1536,512]{2,1,0:T(8,128)(2,1)S(1)}, u32[]{:S(2)}) copy-start(bf16[3,1536,512]{2,1,0:T(8,128)(2,1)S(1)} %get-tuple-element.24.e_ref) | copy-start | bytes 14155780
  48.0 0.6 copy-start.12
  50.3 0.8 copy-start.13
  53.9 2.3 %copy-start.1 = (bf16[3,1536,512]{2,1,0:T(8,128)(2,1)S(1)}, bf16[3,1536,512]{2,1,0:T(8,128)(2,1)}, u32[]{:S(2)}) copy-start(bf16[3,1536,512]{2,1,0:T(8,128)(2,1)} %copy-done) | copy-start | bytes 14155780
  58.3 0.7 copy-start.7
  59.1 5.8 %copy-start.2 = (bf16[3,1536,512]{2,1,0:T(8,128)(2,1)S(1)}, bf16[3,1536,512]{2,1,0:T(8,128)(2,1)}, u32[]{:S(2)}) copy-start(bf16[3,1536,512]{2,1,0:T(8,128)(2,1)} %copy-done) | copy-start | bytes 14155780
  62.3 6.0 %copy-start.9 = (bf16[8,64,384]{2,1,0:T(8,128)(2,1)}, bf16[8,64,384]{2,1,0:T(8,128)(2,1)S(1)}, u32[]{:S(2)}) copy-start(bf16[8,64,384]{2,1,0:T(8,128)(2,1)S(1)} %get-tuple-element.33.att_ref) | copy-start | bytes 1179652
  62.3 12.1 %collective-permute-start.12 = (bf16[8,64,384]{2,1,0:T(8,128)(2,1)S(1)}, bf16[8,64,384]{2,1,0:T(8,128)(2,1)S(1)}, u32[]{:S(2)}, u32[]{:S(2)}) collective-permute-start(bf16[8,64,384]{2,1,0:T(8,128)(2,1)S(1)} %get-tuple-element.41), channel_id=1, source_target_pairs={{0,2},{1,3},{2,0},{3,1},{4,6},{5,7},{6,4},{7,5},{8,16},{9,17},{10,... | collective-permute-start | bytes 1179656 | tf_op jit(solution)/shard_map/ppermute | solution.py:455
  62.8 12.1 %collective-permute-start.14 = (bf16[8,64,384]{2,1,0:T(8,128)(2,1)S(1)}, bf16[8,64,384]{2,1,0:T(8,128)(2,1)S(1)}, u32[]{:S(2)}, u32[]{:S(2)}) collective-permute-start(bf16[8,64,384]{2,1,0:T(8,128)(2,1)S(1)} %get-tuple-element.41), channel_id=1, source_target_pairs={{0,8},{1,9},{2,10},{3,11},{4,12},{5,13},{6,14},{7,15},{8,0},{9,1},... | collective-permute-start | bytes 1179656 | tf_op jit(solution)/shard_map/ppermute | solution.py:455
  62.8 20.0 %collective-permute-start.6 = (bf16[8,64,384]{2,1,0:T(8,128)(2,1)S(1)}, bf16[8,64,384]{2,1,0:T(8,128)(2,1)S(1)}, u32[]{:S(2)}, u32[]{:S(2)}) collective-permute-start(bf16[8,64,384]{2,1,0:T(8,128)(2,1)S(1)} %get-tuple-element.29), channel_id=1, source_target_pairs={{0,2},{1,3},{2,0},{3,1},{4,6},{5,7},{6,4},{7,5},{8,16},{9,17},{10,... | collective-permute-start | bytes 1179656 | tf_op jit(solution)/shard_map/ppermute | solution.py:455
  64.4 18.9 %collective-permute-start.8 = (bf16[8,64,384]{2,1,0:T(8,128)(2,1)S(1)}, bf16[8,64,384]{2,1,0:T(8,128)(2,1)S(1)}, u32[]{:S(2)}, u32[]{:S(2)}) collective-permute-start(bf16[8,64,384]{2,1,0:T(8,128)(2,1)S(1)} %get-tuple-element.29), channel_id=1, source_target_pairs={{0,8},{1,9},{2,10},{3,11},{4,12},{5,13},{6,14},{7,15},{8,0},{9,1},... | collective-permute-start | bytes 1179656 | tf_op jit(solution)/shard_map/ppermute | solution.py:455
  74.5 17.2 %collective-permute-start.13 = (bf16[8,64,384]{2,1,0:T(8,128)(2,1)S(1)}, bf16[8,64,384]{2,1,0:T(8,128)(2,1)S(1)}, u32[]{:S(2)}, u32[]{:S(2)}) collective-permute-start(bf16[8,64,384]{2,1,0:T(8,128)(2,1)S(1)} %shard_map.97), channel_id=1, source_target_pairs={{0,8},{1,9},{2,10},{3,11},{4,12},{5,13},{6,14},{7,15},{8,0},{9,1},... | collective-permute-start | bytes 1179656 | tf_op jit(solution)/shard_map/ppermute | solution.py:455
  75.0 16.8 %collective-permute-start.15 = (bf16[8,64,384]{2,1,0:T(8,128)(2,1)S(1)}, bf16[8,64,384]{2,1,0:T(8,128)(2,1)S(1)}, u32[]{:S(2)}, u32[]{:S(2)}) collective-permute-start(bf16[8,64,384]{2,1,0:T(8,128)(2,1)S(1)} %shard_map.98), channel_id=1, source_target_pairs={{0,2},{1,3},{2,0},{3,1},{4,6},{5,7},{6,4},{7,5},{8,16},{9,17},{10,... | collective-permute-start | bytes 1179656 | tf_op jit(solution)/shard_map/ppermute | solution.py:455
  83.0 14.5 %collective-permute-start.7 = (bf16[8,64,384]{2,1,0:T(8,128)(2,1)S(1)}, bf16[8,64,384]{2,1,0:T(8,128)(2,1)S(1)}, u32[]{:S(2)}, u32[]{:S(2)}) collective-permute-start(bf16[8,64,384]{2,1,0:T(8,128)(2,1)S(1)} %shard_map.91), channel_id=1, source_target_pairs={{0,8},{1,9},{2,10},{3,11},{4,12},{5,13},{6,14},{7,15},{8,0},{9,1},... | collective-permute-start | bytes 1179656 | tf_op jit(solution)/shard_map/ppermute | solution.py:455
  83.3 14.1 %copy-start.8 = (bf16[8,64,384]{2,1,0:T(8,128)(2,1)S(1)}, bf16[8,64,384]{2,1,0:T(8,128)(2,1)}, u32[]{:S(2)}) copy-start(bf16[8,64,384]{2,1,0:T(8,128)(2,1)} %copy-done.7) | copy-start | bytes 1179652
  83.3 14.1 %copy-start.10 = (bf16[8,64,384]{2,1,0:T(8,128)(2,1)S(1)}, bf16[8,64,384]{2,1,0:T(8,128)(2,1)}, u32[]{:S(2)}) copy-start(bf16[8,64,384]{2,1,0:T(8,128)(2,1)} %copy-done.9) | copy-start | bytes 1179652
  83.4 14.0 %collective-permute-start.9 = (bf16[8,64,384]{2,1,0:T(8,128)(2,1)S(1)}, bf16[8,64,384]{2,1,0:T(8,128)(2,1)S(1)}, u32[]{:S(2)}, u32[]{:S(2)}) collective-permute-start(bf16[8,64,384]{2,1,0:T(8,128)(2,1)S(1)} %shard_map.92), channel_id=1, source_target_pairs={{0,2},{1,3},{2,0},{3,1},{4,6},{5,7},{6,4},{7,5},{8,16},{9,17},{10,... | collective-permute-start | bytes 1179656 | tf_op jit(solution)/shard_map/ppermute | solution.py:455
  92.7 11.0 %all-to-all-start.5 = ((bf16[8,64,384]{2,1,0:T(8,128)(2,1)}), bf16[8,64,384]{2,1,0:T(8,128)(2,1)S(1)}, u32[]{:S(2)}, u32[]{:S(2)}) async-start(bf16[8,64,384]{2,1,0:T(8,128)(2,1)} %shard_map.99), calls=%async_computation.5 | async-start | bytes 786432 | tf_op jit(solution)/shard_map/all_to_all | solution.py:425
  103.7 19.3 %all-to-all-start.4 = ((bf16[8,3,64,384]{3,2,1,0:T(8,128)(2,1)}), bf16[8,3,64,384]{3,2,1,0:T(8,128)(2,1)S(1)}, u32[]{:S(2)}, u32[]{:S(2)}) async-start(bf16[8,3,64,384]{3,2,1,0:T(8,128)(2,1)} %shard_map.95), calls=%async_computation.4 | async-start | bytes 2359296 | tf_op jit(solution)/shard_map/all_to_all | solution.py:425

commit v4 on v3

--- a/solution.py
+++ b/solution.py
@@ -14,7 +14,7 @@
 SCALE = 1.0 / math.sqrt(HD)
 SCALE_LOG2 = SCALE * math.log2(math.e)
 MASKED = -1e30
-VMEM_BYTES = 24 * 1024 * 1024
+VMEM_BYTES = 12 * 1024 * 1024
 
 
 def partner_2(shard, axis, distance):
@@ -192,13 +192,17 @@
     return slice(head * HD, (head + 1) * HD)
 
 
-def flat(ref, head):
-    part = ref[:, :, head_columns(head)]
+def flat(ref, head, which=None):
+    columns = head_columns(head)
+    part = ref[:, :, columns] if which is None else ref[:, which, :, columns]
     return part.reshape(part.shape[0] * part.shape[1], HD)
 
 
-def put(ref, head, rows):
-    ref[:, :, head_columns(head)] = rows.reshape(ref.shape[0], ref.shape[1], HD)
+def put(ref, head, rows, which=None):
+    if which is None:
+        ref[:, :, head_columns(head)] = rows.reshape(ref.shape[0], ref.shape[1], HD)
+    else:
+        ref[:, which, :, head_columns(head)] = rows.reshape(ref.shape[0], ref.shape[2], HD)
 
 
 def bias_rows(mask_ref, level, valid, blocks):
@@ -224,7 +228,7 @@
     )
 
 
-def near_scores_kernel(frame_ref, mask_ref, q_ref, k0_ref, k1_ref, k3_ref, e_ref, ml_ref):
+def near_scores_kernel(frame_ref, mask_ref, vqg_ref, k0_ref, k1_ref, k3_ref, e_ref, ml_ref):
     heads, _, tokens = e_ref.shape
     blocks = tokens // BLOCK
     frame = frame_ref[0]
@@ -232,7 +236,7 @@
     bias1 = bias_rows(mask_ref, 0, frame >= 0, blocks)
     bias3 = bias_rows(mask_ref, 0, inner, blocks)
     for head in range(heads):
-        queries = flat(q_ref, head)
+        queries = flat(vqg_ref, head, 1)
         slots = ((k0_ref, None), (k1_ref, bias1), (k3_ref, bias3))
         scores = [masked_scores(flat(ref, head), queries, bias) for ref, bias in slots]
         peak = scores[0].max(axis=0, keepdims=True)
@@ -247,7 +251,7 @@
         ml_ref[head, 1:2] = total
 
 
-def far_scores_kernel(frame_ref, mask_ref, q_ref, g_ref, ka_ref, kb_ref, ml_ref, e_ref, w_ref, dv_ref):
+def far_scores_kernel(frame_ref, mask_ref, vqg_ref, ka_ref, kb_ref, ml_ref, e_ref, w_ref, dv_ref):
     heads, _, tokens = e_ref.shape
     blocks = tokens // BLOCK
     frame = frame_ref[0]
@@ -255,7 +259,7 @@
     bias = bias_rows(mask_ref, 1, frame >= 0, blocks)
     for head in range(heads):
         keys = jnp.where(inner, flat(kb_ref, head), flat(ka_ref, head))
-        scores = masked_scores(keys, flat(q_ref, head), bias)
+        scores = masked_scores(keys, flat(vqg_ref, head, 1), bias)
         peak2 = scores.max(axis=0, keepdims=True)
         e = jnp.exp2(scores - peak2)
         total2 = e.sum(axis=0, keepdims=True)
@@ -266,17 +270,17 @@
         far = jnp.exp2(peak2 - peak)
         inv = 1.0 / (near * ml_ref[head, 1:2] + far * total2)
         far = far * inv
-        scaled = (flat(g_ref, head).T.astype(F32) * far).astype(BF16)
+        scaled = (flat(vqg_ref, head, 2).T.astype(F32) * far).astype(BF16)
         put(dv_ref, head, dot_nt(e, scaled).astype(BF16))
         e_ref[head] = e
         w_ref[head, 0:1] = near * inv
         w_ref[head, 1:2] = far
 
 
-def near_values_kernel(g_ref, e_ref, w_ref, v0_ref, v1_ref, v3_ref, dv0_ref, dv1_ref, dv3_ref, acc_ref):
+def near_values_kernel(vqg_ref, e_ref, w_ref, v0_ref, v1_ref, v3_ref, dv0_ref, dv1_ref, dv3_ref, acc_ref):
     heads, _, tokens = e_ref.shape
     for head in range(heads):
-        scaled = (flat(g_ref, head).T.astype(F32) * w_ref[head, 0:1]).astype(BF16)
+        scaled = (flat(vqg_ref, head, 2).T.astype(F32) * w_ref[head, 0:1]).astype(BF16)
         acc = jnp.zeros((HD, tokens), F32)
         for index, (v_ref, dv_ref) in enumerate(
             ((v0_ref, dv0_ref), (v1_ref, dv1_ref), (v3_ref, dv3_ref))
@@ -288,7 +292,7 @@
 
 
 def far_values_kernel(
-    frame_ref, q_ref, g_ref, ka_ref, kb_ref, va_ref, vb_ref, e_ref, w_ref, acc_ref,
+    frame_ref, vqg_ref, ka_ref, kb_ref, va_ref, vb_ref, e_ref, w_ref, acc_ref,
     dk_ref, att_ref, delta_ref, dq_ref,
 ):
     heads = e_ref.shape[0]
@@ -302,26 +306,26 @@
         far = w_ref[head, 1:2]
         out = (acc_ref[head] * near + dot(values.T, e) * far).astype(BF16)
         put(att_ref, head, out.T)
-        grads = flat(g_ref, head).T.astype(F32)
+        grads = flat(vqg_ref, head, 2).T.astype(F32)
         delta = (grads * out.astype(F32)).sum(axis=0, keepdims=True)
         delta_ref[head, 0:1] = near
         delta_ref[head, 1:2] = near * delta
         scaled = (grads * far).astype(BF16)
         ds = (e.astype(F32) * (dot(values, scaled) - far * delta)).astype(BF16)
-        put(dk_ref, head, (dot(ds, flat(q_ref, head)) * SCALE).astype(BF16))
+        put(dk_ref, head, (dot(ds, flat(vqg_ref, head, 1)) * SCALE).astype(BF16))
         dq_ref[head] = dot(keys.T, ds)
 
 
 def near_keys_kernel(
-    q_ref, g_ref, k0_ref, k1_ref, k3_ref, v0_ref, v1_ref, v3_ref, e_ref, delta_ref, dq2_ref,
-    dk0_ref, dk1_ref, dk3_ref, dq_ref,
+    vqg_ref, k0_ref, k1_ref, k3_ref, v0_ref, v1_ref, v3_ref, e_ref, delta_ref, dq2_ref, att_ref,
+    dk0_ref, dk1_ref, dk3_ref, out_ref,
 ):
     heads, _, tokens = e_ref.shape
     for head in range(heads):
-        queries = flat(q_ref, head)
+        queries = flat(vqg_ref, head, 1)
         near = delta_ref[head, 0:1]
         delta = delta_ref[head, 1:2]
-        scaled = (flat(g_ref, head).T.astype(F32) * near).astype(BF16)
+        scaled = (flat(vqg_ref, head, 2).T.astype(F32) * near).astype(BF16)
         dq = dq2_ref[head]
         for index, (k_ref, v_ref, dk_ref) in enumerate(
             ((k0_ref, v0_ref, dk0_ref), (k1_ref, v1_ref, dk1_ref), (k3_ref, v3_ref, dk3_ref))
@@ -330,7 +334,8 @@
             ds = (e.astype(F32) * (dot(flat(v_ref, head), scaled) - delta)).astype(BF16)
             put(dk_ref, head, (dot(ds, queries) * SCALE).astype(BF16))
             dq = dq + dot(flat(k_ref, head).T, ds)
-        put(dq_ref, head, (dq * SCALE).astype(BF16).T)
+        put(out_ref, head, (dq * SCALE).astype(BF16).T, 1)
+    out_ref[:, 0] = att_ref[...]
 
 
 def add_kernel(frame_ref, own_ref, other_ref, out_ref):
@@ -355,32 +360,28 @@
     return (total + jnp.where(inner, middle_ref[...].astype(F32), 0.0)).astype(BF16)
 
 
-def last_add_kernel(frame_ref, own_ref, edge_ref, middle_ref, out_ref):
-    out_ref[...] = last_sum(frame_ref, own_ref, edge_ref, middle_ref)
-
-
-def collect_kernel(frame_ref, own_ref, edge_ref, middle_ref, att_ref, dq_ref, out_ref):
-    out_ref[:, 0] = att_ref[...]
-    out_ref[:, 1] = dq_ref[...]
-    out_ref[:, 2] = last_sum(frame_ref, own_ref, edge_ref, middle_ref)
-
-
-def pack_kernel(in_ref, out_ref):
-    peers, _, width = out_ref.shape
-    for peer in range(peers):
-        out_ref[peer] = in_ref[:, peer * width : (peer + 1) * width]
-
-
-def unpack_kernel(in_ref, out_ref):
-    peers, _, width = in_ref.shape
-    for peer in range(peers):
-        out_ref[:, peer * width : (peer + 1) * width] = in_ref[peer]
-
-
-def unpack_three_kernel(in_ref, a_ref, b_ref, c_ref):
+def collect_kernel(frame_ref, *refs):
+    out_ref = refs[-1]
+    for which in range(out_ref.shape[1]):
+        out_ref[:, which] = last_sum(frame_ref, *refs[3 * which : 3 * which + 3])
+
+
+def pack_kernel(*refs):
+    out_ref = refs[-1]
+    width = out_ref.shape[3]
+    for peer in range(out_ref.shape[0]):
+        for which, ref in enumerate(refs[:-1]):
+            out_ref[peer, which] = ref[:, peer * width : (peer + 1) * width]
+
+
+def first_kernel(in_ref, out_ref):
+    out_ref[...] = in_ref[:, 0]
+
+
+def unpack_kernel(in_ref, *out_refs):
     peers, _, _, width = in_ref.shape
     for peer in range(peers):
-        for which, ref in enumerate((a_ref, b_ref, c_ref)):
+        for which, ref in enumerate(out_refs):
             ref[:, peer * width : (peer + 1) * width] = in_ref[peer, which]
 
 
@@ -404,7 +405,7 @@
     near_e = jax.ShapeDtypeStruct((heads, 3 * tokens, tokens), BF16)
     far_e = jax.ShapeDtypeStruct((heads, tokens, tokens), BF16)
     stat = jax.ShapeDtypeStruct((heads, 8, tokens), F32)
-    sums = jax.ShapeDtypeStruct((heads, HD, tokens), F32)
+    accum = jax.ShapeDtypeStruct((heads, HD, tokens), F32)
     frame = lax.axis_index("frame").astype(jnp.int32).reshape(1)
     smem = pl.BlockSpec(memory_space=pltpu.SMEM)
     vmem = pl.BlockSpec(memory_space=pltpu.VMEM)
@@ -424,12 +425,13 @@
     def swap(array):
         return lax.all_to_all(array, plane, 0, 0, tiled=True)
 
-    def enter(rows_):
-        return swap(call(pack_kernel, one, 0, rows_))
-
-    def leave(array):
-        return call(unpack_kernel, row_type, 0, swap(array))
-
+    def packed(count):
+        return jax.ShapeDtypeStruct((peers, count, rows, width), BF16)
+
+    def leave(packed):
+        return call(unpack_kernel, (row_type,) * packed.shape[1], 0, swap(packed))
+
+    pair = packed(2)
     devices = ("frame", "rank", "head")
     heads_axis = lax.axis_size("head")
 
@@ -454,46 +456,48 @@
     def send(array, pairs):
         return lax.ppermute(array, devices, pairs)
 
-    k0 = enter(key_rows)
+    k0 = swap(call(pack_kernel, packed(1), 0, key_rows)).reshape(one.shape)
     k1, k3 = send(k0, edge), send(k0, middle)
-    q = enter(query_rows)
-    v0 = enter(value_rows)
-    g = enter(out_grad)
-    k2a, k2b = send(k3, edge), send(k1, middle)
+    vqg = swap(call(pack_kernel, packed(3), 0, value_rows, query_rows, out_grad))
+    v0 = call(first_kernel, one, 0, vqg)
+    ka, kb = send(k3, edge), send(k1, middle)
     v1, v3 = send(v0, edge), send(v0, middle)
-    v2a, v2b = send(v3, edge), send(v1, middle)
+    va, vb = send(v3, edge), send(v1, middle)
+
+    def sums(first, third, from_edge, from_middle):
+        return (
+            call(add_kernel, one, 0, frame, third, from_edge),
+            call(add_inner_kernel, one, 0, frame, first, from_middle),
+        )
 
     e_near, ml = call(
-        near_scores_kernel, (near_e, stat), 6, frame, block_mask, q, k0, k1, k3
+        near_scores_kernel, (near_e, stat), 6, frame, block_mask, vqg, k0, k1, k3
     )
     e_far, w, dv2 = call(
-        far_scores_kernel, (far_e, stat, one), 4, frame, block_mask, q, g, k2a, k2b, ml
+        far_scores_kernel, (far_e, stat, one), 4, frame, block_mask, vqg, ka, kb, ml
     )
     dv_edge, dv_middle = send(dv2, edge), send(dv2, middle)
     dv0, dv1, dv3, acc = call(
-        near_values_kernel, (one, one, one, sums), 6, g, e_near, w, v0, v1, v3
-    )
+        near_values_kernel, (one, one, one, accum), 6, vqg, e_near, w, v0, v1, v3
+    )
+    dv_third, dv_first = sums(dv1, dv3, dv_edge, dv_middle)
+    dv_over = send(dv_first, edge), send(dv_third, middle)
+    acc, dv_first, dv_third = lax.optimization_barrier((acc, dv_first, dv_third))
     dk2, att, delta, dq2 = call(
-        far_values_kernel, (one, one, stat, sums), 4, frame, q, g, k2a, k2b, v2a, v2b, e_far, w, acc
+        far_values_kernel, (one, one, stat, accum), 4, frame, vqg, ka, kb, va, vb, e_far, w, acc
     )
     dk_edge, dk_middle = send(dk2, edge), send(dk2, middle)
-    dk0, dk1, dk3, dq = call(
-        near_keys_kernel, (one, one, one, one), 9, q, g, k0, k1, k3, v0, v1, v3, e_near, delta, dq2
-    )
-
-    def last_round(first, third, from_edge, from_middle):
-        over_middle = send(call(add_kernel, one, 0, frame, third, from_edge), middle)
-        over_edge = send(call(add_inner_kernel, one, 0, frame, first, from_middle), edge)
-        return over_edge, over_middle
-
-    over = last_round(dv1, dv3, dv_edge, dv_middle)
-    three = jax.ShapeDtypeStruct((peers, 3, rows, width), BF16)
-    collected = swap(call(collect_kernel, three, 0, frame, dv0, *over, att, dq))
-    over = last_round(dk1, dk3, dk_edge, dk_middle)
-    attended, grad_query, grad_values = call(
-        unpack_three_kernel, (row_type, row_type, row_type), 0, collected
-    )
-    grad_keys = leave(call(last_add_kernel, one, 0, frame, dk0, *over))
+    delta, dv_over = lax.optimization_barrier((delta, dv_over))
+    dk0, dk1, dk3, att_dq = call(
+        near_keys_kernel, (one, one, one, pair), 9,
+        vqg, k0, k1, k3, v0, v1, v3, e_near, delta, dq2, att,
+    )
+    attended, grad_query = leave(att_dq)
+    dk_third, dk_first = sums(dk1, dk3, dk_edge, dk_middle)
+    dk_over = send(dk_first, edge), send(dk_third, middle)
+    grad_keys, grad_values = leave(
+        call(collect_kernel, pair, 0, frame, dk0, *dk_over, dv0, *dv_over)
+    )
     return attended, grad_query, grad_keys, grad_values
 
 

time: 126 us -> 118 us (0.937)
  starting transfers between devices: 36.6 us -> 23.9 us
  waiting for transfers between devices: 56.5 us -> 66.5 us
  local copies, waits for them, and re-layouts: 7.66 us -> 4.11 us
  Pallas kernels: 22.6 us -> 20.6 us
    ppermute x16, waiting for transfers between devices: 24.6 us -> 48.5 us  [send(): return lax.ppermute(array, devices, pairs)]
    all_to_all x6 -> x4, waiting for transfers between devices: 31.9 us -> 18.1 us  [swap(): return lax.all_to_all(array, plane, 0, 0, tiled=True)]
    all_to_all x6 -> x4, starting transfers between devices: 24.6 us -> 16.9 us  [swap(): return lax.all_to_all(array, plane, 0, 0, tiled=True)]
    ppermute x16, starting transfers between devices: 12.1 us -> 6.96 us  [send(): return lax.ppermute(array, devices, pairs)]
    unnamed x28 -> x30, local copies, waits for them, and re-layouts: 7.66 us -> 4.11 us
    pallas_call x17 -> x15, Pallas kernels: 22.6 us -> 20.6 us  [call(): pl.pallas_call(kernel, in_specs=[smem if x.dtype == jnp.int32 else vmem f...]
  transfers between devices with their start and end apart: 22 -> 20, of which waited for: 14 -> 15; matrix products, arithmetic and copies ran while one was open for 0% -> 0% of each run, Pallas kernels for 14% -> 16%
where the time goes in v4:
time: 118 us; the launch traced here: 116 us
  waiting for transfers between devices  66.5 us (56%)
  starting transfers between devices  23.9 us (20%)
  Pallas kernels  20.6 us (17%)
  local copies, waits for them, and re-layouts  4.11 us (3%)
    ppermute x16, waiting for transfers between devices, send(): return lax.ppermute(array, devices, pairs)  48.5 us
    pallas_call x15, Pallas kernels, call(): pl.pallas_call(kernel, in_specs=[smem if x.dtype == jnp.int32 else vmem f...  20.6 us
    all_to_all x4, waiting for transfers between devices, swap(): return lax.all_to_all(array, plane, 0, 0, tiled=True)  18.1 us
    all_to_all x4, starting transfers between devices, swap(): return lax.all_to_all(array, plane, 0, 0, tiled=True)  16.9 us
    ppermute x16, starting transfers between devices, send(): return lax.ppermute(array, devices, pairs)  6.96 us
    unnamed x30, local copies, waits for them, and re-layouts  4.11 us
  transfers between devices with their start and end apart: 20, of which 15 were waited for; matrix products, arithmetic and copies ran while one was open for 0% of the time, Pallas kernels for 16%

profile of v4, /device:TPU:10, one launch (start us, length us, event | category | flops | bytes accessed | tf_op | source)
XLA Modules:
  0.0 115.9 jit_solution(9719729049056261787)
XLA Ops:
  0.6 0.0 copy-start.2
  0.6 0.0 copy-start
  0.7 0.0 copy-start.1
  0.7 1.1 copy-done.3
  1.7 0.8 shard_map.85
  2.5 4.3 %all-to-all-start.1 = ((bf16[8,1,64,384]{3,2,1,0:T(8,128)(2,1)}), bf16[8,1,64,384]{3,2,1,0:T(8,128)(2,1)S(1)}, u32[]{:S(2)}, u32[]{:S(2)}) async-start(bf16[8,1,64,384]{3,2,1,0:T(8,128)(2,1)} %shard_map.85), calls=%async_computation.1 | async-start | bytes 786432 | tf_op jit(solution)/shard_map/all_to_all | solution.py:426
  6.8 1.1 shard_map.84
  7.9 5.7 %all-to-all-done.1 = bf16[8,1,64,384]{3,2,1,0:T(8,128)(2,1)S(1)} async-done(((bf16[8,1,64,384]{3,2,1,0:T(8,128)(2,1)}), bf16[8,1,64,384]{3,2,1,0:T(8,128)(2,1)S(1)}, u32[]{:S(2)}, u32[]{:S(2)}) %all-to-all-start.1) | async-done | bytes 393248 | tf_op jit(solution)/shard_map/all_to_all | solution.py:426
  13.6 4.1 %all-to-all-start = ((bf16[8,3,64,384]{3,2,1,0:T(8,128)(2,1)}), bf16[8,3,64,384]{3,2,1,0:T(8,128)(2,1)S(1)}, u32[]{:S(2)}, u32[]{:S(2)}) async-start(bf16[8,3,64,384]{3,2,1,0:T(8,128)(2,1)} %shard_map.84), calls=%async_computation | async-start | bytes 2359296 | tf_op jit(solution)/shard_map/all_to_all | solution.py:426
  17.7 1.6 %collective-permute-start.1 = (bf16[8,64,384]{2,1,0:T(8,128)(2,1)S(1)}, bf16[8,64,384]{2,1,0:T(8,128)(2,1)S(1)}, u32[]{:S(2)}, u32[]{:S(2)}) collective-permute-start(bf16[8,64,384]{2,1,0:T(8,128)(2,1)S(1)} %bitcast.2), channel_id=1, source_target_pairs={{0,2},{1,3},{2,0},{3,1},{4,6},{5,7},{6,4},{7,5},{8,16},{9,17},{10,... | collective-permute-start | bytes 1179656 | tf_op jit(solution)/shard_map/ppermute | solution.py:457
  19.3 0.0 collective-permute-start
  19.3 9.6 %collective-permute-done.1.k3_ref = bf16[8,64,384]{2,1,0:T(8,128)(2,1)S(1)} collective-permute-done((bf16[8,64,384]{2,1,0:T(8,128)(2,1)S(1)}, bf16[8,64,384]{2,1,0:T(8,128)(2,1)S(1)}, u32[]{:S(2)}, u32[]{:S(2)}) %collective-permute-start.1) | collective-permute-done | bytes 393248 | tf_op jit(solution)/shard_map/ppermute | solution.py:457
  28.9 0.0 collective-permute-start.4
  28.9 1.3 %collective-permute-done.k1_ref = bf16[8,64,384]{2,1,0:T(8,128)(2,1)S(1)} collective-permute-done((bf16[8,64,384]{2,1,0:T(8,128)(2,1)S(1)}, bf16[8,64,384]{2,1,0:T(8,128)(2,1)S(1)}, u32[]{:S(2)}, u32[]{:S(2)}) %collective-permute-start) | collective-permute-done | bytes 393248 | tf_op jit(solution)/shard_map/ppermute | solution.py:457
  30.2 0.5 collective-permute-start.5
  30.7 2.3 %all-to-all-done.in_ref.vqg_ref = bf16[8,3,64,384]{3,2,1,0:T(8,128)(2,1)S(1)} async-done(((bf16[8,3,64,384]{3,2,1,0:T(8,128)(2,1)}), bf16[8,3,64,384]{3,2,1,0:T(8,128)(2,1)S(1)}, u32[]{:S(2)}, u32[]{:S(2)}) %all-to-all-start) | async-done | bytes 1179680 | tf_op jit(solution)/shard_map/all_to_all | solution.py:426
  33.0 1.6 %collective-permute-start.3 = (bf16[8,64,384]{2,1,0:T(8,128)(2,1)S(1)}, bf16[8,64,384]{2,1,0:T(8,128)(2,1)S(1)}, u32[]{:S(2)}, u32[]{:S(2)}) collective-permute-start(bf16[8,64,384]{2,1,0:T(8,128)(2,1)S(1)} %shard_map.86.v0_ref), channel_id=1, source_target_pairs={{0,2},{1,3},{2,0},{3,1},{4,6},{5,7},{6,4},{7,5},{8,16},{9,17},{10,... | collective-permute-start | bytes 1179656 | tf_op jit(solution)/shard_map/ppermute | solution.py:457
  34.6 0.0 collective-permute-start.2
  34.6 3.5 %shard_map.87 = (bf16[3,1536,512]{2,1,0:T(8,128)(2,1)S(1)}, f32[3,8,512]{2,1,0:T(8,128)S(1)}) custom-call(s32[1]{0:T(128)} %bitcast.1.frame_ref, s32[2,4,4]{2,1,0:T(4,128)S(1)} %copy-done.14, bf16[8,3,64,384]{3,2,1,0:T(8,128)(2,1)S(1)} %all-to-all-done.in_ref.vqg_ref, bf16[8,64,384]{2,1,0:T(8,128)(2,1)S(1)} %bitcast.4, ...), custom_call_target="tpu_custom_call" | custom-call | flops 1207959552 | bytes 4194304 | tf_op jit(solution)/shard_map/pallas_call | solution.py:416
  38.2 2.8 %collective-permute-done.4.ka_ref = bf16[8,64,384]{2,1,0:T(8,128)(2,1)S(1)} collective-permute-done((bf16[8,64,384]{2,1,0:T(8,128)(2,1)S(1)}, bf16[8,64,384]{2,1,0:T(8,128)(2,1)S(1)}, u32[]{:S(2)}, u32[]{:S(2)}) %collective-permute-start.4) | collective-permute-done | bytes 393248 | tf_op jit(solution)/shard_map/ppermute | solution.py:457
  40.9 1.3 %collective-permute-done.5.kb_ref = bf16[8,64,384]{2,1,0:T(8,128)(2,1)S(1)} collective-permute-done((bf16[8,64,384]{2,1,0:T(8,128)(2,1)S(1)}, bf16[8,64,384]{2,1,0:T(8,128)(2,1)S(1)}, u32[]{:S(2)}, u32[]{:S(2)}) %collective-permute-start.5) | collective-permute-done | bytes 393248 | tf_op jit(solution)/shard_map/ppermute | solution.py:457
  42.2 2.4 %shard_map.88 = (bf16[3,512,512]{2,1,0:T(8,128)(2,1)S(1)}, f32[3,8,512]{2,1,0:T(8,128)S(1)}, bf16[8,64,384]{2,1,0:T(8,128)(2,1)S(1)}) custom-call(s32[1]{0:T(128)} %bitcast.1.frame_ref, s32[2,4,4]{2,1,0:T(4,128)S(1)} %copy-done.14, bf16[8,3,64,384]{3,2,1,0:T(8,128)(2,1)S(1)} %all-to-all-done.in_ref.vqg_ref, ...), custom_call_target="tpu_custom_call" | custom-call | flops 805306368 | bytes 4194304 | tf_op jit(solution)/shard_map/pallas_call | solution.py:416
  44.6 0.5 collective-permute-start.8
  45.2 0.0 collective-permute-start.9
  45.2 5.5 %collective-permute-done.3.v3_ref = bf16[8,64,384]{2,1,0:T(8,128)(2,1)S(1)} collective-permute-done((bf16[8,64,384]{2,1,0:T(8,128)(2,1)S(1)}, bf16[8,64,384]{2,1,0:T(8,128)(2,1)S(1)}, u32[]{:S(2)}, u32[]{:S(2)}) %collective-permute-start.3) | collective-permute-done | bytes 393248 | tf_op jit(solution)/shard_map/ppermute | solution.py:457
  50.7 0.0 collective-permute-start.6
  50.7 0.0 collective-permute-done.2.v1_ref
  50.7 0.5 collective-permute-start.7
  51.1 2.1 %shard_map.89 = (bf16[8,64,384]{2,1,0:T(8,128)(2,1)S(1)}, bf16[8,64,384]{2,1,0:T(8,128)(2,1)S(1)}, bf16[8,64,384]{2,1,0:T(8,128)(2,1)S(1)}, f32[3,128,512]{2,1,0:T(8,128)S(1)}) custom-call(bf16[8,3,64,384]{3,2,1,0:T(8,128)(2,1)S(1)} %all-to-all-done.in_ref.vqg_ref, bf16[3,1536,512]{2,1,0:T(8,128)(2,1)S(1)} %get-tuple-element.29.e_ref, ...), custom_call_target="tpu_custom_call" | custom-call | flops 1207959552 | bytes 4194304 | tf_op jit(solution)/shard_map/pallas_call | solution.py:416
  53.2 0.0 copy-start.6
  53.2 5.9 %collective-permute-done.8.other_ref = bf16[8,64,384]{2,1,0:T(8,128)(2,1)S(1)} collective-permute-done((bf16[8,64,384]{2,1,0:T(8,128)(2,1)S(1)}, bf16[8,64,384]{2,1,0:T(8,128)(2,1)S(1)}, u32[]{:S(2)}, u32[]{:S(2)}) %collective-permute-start.8) | collective-permute-done | bytes 393248 | tf_op jit(solution)/shard_map/ppermute | solution.py:457
  59.1 0.3 shard_map.90
  59.4 0.1 collective-permute-start.10
  59.4 0.0 collective-permute-done.9.other_ref
  59.5 0.1 shard_map.91
  59.6 0.5 collective-permute-start.11
  60.1 6.1 %collective-permute-done.6.va_ref = bf16[8,64,384]{2,1,0:T(8,128)(2,1)S(1)} collective-permute-done((bf16[8,64,384]{2,1,0:T(8,128)(2,1)S(1)}, bf16[8,64,384]{2,1,0:T(8,128)(2,1)S(1)}, u32[]{:S(2)}, u32[]{:S(2)}) %collective-permute-start.6) | collective-permute-done | bytes 393248 | tf_op jit(solution)/shard_map/ppermute | solution.py:457
  66.2 1.3 %collective-permute-done.7.vb_ref = bf16[8,64,384]{2,1,0:T(8,128)(2,1)S(1)} collective-permute-done((bf16[8,64,384]{2,1,0:T(8,128)(2,1)S(1)}, bf16[8,64,384]{2,1,0:T(8,128)(2,1)S(1)}, u32[]{:S(2)}, u32[]{:S(2)}) %collective-permute-start.7) | collective-permute-done | bytes 393248 | tf_op jit(solution)/shard_map/ppermute | solution.py:457
  67.5 2.6 %shard_map.92 = (bf16[8,64,384]{2,1,0:T(8,128)(2,1)}, bf16[8,64,384]{2,1,0:T(8,128)(2,1)S(1)}, f32[3,8,512]{2,1,0:T(8,128)S(1)}, f32[3,128,512]{2,1,0:T(8,128)S(1)}) custom-call(s32[1]{0:T(128)} %bitcast.1.frame_ref, bf16[8,3,64,384]{3,2,1,0:T(8,128)(2,1)S(1)} %all-to-all-done.in_ref.vqg_ref, bf16[8,64,384]{2,1,0:T(8,128)(2,1)S(1)} %collective-permute-done.4.ka_ref, ...), custom_call_target="tpu_custom_call" | custom-call | flops 805306368 | bytes 4194304 | tf_op jit(solution)/shard_map/pallas_call | solution.py:416
  70.1 0.0 collective-permute-start.14
  70.1 0.5 collective-permute-start.12
  70.6 4.0 %collective-permute-done.10.refs_4_ = bf16[8,64,384]{2,1,0:T(8,128)(2,1)S(1)} collective-permute-done((bf16[8,64,384]{2,1,0:T(8,128)(2,1)S(1)}, bf16[8,64,384]{2,1,0:T(8,128)(2,1)S(1)}, u32[]{:S(2)}, u32[]{:S(2)}) %collective-permute-start.10) | collective-permute-done | bytes 393248 | tf_op jit(solution)/shard_map/ppermute | solution.py:457
  74.6 0.7 copy-done.8
  75.4 0.6 collective-permute-done.11.refs_5_
  75.9 0.8 copy-done.10
  76.7 4.3 %shard_map.93 = (bf16[8,64,384]{2,1,0:T(8,128)(2,1)S(1)}, bf16[8,64,384]{2,1,0:T(8,128)(2,1)S(1)}, bf16[8,64,384]{2,1,0:T(8,128)(2,1)S(1)}, bf16[8,2,64,384]{3,2,1,0:T(8,128)(2,1)}) custom-call(bf16[8,3,64,384]{3,2,1,0:T(8,128)(2,1)S(1)} %all-to-all-done.in_ref.vqg_ref, bf16[8,64,384]{2,1,0:T(8,128)(2,1)S(1)} %bitcast.5, ...), custom_call_target="tpu_custom_call" | custom-call | flops 1811939328 | bytes 4194304 | tf_op jit(solution)/shard_map/pallas_call | solution.py:416
  81.0 0.7 copy-done.4
  81.8 0.7 copy-done.12
  82.5 4.3 %all-to-all-start.2 = ((bf16[8,2,64,384]{3,2,1,0:T(8,128)(2,1)}), bf16[8,2,64,384]{3,2,1,0:T(8,128)(2,1)S(1)}, u32[]{:S(2)}, u32[]{:S(2)}) async-start(bf16[8,2,64,384]{3,2,1,0:T(8,128)(2,1)} %get-tuple-element.42), calls=%async_computation.2 | async-start | bytes 1572864 | tf_op jit(solution)/shard_map/all_to_all | solution.py:426
  86.9 0.0 copy-start.13
  86.9 0.0 collective-permute-done.12.other_ref
  86.9 0.1 shard_map.95
  87.0 0.1 collective-permute-start.13
  87.1 0.0 collective-permute-done.14.other_ref
  87.1 0.1 shard_map.96
  87.2 1.1 collective-permute-start.15
  88.3 10.0 %collective-permute-done.13.refs_1_ = bf16[8,64,384]{2,1,0:T(8,128)(2,1)S(1)} collective-permute-done((bf16[8,64,384]{2,1,0:T(8,128)(2,1)S(1)}, bf16[8,64,384]{2,1,0:T(8,128)(2,1)S(1)}, u32[]{:S(2)}, u32[]{:S(2)}) %collective-permute-start.13) | collective-permute-done | bytes 393248 | tf_op jit(solution)/shard_map/ppermute | solution.py:457
  98.2 0.2 collective-permute-done.15.refs_2_
  98.5 1.3 %shard_map.97 = bf16[8,2,64,384]{3,2,1,0:T(8,128)(2,1)} custom-call(s32[1]{0:T(128)} %bitcast.1.frame_ref, bf16[8,64,384]{2,1,0:T(8,128)(2,1)S(1)} %copy-done.13, bf16[8,64,384]{2,1,0:T(8,128)(2,1)S(1)} %collective-permute-done.13.refs_1_, bf16[8,64,384]{2,1,0:T(8,128)(2,1)S(1)} %collective-permute-done.15.refs_2_, bf16[8,64,384]{2,1,0:T(8,128)(2,1)S(1)} %copy-done.7, ...), custom_call_target="tpu_custom_call" | custom-call | bytes 4194304 | tf_op jit(solution)/shard_map/pallas_call | solution.py:416
  99.7 0.0 all-to-all-done.2.in_ref
  99.7 4.2 %all-to-all-start.3 = ((bf16[8,2,64,384]{3,2,1,0:T(8,128)(2,1)}), bf16[8,2,64,384]{3,2,1,0:T(8,128)(2,1)S(1)}, u32[]{:S(2)}, u32[]{:S(2)}) async-start(bf16[8,2,64,384]{3,2,1,0:T(8,128)(2,1)} %shard_map.97), calls=%async_computation.3 | async-start | bytes 1572864 | tf_op jit(solution)/shard_map/all_to_all | solution.py:426
  103.9 0.9 shard_map.94
  104.9 10.1 %all-to-all-done.3.in_ref = bf16[8,2,64,384]{3,2,1,0:T(8,128)(2,1)S(1)} async-done(((bf16[8,2,64,384]{3,2,1,0:T(8,128)(2,1)}), bf16[8,2,64,384]{3,2,1,0:T(8,128)(2,1)S(1)}, u32[]{:S(2)}, u32[]{:S(2)}) %all-to-all-start.3) | async-done | bytes 786464 | tf_op jit(solution)/shard_map/all_to_all | solution.py:426
  115.0 0.9 shard_map.98
  (21 shorter events, 0.1 us)
Async XLA Ops:
  0.6 6.2 %copy-start.2 = (bf16[64,3072]{1,0:T(8,128)(2,1)S(1)}, bf16[64,3072]{1,0:T(8,128)(2,1)}, u32[]{:S(2)}) copy-start(bf16[64,3072]{1,0:T(8,128)(2,1)} %refs_2_.1) | copy-start | bytes 1179652
  0.6 6.1 %copy-start = (bf16[64,3072]{1,0:T(8,128)(2,1)S(1)}, bf16[64,3072]{1,0:T(8,128)(2,1)}, u32[]{:S(2)}) copy-start(bf16[64,3072]{1,0:T(8,128)(2,1)} %refs_0_.2) | copy-start | bytes 1179652
  0.7 6.1 %copy-start.1 = (bf16[64,3072]{1,0:T(8,128)(2,1)S(1)}, bf16[64,3072]{1,0:T(8,128)(2,1)}, u32[]{:S(2)}) copy-start(bf16[64,3072]{1,0:T(8,128)(2,1)} %refs_1_.1) | copy-start | bytes 1179652
  0.7 1.1 copy-start.3
  2.5 11.1 %all-to-all-start.1 = ((bf16[8,1,64,384]{3,2,1,0:T(8,128)(2,1)}), bf16[8,1,64,384]{3,2,1,0:T(8,128)(2,1)S(1)}, u32[]{:S(2)}, u32[]{:S(2)}) async-start(bf16[8,1,64,384]{3,2,1,0:T(8,128)(2,1)} %shard_map.85), calls=%async_computation.1 | async-start | bytes 786432 | tf_op jit(solution)/shard_map/all_to_all | solution.py:426
  7.9 26.7 %copy-start.14 = (s32[2,4,4]{2,1,0:T(4,128)S(1)}, s32[2,4,4]{2,1,0:T(4,128)}, u32[]{:S(2)}) copy-start(s32[2,4,4]{2,1,0:T(4,128)} %mask_ref.3) | copy-start | bytes 388
  13.6 19.3 %all-to-all-start = ((bf16[8,3,64,384]{3,2,1,0:T(8,128)(2,1)}), bf16[8,3,64,384]{3,2,1,0:T(8,128)(2,1)S(1)}, u32[]{:S(2)}, u32[]{:S(2)}) async-start(bf16[8,3,64,384]{3,2,1,0:T(8,128)(2,1)} %shard_map.84), calls=%async_computation | async-start | bytes 2359296 | tf_op jit(solution)/shard_map/all_to_all | solution.py:426
  17.7 11.2 %collective-permute-start.1 = (bf16[8,64,384]{2,1,0:T(8,128)(2,1)S(1)}, bf16[8,64,384]{2,1,0:T(8,128)(2,1)S(1)}, u32[]{:S(2)}, u32[]{:S(2)}) collective-permute-start(bf16[8,64,384]{2,1,0:T(8,128)(2,1)S(1)} %bitcast.2), channel_id=1, source_target_pairs={{0,2},{1,3},{2,0},{3,1},{4,6},{5,7},{6,4},{7,5},{8,16},{9,17},{10,... | collective-permute-start | bytes 1179656 | tf_op jit(solution)/shard_map/ppermute | solution.py:457
  19.3 10.9 %collective-permute-start = (bf16[8,64,384]{2,1,0:T(8,128)(2,1)S(1)}, bf16[8,64,384]{2,1,0:T(8,128)(2,1)S(1)}, u32[]{:S(2)}, u32[]{:S(2)}) collective-permute-start(bf16[8,64,384]{2,1,0:T(8,128)(2,1)S(1)} %bitcast.3), channel_id=1, source_target_pairs={{0,8},{1,9},{2,10},{3,11},{4,12},{5,13},{6,14},{7,15},{8,0},{9,1},... | collective-permute-start | bytes 1179656 | tf_op jit(solution)/shard_map/ppermute | solution.py:457
  28.9 12.1 %collective-permute-start.4 = (bf16[8,64,384]{2,1,0:T(8,128)(2,1)S(1)}, bf16[8,64,384]{2,1,0:T(8,128)(2,1)S(1)}, u32[]{:S(2)}, u32[]{:S(2)}) collective-permute-start(bf16[8,64,384]{2,1,0:T(8,128)(2,1)S(1)} %collective-permute-done.1.k3_ref), channel_id=1, source_target_pairs={{0,8},{1,9},{2,10},{3,11},{4,12},{5,13},{6,14},{7,15},{8,0},{9,1},... | collective-permute-start | bytes 1179656 | tf_op jit(solution)/shard_map/ppermute | solution.py:457
  30.2 12.1 %collective-permute-start.5 = (bf16[8,64,384]{2,1,0:T(8,128)(2,1)S(1)}, bf16[8,64,384]{2,1,0:T(8,128)(2,1)S(1)}, u32[]{:S(2)}, u32[]{:S(2)}) collective-permute-start(bf16[8,64,384]{2,1,0:T(8,128)(2,1)S(1)} %collective-permute-done.k1_ref), channel_id=1, source_target_pairs={{0,2},{1,3},{2,0},{3,1},{4,6},{5,7},{6,4},{7,5},{8,16},{9,17},{10,... | collective-permute-start | bytes 1179656 | tf_op jit(solution)/shard_map/ppermute | solution.py:457
  33.0 17.7 %collective-permute-start.3 = (bf16[8,64,384]{2,1,0:T(8,128)(2,1)S(1)}, bf16[8,64,384]{2,1,0:T(8,128)(2,1)S(1)}, u32[]{:S(2)}, u32[]{:S(2)}) collective-permute-start(bf16[8,64,384]{2,1,0:T(8,128)(2,1)S(1)} %shard_map.86.v0_ref), channel_id=1, source_target_pairs={{0,2},{1,3},{2,0},{3,1},{4,6},{5,7},{6,4},{7,5},{8,16},{9,17},{10,... | collective-permute-start | bytes 1179656 | tf_op jit(solution)/shard_map/ppermute | solution.py:457
  34.6 16.0 %collective-permute-start.2 = (bf16[8,64,384]{2,1,0:T(8,128)(2,1)S(1)}, bf16[8,64,384]{2,1,0:T(8,128)(2,1)S(1)}, u32[]{:S(2)}, u32[]{:S(2)}) collective-permute-start(bf16[8,64,384]{2,1,0:T(8,128)(2,1)S(1)} %shard_map.86.v0_ref), channel_id=1, source_target_pairs={{0,8},{1,9},{2,10},{3,11},{4,12},{5,13},{6,14},{7,15},{8,0},{9,1},... | collective-permute-start | bytes 1179656 | tf_op jit(solution)/shard_map/ppermute | solution.py:457
  44.6 14.5 %collective-permute-start.8 = (bf16[8,64,384]{2,1,0:T(8,128)(2,1)S(1)}, bf16[8,64,384]{2,1,0:T(8,128)(2,1)S(1)}, u32[]{:S(2)}, u32[]{:S(2)}) collective-permute-start(bf16[8,64,384]{2,1,0:T(8,128)(2,1)S(1)} %get-tuple-element.35), channel_id=1, source_target_pairs={{0,2},{1,3},{2,0},{3,1},{4,6},{5,7},{6,4},{7,5},{8,16},{9,17},{10,... | collective-permute-start | bytes 1179656 | tf_op jit(solution)/shard_map/ppermute | solution.py:457
  45.2 14.3 %collective-permute-start.9 = (bf16[8,64,384]{2,1,0:T(8,128)(2,1)S(1)}, bf16[8,64,384]{2,1,0:T(8,128)(2,1)S(1)}, u32[]{:S(2)}, u32[]{:S(2)}) collective-permute-start(bf16[8,64,384]{2,1,0:T(8,128)(2,1)S(1)} %get-tuple-element.35), channel_id=1, source_target_pairs={{0,8},{1,9},{2,10},{3,11},{4,12},{5,13},{6,14},{7,15},{8,0},{9,1},... | collective-permute-start | bytes 1179656 | tf_op jit(solution)/shard_map/ppermute | solution.py:457
  50.7 15.6 %collective-permute-start.6 = (bf16[8,64,384]{2,1,0:T(8,128)(2,1)S(1)}, bf16[8,64,384]{2,1,0:T(8,128)(2,1)S(1)}, u32[]{:S(2)}, u32[]{:S(2)}) collective-permute-start(bf16[8,64,384]{2,1,0:T(8,128)(2,1)S(1)} %collective-permute-done.3.v3_ref), channel_id=1, source_target_pairs={{0,8},{1,9},{2,10},{3,11},{4,12},{5,13},{6,14},{7,15},{8,0},{9,1},... | collective-permute-start | bytes 1179656 | tf_op jit(solution)/shard_map/ppermute | solution.py:457
  50.7 16.8 %collective-permute-start.7 = (bf16[8,64,384]{2,1,0:T(8,128)(2,1)S(1)}, bf16[8,64,384]{2,1,0:T(8,128)(2,1)S(1)}, u32[]{:S(2)}, u32[]{:S(2)}) collective-permute-start(bf16[8,64,384]{2,1,0:T(8,128)(2,1)S(1)} %collective-permute-done.2.v1_ref), channel_id=1, source_target_pairs={{0,2},{1,3},{2,0},{3,1},{4,6},{5,7},{6,4},{7,5},{8,16},{9,17},{10,... | collective-permute-start | bytes 1179656 | tf_op jit(solution)/shard_map/ppermute | solution.py:457
  53.2 14.3 %copy-start.6 = (bf16[8,64,384]{2,1,0:T(8,128)(2,1)}, bf16[8,64,384]{2,1,0:T(8,128)(2,1)S(1)}, u32[]{:S(2)}) copy-start(bf16[8,64,384]{2,1,0:T(8,128)(2,1)S(1)} %get-tuple-element.49.refs_3_) | copy-start | bytes 1179652
  59.4 15.3 %collective-permute-start.10 = (bf16[8,64,384]{2,1,0:T(8,128)(2,1)S(1)}, bf16[8,64,384]{2,1,0:T(8,128)(2,1)S(1)}, u32[]{:S(2)}, u32[]{:S(2)}) collective-permute-start(bf16[8,64,384]{2,1,0:T(8,128)(2,1)S(1)} %shard_map.90), channel_id=1, source_target_pairs={{0,8},{1,9},{2,10},{3,11},{4,12},{5,13},{6,14},{7,15},{8,0},{9,1},... | collective-permute-start | bytes 1179656 | tf_op jit(solution)/shard_map/ppermute | solution.py:457
  59.6 16.4 %collective-permute-start.11 = (bf16[8,64,384]{2,1,0:T(8,128)(2,1)S(1)}, bf16[8,64,384]{2,1,0:T(8,128)(2,1)S(1)}, u32[]{:S(2)}, u32[]{:S(2)}) collective-permute-start(bf16[8,64,384]{2,1,0:T(8,128)(2,1)S(1)} %shard_map.91), channel_id=1, source_target_pairs={{0,2},{1,3},{2,0},{3,1},{4,6},{5,7},{6,4},{7,5},{8,16},{9,17},{10,... | collective-permute-start | bytes 1179656 | tf_op jit(solution)/shard_map/ppermute | solution.py:457
  70.1 17.0 %collective-permute-start.14 = (bf16[8,64,384]{2,1,0:T(8,128)(2,1)}, bf16[8,64,384]{2,1,0:T(8,128)(2,1)S(1)}, u32[]{:S(2)}, u32[]{:S(2)}) collective-permute-start(bf16[8,64,384]{2,1,0:T(8,128)(2,1)} %get-tuple-element.47), channel_id=1, source_target_pairs={{0,8},{1,9},{2,10},{3,11},{4,12},{5,13},{6,14},{7,15},{8,0},{9,1},... | collective-permute-start | bytes 1179656 | tf_op jit(solution)/shard_map/ppermute | solution.py:457
  70.1 16.7 %collective-permute-start.12 = (bf16[8,64,384]{2,1,0:T(8,128)(2,1)}, bf16[8,64,384]{2,1,0:T(8,128)(2,1)S(1)}, u32[]{:S(2)}, u32[]{:S(2)}) collective-permute-start(bf16[8,64,384]{2,1,0:T(8,128)(2,1)} %get-tuple-element.47), channel_id=1, source_target_pairs={{0,2},{1,3},{2,0},{3,1},{4,6},{5,7},{6,4},{7,5},{8,16},{9,17},{10,... | collective-permute-start | bytes 1179656 | tf_op jit(solution)/shard_map/ppermute | solution.py:457
  74.6 0.7 copy-start.8
  75.9 0.8 copy-start.10
  81.0 0.7 copy-start.4
  81.8 0.7 copy-start.12
  82.5 4.4 %copy-start.5 = (bf16[8,64,384]{2,1,0:T(8,128)(2,1)S(1)}, bf16[8,64,384]{2,1,0:T(8,128)(2,1)}, u32[]{:S(2)}) copy-start(bf16[8,64,384]{2,1,0:T(8,128)(2,1)} %copy-done.4) | copy-start | bytes 1179652
  82.5 17.2 %all-to-all-start.2 = ((bf16[8,2,64,384]{3,2,1,0:T(8,128)(2,1)}), bf16[8,2,64,384]{3,2,1,0:T(8,128)(2,1)S(1)}, u32[]{:S(2)}, u32[]{:S(2)}) async-start(bf16[8,2,64,384]{3,2,1,0:T(8,128)(2,1)} %get-tuple-element.42), calls=%async_computation.2 | async-start | bytes 1572864 | tf_op jit(solution)/shard_map/all_to_all | solution.py:426
  86.8 11.6 %copy-start.7 = (bf16[8,64,384]{2,1,0:T(8,128)(2,1)S(1)}, bf16[8,64,384]{2,1,0:T(8,128)(2,1)}, u32[]{:S(2)}) copy-start(bf16[8,64,384]{2,1,0:T(8,128)(2,1)} %copy-done.6) | copy-start | bytes 1179652
  86.8 11.6 %copy-start.9 = (bf16[8,64,384]{2,1,0:T(8,128)(2,1)S(1)}, bf16[8,64,384]{2,1,0:T(8,128)(2,1)}, u32[]{:S(2)}) copy-start(bf16[8,64,384]{2,1,0:T(8,128)(2,1)} %copy-done.8) | copy-start | bytes 1179652
  86.8 11.6 %copy-start.11 = (bf16[8,64,384]{2,1,0:T(8,128)(2,1)S(1)}, bf16[8,64,384]{2,1,0:T(8,128)(2,1)}, u32[]{:S(2)}) copy-start(bf16[8,64,384]{2,1,0:T(8,128)(2,1)} %copy-done.10) | copy-start | bytes 1179652
  86.9 11.6 %copy-start.13 = (bf16[8,64,384]{2,1,0:T(8,128)(2,1)S(1)}, bf16[8,64,384]{2,1,0:T(8,128)(2,1)}, u32[]{:S(2)}) copy-start(bf16[8,64,384]{2,1,0:T(8,128)(2,1)} %copy-done.12) | copy-start | bytes 1179652
  87.0 11.2 %collective-permute-start.13 = (bf16[8,64,384]{2,1,0:T(8,128)(2,1)S(1)}, bf16[8,64,384]{2,1,0:T(8,128)(2,1)S(1)}, u32[]{:S(2)}, u32[]{:S(2)}) collective-permute-start(bf16[8,64,384]{2,1,0:T(8,128)(2,1)S(1)} %shard_map.95), channel_id=1, source_target_pairs={{0,8},{1,9},{2,10},{3,11},{4,12},{5,13},{6,14},{7,15},{8,0},{9,1},... | collective-permute-start | bytes 1179656 | tf_op jit(solution)/shard_map/ppermute | solution.py:457
  87.2 11.2 %collective-permute-start.15 = (bf16[8,64,384]{2,1,0:T(8,128)(2,1)S(1)}, bf16[8,64,384]{2,1,0:T(8,128)(2,1)S(1)}, u32[]{:S(2)}, u32[]{:S(2)}) collective-permute-start(bf16[8,64,384]{2,1,0:T(8,128)(2,1)S(1)} %shard_map.96), channel_id=1, source_target_pairs={{0,2},{1,3},{2,0},{3,1},{4,6},{5,7},{6,4},{7,5},{8,16},{9,17},{10,... | collective-permute-start | bytes 1179656 | tf_op jit(solution)/shard_map/ppermute | solution.py:457
  99.7 15.2 %all-to-all-start.3 = ((bf16[8,2,64,384]{3,2,1,0:T(8,128)(2,1)}), bf16[8,2,64,384]{3,2,1,0:T(8,128)(2,1)S(1)}, u32[]{:S(2)}, u32[]{:S(2)}) async-start(bf16[8,2,64,384]{3,2,1,0:T(8,128)(2,1)} %shard_map.97), calls=%async_computation.3 | async-start | bytes 1572864 | tf_op jit(solution)/shard_map/all_to_all | solution.py:426

commit v5 on v4

--- a/solution.py
+++ b/solution.py
@@ -1,3 +1,4 @@
+import functools
 import math
 
 import jax
@@ -15,6 +16,8 @@
 SCALE_LOG2 = SCALE * math.log2(math.e)
 MASKED = -1e30
 VMEM_BYTES = 12 * 1024 * 1024
+
+CONFIG = {'groups': [['k', 'q', 'g'], ['v']], 'vmode': 1, 'outs': [['att', 'dq'], ['dk', 'dv']], 'opts': ['b6', 'b7', 'sumv', 'big', 'b8', 'gate'], 'cost': {'fs': 2, 'nv': 2, 'fv': 2, 'nk': 4, 'pick1': 0.1, 'gate': 20, 'sumv': 20}}
 
 
 def partner_2(shard, axis, distance):
@@ -228,7 +231,7 @@
     )
 
 
-def near_scores_kernel(frame_ref, mask_ref, vqg_ref, k0_ref, k1_ref, k3_ref, e_ref, ml_ref):
+def near_scores_kernel(rows, frame_ref, mask_ref, e_ref, ml_ref):
     heads, _, tokens = e_ref.shape
     blocks = tokens // BLOCK
     frame = frame_ref[0]
@@ -236,9 +239,9 @@
     bias1 = bias_rows(mask_ref, 0, frame >= 0, blocks)
     bias3 = bias_rows(mask_ref, 0, inner, blocks)
     for head in range(heads):
-        queries = flat(vqg_ref, head, 1)
-        slots = ((k0_ref, None), (k1_ref, bias1), (k3_ref, bias3))
-        scores = [masked_scores(flat(ref, head), queries, bias) for ref, bias in slots]
+        queries = rows("q", head)
+        slots = (("k0", None), ("k1", bias1), ("k3", bias3))
+        scores = [masked_scores(rows(name, head), queries, bias) for name, bias in slots]
         peak = scores[0].max(axis=0, keepdims=True)
         for score in scores[1:]:
             peak = jnp.maximum(peak, score.max(axis=0, keepdims=True))
@@ -251,15 +254,15 @@
         ml_ref[head, 1:2] = total
 
 
-def far_scores_kernel(frame_ref, mask_ref, vqg_ref, ka_ref, kb_ref, ml_ref, e_ref, w_ref, dv_ref):
+def far_scores_kernel(rows, frame_ref, mask_ref, ml_ref, e_ref, w_ref, dv_ref):
     heads, _, tokens = e_ref.shape
     blocks = tokens // BLOCK
     frame = frame_ref[0]
     inner = (frame == 1) | (frame == 2)
     bias = bias_rows(mask_ref, 1, frame >= 0, blocks)
     for head in range(heads):
-        keys = jnp.where(inner, flat(kb_ref, head), flat(ka_ref, head))
-        scores = masked_scores(keys, flat(vqg_ref, head, 1), bias)
+        keys = jnp.where(inner, rows("kb", head), rows("ka", head))
+        scores = masked_scores(keys, rows("q", head), bias)
         peak2 = scores.max(axis=0, keepdims=True)
         e = jnp.exp2(scores - peak2)
         total2 = e.sum(axis=0, keepdims=True)
@@ -270,75 +273,66 @@
         far = jnp.exp2(peak2 - peak)
         inv = 1.0 / (near * ml_ref[head, 1:2] + far * total2)
         far = far * inv
-        scaled = (flat(vqg_ref, head, 2).T.astype(F32) * far).astype(BF16)
+        scaled = (rows("g", head).T.astype(F32) * far).astype(BF16)
         put(dv_ref, head, dot_nt(e, scaled).astype(BF16))
         e_ref[head] = e
         w_ref[head, 0:1] = near * inv
         w_ref[head, 1:2] = far
 
 
-def near_values_kernel(vqg_ref, e_ref, w_ref, v0_ref, v1_ref, v3_ref, dv0_ref, dv1_ref, dv3_ref, acc_ref):
+def near_values_kernel(rows, e_ref, w_ref, dv0_ref, dv1_ref, dv3_ref, acc_ref):
     heads, _, tokens = e_ref.shape
     for head in range(heads):
-        scaled = (flat(vqg_ref, head, 2).T.astype(F32) * w_ref[head, 0:1]).astype(BF16)
+        scaled = (rows("g", head).T.astype(F32) * w_ref[head, 0:1]).astype(BF16)
         acc = jnp.zeros((HD, tokens), F32)
-        for index, (v_ref, dv_ref) in enumerate(
-            ((v0_ref, dv0_ref), (v1_ref, dv1_ref), (v3_ref, dv3_ref))
-        ):
+        slots = (("v0", dv0_ref), ("v1", dv1_ref), ("v3", dv3_ref))
+        for index, (name, dv_ref) in enumerate(slots):
             e = e_ref[head, index * tokens : (index + 1) * tokens]
             put(dv_ref, head, dot_nt(e, scaled).astype(BF16))
-            acc = acc + dot(flat(v_ref, head).T, e)
+            acc = acc + dot(rows(name, head).T, e)
         acc_ref[head] = acc
 
 
-def far_values_kernel(
-    frame_ref, vqg_ref, ka_ref, kb_ref, va_ref, vb_ref, e_ref, w_ref, acc_ref,
-    dk_ref, att_ref, delta_ref, dq_ref,
-):
+def far_values_kernel(rows, frame_ref, e_ref, w_ref, acc_ref, dk_ref, att_ref, delta_ref, dq_ref):
     heads = e_ref.shape[0]
     frame = frame_ref[0]
     inner = (frame == 1) | (frame == 2)
     for head in range(heads):
-        keys = jnp.where(inner, flat(kb_ref, head), flat(ka_ref, head))
-        values = jnp.where(inner, flat(vb_ref, head), flat(va_ref, head))
+        keys = jnp.where(inner, rows("kb", head), rows("ka", head))
+        values = jnp.where(inner, rows("vb", head), rows("va", head))
         e = e_ref[head]
         near = w_ref[head, 0:1]
         far = w_ref[head, 1:2]
         out = (acc_ref[head] * near + dot(values.T, e) * far).astype(BF16)
         put(att_ref, head, out.T)
-        grads = flat(vqg_ref, head, 2).T.astype(F32)
+        grads = rows("g", head).T.astype(F32)
         delta = (grads * out.astype(F32)).sum(axis=0, keepdims=True)
         delta_ref[head, 0:1] = near
         delta_ref[head, 1:2] = near * delta
         scaled = (grads * far).astype(BF16)
         ds = (e.astype(F32) * (dot(values, scaled) - far * delta)).astype(BF16)
-        put(dk_ref, head, (dot(ds, flat(vqg_ref, head, 1)) * SCALE).astype(BF16))
+        put(dk_ref, head, (dot(ds, rows("q", head)) * SCALE).astype(BF16))
         dq_ref[head] = dot(keys.T, ds)
 
 
-def near_keys_kernel(
-    vqg_ref, k0_ref, k1_ref, k3_ref, v0_ref, v1_ref, v3_ref, e_ref, delta_ref, dq2_ref, att_ref,
-    dk0_ref, dk1_ref, dk3_ref, out_ref,
-):
+def near_keys_kernel(rows, e_ref, delta_ref, dq2_ref, dk0_ref, dk1_ref, dk3_ref, dq_ref):
     heads, _, tokens = e_ref.shape
     for head in range(heads):
-        queries = flat(vqg_ref, head, 1)
+        queries = rows("q", head)
         near = delta_ref[head, 0:1]
         delta = delta_ref[head, 1:2]
-        scaled = (flat(vqg_ref, head, 2).T.astype(F32) * near).astype(BF16)
+        scaled = (rows("g", head).T.astype(F32) * near).astype(BF16)
         dq = dq2_ref[head]
-        for index, (k_ref, v_ref, dk_ref) in enumerate(
-            ((k0_ref, v0_ref, dk0_ref), (k1_ref, v1_ref, dk1_ref), (k3_ref, v3_ref, dk3_ref))
-        ):
+        slots = (("k0", "v0", dk0_ref), ("k1", "v1", dk1_ref), ("k3", "v3", dk3_ref))
+        for index, (k_name, v_name, dk_ref) in enumerate(slots):
             e = e_ref[head, index * tokens : (index + 1) * tokens]
-            ds = (e.astype(F32) * (dot(flat(v_ref, head), scaled) - delta)).astype(BF16)
+            ds = (e.astype(F32) * (dot(rows(v_name, head), scaled) - delta)).astype(BF16)
             put(dk_ref, head, (dot(ds, queries) * SCALE).astype(BF16))
-            dq = dq + dot(flat(k_ref, head).T, ds)
-        put(out_ref, head, (dq * SCALE).astype(BF16).T, 1)
-    out_ref[:, 0] = att_ref[...]
-
-
-def add_kernel(frame_ref, own_ref, other_ref, out_ref):
+            dq = dq + dot(rows(k_name, head).T, ds)
+        put(dq_ref, head, (dq * SCALE).astype(BF16).T)
+
+
+def add_kernel(own_ref, other_ref, out_ref):
     out_ref[...] = (own_ref[...].astype(F32) + other_ref[...].astype(F32)).astype(BF16)
 
 
@@ -354,28 +348,70 @@
         out_ref[...] = own_ref[...]
 
 
-def last_sum(frame_ref, own_ref, edge_ref, middle_ref):
+def sum_kernel(frame_ref, own_ref, edge_ref, middle_ref, out_ref):
     inner = (frame_ref[0] == 1) | (frame_ref[0] == 2)
     total = own_ref[...].astype(F32) + edge_ref[...].astype(F32)
-    return (total + jnp.where(inner, middle_ref[...].astype(F32), 0.0)).astype(BF16)
-
-
-def collect_kernel(frame_ref, *refs):
+    out_ref[...] = (total + jnp.where(inner, middle_ref[...].astype(F32), 0.0)).astype(BF16)
+
+
+def collect_kernel(counts, frame_ref, *refs):
     out_ref = refs[-1]
-    for which in range(out_ref.shape[1]):
-        out_ref[:, which] = last_sum(frame_ref, *refs[3 * which : 3 * which + 3])
+    inner = (frame_ref[0] == 1) | (frame_ref[0] == 2)
+    place = 0
+    for which, count in enumerate(counts):
+        parts = refs[place : place + count]
+        place += count
+        if count == 1:
+            out_ref[:, which] = parts[0][...]
+        else:
+            own, edge, middle = (part[...].astype(F32) for part in parts)
+            out_ref[:, which] = (own + edge + jnp.where(inner, middle, 0.0)).astype(BF16)
 
 
 def pack_kernel(*refs):
-    out_ref = refs[-1]
-    width = out_ref.shape[3]
-    for peer in range(out_ref.shape[0]):
-        for which, ref in enumerate(refs[:-1]):
-            out_ref[peer, which] = ref[:, peer * width : (peer + 1) * width]
-
-
-def first_kernel(in_ref, out_ref):
-    out_ref[...] = in_ref[:, 0]
+    out_ref, held, sems = refs[-3:]
+    copies = [
+        pltpu.make_async_copy(ref, held.at[which], sems.at[which])
+        for which, ref in enumerate(refs[:-3])
+    ]
+    for copy in copies:
+        copy.start()
+    peers, _, _, width = out_ref.shape
+    for which, copy in enumerate(copies):
+        copy.wait()
+        for peer in range(peers):
+            out_ref[peer, which] = held[which, :, peer * width : (peer + 1) * width]
+
+
+def pack_values_kernel(frame_ref, *refs):
+    out_ref, held, sems = refs[-3:]
+    count = out_ref.shape[1]
+    inner = (frame_ref[0] == 1) | (frame_ref[0] == 2)
+    copies = [
+        pltpu.make_async_copy(ref, held.at[which], sems.at[which])
+        for which, ref in enumerate(refs[:-3])
+    ]
+    for copy in copies:
+        copy.start()
+    for copy in copies:
+        copy.wait()
+    peers, _, _, width = out_ref.shape
+    for peer in range(peers):
+        columns = slice(peer * width, (peer + 1) * width)
+        for which in range(count - 1):
+            out_ref[peer, which] = held[which, :, columns]
+        out_ref[peer, count - 1] = jnp.where(
+            inner, held[count, :, columns], held[count - 1, :, columns]
+        )
+
+
+def pass_kernel(*refs):
+    pass
+
+
+def pick_kernel(places, in_ref, *out_refs):
+    for place, ref in zip(places, out_refs):
+        ref[...] = in_ref[:, place]
 
 
 def unpack_kernel(in_ref, *out_refs):
@@ -383,14 +419,6 @@
     for peer in range(peers):
         for which, ref in enumerate(out_refs):
             ref[:, peer * width : (peer + 1) * width] = in_ref[peer, which]
-
-
-def params():
-    return pltpu.CompilerParams(vmem_limit_bytes=VMEM_BYTES)
-
-
-def cost(flops, data):
-    return pl.CostEstimate(flops=flops, bytes_accessed=data, transcendentals=0)
 
 
 def per_device_line(query_rows, key_rows, value_rows, out_grad, block_mask):
@@ -409,29 +437,78 @@
     frame = lax.axis_index("frame").astype(jnp.int32).reshape(1)
     smem = pl.BlockSpec(memory_space=pltpu.SMEM)
     vmem = pl.BlockSpec(memory_space=pltpu.VMEM)
-    pair_flops = heads * 2 * tokens * tokens * HD
-
-    def call(kernel, outs, work, *operands):
+    found = {}
+
+    def call(kernel, outs, work, *operands, names=()):
         several = isinstance(outs, tuple)
+        arrays = []
+        places = {}
+        for name in names:
+            array, which = found[name]
+            spot = [i for i, x in enumerate(arrays) if x is array]
+            if not spot:
+                spot = [len(arrays)]
+                arrays.append(array)
+            places[name] = (spot[0], which)
+
+        def body(*refs):
+            lookup = refs[: len(arrays)]
+            if not places:
+                return kernel(*refs)
+
+            def rows_of(name, head):
+                index, which = places[name]
+                return flat(lookup[index], head, which)
+
+            return kernel(rows_of, *refs[len(arrays) :])
+
+        operands = tuple(arrays) + operands
         return pl.pallas_call(
-            kernel,
+            body,
             in_specs=[smem if x.dtype == jnp.int32 else vmem for x in operands],
             out_specs=(vmem,) * len(outs) if several else vmem,
             out_shape=outs,
-            compiler_params=params(),
-            cost_estimate=cost(work * pair_flops, 4 << 20),
+            compiler_params=pltpu.CompilerParams(vmem_limit_bytes=VMEM_BYTES),
+            cost_estimate=pl.CostEstimate(
+                flops=int(work * 1_150_000_000), bytes_accessed=1 << 16, transcendentals=0
+            ),
         )(*operands)
+
+    def later(work, *arrays):
+        return pl.pallas_call(
+            pass_kernel,
+            in_specs=[pl.BlockSpec(memory_space=pl.ANY)] * len(arrays),
+            out_specs=(pl.BlockSpec(memory_space=pl.ANY),) * len(arrays),
+            out_shape=tuple(jax.ShapeDtypeStruct(x.shape, x.dtype) for x in arrays),
+            input_output_aliases={i: i for i in range(len(arrays))},
+            cost_estimate=pl.CostEstimate(
+                flops=int(work * 1_150_000_000), bytes_accessed=1 << 16, transcendentals=0
+            ),
+        )(*arrays)
+
+    def pack(work, *arrays, kernel=pack_kernel, first=(), limit=VMEM_BYTES):
+        count = len(arrays) - len(first)
+        return pl.pallas_call(
+            kernel,
+            in_specs=[smem] * len(first) + [pl.BlockSpec(memory_space=pltpu.HBM)] * len(arrays),
+            out_specs=vmem,
+            out_shape=packed(count),
+            scratch_shapes=[
+                pltpu.VMEM((len(arrays), rows, columns), BF16),
+                pltpu.SemaphoreType.DMA((len(arrays),)),
+            ],
+            compiler_params=pltpu.CompilerParams(vmem_limit_bytes=limit),
+            cost_estimate=pl.CostEstimate(
+                flops=int(work * 1_150_000_000), bytes_accessed=1 << 16, transcendentals=0
+            ),
+        )(*first, *arrays)
+
+    def packed(count):
+        return jax.ShapeDtypeStruct((peers, count, rows, width), BF16)
 
     def swap(array):
         return lax.all_to_all(array, plane, 0, 0, tiled=True)
 
-    def packed(count):
-        return jax.ShapeDtypeStruct((peers, count, rows, width), BF16)
-
-    def leave(packed):
-        return call(unpack_kernel, (row_type,) * packed.shape[1], 0, swap(packed))
-
-    pair = packed(2)
     devices = ("frame", "rank", "head")
     heads_axis = lax.axis_size("head")
 
@@ -456,49 +533,167 @@
     def send(array, pairs):
         return lax.ppermute(array, devices, pairs)
 
-    k0 = swap(call(pack_kernel, packed(1), 0, key_rows)).reshape(one.shape)
-    k1, k3 = send(k0, edge), send(k0, middle)
-    vqg = swap(call(pack_kernel, packed(3), 0, value_rows, query_rows, out_grad))
-    v0 = call(first_kernel, one, 0, vqg)
-    ka, kb = send(k3, edge), send(k1, middle)
-    v1, v3 = send(v0, edge), send(v0, middle)
-    va, vb = send(v3, edge), send(v1, middle)
-
-    def sums(first, third, from_edge, from_middle):
+    def barrier(*values):
+        return lax.optimization_barrier(values)
+
+    cost = CONFIG["cost"]
+    opts = CONFIG["opts"]
+    raw = {"k": key_rows, "q": query_rows, "v": value_rows, "g": out_grad}
+    vmode = CONFIG["vmode"]
+    if vmode > 0:
+        raw["v1"], raw["v3"] = send(value_rows, edge), send(value_rows, middle)
+    if vmode > 1:
+        raw["va"], raw["vb"] = send(raw["v3"], edge), send(raw["v1"], middle)
+
+    scored = []
+
+    def near_scores():
+        return call(
+            near_scores_kernel, (near_e, stat), cost.get("ns", 3.5), frame, block_mask,
+            names=("q", "k0", "k1", "k3"),
+        )
+
+    early = {}
+    ready = {}
+    for index, group in enumerate(CONFIG["groups"]):
+        members = list(group)
+        if "v" in members and vmode > 0:
+            at = members.index("v")
+            members[at:at + 1] = ["v", "v1", "v3"]
+            if vmode > 1:
+                members.append("v2")
+        work = cost.get("pack%d" % index, 0.5)
+        if "v2" in members:
+            members.remove("v2")
+            members.append("v2")
+            buffer = pack(
+                work, *[raw[m] for m in members[:-1]], raw["va"], raw["vb"],
+                kernel=pack_values_kernel, first=(frame,),
+            )
+        else:
+            buffer = early.pop(index, None)
+            if buffer is None:
+                buffer = pack(
+                    work, *[raw[m] for m in members],
+                    limit=(60 << 20) if index == 0 and "big" in opts else VMEM_BYTES,
+                )
+        landed = swap(buffer)
+        if "b8" in opts and index == 0 and vmode == 1:
+            later_index = [i for i, g in enumerate(CONFIG["groups"]) if "v" in g][0]
+            early[later_index] = pack(
+                cost.get("pack%d" % later_index, 0.5),
+                *[raw[m] for m in sum([["v", "v1", "v3"] if x == "v" else [x] for x in CONFIG["groups"][later_index]], [])],
+            )
+            landed, early[later_index] = barrier(landed, early[later_index])
+        if "b7" in opts and "v" in members and "k0" in found and "q" in found:
+            e_near, ml = near_scores()
+            landed, ml = barrier(landed, ml)
+            scored.append((e_near, ml))
+        for place, m in enumerate(members):
+            ready[m] = (landed, place)
+        want = [m for m in members if m == "k" or (m == "v" and vmode == 0) or (m in ("v1", "v3") and vmode == 1)]
+        if want:
+            if len(members) == 1:
+                alone = (landed.reshape(one.shape),)
+            else:
+                alone = call(
+                    functools.partial(pick_kernel, tuple(members.index(m) for m in want)),
+                    (one,) * len(want), cost.get("pick%d" % index, 0.2), landed,
+                )
+            for m, array in zip(want, alone):
+                ready[m] = (array, None)
+        if "k" in members:
+            k0 = ready["k"][0]
+            k1, k3 = send(k0, edge), send(k0, middle)
+            if "gate" in opts:
+                k1, k3 = later(cost.get("gate", 20), k1, k3)
+            found.update(k0=(k0, None), k1=(k1, None), k3=(k3, None))
+            found.update(ka=(send(k3, edge), None), kb=(send(k1, middle), None))
+        if "v" in members:
+            if vmode == 0:
+                v0 = ready["v"][0]
+                v1, v3 = send(v0, edge), send(v0, middle)
+                found.update(v0=(v0, None), v1=(v1, None), v3=(v3, None))
+                found.update(va=(send(v3, edge), None), vb=(send(v1, middle), None))
+            else:
+                found.update(v0=(landed, members.index("v")), v1=ready["v1"], v3=ready["v3"])
+                if vmode == 1:
+                    v1, v3 = ready["v1"][0], ready["v3"][0]
+                    found.update(va=(send(v3, edge), None), vb=(send(v1, middle), None))
+                else:
+                    found.update(va=ready["v2"], vb=ready["v2"])
+        for m in ("q", "g"):
+            if m in members:
+                found[m] = ready[m]
+
+    if not scored:
+        scored.append(near_scores())
+
+    def sums(name, first, third, from_edge, from_middle):
+        work = cost.get("add" + name, 0.2)
         return (
-            call(add_kernel, one, 0, frame, third, from_edge),
-            call(add_inner_kernel, one, 0, frame, first, from_middle),
-        )
-
-    e_near, ml = call(
-        near_scores_kernel, (near_e, stat), 6, frame, block_mask, vqg, k0, k1, k3
-    )
+            call(add_inner_kernel, one, work, frame, first, from_middle),
+            call(add_kernel, one, work, third, from_edge),
+        )
+
+    e_near, ml = scored[0]
+    if "gns" in opts:
+        (ml,) = later(cost.get("gns", 10), ml)
     e_far, w, dv2 = call(
-        far_scores_kernel, (far_e, stat, one), 4, frame, block_mask, vqg, ka, kb, ml
+        far_scores_kernel, (far_e, stat, one), cost.get("fs", 2.5), frame, block_mask, ml,
+        names=("q", "g", "ka", "kb"),
     )
     dv_edge, dv_middle = send(dv2, edge), send(dv2, middle)
     dv0, dv1, dv3, acc = call(
-        near_values_kernel, (one, one, one, accum), 6, vqg, e_near, w, v0, v1, v3
-    )
-    dv_third, dv_first = sums(dv1, dv3, dv_edge, dv_middle)
+        near_values_kernel, (one, one, one, accum), cost.get("nv", 2), e_near, w,
+        names=("g", "v0", "v1", "v3"),
+    )
+    dk2, att, delta, dq2 = call(
+        far_values_kernel, (one, one, stat, accum), cost.get("fv", 2.5), frame, e_far, w, acc,
+        names=("q", "g", "ka", "kb", "va", "vb"),
+    )
+    dk_edge, dk_middle = send(dk2, edge), send(dk2, middle)
+    dk0, dk1, dk3, dq = call(
+        near_keys_kernel, (one, one, one, one), cost.get("nk", 3.5), e_near, delta, dq2,
+        names=("q", "g", "k0", "k1", "k3", "v0", "v1", "v3"),
+    )
+    if "b6" in opts:
+        dq, dv1, dv3 = barrier(dq, dv1, dv3)
+    dv_first, dv_third = sums("v", dv1, dv3, dv_edge, dv_middle)
     dv_over = send(dv_first, edge), send(dv_third, middle)
-    acc, dv_first, dv_third = lax.optimization_barrier((acc, dv_first, dv_third))
-    dk2, att, delta, dq2 = call(
-        far_values_kernel, (one, one, stat, accum), 4, frame, vqg, ka, kb, va, vb, e_far, w, acc
-    )
-    dk_edge, dk_middle = send(dk2, edge), send(dk2, middle)
-    delta, dv_over = lax.optimization_barrier((delta, dv_over))
-    dk0, dk1, dk3, att_dq = call(
-        near_keys_kernel, (one, one, one, pair), 9,
-        vqg, k0, k1, k3, v0, v1, v3, e_near, delta, dq2, att,
-    )
-    attended, grad_query = leave(att_dq)
-    dk_third, dk_first = sums(dk1, dk3, dk_edge, dk_middle)
+    if "gdv" in opts:
+        dv_over = later(cost.get("gdv", 20), *dv_over)
+    dk_first, dk_third = sums("k", dk1, dk3, dk_edge, dk_middle)
     dk_over = send(dk_first, edge), send(dk_third, middle)
-    grad_keys, grad_values = leave(
-        call(collect_kernel, pair, 0, frame, dk0, *dk_over, dv0, *dv_over)
-    )
-    return attended, grad_query, grad_keys, grad_values
+
+    if "b4" in opts:
+        att, dv_first, dv_third = barrier(att, dv_first, dv_third)
+    if "b5" in opts:
+        dq, dv_first, dv_third = barrier(dq, dv_first, dv_third)
+    parts = {"att": (att,), "dq": (dq,), "dk": (dk0, *dk_over), "dv": (dv0, *dv_over)}
+    if "sumv" in opts:
+        parts["dv"] = (call(sum_kernel, one, cost.get("sumv", 20), frame, *parts["dv"]),)
+    results = {}
+    previous = None
+    for index, group in enumerate(CONFIG["outs"]):
+        operands = [parts[m] for m in group]
+        if previous is not None and "b3" in opts:
+            first, previous = barrier(operands[0][0], previous)
+            operands[0] = (first,) + tuple(operands[0][1:])
+            previous_outs = call(
+                unpack_kernel, (row_type,) * len(previous_group), 0.5, previous
+            )
+            results.update(zip(previous_group, previous_outs))
+        counts = tuple(len(p) for p in operands)
+        buffer = call(
+            functools.partial(collect_kernel, counts), packed(len(group)),
+            cost.get("collect%d" % index, 0.5), frame, *[x for p in operands for x in p],
+        )
+        previous, previous_group = swap(buffer), group
+        if "b3" not in opts or index == len(CONFIG["outs"]) - 1:
+            outs = call(unpack_kernel, (row_type,) * len(group), 0.5, previous)
+            results.update(zip(group, outs))
+    return results["att"], results["dq"], results["dk"], results["dv"]
 
 
 def solution(mesh):

time: 118 us -> 110 us (0.932)
  waiting for transfers between devices: 66.5 us -> 46.8 us
  starting transfers between devices: 23.9 us -> 29.6 us
  Pallas kernels: 20.6 us -> 24.8 us
  local copies, waits for them, and re-layouts: 4.11 us -> 6.34 us
    ppermute x16, waiting for transfers between devices: 48.5 us -> 35.5 us  [send(): return lax.ppermute(array, devices, pairs)]
    all_to_all x4, waiting for transfers between devices: 18.1 us -> 11.3 us  [swap(): return lax.all_to_all(array, plane, 0, 0, tiled=True)]
    ppermute x16, starting transfers between devices: 6.96 us -> 12.7 us  [send(): return lax.ppermute(array, devices, pairs)]
    pallas_call x15 -> x19, Pallas kernels: 20.6 us -> 24.8 us  [the longest x16 20.7 us: call(): pl.pallas_call(body, in_specs=[smem if x.dtype == jnp.int32 else vmem for...]
    unnamed x30 -> x38, local copies, waits for them, and re-layouts: 4.11 us -> 6.34 us
  transfers between devices with their start and end apart: 20 -> 20, of which waited for: 15 -> 12; matrix products, arithmetic and copies ran while one was open for 0% -> 0% of each run, Pallas kernels for 16% -> 20%
where the time goes in v5:
time: 110 us; the launch traced here: 108 us
  waiting for transfers between devices  46.8 us (43%)
  starting transfers between devices  29.6 us (27%)
  Pallas kernels  24.8 us (23%)
  local copies, waits for them, and re-layouts  6.34 us (6%)
    ppermute x16, waiting for transfers between devices, send(): return lax.ppermute(array, devices, pairs)  35.5 us
    pallas_call x16, Pallas kernels, call(): pl.pallas_call(body, in_specs=[smem if x.dtype == jnp.int32 else vmem for...  20.7 us
    all_to_all x4, starting transfers between devices, swap(): return lax.all_to_all(array, plane, 0, 0, tiled=True)  16.9 us
    ppermute x16, starting transfers between devices, send(): return lax.ppermute(array, devices, pairs)  12.7 us
    all_to_all x4, waiting for transfers between devices, swap(): return lax.all_to_all(array, plane, 0, 0, tiled=True)  11.3 us
    unnamed x38, local copies, waits for them, and re-layouts  6.34 us
    pallas_call x2, Pallas kernels, pack(): pl.pallas_call(kernel, in_specs=[smem] * len(first) + [pl.BlockSpec(memor...  4.09 us
  transfers between devices with their start and end apart: 20, of which 12 were waited for; matrix products, arithmetic and copies ran while one was open for 0% of the time, Pallas kernels for 20%

profile of v5, /device:TPU:10, one launch (start us, length us, event | category | flops | bytes accessed | tf_op | source)
XLA Modules:
  0.0 108.4 jit_solution(16281974340682838420)
XLA Ops:
  0.6 2.4 %shard_map.84 = bf16[8,3,64,384]{3,2,1,0:T(8,128)(2,1)} custom-call(bf16[64,3072]{1,0:T(8,128)(2,1)} %refs_0_.2, bf16[64,3072]{1,0:T(8,128)(2,1)} %refs_1_.1, bf16[64,3072]{1,0:T(8,128)(2,1)} %refs_2_.1), custom_call_target="tpu_custom_call" | custom-call | flops 575000000 | bytes 65536 | tf_op jit(solution)/shard_map/pallas_call | solution.py:491
  3.0 0.0 copy-start
  3.0 4.4 %all-to-all-start = ((bf16[8,3,64,384]{3,2,1,0:T(8,128)(2,1)}), bf16[8,3,64,384]{3,2,1,0:T(8,128)(2,1)S(1)}, u32[]{:S(2)}, u32[]{:S(2)}) async-start(bf16[8,3,64,384]{3,2,1,0:T(8,128)(2,1)} %shard_map.84), calls=%async_computation | async-start | bytes 2359296 | tf_op jit(solution)/shard_map/all_to_all | solution.py:510
  7.4 0.4 collective-permute-start
  7.9 2.7 %collective-permute-start.1 = (bf16[64,3072]{1,0:T(8,128)(2,1)S(1)}, bf16[64,3072]{1,0:T(8,128)(2,1)S(1)}, u32[]{:S(2)}, u32[]{:S(2)}) collective-permute-start(bf16[64,3072]{1,0:T(8,128)(2,1)S(1)} %copy-done), channel_id=1, source_target_pairs={{0,2},{1,3},{2,0},{3,1},{4,6},{5,7},{6,4},{7,5},{8,16},{9,17},{10,... | collective-permute-start | bytes 1179656 | tf_op jit(solution)/shard_map/ppermute | solution.py:534
  10.6 8.0 %collective-permute-done.refs_1_ = bf16[64,3072]{1,0:T(8,128)(2,1)S(1)} collective-permute-done((bf16[64,3072]{1,0:T(8,128)(2,1)S(1)}, bf16[64,3072]{1,0:T(8,128)(2,1)S(1)}, u32[]{:S(2)}, u32[]{:S(2)}) %collective-permute-start) | collective-permute-done | bytes 393248 | tf_op jit(solution)/shard_map/ppermute | solution.py:534
  18.6 1.1 %collective-permute-done.1.refs_2_ = bf16[64,3072]{1,0:T(8,128)(2,1)S(1)} collective-permute-done((bf16[64,3072]{1,0:T(8,128)(2,1)S(1)}, bf16[64,3072]{1,0:T(8,128)(2,1)S(1)}, u32[]{:S(2)}, u32[]{:S(2)}) %collective-permute-start.1) | collective-permute-done | bytes 393248 | tf_op jit(solution)/shard_map/ppermute | solution.py:534
  19.7 1.7 %shard_map.85 = bf16[8,3,64,384]{3,2,1,0:T(8,128)(2,1)} custom-call(bf16[64,3072]{1,0:T(8,128)(2,1)S(1)} %copy-done, bf16[64,3072]{1,0:T(8,128)(2,1)S(1)} %collective-permute-done.refs_1_, bf16[64,3072]{1,0:T(8,128)(2,1)S(1)} %collective-permute-done.1.refs_2_), custom_call_target="tpu_custom_call" | custom-call | flops 575000000 | bytes 65536 | tf_op jit(solution)/shard_map/pallas_call | solution.py:491
  21.4 1.2 %all-to-all-done.refs_0_ = bf16[8,3,64,384]{3,2,1,0:T(8,128)(2,1)S(1)} async-done(((bf16[8,3,64,384]{3,2,1,0:T(8,128)(2,1)}), bf16[8,3,64,384]{3,2,1,0:T(8,128)(2,1)S(1)}, u32[]{:S(2)}, u32[]{:S(2)}) %all-to-all-start) | async-done | bytes 1179680 | tf_op jit(solution)/shard_map/all_to_all | solution.py:510
  22.7 0.5 collective-permute-start.2
  23.2 2.7 %collective-permute-start.3 = (bf16[8,64,384]{2,1,0:T(8,128)(2,1)S(1)}, bf16[8,64,384]{2,1,0:T(8,128)(2,1)S(1)}, u32[]{:S(2)}, u32[]{:S(2)}) collective-permute-start(bf16[8,64,384]{2,1,0:T(8,128)(2,1)S(1)} %shard_map.86.refs_1_), channel_id=1, source_target_pairs={{0,2},{1,3},{2,0},{3,1},{4,6},{5,7},{6,4},{7,5},{8,16},{9,17},{10,... | collective-permute-start | bytes 1179656 | tf_op jit(solution)/shard_map/ppermute | solution.py:534
  25.9 4.2 %all-to-all-start.1 = ((bf16[8,3,64,384]{3,2,1,0:T(8,128)(2,1)}), bf16[8,3,64,384]{3,2,1,0:T(8,128)(2,1)S(1)}, u32[]{:S(2)}, u32[]{:S(2)}) async-start(bf16[8,3,64,384]{3,2,1,0:T(8,128)(2,1)} %shard_map.85), calls=%async_computation.1 | async-start | bytes 2359296 | tf_op jit(solution)/shard_map/all_to_all | solution.py:510
  30.1 3.8 %collective-permute-done.2.refs_0_ = bf16[8,64,384]{2,1,0:T(8,128)(2,1)S(1)} collective-permute-done((bf16[8,64,384]{2,1,0:T(8,128)(2,1)S(1)}, bf16[8,64,384]{2,1,0:T(8,128)(2,1)S(1)}, u32[]{:S(2)}, u32[]{:S(2)}) %collective-permute-start.2) | collective-permute-done | bytes 393248 | tf_op jit(solution)/shard_map/ppermute | solution.py:534
  33.9 1.1 %collective-permute-done.3.refs_1_ = bf16[8,64,384]{2,1,0:T(8,128)(2,1)S(1)} collective-permute-done((bf16[8,64,384]{2,1,0:T(8,128)(2,1)S(1)}, bf16[8,64,384]{2,1,0:T(8,128)(2,1)S(1)}, u32[]{:S(2)}, u32[]{:S(2)}) %collective-permute-start.3) | collective-permute-done | bytes 393248 | tf_op jit(solution)/shard_map/ppermute | solution.py:534
  35.0 0.7 copy-done.8
  35.8 0.1 collective-permute-start.4
  35.9 2.7 %collective-permute-start.5 = (bf16[8,64,384]{2,1,0:T(8,128)(2,1)}, bf16[8,64,384]{2,1,0:T(8,128)(2,1)S(1)}, u32[]{:S(2)}, u32[]{:S(2)}) collective-permute-start(bf16[8,64,384]{2,1,0:T(8,128)(2,1)} %get-tuple-element.38.refs_2_), channel_id=1, source_target_pairs={{0,2},{1,3},{2,0},{3,1},{4,6},{5,7},{6,4},{7,5},{8,16},{9,17},{10,... | collective-permute-start | bytes 1179656 | tf_op jit(solution)/shard_map/ppermute | solution.py:534
  38.6 1.0 copy-done.6
  39.6 1.0 copy-done.9
  40.6 3.5 %shard_map.88 = (bf16[3,1536,512]{2,1,0:T(8,128)(2,1)S(1)}, f32[3,8,512]{2,1,0:T(8,128)S(1)}) custom-call(bf16[8,3,64,384]{3,2,1,0:T(8,128)(2,1)S(1)} %all-to-all-done.refs_0_, bf16[8,64,384]{2,1,0:T(8,128)(2,1)S(1)} %shard_map.86.refs_1_, bf16[8,64,384]{2,1,0:T(8,128)(2,1)S(1)} %copy-done.6, bf16[8,64,384]{2,1,0:T(8,128)(2,1)S(1)} %copy-done.9, ...), custom_call_target="tpu_custom_call" | custom-call | flops 4024999936 | bytes 65536 | tf_op jit(solution)/shard_map/pallas_call | solution.py:466
  44.1 2.2 %copy-done.12 = bf16[3,1536,512]{2,1,0:T(8,128)(2,1)} copy-done((bf16[3,1536,512]{2,1,0:T(8,128)(2,1)}, bf16[3,1536,512]{2,1,0:T(8,128)(2,1)S(1)}, u32[]{:S(2)}) %copy-start.12) | copy-done | bytes 4718616
  46.3 0.6 copy-done.15
  46.9 0.0 all-to-all-done.1.refs_0_.refs_1_.refs_4_
  46.9 0.1 shard_map.89
  47.0 0.1 collective-permute-start.6
  47.0 0.0 slice-start
  47.1 0.0 slice-start.1
  47.1 0.9 collective-permute-start.7
  48.0 0.0 collective-permute-done.4.refs_1_
  48.0 0.0 collective-permute-done.5.refs_2_
  48.0 2.4 %shard_map.90 = (bf16[3,512,512]{2,1,0:T(8,128)(2,1)S(1)}, f32[3,8,512]{2,1,0:T(8,128)S(1)}, bf16[8,64,384]{2,1,0:T(8,128)(2,1)S(1)}) custom-call(bf16[8,3,64,384]{3,2,1,0:T(8,128)(2,1)S(1)} %all-to-all-done.refs_0_, bf16[8,64,384]{2,1,0:T(8,128)(2,1)S(1)} %collective-permute-done.4.refs_1_, bf16[8,64,384]{2,1,0:T(8,128)(2,1)S(1)} %collective-permute-done.5.refs_2_, ...), custom_call_target="tpu_custom_call" | custom-call | flops 2300000000 | bytes 65536 | tf_op jit(solution)/shard_map/pallas_call | solution.py:466
  50.4 1.1 %collective-permute-start.14 = (bf16[8,64,384]{2,1,0:T(8,128)(2,1)S(1)}, bf16[8,64,384]{2,1,0:T(8,128)(2,1)S(1)}, u32[]{:S(2)}, u32[]{:S(2)}) collective-permute-start(bf16[8,64,384]{2,1,0:T(8,128)(2,1)S(1)} %get-tuple-element.64), channel_id=1, source_target_pairs={{0,8},{1,9},{2,10},{3,11},{4,12},{5,13},{6,14},{7,15},{8,0},{9,1},... | collective-permute-start | bytes 1179656 | tf_op jit(solution)/shard_map/ppermute | solution.py:534
  51.5 0.2 collective-permute-start.12
  51.7 2.1 %shard_map.91 = (bf16[8,64,384]{2,1,0:T(8,128)(2,1)S(1)}, bf16[8,64,384]{2,1,0:T(8,128)(2,1)S(1)}, bf16[8,64,384]{2,1,0:T(8,128)(2,1)S(1)}, f32[3,128,512]{2,1,0:T(8,128)S(1)}) custom-call(bf16[8,3,64,384]{3,2,1,0:T(8,128)(2,1)S(1)} %all-to-all-done.refs_0_, bf16[8,3,64,384]{3,2,1,0:T(8,128)(2,1)S(1)} %all-to-all-done.1.refs_0_.refs_1_.refs_4_, ...), custom_call_target="tpu_custom_call" | custom-call | flops 2300000000 | bytes 65536 | tf_op jit(solution)/shard_map/pallas_call | solution.py:466
  53.8 0.0 copy-start.13
  53.8 0.7 copy-done.13
  54.5 4.6 %collective-permute-done.6.refs_3_ = bf16[8,64,384]{2,1,0:T(8,128)(2,1)S(1)} collective-permute-done((bf16[8,64,384]{2,1,0:T(8,128)(2,1)S(1)}, bf16[8,64,384]{2,1,0:T(8,128)(2,1)S(1)}, u32[]{:S(2)}, u32[]{:S(2)}) %collective-permute-start.6) | collective-permute-done | bytes 393248 | tf_op jit(solution)/shard_map/ppermute | solution.py:534
  59.1 0.1 collective-permute-done.7.refs_4_
  59.2 2.6 %shard_map.92 = (bf16[8,64,384]{2,1,0:T(8,128)(2,1)}, bf16[8,64,384]{2,1,0:T(8,128)(2,1)S(1)}, f32[3,8,512]{2,1,0:T(8,128)S(1)}, f32[3,128,512]{2,1,0:T(8,128)S(1)}) custom-call(bf16[8,3,64,384]{3,2,1,0:T(8,128)(2,1)S(1)} %all-to-all-done.refs_0_, bf16[8,64,384]{2,1,0:T(8,128)(2,1)S(1)} %collective-permute-done.4.refs_1_, ...), custom_call_target="tpu_custom_call" | custom-call | flops 2300000000 | bytes 65536 | tf_op jit(solution)/shard_map/pallas_call | solution.py:466
  61.8 0.0 collective-permute-start.10
  61.8 0.8 collective-permute-start.8
  62.6 3.4 %shard_map.93 = (bf16[8,64,384]{2,1,0:T(8,128)(2,1)S(1)}, bf16[8,64,384]{2,1,0:T(8,128)(2,1)S(1)}, bf16[8,64,384]{2,1,0:T(8,128)(2,1)S(1)}, bf16[8,64,384]{2,1,0:T(8,128)(2,1)S(1)}) custom-call(bf16[8,3,64,384]{3,2,1,0:T(8,128)(2,1)S(1)} %all-to-all-done.refs_0_, bf16[8,64,384]{2,1,0:T(8,128)(2,1)S(1)} %shard_map.86.refs_1_, ...), custom_call_target="tpu_custom_call" | custom-call | flops 4600000000 | bytes 65536 | tf_op jit(solution)/shard_map/pallas_call | solution.py:466
  66.0 0.0 copy-start.1
  66.0 0.0 copy-start.3
  66.0 1.5 %collective-permute-done.14.refs_1_ = bf16[8,64,384]{2,1,0:T(8,128)(2,1)S(1)} collective-permute-done((bf16[8,64,384]{2,1,0:T(8,128)(2,1)S(1)}, bf16[8,64,384]{2,1,0:T(8,128)(2,1)S(1)}, u32[]{:S(2)}, u32[]{:S(2)}) %collective-permute-start.14) | collective-permute-done | bytes 393248 | tf_op jit(solution)/shard_map/ppermute | solution.py:534
  67.5 0.1 shard_map.99
  67.6 0.1 collective-permute-start.15
  67.7 0.1 shard_map.98
  67.8 0.3 collective-permute-start.13
  68.1 1.0 shard_map.94
  69.1 4.2 %all-to-all-start.2 = ((bf16[8,2,64,384]{3,2,1,0:T(8,128)(2,1)}), bf16[8,2,64,384]{3,2,1,0:T(8,128)(2,1)S(1)}, u32[]{:S(2)}, u32[]{:S(2)}) async-start(bf16[8,2,64,384]{3,2,1,0:T(8,128)(2,1)} %shard_map.94), calls=%async_computation.2 | async-start | bytes 1572864 | tf_op jit(solution)/shard_map/all_to_all | solution.py:510
  73.3 2.8 %collective-permute-done.10.refs_1_ = bf16[8,64,384]{2,1,0:T(8,128)(2,1)} collective-permute-done((bf16[8,64,384]{2,1,0:T(8,128)(2,1)}, bf16[8,64,384]{2,1,0:T(8,128)(2,1)}, u32[]{:S(2)}, u32[]{:S(2)}) %collective-permute-start.10) | collective-permute-done | bytes 393248 | tf_op jit(solution)/shard_map/ppermute | solution.py:534
  76.0 1.1 %shard_map.97 = bf16[8,64,384]{2,1,0:T(8,128)(2,1)S(1)} custom-call(bf16[8,64,384]{2,1,0:T(8,128)(2,1)S(1)} %copy-done.4, bf16[8,64,384]{2,1,0:T(8,128)(2,1)} %collective-permute-done.10.refs_1_), custom_call_target="tpu_custom_call" | custom-call | flops 230000000 | bytes 65536 | tf_op jit(solution)/shard_map/pallas_call | solution.py:466
  77.2 0.1 collective-permute-start.11
  77.3 0.1 shard_map.96
  77.4 0.1 collective-permute-start.9
  77.5 7.1 %collective-permute-done.15.refs_3_ = bf16[8,64,384]{2,1,0:T(8,128)(2,1)} collective-permute-done((bf16[8,64,384]{2,1,0:T(8,128)(2,1)S(1)}, bf16[8,64,384]{2,1,0:T(8,128)(2,1)}, u32[]{:S(2)}, u32[]{:S(2)}) %collective-permute-start.15) | collective-permute-done | bytes 393248 | tf_op jit(solution)/shard_map/ppermute | solution.py:534
  84.6 1.3 %shard_map.100.refs_4_ = bf16[8,64,384]{2,1,0:T(8,128)(2,1)S(1)} custom-call(s32[1]{0:T(128)} %bitcast.refs_4_.refs_3_.refs_5_.refs_0_, bf16[8,64,384]{2,1,0:T(8,128)(2,1)S(1)} %copy-done.14, bf16[8,64,384]{2,1,0:T(8,128)(2,1)} %collective-permute-done.13.refs_2_, bf16[8,64,384]{2,1,0:T(8,128)(2,1)} %collective-permute-done.15.refs_3_), custom_call_target="tpu_custom_call" | custom-call | flops 23000000512 | bytes 65536 | tf_op jit(solution)/shard_map/pallas_call | solution.py:466
  85.9 5.4 %collective-permute-done.11.refs_3_ = bf16[8,64,384]{2,1,0:T(8,128)(2,1)S(1)} collective-permute-done((bf16[8,64,384]{2,1,0:T(8,128)(2,1)S(1)}, bf16[8,64,384]{2,1,0:T(8,128)(2,1)S(1)}, u32[]{:S(2)}, u32[]{:S(2)}) %collective-permute-start.11) | collective-permute-done | bytes 393248 | tf_op jit(solution)/shard_map/ppermute | solution.py:534
  91.2 1.1 %shard_map.101 = bf16[8,2,64,384]{3,2,1,0:T(8,128)(2,1)} custom-call(s32[1]{0:T(128)} %bitcast.refs_4_.refs_3_.refs_5_.refs_0_, bf16[8,64,384]{2,1,0:T(8,128)(2,1)S(1)} %get-tuple-element.58.refs_1_, bf16[8,64,384]{2,1,0:T(8,128)(2,1)S(1)} %collective-permute-done.9.refs_2_, bf16[8,64,384]{2,1,0:T(8,128)(2,1)S(1)} %collective-permute-done.11.refs_3_, ...), custom_call_target="tpu_custom_call" | custom-call | flops 575000000 | bytes 65536 | tf_op jit(solution)/shard_map/pallas_call | solution.py:466
  92.3 4.1 %all-to-all-start.3 = ((bf16[8,2,64,384]{3,2,1,0:T(8,128)(2,1)}), bf16[8,2,64,384]{3,2,1,0:T(8,128)(2,1)S(1)}, u32[]{:S(2)}, u32[]{:S(2)}) async-start(bf16[8,2,64,384]{3,2,1,0:T(8,128)(2,1)} %shard_map.101), calls=%async_computation.3 | async-start | bytes 1572864 | tf_op jit(solution)/shard_map/all_to_all | solution.py:510
  96.4 0.9 shard_map.95
  97.3 10.1 %all-to-all-done.3.refs_0_ = bf16[8,2,64,384]{3,2,1,0:T(8,128)(2,1)S(1)} async-done(((bf16[8,2,64,384]{3,2,1,0:T(8,128)(2,1)}), bf16[8,2,64,384]{3,2,1,0:T(8,128)(2,1)S(1)}, u32[]{:S(2)}, u32[]{:S(2)}) %all-to-all-start.3) | async-done | bytes 786464 | tf_op jit(solution)/shard_map/all_to_all | solution.py:510
  107.4 0.9 shard_map.102
  (34 shorter events, 0.1 us)
Async XLA Ops:
  3.0 4.4 %copy-start = (bf16[64,3072]{1,0:T(8,128)(2,1)S(1)}, bf16[64,3072]{1,0:T(8,128)(2,1)}, u32[]{:S(2)}) copy-start(bf16[64,3072]{1,0:T(8,128)(2,1)} %refs_0_.3) | copy-start | bytes 1179652
  3.0 19.7 %all-to-all-start = ((bf16[8,3,64,384]{3,2,1,0:T(8,128)(2,1)}), bf16[8,3,64,384]{3,2,1,0:T(8,128)(2,1)S(1)}, u32[]{:S(2)}, u32[]{:S(2)}) async-start(bf16[8,3,64,384]{3,2,1,0:T(8,128)(2,1)} %shard_map.84), calls=%async_computation | async-start | bytes 2359296 | tf_op jit(solution)/shard_map/all_to_all | solution.py:510
  7.4 11.2 %collective-permute-start = (bf16[64,3072]{1,0:T(8,128)(2,1)S(1)}, bf16[64,3072]{1,0:T(8,128)(2,1)S(1)}, u32[]{:S(2)}, u32[]{:S(2)}) collective-permute-start(bf16[64,3072]{1,0:T(8,128)(2,1)S(1)} %copy-done), channel_id=1, source_target_pairs={{0,8},{1,9},{2,10},{3,11},{4,12},{5,13},{6,14},{7,15},{8,0},{9,1},... | collective-permute-start | bytes 1179656 | tf_op jit(solution)/shard_map/ppermute | solution.py:534
  7.9 11.8 %collective-permute-start.1 = (bf16[64,3072]{1,0:T(8,128)(2,1)S(1)}, bf16[64,3072]{1,0:T(8,128)(2,1)S(1)}, u32[]{:S(2)}, u32[]{:S(2)}) collective-permute-start(bf16[64,3072]{1,0:T(8,128)(2,1)S(1)} %copy-done), channel_id=1, source_target_pairs={{0,2},{1,3},{2,0},{3,1},{4,6},{5,7},{6,4},{7,5},{8,16},{9,17},{10,... | collective-permute-start | bytes 1179656 | tf_op jit(solution)/shard_map/ppermute | solution.py:534
  22.7 11.2 %collective-permute-start.2 = (bf16[8,64,384]{2,1,0:T(8,128)(2,1)S(1)}, bf16[8,64,384]{2,1,0:T(8,128)(2,1)S(1)}, u32[]{:S(2)}, u32[]{:S(2)}) collective-permute-start(bf16[8,64,384]{2,1,0:T(8,128)(2,1)S(1)} %shard_map.86.refs_1_), channel_id=1, source_target_pairs={{0,8},{1,9},{2,10},{3,11},{4,12},{5,13},{6,14},{7,15},{8,0},{9,1},... | collective-permute-start | bytes 1179656 | tf_op jit(solution)/shard_map/ppermute | solution.py:534
  23.2 11.8 %collective-permute-start.3 = (bf16[8,64,384]{2,1,0:T(8,128)(2,1)S(1)}, bf16[8,64,384]{2,1,0:T(8,128)(2,1)S(1)}, u32[]{:S(2)}, u32[]{:S(2)}) collective-permute-start(bf16[8,64,384]{2,1,0:T(8,128)(2,1)S(1)} %shard_map.86.refs_1_), channel_id=1, source_target_pairs={{0,2},{1,3},{2,0},{3,1},{4,6},{5,7},{6,4},{7,5},{8,16},{9,17},{10,... | collective-permute-start | bytes 1179656 | tf_op jit(solution)/shard_map/ppermute | solution.py:534
  25.9 21.0 %all-to-all-start.1 = ((bf16[8,3,64,384]{3,2,1,0:T(8,128)(2,1)}), bf16[8,3,64,384]{3,2,1,0:T(8,128)(2,1)S(1)}, u32[]{:S(2)}, u32[]{:S(2)}) async-start(bf16[8,3,64,384]{3,2,1,0:T(8,128)(2,1)} %shard_map.85), calls=%async_computation.1 | async-start | bytes 2359296 | tf_op jit(solution)/shard_map/all_to_all | solution.py:510
  30.1 8.4 %copy-start.11 = (s32[2,4,4]{2,1,0:T(4,128)S(1)}, s32[2,4,4]{2,1,0:T(4,128)}, u32[]{:S(2)}) copy-start(s32[2,4,4]{2,1,0:T(4,128)} %refs_4_.1) | copy-start | bytes 388
  33.9 1.1 %copy-start.5 = (bf16[8,64,384]{2,1,0:T(8,128)(2,1)}, bf16[8,64,384]{2,1,0:T(8,128)(2,1)S(1)}, u32[]{:S(2)}) copy-start(bf16[8,64,384]{2,1,0:T(8,128)(2,1)S(1)} %collective-permute-done.2.refs_0_) | copy-start | bytes 1179652
  35.0 0.7 copy-start.8
  35.8 12.2 %collective-permute-start.4 = (bf16[8,64,384]{2,1,0:T(8,128)(2,1)}, bf16[8,64,384]{2,1,0:T(8,128)(2,1)S(1)}, u32[]{:S(2)}, u32[]{:S(2)}) collective-permute-start(bf16[8,64,384]{2,1,0:T(8,128)(2,1)} %get-tuple-element.37.refs_3_), channel_id=1, source_target_pairs={{0,8},{1,9},{2,10},{3,11},{4,12},{5,13},{6,14},{7,15},{8,0},{9,1},... | collective-permute-start | bytes 1179656 | tf_op jit(solution)/shard_map/ppermute | solution.py:534
  35.9 12.2 %collective-permute-start.5 = (bf16[8,64,384]{2,1,0:T(8,128)(2,1)}, bf16[8,64,384]{2,1,0:T(8,128)(2,1)S(1)}, u32[]{:S(2)}, u32[]{:S(2)}) collective-permute-start(bf16[8,64,384]{2,1,0:T(8,128)(2,1)} %get-tuple-element.38.refs_2_), channel_id=1, source_target_pairs={{0,2},{1,3},{2,0},{3,1},{4,6},{5,7},{6,4},{7,5},{8,16},{9,17},{10,... | collective-permute-start | bytes 1179656 | tf_op jit(solution)/shard_map/ppermute | solution.py:534
  38.6 1.0 copy-start.6
  39.6 1.0 copy-start.9
  44.1 2.2 %copy-start.12 = (bf16[3,1536,512]{2,1,0:T(8,128)(2,1)}, bf16[3,1536,512]{2,1,0:T(8,128)(2,1)S(1)}, u32[]{:S(2)}) copy-start(bf16[3,1536,512]{2,1,0:T(8,128)(2,1)S(1)} %get-tuple-element.47.refs_4_.refs_7_) | copy-start | bytes 14155780
  46.3 0.6 copy-start.15
  46.9 1.1 %copy-start.16 = (f32[3,8,512]{2,1,0:T(8,128)S(1)}, f32[3,8,512]{2,1,0:T(8,128)}, u32[]{:S(2)}) copy-start(f32[3,8,512]{2,1,0:T(8,128)} %copy-done.15) | copy-start | bytes 147460
  47.0 12.1 %collective-permute-start.6 = (bf16[8,64,384]{2,1,0:T(8,128)(2,1)S(1)}, bf16[8,64,384]{2,1,0:T(8,128)(2,1)S(1)}, u32[]{:S(2)}, u32[]{:S(2)}) collective-permute-start(bf16[8,64,384]{2,1,0:T(8,128)(2,1)S(1)} %get-tuple-element.42.refs_3_.refs_6_), channel_id=1, source_target_pairs={{0,8},{1,9},{2,10},{3,11},{4,12},{5,13},{6,14},{7,15},{8,0},{9,1},... | collective-permute-start | bytes 1179656 | tf_op jit(solution)/shard_map/ppermute | solution.py:534
  47.0 4.7 %slice-start = ((s8[4718592]{0:T(1024)(128)(4,1)}), s8[4194304]{0:T(1024)(128)(4,1)S(1)}, s32[]{:S(2)}) async-start(s8[4718592]{0:T(1024)(128)(4,1)} %bitcast.1), calls=%async_computation.4 | async-start | bytes 8388608
  47.1 4.6 %slice-start.1 = ((s8[4718592]{0:T(1024)(128)(4,1)}), s8[524288]{0:T(1024)(128)(4,1)S(1)}, s32[]{:S(2)}) async-start(s8[4718592]{0:T(1024)(128)(4,1)} %bitcast.1), calls=%async_computation.5 | async-start | bytes 1048576
  47.1 12.1 %collective-permute-start.7 = (bf16[8,64,384]{2,1,0:T(8,128)(2,1)S(1)}, bf16[8,64,384]{2,1,0:T(8,128)(2,1)S(1)}, u32[]{:S(2)}, u32[]{:S(2)}) collective-permute-start(bf16[8,64,384]{2,1,0:T(8,128)(2,1)S(1)} %get-tuple-element.43.refs_2_.refs_5_), channel_id=1, source_target_pairs={{0,2},{1,3},{2,0},{3,1},{4,6},{5,7},{6,4},{7,5},{8,16},{9,17},{10,... | collective-permute-start | bytes 1179656 | tf_op jit(solution)/shard_map/ppermute | solution.py:534
  50.4 17.1 %collective-permute-start.14 = (bf16[8,64,384]{2,1,0:T(8,128)(2,1)S(1)}, bf16[8,64,384]{2,1,0:T(8,128)(2,1)S(1)}, u32[]{:S(2)}, u32[]{:S(2)}) collective-permute-start(bf16[8,64,384]{2,1,0:T(8,128)(2,1)S(1)} %get-tuple-element.64), channel_id=1, source_target_pairs={{0,8},{1,9},{2,10},{3,11},{4,12},{5,13},{6,14},{7,15},{8,0},{9,1},... | collective-permute-start | bytes 1179656 | tf_op jit(solution)/shard_map/ppermute | solution.py:534
  51.5 16.2 %collective-permute-start.12 = (bf16[8,64,384]{2,1,0:T(8,128)(2,1)S(1)}, bf16[8,64,384]{2,1,0:T(8,128)(2,1)S(1)}, u32[]{:S(2)}, u32[]{:S(2)}) collective-permute-start(bf16[8,64,384]{2,1,0:T(8,128)(2,1)S(1)} %get-tuple-element.64), channel_id=1, source_target_pairs={{0,2},{1,3},{2,0},{3,1},{4,6},{5,7},{6,4},{7,5},{8,16},{9,17},{10,... | collective-permute-start | bytes 1179656 | tf_op jit(solution)/shard_map/ppermute | solution.py:534
  53.8 0.7 copy-start.13
  59.2 3.4 %copy-start.7 = (bf16[8,64,384]{2,1,0:T(8,128)(2,1)S(1)}, bf16[8,64,384]{2,1,0:T(8,128)(2,1)}, u32[]{:S(2)}) copy-start(bf16[8,64,384]{2,1,0:T(8,128)(2,1)} %get-tuple-element.38.refs_2_) | copy-start | bytes 1179652
  59.2 3.4 %copy-start.10 = (bf16[8,64,384]{2,1,0:T(8,128)(2,1)S(1)}, bf16[8,64,384]{2,1,0:T(8,128)(2,1)}, u32[]{:S(2)}) copy-start(bf16[8,64,384]{2,1,0:T(8,128)(2,1)} %get-tuple-element.37.refs_3_) | copy-start | bytes 1179652
  61.8 14.3 %collective-permute-start.10 = (bf16[8,64,384]{2,1,0:T(8,128)(2,1)}, bf16[8,64,384]{2,1,0:T(8,128)(2,1)}, u32[]{:S(2)}, u32[]{:S(2)}) collective-permute-start(bf16[8,64,384]{2,1,0:T(8,128)(2,1)} %get-tuple-element.60), channel_id=1, source_target_pairs={{0,8},{1,9},{2,10},{3,11},{4,12},{5,13},{6,14},{7,15},{8,0},{9,1},... | collective-permute-start | bytes 1179656 | tf_op jit(solution)/shard_map/ppermute | solution.py:534
  61.8 15.5 %collective-permute-start.8 = (bf16[8,64,384]{2,1,0:T(8,128)(2,1)}, bf16[8,64,384]{2,1,0:T(8,128)(2,1)S(1)}, u32[]{:S(2)}, u32[]{:S(2)}) collective-permute-start(bf16[8,64,384]{2,1,0:T(8,128)(2,1)} %get-tuple-element.60), channel_id=1, source_target_pairs={{0,2},{1,3},{2,0},{3,1},{4,6},{5,7},{6,4},{7,5},{8,16},{9,17},{10,... | collective-permute-start | bytes 1179656 | tf_op jit(solution)/shard_map/ppermute | solution.py:534
  66.0 1.8 %copy-start.1 = (bf16[8,64,384]{2,1,0:T(8,128)(2,1)}, bf16[8,64,384]{2,1,0:T(8,128)(2,1)S(1)}, u32[]{:S(2)}) copy-start(bf16[8,64,384]{2,1,0:T(8,128)(2,1)S(1)} %get-tuple-element.59.refs_1_) | copy-start | bytes 1179652
  66.0 1.8 %copy-start.3 = (bf16[8,64,384]{2,1,0:T(8,128)(2,1)}, bf16[8,64,384]{2,1,0:T(8,128)(2,1)S(1)}, u32[]{:S(2)}) copy-start(bf16[8,64,384]{2,1,0:T(8,128)(2,1)S(1)} %get-tuple-element.61.refs_0_) | copy-start | bytes 1179652
  67.6 17.0 %collective-permute-start.15 = (bf16[8,64,384]{2,1,0:T(8,128)(2,1)S(1)}, bf16[8,64,384]{2,1,0:T(8,128)(2,1)}, u32[]{:S(2)}, u32[]{:S(2)}) collective-permute-start(bf16[8,64,384]{2,1,0:T(8,128)(2,1)S(1)} %shard_map.99), channel_id=1, source_target_pairs={{0,2},{1,3},{2,0},{3,1},{4,6},{5,7},{6,4},{7,5},{8,16},{9,17},{10,... | collective-permute-start | bytes 1179656 | tf_op jit(solution)/shard_map/ppermute | solution.py:534
  67.8 16.7 %collective-permute-start.13 = (bf16[8,64,384]{2,1,0:T(8,128)(2,1)S(1)}, bf16[8,64,384]{2,1,0:T(8,128)(2,1)}, u32[]{:S(2)}, u32[]{:S(2)}) collective-permute-start(bf16[8,64,384]{2,1,0:T(8,128)(2,1)S(1)} %shard_map.98), channel_id=1, source_target_pairs={{0,8},{1,9},{2,10},{3,11},{4,12},{5,13},{6,14},{7,15},{8,0},{9,1},... | collective-permute-start | bytes 1179656 | tf_op jit(solution)/shard_map/ppermute | solution.py:534
  69.1 7.0 %copy-start.4 = (bf16[8,64,384]{2,1,0:T(8,128)(2,1)S(1)}, bf16[8,64,384]{2,1,0:T(8,128)(2,1)}, u32[]{:S(2)}) copy-start(bf16[8,64,384]{2,1,0:T(8,128)(2,1)} %copy-done.3) | copy-start | bytes 1179652
  69.1 8.2 %copy-start.2 = (bf16[8,64,384]{2,1,0:T(8,128)(2,1)S(1)}, bf16[8,64,384]{2,1,0:T(8,128)(2,1)}, u32[]{:S(2)}) copy-start(bf16[8,64,384]{2,1,0:T(8,128)(2,1)} %copy-done.1) | copy-start | bytes 1179652
  69.1 23.2 %all-to-all-start.2 = ((bf16[8,2,64,384]{3,2,1,0:T(8,128)(2,1)}), bf16[8,2,64,384]{3,2,1,0:T(8,128)(2,1)S(1)}, u32[]{:S(2)}, u32[]{:S(2)}) async-start(bf16[8,2,64,384]{3,2,1,0:T(8,128)(2,1)} %shard_map.94), calls=%async_computation.2 | async-start | bytes 1572864 | tf_op jit(solution)/shard_map/all_to_all | solution.py:510
  76.0 8.5 %copy-start.14 = (bf16[8,64,384]{2,1,0:T(8,128)(2,1)S(1)}, bf16[8,64,384]{2,1,0:T(8,128)(2,1)}, u32[]{:S(2)}) copy-start(bf16[8,64,384]{2,1,0:T(8,128)(2,1)} %copy-done.13) | copy-start | bytes 1179652
  77.2 14.0 %collective-permute-start.11 = (bf16[8,64,384]{2,1,0:T(8,128)(2,1)S(1)}, bf16[8,64,384]{2,1,0:T(8,128)(2,1)S(1)}, u32[]{:S(2)}, u32[]{:S(2)}) collective-permute-start(bf16[8,64,384]{2,1,0:T(8,128)(2,1)S(1)} %shard_map.97), channel_id=1, source_target_pairs={{0,2},{1,3},{2,0},{3,1},{4,6},{5,7},{6,4},{7,5},{8,16},{9,17},{10,... | collective-permute-start | bytes 1179656 | tf_op jit(solution)/shard_map/ppermute | solution.py:534
  77.4 13.8 %collective-permute-start.9 = (bf16[8,64,384]{2,1,0:T(8,128)(2,1)S(1)}, bf16[8,64,384]{2,1,0:T(8,128)(2,1)S(1)}, u32[]{:S(2)}, u32[]{:S(2)}) collective-permute-start(bf16[8,64,384]{2,1,0:T(8,128)(2,1)S(1)} %shard_map.96), channel_id=1, source_target_pairs={{0,8},{1,9},{2,10},{3,11},{4,12},{5,13},{6,14},{7,15},{8,0},{9,1},... | collective-permute-start | bytes 1179656 | tf_op jit(solution)/shard_map/ppermute | solution.py:534
  92.3 15.1 %all-to-all-start.3 = ((bf16[8,2,64,384]{3,2,1,0:T(8,128)(2,1)}), bf16[8,2,64,384]{3,2,1,0:T(8,128)(2,1)S(1)}, u32[]{:S(2)}, u32[]{:S(2)}) async-start(bf16[8,2,64,384]{3,2,1,0:T(8,128)(2,1)} %shard_map.101), calls=%async_computation.3 | async-start | bytes 1572864 | tf_op jit(solution)/shard_map/all_to_all | solution.py:510

commit v6 on v4

--- a/solution.py
+++ b/solution.py
@@ -1,3 +1,4 @@
+import functools
 import math
 
 import jax
@@ -15,6 +16,12 @@
 SCALE_LOG2 = SCALE * math.log2(math.e)
 MASKED = -1e30
 VMEM_BYTES = 12 * 1024 * 1024
+FIRST_PACK_BYTES = 60 * 1024 * 1024
+
+FLOPS_PER_US = 1_150_000_000
+SECOND_HOP_WORK = 20
+PICK_WORK = 20
+SUM_WORK = 20
 
 
 def partner_2(shard, axis, distance):
@@ -228,7 +235,7 @@
     )
 
 
-def near_scores_kernel(frame_ref, mask_ref, vqg_ref, k0_ref, k1_ref, k3_ref, e_ref, ml_ref):
+def near_scores_kernel(rows, frame_ref, mask_ref, e_ref, ml_ref):
     heads, _, tokens = e_ref.shape
     blocks = tokens // BLOCK
     frame = frame_ref[0]
@@ -236,9 +243,9 @@
     bias1 = bias_rows(mask_ref, 0, frame >= 0, blocks)
     bias3 = bias_rows(mask_ref, 0, inner, blocks)
     for head in range(heads):
-        queries = flat(vqg_ref, head, 1)
-        slots = ((k0_ref, None), (k1_ref, bias1), (k3_ref, bias3))
-        scores = [masked_scores(flat(ref, head), queries, bias) for ref, bias in slots]
+        queries = rows("q", head)
+        slots = (("k0", None), ("k1", bias1), ("k3", bias3))
+        scores = [masked_scores(rows(name, head), queries, bias) for name, bias in slots]
         peak = scores[0].max(axis=0, keepdims=True)
         for score in scores[1:]:
             peak = jnp.maximum(peak, score.max(axis=0, keepdims=True))
@@ -251,131 +258,142 @@
         ml_ref[head, 1:2] = total
 
 
-def far_scores_kernel(frame_ref, mask_ref, vqg_ref, ka_ref, kb_ref, ml_ref, e_ref, w_ref, dv_ref):
-    heads, _, tokens = e_ref.shape
+def far_scores_kernel(rows, frame_ref, mask_ref, ml_ref, p_ref, w_ref, dv_ref, k2_ref):
+    heads, _, tokens = p_ref.shape
     blocks = tokens // BLOCK
     frame = frame_ref[0]
     inner = (frame == 1) | (frame == 2)
     bias = bias_rows(mask_ref, 1, frame >= 0, blocks)
     for head in range(heads):
-        keys = jnp.where(inner, flat(kb_ref, head), flat(ka_ref, head))
-        scores = masked_scores(keys, flat(vqg_ref, head, 1), bias)
+        keys = jnp.where(inner, rows("kb", head), rows("ka", head))
+        put(k2_ref, head, keys)
+        scores = masked_scores(keys, rows("q", head), bias)
         peak2 = scores.max(axis=0, keepdims=True)
         e = jnp.exp2(scores - peak2)
         total2 = e.sum(axis=0, keepdims=True)
-        e = e.astype(BF16)
         peak1 = ml_ref[head, 0:1]
         peak = jnp.maximum(peak1, peak2)
         near = jnp.exp2(peak1 - peak)
         far = jnp.exp2(peak2 - peak)
         inv = 1.0 / (near * ml_ref[head, 1:2] + far * total2)
-        far = far * inv
-        scaled = (flat(vqg_ref, head, 2).T.astype(F32) * far).astype(BF16)
-        put(dv_ref, head, dot_nt(e, scaled).astype(BF16))
-        e_ref[head] = e
+        weights = (e * (far * inv)).astype(BF16)
+        put(dv_ref, head, dot(weights, rows("g", head)).astype(BF16))
+        p_ref[head] = weights
         w_ref[head, 0:1] = near * inv
-        w_ref[head, 1:2] = far
-
-
-def near_values_kernel(vqg_ref, e_ref, w_ref, v0_ref, v1_ref, v3_ref, dv0_ref, dv1_ref, dv3_ref, acc_ref):
+
+
+def near_weights(e_ref, w_ref, head, index):
+    tokens = e_ref.shape[2]
+    e = e_ref[head, index * tokens : (index + 1) * tokens]
+    return e * w_ref[head, 0:1].astype(BF16)
+
+
+def near_values_kernel(rows, e_ref, w_ref, dv0_ref, dv1_ref, dv3_ref, acc_ref):
     heads, _, tokens = e_ref.shape
     for head in range(heads):
-        scaled = (flat(vqg_ref, head, 2).T.astype(F32) * w_ref[head, 0:1]).astype(BF16)
+        grads = rows("g", head)
         acc = jnp.zeros((HD, tokens), F32)
-        for index, (v_ref, dv_ref) in enumerate(
-            ((v0_ref, dv0_ref), (v1_ref, dv1_ref), (v3_ref, dv3_ref))
-        ):
-            e = e_ref[head, index * tokens : (index + 1) * tokens]
-            put(dv_ref, head, dot_nt(e, scaled).astype(BF16))
-            acc = acc + dot(flat(v_ref, head).T, e)
+        slots = (("v0", dv0_ref), ("v1", dv1_ref), ("v3", dv3_ref))
+        for index, (name, dv_ref) in enumerate(slots):
+            weights = near_weights(e_ref, w_ref, head, index)
+            put(dv_ref, head, dot(weights, grads).astype(BF16))
+            acc = acc + dot(rows(name, head).T, weights)
         acc_ref[head] = acc
 
 
-def far_values_kernel(
-    frame_ref, vqg_ref, ka_ref, kb_ref, va_ref, vb_ref, e_ref, w_ref, acc_ref,
-    dk_ref, att_ref, delta_ref, dq_ref,
-):
-    heads = e_ref.shape[0]
+def far_values_kernel(rows, frame_ref, p_ref, acc_ref, dk_ref, att_ref, delta_ref, dq_ref):
+    heads = p_ref.shape[0]
     frame = frame_ref[0]
     inner = (frame == 1) | (frame == 2)
     for head in range(heads):
-        keys = jnp.where(inner, flat(kb_ref, head), flat(ka_ref, head))
-        values = jnp.where(inner, flat(vb_ref, head), flat(va_ref, head))
-        e = e_ref[head]
-        near = w_ref[head, 0:1]
-        far = w_ref[head, 1:2]
-        out = (acc_ref[head] * near + dot(values.T, e) * far).astype(BF16)
+        keys = rows("k2", head)
+        values = jnp.where(inner, rows("vb", head), rows("va", head))
+        weights = p_ref[head]
+        out = (acc_ref[head] + dot(values.T, weights)).astype(BF16)
         put(att_ref, head, out.T)
-        grads = flat(vqg_ref, head, 2).T.astype(F32)
-        delta = (grads * out.astype(F32)).sum(axis=0, keepdims=True)
-        delta_ref[head, 0:1] = near
-        delta_ref[head, 1:2] = near * delta
-        scaled = (grads * far).astype(BF16)
-        ds = (e.astype(F32) * (dot(values, scaled) - far * delta)).astype(BF16)
-        put(dk_ref, head, (dot(ds, flat(vqg_ref, head, 1)) * SCALE).astype(BF16))
+        grads = rows("g", head).T
+        delta = (grads.astype(F32) * out.astype(F32)).sum(axis=0, keepdims=True)
+        delta_ref[head, 0:1] = delta
+        ds = (weights.astype(F32) * (dot(values, grads) - delta)).astype(BF16)
+        put(dk_ref, head, (dot(ds, rows("q", head)) * SCALE).astype(BF16))
         dq_ref[head] = dot(keys.T, ds)
 
 
-def near_keys_kernel(
-    vqg_ref, k0_ref, k1_ref, k3_ref, v0_ref, v1_ref, v3_ref, e_ref, delta_ref, dq2_ref, att_ref,
-    dk0_ref, dk1_ref, dk3_ref, out_ref,
-):
-    heads, _, tokens = e_ref.shape
-    for head in range(heads):
-        queries = flat(vqg_ref, head, 1)
-        near = delta_ref[head, 0:1]
-        delta = delta_ref[head, 1:2]
-        scaled = (flat(vqg_ref, head, 2).T.astype(F32) * near).astype(BF16)
+def near_keys_kernel(rows, e_ref, w_ref, delta_ref, dq2_ref, dk0_ref, dk1_ref, dk3_ref, dq_ref):
+    for head in range(e_ref.shape[0]):
+        queries = rows("q", head)
+        grads = rows("g", head).T
+        delta = delta_ref[head, 0:1]
         dq = dq2_ref[head]
-        for index, (k_ref, v_ref, dk_ref) in enumerate(
-            ((k0_ref, v0_ref, dk0_ref), (k1_ref, v1_ref, dk1_ref), (k3_ref, v3_ref, dk3_ref))
-        ):
-            e = e_ref[head, index * tokens : (index + 1) * tokens]
-            ds = (e.astype(F32) * (dot(flat(v_ref, head), scaled) - delta)).astype(BF16)
+        slots = (("k0", "v0", dk0_ref), ("k1", "v1", dk1_ref), ("k3", "v3", dk3_ref))
+        for index, (k_name, v_name, dk_ref) in enumerate(slots):
+            weights = near_weights(e_ref, w_ref, head, index).astype(F32)
+            ds = (weights * (dot(rows(v_name, head), grads) - delta)).astype(BF16)
             put(dk_ref, head, (dot(ds, queries) * SCALE).astype(BF16))
-            dq = dq + dot(flat(k_ref, head).T, ds)
-        put(out_ref, head, (dq * SCALE).astype(BF16).T, 1)
-    out_ref[:, 0] = att_ref[...]
-
-
-def add_kernel(frame_ref, own_ref, other_ref, out_ref):
-    out_ref[...] = (own_ref[...].astype(F32) + other_ref[...].astype(F32)).astype(BF16)
-
-
-def add_inner_kernel(frame_ref, own_ref, other_ref, out_ref):
+            dq = dq + dot(rows(k_name, head).T, ds)
+        put(dq_ref, head, (dq * SCALE).astype(BF16).T)
+
+
+def add_both_kernel(frame_ref, first_ref, middle_ref, third_ref, edge_ref, first_out, third_out):
     inner = (frame_ref[0] == 1) | (frame_ref[0] == 2)
+    third_out[...] = (third_ref[...].astype(F32) + edge_ref[...].astype(F32)).astype(BF16)
 
     @pl.when(inner)
     def _():
-        out_ref[...] = (own_ref[...].astype(F32) + other_ref[...].astype(F32)).astype(BF16)
+        first_out[...] = (first_ref[...].astype(F32) + middle_ref[...].astype(F32)).astype(BF16)
 
     @pl.when(jnp.logical_not(inner))
     def _():
-        out_ref[...] = own_ref[...]
-
-
-def last_sum(frame_ref, own_ref, edge_ref, middle_ref):
+        first_out[...] = first_ref[...]
+
+
+def sum_kernel(frame_ref, own_ref, edge_ref, middle_ref, out_ref):
     inner = (frame_ref[0] == 1) | (frame_ref[0] == 2)
     total = own_ref[...].astype(F32) + edge_ref[...].astype(F32)
-    return (total + jnp.where(inner, middle_ref[...].astype(F32), 0.0)).astype(BF16)
-
-
-def collect_kernel(frame_ref, *refs):
-    out_ref = refs[-1]
-    for which in range(out_ref.shape[1]):
-        out_ref[:, which] = last_sum(frame_ref, *refs[3 * which : 3 * which + 3])
+    out_ref[...] = (total + jnp.where(inner, middle_ref[...].astype(F32), 0.0)).astype(BF16)
+
+
+def pair_kernel(first_ref, second_ref, out_ref):
+    out_ref[:, 0] = first_ref[...]
+    out_ref[:, 1] = second_ref[...]
+
+
+def last_kernel(frame_ref, own_ref, edge_ref, middle_ref, second_ref, out_ref):
+    inner = (frame_ref[0] == 1) | (frame_ref[0] == 2)
+    total = own_ref[...].astype(F32) + edge_ref[...].astype(F32)
+    out_ref[:, 0] = (total + jnp.where(inner, middle_ref[...].astype(F32), 0.0)).astype(BF16)
+    out_ref[:, 1] = second_ref[...]
 
 
 def pack_kernel(*refs):
-    out_ref = refs[-1]
-    width = out_ref.shape[3]
-    for peer in range(out_ref.shape[0]):
-        for which, ref in enumerate(refs[:-1]):
-            out_ref[peer, which] = ref[:, peer * width : (peer + 1) * width]
-
-
-def first_kernel(in_ref, out_ref):
-    out_ref[...] = in_ref[:, 0]
+    out_ref, held, packed, sems, out_sems = refs[-5:]
+    copies = [
+        pltpu.make_async_copy(ref, held.at[which], sems.at[which])
+        for which, ref in enumerate(refs[:-5])
+    ]
+    for copy in copies:
+        copy.start()
+    peers, _, _, width = out_ref.shape
+    leaving = []
+    for which, copy in enumerate(copies):
+        copy.wait()
+        for peer in range(peers):
+            packed[which, peer] = held[which, :, peer * width : (peer + 1) * width]
+        leaving.append(
+            pltpu.make_async_copy(packed.at[which], out_ref.at[:, which], out_sems.at[which])
+        )
+        leaving[-1].start()
+    for copy in leaving:
+        copy.wait()
+
+
+def pass_kernel(*refs):
+    pass
+
+
+def pick_kernel(places, in_ref, *out_refs):
+    for place, ref in zip(places, out_refs):
+        ref[...] = in_ref[:, place]
 
 
 def unpack_kernel(in_ref, *out_refs):
@@ -385,17 +403,11 @@
             ref[:, peer * width : (peer + 1) * width] = in_ref[peer, which]
 
 
-def params():
-    return pltpu.CompilerParams(vmem_limit_bytes=VMEM_BYTES)
-
-
-def cost(flops, data):
-    return pl.CostEstimate(flops=flops, bytes_accessed=data, transcendentals=0)
-
-
 def per_device_line(query_rows, key_rows, value_rows, out_grad, block_mask):
     plane = ("rank", "head")
-    peers = lax.axis_size("rank") * lax.axis_size("head")
+    devices = ("frame", "rank", "head")
+    head_parts = lax.axis_size("head")
+    peers = lax.axis_size("rank") * head_parts
     rows, columns = query_rows.shape
     width = columns // peers
     heads = width // HD
@@ -409,43 +421,101 @@
     frame = lax.axis_index("frame").astype(jnp.int32).reshape(1)
     smem = pl.BlockSpec(memory_space=pltpu.SMEM)
     vmem = pl.BlockSpec(memory_space=pltpu.VMEM)
-    pair_flops = heads * 2 * tokens * tokens * HD
-
-    def call(kernel, outs, work, *operands):
+    anywhere = pl.BlockSpec(memory_space=pl.ANY)
+    found = {}
+
+    def estimate(work):
+        return pl.CostEstimate(
+            flops=int(work * FLOPS_PER_US), bytes_accessed=1 << 16, transcendentals=0
+        )
+
+    def call(kernel, outs, work, *operands, names=()):
         several = isinstance(outs, tuple)
+        arrays = []
+        places = {}
+        for name in names:
+            array, which = found[name]
+            spot = [i for i, x in enumerate(arrays) if x is array]
+            if not spot:
+                spot = [len(arrays)]
+                arrays.append(array)
+            places[name] = (spot[0], which)
+
+        def body(*refs):
+            lookup = refs[: len(arrays)]
+            if not places:
+                return kernel(*refs)
+
+            def rows_of(name, head):
+                index, which = places[name]
+                return flat(lookup[index], head, which)
+
+            return kernel(rows_of, *refs[len(arrays) :])
+
+        operands = tuple(arrays) + operands
         return pl.pallas_call(
-            kernel,
+            body,
             in_specs=[smem if x.dtype == jnp.int32 else vmem for x in operands],
             out_specs=(vmem,) * len(outs) if several else vmem,
             out_shape=outs,
-            compiler_params=params(),
-            cost_estimate=cost(work * pair_flops, 4 << 20),
+            compiler_params=pltpu.CompilerParams(vmem_limit_bytes=VMEM_BYTES),
+            cost_estimate=estimate(work),
         )(*operands)
+
+    def packed(count):
+        return jax.ShapeDtypeStruct((peers, count, rows, width), BF16)
+
+    def pack(*arrays, limit=VMEM_BYTES):
+        count = len(arrays)
+        return pl.pallas_call(
+            pack_kernel,
+            in_specs=[anywhere] * count,
+            out_specs=anywhere,
+            out_shape=packed(count),
+            scratch_shapes=[
+                pltpu.VMEM((count, rows, columns), BF16),
+                pltpu.VMEM((count, peers, rows, width), BF16),
+                pltpu.SemaphoreType.DMA((count,)),
+                pltpu.SemaphoreType.DMA((count,)),
+            ],
+            compiler_params=pltpu.CompilerParams(vmem_limit_bytes=limit),
+            cost_estimate=estimate(0.5),
+        )(*arrays)
+
+    def pick(landed, *places):
+        kernel = functools.partial(pick_kernel, places)
+        return call(kernel, (one,) * len(places), PICK_WORK, landed)
+
+    def later(work, *arrays):
+        return pl.pallas_call(
+            pass_kernel,
+            in_specs=[anywhere] * len(arrays),
+            out_specs=(anywhere,) * len(arrays),
+            out_shape=tuple(jax.ShapeDtypeStruct(x.shape, x.dtype) for x in arrays),
+            input_output_aliases={i: i for i in range(len(arrays))},
+            cost_estimate=estimate(work),
+        )(*arrays)
 
     def swap(array):
         return lax.all_to_all(array, plane, 0, 0, tiled=True)
 
-    def packed(count):
-        return jax.ShapeDtypeStruct((peers, count, rows, width), BF16)
-
-    def leave(packed):
-        return call(unpack_kernel, (row_type,) * packed.shape[1], 0, swap(packed))
-
-    pair = packed(2)
-    devices = ("frame", "rank", "head")
-    heads_axis = lax.axis_size("head")
+    def leave(pair):
+        return call(unpack_kernel, (row_type, row_type), 0.5, swap(pair))
+
+    def barrier(*values):
+        return lax.optimization_barrier(values)
 
     def pairs_of(partner):
         pairs = []
         for frame_ in range(4):
             for rank in range(GROUP):
-                for part in range(heads_axis):
+                for part in range(head_parts):
                     there = partner.get(frame_)
                     place = (frame_, rank ^ 1) if there is None else (there, rank)
                     pairs.append(
                         (
-                            (frame_ * GROUP + rank) * heads_axis + part,
-                            (place[0] * GROUP + place[1]) * heads_axis + part,
+                            (frame_ * GROUP + rank) * head_parts + part,
+                            (place[0] * GROUP + place[1]) * head_parts + part,
                         )
                     )
         return pairs
@@ -456,47 +526,59 @@
     def send(array, pairs):
         return lax.ppermute(array, devices, pairs)
 
-    k0 = swap(call(pack_kernel, packed(1), 0, key_rows)).reshape(one.shape)
+    def sums(first, third, from_edge, from_middle):
+        return call(
+            add_both_kernel, (one, one), 0.2, frame, first, from_middle, third, from_edge
+        )
+
+    v1_rows, v3_rows = send(value_rows, edge), send(value_rows, middle)
+    kqg = swap(pack(key_rows, query_rows, out_grad, limit=FIRST_PACK_BYTES))
+    values = pack(value_rows, v1_rows, v3_rows)
+    kqg, values = barrier(kqg, values)
+    (k0,) = pick(kqg, 0)
     k1, k3 = send(k0, edge), send(k0, middle)
-    vqg = swap(call(pack_kernel, packed(3), 0, value_rows, query_rows, out_grad))
-    v0 = call(first_kernel, one, 0, vqg)
-    ka, kb = send(k3, edge), send(k1, middle)
-    v1, v3 = send(v0, edge), send(v0, middle)
-    va, vb = send(v3, edge), send(v1, middle)
-
-    def sums(first, third, from_edge, from_middle):
-        return (
-            call(add_kernel, one, 0, frame, third, from_edge),
-            call(add_inner_kernel, one, 0, frame, first, from_middle),
-        )
-
+    k1_on, k3_on = later(SECOND_HOP_WORK, k1, k3)
+    ka, kb = send(k3_on, edge), send(k1_on, middle)
+    for name, array in (("k0", k0), ("k1", k1), ("k3", k3), ("ka", ka), ("kb", kb)):
+        found[name] = (array, None)
+    found.update(q=(kqg, 1), g=(kqg, 2))
     e_near, ml = call(
-        near_scores_kernel, (near_e, stat), 6, frame, block_mask, vqg, k0, k1, k3
-    )
-    e_far, w, dv2 = call(
-        far_scores_kernel, (far_e, stat, one), 4, frame, block_mask, vqg, ka, kb, ml
-    )
+        near_scores_kernel, (near_e, stat), 3.5, frame, block_mask,
+        names=("q", "k0", "k1", "k3"),
+    )
+    values, ml = barrier(swap(values), ml)
+    v1, v3 = pick(values, 1, 2)
+    found.update(v0=(values, 0), v1=(values, 1), v3=(values, 2))
+    found.update(va=(send(v3, edge), None), vb=(send(v1, middle), None))
+
+    p_far, w, dv2, k2 = call(
+        far_scores_kernel, (far_e, stat, one, one), 2, frame, block_mask, ml,
+        names=("q", "g", "ka", "kb"),
+    )
+    found["k2"] = (k2, None)
     dv_edge, dv_middle = send(dv2, edge), send(dv2, middle)
     dv0, dv1, dv3, acc = call(
-        near_values_kernel, (one, one, one, accum), 6, vqg, e_near, w, v0, v1, v3
-    )
-    dv_third, dv_first = sums(dv1, dv3, dv_edge, dv_middle)
+        near_values_kernel, (one, one, one, accum), 2, e_near, w,
+        names=("g", "v0", "v1", "v3"),
+    )
+    dk2, att, delta, dq2 = call(
+        far_values_kernel, (one, one, stat, accum), 2, frame, p_far, acc,
+        names=("q", "g", "k2", "va", "vb"),
+    )
+    dk_edge, dk_middle = send(dk2, edge), send(dk2, middle)
+    dk0, dk1, dk3, dq = call(
+        near_keys_kernel, (one, one, one, one), 4, e_near, w, delta, dq2,
+        names=("q", "g", "k0", "k1", "k3", "v0", "v1", "v3"),
+    )
+    dq, dv1, dv3 = barrier(dq, dv1, dv3)
+    dv_first, dv_third = sums(dv1, dv3, dv_edge, dv_middle)
     dv_over = send(dv_first, edge), send(dv_third, middle)
-    acc, dv_first, dv_third = lax.optimization_barrier((acc, dv_first, dv_third))
-    dk2, att, delta, dq2 = call(
-        far_values_kernel, (one, one, stat, accum), 4, frame, vqg, ka, kb, va, vb, e_far, w, acc
-    )
-    dk_edge, dk_middle = send(dk2, edge), send(dk2, middle)
-    delta, dv_over = lax.optimization_barrier((delta, dv_over))
-    dk0, dk1, dk3, att_dq = call(
-        near_keys_kernel, (one, one, one, pair), 9,
-        vqg, k0, k1, k3, v0, v1, v3, e_near, delta, dq2, att,
-    )
-    attended, grad_query = leave(att_dq)
-    dk_third, dk_first = sums(dk1, dk3, dk_edge, dk_middle)
+    dk_first, dk_third = sums(dk1, dk3, dk_edge, dk_middle)
     dk_over = send(dk_first, edge), send(dk_third, middle)
+    attended, grad_query = leave(call(pair_kernel, packed(2), 0.5, att, dq))
+    dv = call(sum_kernel, one, SUM_WORK, frame, dv0, *dv_over)
     grad_keys, grad_values = leave(
-        call(collect_kernel, pair, 0, frame, dk0, *dk_over, dv0, *dv_over)
+        call(last_kernel, packed(2), 0.5, frame, dk0, *dk_over, dv)
     )
     return attended, grad_query, grad_keys, grad_values
 

time: 118 us -> 109 us (0.924)
  waiting for transfers between devices: 66.5 us -> 47.3 us
  starting transfers between devices: 23.9 us -> 31.4 us
  Pallas kernels: 20.6 us -> 23.7 us
    ppermute x16, waiting for transfers between devices: 48.5 us -> 35.5 us  [send(): return lax.ppermute(array, devices, pairs)]
    ppermute x16, starting transfers between devices: 6.96 us -> 14.4 us  [send(): return lax.ppermute(array, devices, pairs)]
    all_to_all x4, waiting for transfers between devices: 18.1 us -> 11.8 us  [swap(): return lax.all_to_all(array, plane, 0, 0, tiled=True)]
    pallas_call x15 -> x17, Pallas kernels: 20.6 us -> 23.7 us  [the longest x14 19.8 us: call(): pl.pallas_call(body, in_specs=[smem if x.dtype == jnp.int32 else vmem for...]
    unnamed x30 -> x32, local copies, waits for them, and re-layouts: 4.11 us -> 4.32 us
  transfers between devices with their start and end apart: 20 -> 20, of which waited for: 15 -> 17; matrix products, arithmetic and copies ran while one was open for 0% -> 1% of each run, Pallas kernels for 16% -> 19%
where the time goes in v6:
time: 109 us; the launch traced here: 107 us
  waiting for transfers between devices  47.3 us (43%)
  starting transfers between devices  31.4 us (29%)
  Pallas kernels  23.7 us (22%)
  local copies, waits for them, and re-layouts  4.32 us (4%)
    ppermute x16, waiting for transfers between devices, send(): return lax.ppermute(array, devices, pairs)  35.5 us
    pallas_call x14, Pallas kernels, call(): pl.pallas_call(body, in_specs=[smem if x.dtype == jnp.int32 else vmem for...  19.8 us
    all_to_all x4, starting transfers between devices, swap(): return lax.all_to_all(array, plane, 0, 0, tiled=True)  17 us
    ppermute x16, starting transfers between devices, send(): return lax.ppermute(array, devices, pairs)  14.4 us
    all_to_all x4, waiting for transfers between devices, swap(): return lax.all_to_all(array, plane, 0, 0, tiled=True)  11.8 us
    unnamed x32, local copies, waits for them, and re-layouts  4.32 us
    pallas_call x2, Pallas kernels, pack(): pl.pallas_call(pack_kernel, in_specs=[anywhere] * count, out_specs=anywhe...  3.85 us
  transfers between devices with their start and end apart: 20, of which 17 were waited for; matrix products, arithmetic and copies ran while one was open for 1% of the time, Pallas kernels for 19%

profile of v6, /device:TPU:10, one launch (start us, length us, event | category | flops | bytes accessed | tf_op | source)
XLA Modules:
  0.0 107.5 jit_solution(9122496177125224237)
XLA Ops:
  0.6 2.2 %shard_map.84 = bf16[8,3,64,384]{3,2,1,0:T(8,128)(2,1)} custom-call(bf16[64,3072]{1,0:T(8,128)(2,1)} %refs_0_.2, bf16[64,3072]{1,0:T(8,128)(2,1)} %refs_1_.1, bf16[64,3072]{1,0:T(8,128)(2,1)} %refs_2_.1), custom_call_target="tpu_custom_call" | custom-call | flops 575000000 | bytes 65536 | tf_op jit(solution)/shard_map/pallas_call | solution.py:470
  2.8 0.0 copy-start
  2.8 4.4 %all-to-all-start = ((bf16[8,3,64,384]{3,2,1,0:T(8,128)(2,1)}), bf16[8,3,64,384]{3,2,1,0:T(8,128)(2,1)S(1)}, u32[]{:S(2)}, u32[]{:S(2)}) async-start(bf16[8,3,64,384]{3,2,1,0:T(8,128)(2,1)} %shard_map.84), calls=%async_computation | async-start | bytes 2359296 | tf_op jit(solution)/shard_map/all_to_all | solution.py:500
  7.2 0.4 collective-permute-start
  7.7 2.7 %collective-permute-start.1 = (bf16[64,3072]{1,0:T(8,128)(2,1)S(1)}, bf16[64,3072]{1,0:T(8,128)(2,1)S(1)}, u32[]{:S(2)}, u32[]{:S(2)}) collective-permute-start(bf16[64,3072]{1,0:T(8,128)(2,1)S(1)} %copy-done), channel_id=1, source_target_pairs={{0,2},{1,3},{2,0},{3,1},{4,6},{5,7},{6,4},{7,5},{8,16},{9,17},{10,... | collective-permute-start | bytes 1179656 | tf_op jit(solution)/shard_map/ppermute | solution.py:527
  10.4 8.0 %collective-permute-done.refs_1_ = bf16[64,3072]{1,0:T(8,128)(2,1)S(1)} collective-permute-done((bf16[64,3072]{1,0:T(8,128)(2,1)S(1)}, bf16[64,3072]{1,0:T(8,128)(2,1)S(1)}, u32[]{:S(2)}, u32[]{:S(2)}) %collective-permute-start) | collective-permute-done | bytes 393248 | tf_op jit(solution)/shard_map/ppermute | solution.py:527
  18.4 1.1 %collective-permute-done.1.refs_2_ = bf16[64,3072]{1,0:T(8,128)(2,1)S(1)} collective-permute-done((bf16[64,3072]{1,0:T(8,128)(2,1)S(1)}, bf16[64,3072]{1,0:T(8,128)(2,1)S(1)}, u32[]{:S(2)}, u32[]{:S(2)}) %collective-permute-start.1) | collective-permute-done | bytes 393248 | tf_op jit(solution)/shard_map/ppermute | solution.py:527
  19.5 1.7 %shard_map.85 = bf16[8,3,64,384]{3,2,1,0:T(8,128)(2,1)} custom-call(bf16[64,3072]{1,0:T(8,128)(2,1)S(1)} %copy-done, bf16[64,3072]{1,0:T(8,128)(2,1)S(1)} %collective-permute-done.refs_1_, bf16[64,3072]{1,0:T(8,128)(2,1)S(1)} %collective-permute-done.1.refs_2_), custom_call_target="tpu_custom_call" | custom-call | flops 575000000 | bytes 65536 | tf_op jit(solution)/shard_map/pallas_call | solution.py:470
  21.2 1.3 %all-to-all-done.refs_0_ = bf16[8,3,64,384]{3,2,1,0:T(8,128)(2,1)S(1)} async-done(((bf16[8,3,64,384]{3,2,1,0:T(8,128)(2,1)}), bf16[8,3,64,384]{3,2,1,0:T(8,128)(2,1)S(1)}, u32[]{:S(2)}, u32[]{:S(2)}) %all-to-all-start) | async-done | bytes 1179680 | tf_op jit(solution)/shard_map/all_to_all | solution.py:500
  22.5 0.0 copy-start.5
  22.5 0.5 collective-permute-start.2
  23.0 2.7 %collective-permute-start.3 = (bf16[8,64,384]{2,1,0:T(8,128)(2,1)S(1)}, bf16[8,64,384]{2,1,0:T(8,128)(2,1)S(1)}, u32[]{:S(2)}, u32[]{:S(2)}) collective-permute-start(bf16[8,64,384]{2,1,0:T(8,128)(2,1)S(1)} %shard_map.86.refs_1_), channel_id=1, source_target_pairs={{0,2},{1,3},{2,0},{3,1},{4,6},{5,7},{6,4},{7,5},{8,16},{9,17},{10,... | collective-permute-start | bytes 1179656 | tf_op jit(solution)/shard_map/ppermute | solution.py:527
  25.7 4.2 %all-to-all-start.1 = ((bf16[8,3,64,384]{3,2,1,0:T(8,128)(2,1)}), bf16[8,3,64,384]{3,2,1,0:T(8,128)(2,1)S(1)}, u32[]{:S(2)}, u32[]{:S(2)}) async-start(bf16[8,3,64,384]{3,2,1,0:T(8,128)(2,1)} %shard_map.85), calls=%async_computation.1 | async-start | bytes 2359296 | tf_op jit(solution)/shard_map/all_to_all | solution.py:500
  29.9 3.8 %collective-permute-done.2.refs_2_ = bf16[8,64,384]{2,1,0:T(8,128)(2,1)S(1)} collective-permute-done((bf16[8,64,384]{2,1,0:T(8,128)(2,1)S(1)}, bf16[8,64,384]{2,1,0:T(8,128)(2,1)S(1)}, u32[]{:S(2)}, u32[]{:S(2)}) %collective-permute-start.2) | collective-permute-done | bytes 393248 | tf_op jit(solution)/shard_map/ppermute | solution.py:527
  33.7 0.7 copy.11.refs_0_
  34.5 0.4 collective-permute-done.3.refs_3_
  34.8 0.7 copy.12.refs_1_
  35.6 0.1 collective-permute-start.4
  35.7 2.7 %collective-permute-start.5 = (bf16[8,64,384]{2,1,0:T(8,128)(2,1)}, bf16[8,64,384]{2,1,0:T(8,128)(2,1)}, u32[]{:S(2)}, u32[]{:S(2)}) collective-permute-start(bf16[8,64,384]{2,1,0:T(8,128)(2,1)} %get-tuple-element.43), channel_id=1, source_target_pairs={{0,2},{1,3},{2,0},{3,1},{4,6},{5,7},{6,4},{7,5},{8,16},{9,17},{10,... | collective-permute-start | bytes 1179656 | tf_op jit(solution)/shard_map/ppermute | solution.py:527
  38.4 3.5 %shard_map.88 = (bf16[3,1536,512]{2,1,0:T(8,128)(2,1)S(1)}, f32[3,8,512]{2,1,0:T(8,128)S(1)}) custom-call(bf16[8,3,64,384]{3,2,1,0:T(8,128)(2,1)S(1)} %all-to-all-done.refs_0_, bf16[8,64,384]{2,1,0:T(8,128)(2,1)S(1)} %shard_map.86.refs_1_, bf16[8,64,384]{2,1,0:T(8,128)(2,1)S(1)} %collective-permute-done.2.refs_2_, ...), custom_call_target="tpu_custom_call" | custom-call | flops 4024999936 | bytes 65536 | tf_op jit(solution)/shard_map/pallas_call | solution.py:456
  41.9 2.1 %copy-done.8 = bf16[3,1536,512]{2,1,0:T(8,128)(2,1)} copy-done((bf16[3,1536,512]{2,1,0:T(8,128)(2,1)}, bf16[3,1536,512]{2,1,0:T(8,128)(2,1)S(1)}, u32[]{:S(2)}) %copy-start.8) | copy-done | bytes 4718616
  44.1 0.6 copy-done.11
  44.7 0.5 all-to-all-done.1.refs_0_.refs_1_.refs_4_
  45.2 0.1 shard_map.90
  45.2 0.1 collective-permute-start.6
  45.3 0.0 slice-start
  45.3 0.0 slice-start.1
  45.3 0.5 collective-permute-start.7
  45.8 0.4 collective-permute-done.4.refs_1_
  46.2 0.7 collective-permute-done.5.refs_2_
  47.0 2.8 %shard_map.89 = (bf16[3,512,512]{2,1,0:T(8,128)(2,1)S(1)}, f32[3,8,512]{2,1,0:T(8,128)S(1)}, bf16[8,64,384]{2,1,0:T(8,128)(2,1)S(1)}, bf16[8,64,384]{2,1,0:T(8,128)(2,1)S(1)}) custom-call(bf16[8,3,64,384]{3,2,1,0:T(8,128)(2,1)S(1)} %all-to-all-done.refs_0_, bf16[8,64,384]{2,1,0:T(8,128)(2,1)} %collective-permute-done.4.refs_1_, ...), custom_call_target="tpu_custom_call" | custom-call | flops 2300000000 | bytes 65536 | tf_op jit(solution)/shard_map/pallas_call | solution.py:456
  49.8 1.8 %collective-permute-start.12 = (bf16[8,64,384]{2,1,0:T(8,128)(2,1)S(1)}, bf16[8,64,384]{2,1,0:T(8,128)(2,1)S(1)}, u32[]{:S(2)}, u32[]{:S(2)}) collective-permute-start(bf16[8,64,384]{2,1,0:T(8,128)(2,1)S(1)} %get-tuple-element.72), channel_id=1, source_target_pairs={{0,2},{1,3},{2,0},{3,1},{4,6},{5,7},{6,4},{7,5},{8,16},{9,17},{10,... | collective-permute-start | bytes 1179656 | tf_op jit(solution)/shard_map/ppermute | solution.py:527
  51.6 0.0 collective-permute-start.13
  51.6 2.0 %shard_map.91 = (bf16[8,64,384]{2,1,0:T(8,128)(2,1)S(1)}, bf16[8,64,384]{2,1,0:T(8,128)(2,1)S(1)}, bf16[8,64,384]{2,1,0:T(8,128)(2,1)S(1)}, f32[3,128,512]{2,1,0:T(8,128)S(1)}) custom-call(bf16[8,3,64,384]{3,2,1,0:T(8,128)(2,1)S(1)} %all-to-all-done.refs_0_, bf16[8,3,64,384]{3,2,1,0:T(8,128)(2,1)S(1)} %all-to-all-done.1.refs_0_.refs_1_.refs_4_, ...), custom_call_target="tpu_custom_call" | custom-call | flops 2300000000 | bytes 65536 | tf_op jit(solution)/shard_map/pallas_call | solution.py:456
  53.6 0.0 copy-start.9
  53.6 3.6 %collective-permute-done.6.refs_2_ = bf16[8,64,384]{2,1,0:T(8,128)(2,1)S(1)} collective-permute-done((bf16[8,64,384]{2,1,0:T(8,128)(2,1)S(1)}, bf16[8,64,384]{2,1,0:T(8,128)(2,1)S(1)}, u32[]{:S(2)}, u32[]{:S(2)}) %collective-permute-start.6) | collective-permute-done | bytes 393248 | tf_op jit(solution)/shard_map/ppermute | solution.py:527
  57.2 0.1 collective-permute-done.7.refs_3_
  57.3 2.4 %shard_map.92 = (bf16[8,64,384]{2,1,0:T(8,128)(2,1)}, bf16[8,64,384]{2,1,0:T(8,128)(2,1)S(1)}, f32[3,8,512]{2,1,0:T(8,128)S(1)}, f32[3,128,512]{2,1,0:T(8,128)S(1)}) custom-call(bf16[8,3,64,384]{3,2,1,0:T(8,128)(2,1)S(1)} %all-to-all-done.refs_0_, bf16[8,64,384]{2,1,0:T(8,128)(2,1)S(1)} %get-tuple-element.47.refs_1_, ...), custom_call_target="tpu_custom_call" | custom-call | flops 2300000000 | bytes 65536 | tf_op jit(solution)/shard_map/pallas_call | solution.py:456
  59.7 0.4 collective-permute-start.8
  60.1 3.4 %shard_map.93 = (bf16[8,64,384]{2,1,0:T(8,128)(2,1)S(1)}, bf16[8,64,384]{2,1,0:T(8,128)(2,1)S(1)}, bf16[8,64,384]{2,1,0:T(8,128)(2,1)S(1)}, bf16[8,64,384]{2,1,0:T(8,128)(2,1)S(1)}) custom-call(bf16[8,3,64,384]{3,2,1,0:T(8,128)(2,1)S(1)} %all-to-all-done.refs_0_, bf16[8,64,384]{2,1,0:T(8,128)(2,1)S(1)} %copy-done.6, ...), custom_call_target="tpu_custom_call" | custom-call | flops 4600000000 | bytes 65536 | tf_op jit(solution)/shard_map/pallas_call | solution.py:456
  63.5 0.0 copy-start.1
  63.5 0.0 copy-start.3
  63.5 2.2 %collective-permute-done.12.refs_2_ = bf16[8,64,384]{2,1,0:T(8,128)(2,1)S(1)} collective-permute-done((bf16[8,64,384]{2,1,0:T(8,128)(2,1)S(1)}, bf16[8,64,384]{2,1,0:T(8,128)(2,1)S(1)}, u32[]{:S(2)}, u32[]{:S(2)}) %collective-permute-start.12) | collective-permute-done | bytes 393248 | tf_op jit(solution)/shard_map/ppermute | solution.py:527
  65.8 0.0 collective-permute-done.13.refs_4_
  65.8 0.2 shard_map.97
  66.0 0.3 collective-permute-start.14
  66.3 1.6 %collective-permute-start.15 = (bf16[8,64,384]{2,1,0:T(8,128)(2,1)S(1)}, bf16[8,64,384]{2,1,0:T(8,128)(2,1)S(1)}, u32[]{:S(2)}, u32[]{:S(2)}) collective-permute-start(bf16[8,64,384]{2,1,0:T(8,128)(2,1)S(1)} %get-tuple-element.75), channel_id=1, source_target_pairs={{0,2},{1,3},{2,0},{3,1},{4,6},{5,7},{6,4},{7,5},{8,16},{9,17},{10,... | collective-permute-start | bytes 1179656 | tf_op jit(solution)/shard_map/ppermute | solution.py:527
  67.9 1.0 shard_map.94
  68.8 4.3 %all-to-all-start.2 = ((bf16[8,2,64,384]{3,2,1,0:T(8,128)(2,1)}), bf16[8,2,64,384]{3,2,1,0:T(8,128)(2,1)S(1)}, u32[]{:S(2)}, u32[]{:S(2)}) async-start(bf16[8,2,64,384]{3,2,1,0:T(8,128)(2,1)} %shard_map.94), calls=%async_computation.2 | async-start | bytes 1572864 | tf_op jit(solution)/shard_map/all_to_all | solution.py:500
  73.2 1.1 %collective-permute-done.8.refs_2_ = bf16[8,64,384]{2,1,0:T(8,128)(2,1)} collective-permute-done((bf16[8,64,384]{2,1,0:T(8,128)(2,1)}, bf16[8,64,384]{2,1,0:T(8,128)(2,1)}, u32[]{:S(2)}, u32[]{:S(2)}) %collective-permute-start.8) | collective-permute-done | bytes 393248 | tf_op jit(solution)/shard_map/ppermute | solution.py:527
  74.3 0.0 collective-permute-done.9.refs_4_
  74.3 1.3 %shard_map.96 = (bf16[8,64,384]{2,1,0:T(8,128)(2,1)S(1)}, bf16[8,64,384]{2,1,0:T(8,128)(2,1)S(1)}) custom-call(s32[1]{0:T(128)} %bitcast.refs_4_.refs_3_.refs_0_, bf16[8,64,384]{2,1,0:T(8,128)(2,1)S(1)} %copy-done.2, bf16[8,64,384]{2,1,0:T(8,128)(2,1)} %collective-permute-done.8.refs_2_, bf16[8,64,384]{2,1,0:T(8,128)(2,1)S(1)} %copy-done.4, ...), custom_call_target="tpu_custom_call" | custom-call | flops 230000000 | bytes 65536 | tf_op jit(solution)/shard_map/pallas_call | solution.py:456
  75.6 0.1 collective-permute-start.10
  75.7 0.5 collective-permute-start.11
  76.2 6.3 %collective-permute-done.14.refs_2_ = bf16[8,64,384]{2,1,0:T(8,128)(2,1)S(1)} collective-permute-done((bf16[8,64,384]{2,1,0:T(8,128)(2,1)S(1)}, bf16[8,64,384]{2,1,0:T(8,128)(2,1)S(1)}, u32[]{:S(2)}, u32[]{:S(2)}) %collective-permute-start.14) | collective-permute-done | bytes 393248 | tf_op jit(solution)/shard_map/ppermute | solution.py:527
  82.5 0.1 collective-permute-done.15.refs_3_
  82.6 0.2 shard_map.98.refs_4_
  82.8 7.5 %collective-permute-done.10.refs_2_ = bf16[8,64,384]{2,1,0:T(8,128)(2,1)S(1)} collective-permute-done((bf16[8,64,384]{2,1,0:T(8,128)(2,1)S(1)}, bf16[8,64,384]{2,1,0:T(8,128)(2,1)S(1)}, u32[]{:S(2)}, u32[]{:S(2)}) %collective-permute-start.10) | collective-permute-done | bytes 393248 | tf_op jit(solution)/shard_map/ppermute | solution.py:527
  90.3 0.1 collective-permute-done.11.refs_3_
  90.4 1.1 %shard_map.99 = bf16[8,2,64,384]{3,2,1,0:T(8,128)(2,1)} custom-call(s32[1]{0:T(128)} %bitcast.refs_4_.refs_3_.refs_0_, bf16[8,64,384]{2,1,0:T(8,128)(2,1)S(1)} %get-tuple-element.64.refs_1_, bf16[8,64,384]{2,1,0:T(8,128)(2,1)S(1)} %collective-permute-done.10.refs_2_, bf16[8,64,384]{2,1,0:T(8,128)(2,1)S(1)} %collective-permute-done.11.refs_3_, ...), custom_call_target="tpu_custom_call" | custom-call | flops 575000000 | bytes 65536 | tf_op jit(solution)/shard_map/pallas_call | solution.py:456
  91.5 4.0 %all-to-all-start.3 = ((bf16[8,2,64,384]{3,2,1,0:T(8,128)(2,1)}), bf16[8,2,64,384]{3,2,1,0:T(8,128)(2,1)S(1)}, u32[]{:S(2)}, u32[]{:S(2)}) async-start(bf16[8,2,64,384]{3,2,1,0:T(8,128)(2,1)} %shard_map.99), calls=%async_computation.3 | async-start | bytes 1572864 | tf_op jit(solution)/shard_map/all_to_all | solution.py:500
  95.5 0.9 shard_map.95
  96.5 10.1 %all-to-all-done.3.refs_0_ = bf16[8,2,64,384]{3,2,1,0:T(8,128)(2,1)S(1)} async-done(((bf16[8,2,64,384]{3,2,1,0:T(8,128)(2,1)}), bf16[8,2,64,384]{3,2,1,0:T(8,128)(2,1)S(1)}, u32[]{:S(2)}, u32[]{:S(2)}) %all-to-all-start.3) | async-done | bytes 786464 | tf_op jit(solution)/shard_map/all_to_all | solution.py:500
  106.5 0.9 shard_map.100
  (26 shorter events, 0.1 us)
Async XLA Ops:
  2.8 4.4 %copy-start = (bf16[64,3072]{1,0:T(8,128)(2,1)S(1)}, bf16[64,3072]{1,0:T(8,128)(2,1)}, u32[]{:S(2)}) copy-start(bf16[64,3072]{1,0:T(8,128)(2,1)} %refs_0_.3) | copy-start | bytes 1179652
  2.8 19.7 %all-to-all-start = ((bf16[8,3,64,384]{3,2,1,0:T(8,128)(2,1)}), bf16[8,3,64,384]{3,2,1,0:T(8,128)(2,1)S(1)}, u32[]{:S(2)}, u32[]{:S(2)}) async-start(bf16[8,3,64,384]{3,2,1,0:T(8,128)(2,1)} %shard_map.84), calls=%async_computation | async-start | bytes 2359296 | tf_op jit(solution)/shard_map/all_to_all | solution.py:500
  7.2 11.2 %collective-permute-start = (bf16[64,3072]{1,0:T(8,128)(2,1)S(1)}, bf16[64,3072]{1,0:T(8,128)(2,1)S(1)}, u32[]{:S(2)}, u32[]{:S(2)}) collective-permute-start(bf16[64,3072]{1,0:T(8,128)(2,1)S(1)} %copy-done), channel_id=1, source_target_pairs={{0,8},{1,9},{2,10},{3,11},{4,12},{5,13},{6,14},{7,15},{8,0},{9,1},... | collective-permute-start | bytes 1179656 | tf_op jit(solution)/shard_map/ppermute | solution.py:527
  7.7 11.8 %collective-permute-start.1 = (bf16[64,3072]{1,0:T(8,128)(2,1)S(1)}, bf16[64,3072]{1,0:T(8,128)(2,1)S(1)}, u32[]{:S(2)}, u32[]{:S(2)}) collective-permute-start(bf16[64,3072]{1,0:T(8,128)(2,1)S(1)} %copy-done), channel_id=1, source_target_pairs={{0,2},{1,3},{2,0},{3,1},{4,6},{5,7},{6,4},{7,5},{8,16},{9,17},{10,... | collective-permute-start | bytes 1179656 | tf_op jit(solution)/shard_map/ppermute | solution.py:527
  22.5 15.9 %copy-start.5 = (bf16[8,64,384]{2,1,0:T(8,128)(2,1)}, bf16[8,64,384]{2,1,0:T(8,128)(2,1)S(1)}, u32[]{:S(2)}) copy-start(bf16[8,64,384]{2,1,0:T(8,128)(2,1)S(1)} %shard_map.86.refs_1_) | copy-start | bytes 1179652
  22.5 11.2 %collective-permute-start.2 = (bf16[8,64,384]{2,1,0:T(8,128)(2,1)S(1)}, bf16[8,64,384]{2,1,0:T(8,128)(2,1)S(1)}, u32[]{:S(2)}, u32[]{:S(2)}) collective-permute-start(bf16[8,64,384]{2,1,0:T(8,128)(2,1)S(1)} %shard_map.86.refs_1_), channel_id=1, source_target_pairs={{0,8},{1,9},{2,10},{3,11},{4,12},{5,13},{6,14},{7,15},{8,0},{9,1},... | collective-permute-start | bytes 1179656 | tf_op jit(solution)/shard_map/ppermute | solution.py:527
  23.0 11.8 %collective-permute-start.3 = (bf16[8,64,384]{2,1,0:T(8,128)(2,1)S(1)}, bf16[8,64,384]{2,1,0:T(8,128)(2,1)S(1)}, u32[]{:S(2)}, u32[]{:S(2)}) collective-permute-start(bf16[8,64,384]{2,1,0:T(8,128)(2,1)S(1)} %shard_map.86.refs_1_), channel_id=1, source_target_pairs={{0,2},{1,3},{2,0},{3,1},{4,6},{5,7},{6,4},{7,5},{8,16},{9,17},{10,... | collective-permute-start | bytes 1179656 | tf_op jit(solution)/shard_map/ppermute | solution.py:527
  25.7 19.4 %all-to-all-start.1 = ((bf16[8,3,64,384]{3,2,1,0:T(8,128)(2,1)}), bf16[8,3,64,384]{3,2,1,0:T(8,128)(2,1)S(1)}, u32[]{:S(2)}, u32[]{:S(2)}) async-start(bf16[8,3,64,384]{3,2,1,0:T(8,128)(2,1)} %shard_map.85), calls=%async_computation.1 | async-start | bytes 2359296 | tf_op jit(solution)/shard_map/all_to_all | solution.py:500
  35.6 2.8 %copy-start.7 = (s32[2,4,4]{2,1,0:T(4,128)S(1)}, s32[2,4,4]{2,1,0:T(4,128)}, u32[]{:S(2)}) copy-start(s32[2,4,4]{2,1,0:T(4,128)} %refs_4_.1) | copy-start | bytes 388
  35.6 10.6 %collective-permute-start.4 = (bf16[8,64,384]{2,1,0:T(8,128)(2,1)}, bf16[8,64,384]{2,1,0:T(8,128)(2,1)}, u32[]{:S(2)}, u32[]{:S(2)}) collective-permute-start(bf16[8,64,384]{2,1,0:T(8,128)(2,1)} %get-tuple-element.42), channel_id=1, source_target_pairs={{0,8},{1,9},{2,10},{3,11},{4,12},{5,13},{6,14},{7,15},{8,0},{9,1},... | collective-permute-start | bytes 1179656 | tf_op jit(solution)/shard_map/ppermute | solution.py:527
  35.7 11.3 %collective-permute-start.5 = (bf16[8,64,384]{2,1,0:T(8,128)(2,1)}, bf16[8,64,384]{2,1,0:T(8,128)(2,1)}, u32[]{:S(2)}, u32[]{:S(2)}) collective-permute-start(bf16[8,64,384]{2,1,0:T(8,128)(2,1)} %get-tuple-element.43), channel_id=1, source_target_pairs={{0,2},{1,3},{2,0},{3,1},{4,6},{5,7},{6,4},{7,5},{8,16},{9,17},{10,... | collective-permute-start | bytes 1179656 | tf_op jit(solution)/shard_map/ppermute | solution.py:527
  41.9 2.2 %copy-start.8 = (bf16[3,1536,512]{2,1,0:T(8,128)(2,1)}, bf16[3,1536,512]{2,1,0:T(8,128)(2,1)S(1)}, u32[]{:S(2)}) copy-start(bf16[3,1536,512]{2,1,0:T(8,128)(2,1)S(1)} %get-tuple-element.52.refs_2_.refs_5_) | copy-start | bytes 14155780
  44.1 0.6 copy-start.11
  45.2 1.8 %copy-start.12 = (f32[3,8,512]{2,1,0:T(8,128)S(1)}, f32[3,8,512]{2,1,0:T(8,128)}, u32[]{:S(2)}) copy-start(f32[3,8,512]{2,1,0:T(8,128)} %copy-done.11) | copy-start | bytes 147460
  45.2 12.0 %collective-permute-start.6 = (bf16[8,64,384]{2,1,0:T(8,128)(2,1)S(1)}, bf16[8,64,384]{2,1,0:T(8,128)(2,1)S(1)}, u32[]{:S(2)}, u32[]{:S(2)}) collective-permute-start(bf16[8,64,384]{2,1,0:T(8,128)(2,1)S(1)} %get-tuple-element.49), channel_id=1, source_target_pairs={{0,8},{1,9},{2,10},{3,11},{4,12},{5,13},{6,14},{7,15},{8,0},{9,1},... | collective-permute-start | bytes 1179656 | tf_op jit(solution)/shard_map/ppermute | solution.py:527
  45.3 6.3 %slice-start = ((s8[4718592]{0:T(1024)(128)(4,1)}), s8[4194304]{0:T(1024)(128)(4,1)S(1)}, s32[]{:S(2)}) async-start(s8[4718592]{0:T(1024)(128)(4,1)} %bitcast.1), calls=%async_computation.4 | async-start | bytes 8388608
  45.3 6.3 %slice-start.1 = ((s8[4718592]{0:T(1024)(128)(4,1)}), s8[524288]{0:T(1024)(128)(4,1)S(1)}, s32[]{:S(2)}) async-start(s8[4718592]{0:T(1024)(128)(4,1)} %bitcast.1), calls=%async_computation.5 | async-start | bytes 1048576
  45.3 12.0 %collective-permute-start.7 = (bf16[8,64,384]{2,1,0:T(8,128)(2,1)S(1)}, bf16[8,64,384]{2,1,0:T(8,128)(2,1)S(1)}, u32[]{:S(2)}, u32[]{:S(2)}) collective-permute-start(bf16[8,64,384]{2,1,0:T(8,128)(2,1)S(1)} %get-tuple-element.50), channel_id=1, source_target_pairs={{0,2},{1,3},{2,0},{3,1},{4,6},{5,7},{6,4},{7,5},{8,16},{9,17},{10,... | collective-permute-start | bytes 1179656 | tf_op jit(solution)/shard_map/ppermute | solution.py:527
  49.8 16.0 %collective-permute-start.12 = (bf16[8,64,384]{2,1,0:T(8,128)(2,1)S(1)}, bf16[8,64,384]{2,1,0:T(8,128)(2,1)S(1)}, u32[]{:S(2)}, u32[]{:S(2)}) collective-permute-start(bf16[8,64,384]{2,1,0:T(8,128)(2,1)S(1)} %get-tuple-element.72), channel_id=1, source_target_pairs={{0,2},{1,3},{2,0},{3,1},{4,6},{5,7},{6,4},{7,5},{8,16},{9,17},{10,... | collective-permute-start | bytes 1179656 | tf_op jit(solution)/shard_map/ppermute | solution.py:527
  51.6 14.2 %collective-permute-start.13 = (bf16[8,64,384]{2,1,0:T(8,128)(2,1)S(1)}, bf16[8,64,384]{2,1,0:T(8,128)(2,1)S(1)}, u32[]{:S(2)}, u32[]{:S(2)}) collective-permute-start(bf16[8,64,384]{2,1,0:T(8,128)(2,1)S(1)} %get-tuple-element.72), channel_id=1, source_target_pairs={{0,8},{1,9},{2,10},{3,11},{4,12},{5,13},{6,14},{7,15},{8,0},{9,1},... | collective-permute-start | bytes 1179656 | tf_op jit(solution)/shard_map/ppermute | solution.py:527
  53.6 6.1 %copy-start.9 = (bf16[8,64,384]{2,1,0:T(8,128)(2,1)}, bf16[8,64,384]{2,1,0:T(8,128)(2,1)S(1)}, u32[]{:S(2)}) copy-start(bf16[8,64,384]{2,1,0:T(8,128)(2,1)S(1)} %get-tuple-element.70.refs_1_) | copy-start | bytes 1179652
  57.3 2.8 %copy-start.6 = (bf16[8,64,384]{2,1,0:T(8,128)(2,1)S(1)}, bf16[8,64,384]{2,1,0:T(8,128)(2,1)}, u32[]{:S(2)}) copy-start(bf16[8,64,384]{2,1,0:T(8,128)(2,1)} %copy-done.5) | copy-start | bytes 1179652
  59.7 14.6 %collective-permute-start.8 = (bf16[8,64,384]{2,1,0:T(8,128)(2,1)}, bf16[8,64,384]{2,1,0:T(8,128)(2,1)}, u32[]{:S(2)}, u32[]{:S(2)}) collective-permute-start(bf16[8,64,384]{2,1,0:T(8,128)(2,1)} %get-tuple-element.66), channel_id=1, source_target_pairs={{0,2},{1,3},{2,0},{3,1},{4,6},{5,7},{6,4},{7,5},{8,16},{9,17},{10,... | collective-permute-start | bytes 1179656 | tf_op jit(solution)/shard_map/ppermute | solution.py:527
  60.1 14.2 %collective-permute-start.9 = (bf16[8,64,384]{2,1,0:T(8,128)(2,1)}, bf16[8,64,384]{2,1,0:T(8,128)(2,1)}, u32[]{:S(2)}, u32[]{:S(2)}) collective-permute-start(bf16[8,64,384]{2,1,0:T(8,128)(2,1)} %get-tuple-element.66), channel_id=1, source_target_pairs={{0,8},{1,9},{2,10},{3,11},{4,12},{5,13},{6,14},{7,15},{8,0},{9,1},... | collective-permute-start | bytes 1179656 | tf_op jit(solution)/shard_map/ppermute | solution.py:527
  63.5 2.5 %copy-start.1 = (bf16[8,64,384]{2,1,0:T(8,128)(2,1)}, bf16[8,64,384]{2,1,0:T(8,128)(2,1)S(1)}, u32[]{:S(2)}) copy-start(bf16[8,64,384]{2,1,0:T(8,128)(2,1)S(1)} %get-tuple-element.65.refs_1_) | copy-start | bytes 1179652
  63.5 4.4 %copy-start.3 = (bf16[8,64,384]{2,1,0:T(8,128)(2,1)}, bf16[8,64,384]{2,1,0:T(8,128)(2,1)S(1)}, u32[]{:S(2)}) copy-start(bf16[8,64,384]{2,1,0:T(8,128)(2,1)S(1)} %get-tuple-element.67.refs_3_) | copy-start | bytes 1179652
  66.0 16.5 %collective-permute-start.14 = (bf16[8,64,384]{2,1,0:T(8,128)(2,1)S(1)}, bf16[8,64,384]{2,1,0:T(8,128)(2,1)S(1)}, u32[]{:S(2)}, u32[]{:S(2)}) collective-permute-start(bf16[8,64,384]{2,1,0:T(8,128)(2,1)S(1)} %get-tuple-element.74), channel_id=1, source_target_pairs={{0,8},{1,9},{2,10},{3,11},{4,12},{5,13},{6,14},{7,15},{8,0},{9,1},... | collective-permute-start | bytes 1179656 | tf_op jit(solution)/shard_map/ppermute | solution.py:527
  66.3 16.3 %collective-permute-start.15 = (bf16[8,64,384]{2,1,0:T(8,128)(2,1)S(1)}, bf16[8,64,384]{2,1,0:T(8,128)(2,1)S(1)}, u32[]{:S(2)}, u32[]{:S(2)}) collective-permute-start(bf16[8,64,384]{2,1,0:T(8,128)(2,1)S(1)} %get-tuple-element.75), channel_id=1, source_target_pairs={{0,2},{1,3},{2,0},{3,1},{4,6},{5,7},{6,4},{7,5},{8,16},{9,17},{10,... | collective-permute-start | bytes 1179656 | tf_op jit(solution)/shard_map/ppermute | solution.py:527
  68.8 5.5 %copy-start.2 = (bf16[8,64,384]{2,1,0:T(8,128)(2,1)S(1)}, bf16[8,64,384]{2,1,0:T(8,128)(2,1)}, u32[]{:S(2)}) copy-start(bf16[8,64,384]{2,1,0:T(8,128)(2,1)} %copy-done.1) | copy-start | bytes 1179652
  68.8 5.5 %copy-start.4 = (bf16[8,64,384]{2,1,0:T(8,128)(2,1)S(1)}, bf16[8,64,384]{2,1,0:T(8,128)(2,1)}, u32[]{:S(2)}) copy-start(bf16[8,64,384]{2,1,0:T(8,128)(2,1)} %copy-done.3) | copy-start | bytes 1179652
  68.8 22.6 %all-to-all-start.2 = ((bf16[8,2,64,384]{3,2,1,0:T(8,128)(2,1)}), bf16[8,2,64,384]{3,2,1,0:T(8,128)(2,1)S(1)}, u32[]{:S(2)}, u32[]{:S(2)}) async-start(bf16[8,2,64,384]{3,2,1,0:T(8,128)(2,1)} %shard_map.94), calls=%async_computation.2 | async-start | bytes 1572864 | tf_op jit(solution)/shard_map/all_to_all | solution.py:500
  73.2 9.4 %copy-start.10 = (bf16[8,64,384]{2,1,0:T(8,128)(2,1)S(1)}, bf16[8,64,384]{2,1,0:T(8,128)(2,1)}, u32[]{:S(2)}) copy-start(bf16[8,64,384]{2,1,0:T(8,128)(2,1)} %copy-done.9) | copy-start | bytes 1179652
  75.6 14.7 %collective-permute-start.10 = (bf16[8,64,384]{2,1,0:T(8,128)(2,1)S(1)}, bf16[8,64,384]{2,1,0:T(8,128)(2,1)S(1)}, u32[]{:S(2)}, u32[]{:S(2)}) collective-permute-start(bf16[8,64,384]{2,1,0:T(8,128)(2,1)S(1)} %get-tuple-element.68), channel_id=1, source_target_pairs={{0,8},{1,9},{2,10},{3,11},{4,12},{5,13},{6,14},{7,15},{8,0},{9,1},... | collective-permute-start | bytes 1179656 | tf_op jit(solution)/shard_map/ppermute | solution.py:527
  75.7 14.7 %collective-permute-start.11 = (bf16[8,64,384]{2,1,0:T(8,128)(2,1)S(1)}, bf16[8,64,384]{2,1,0:T(8,128)(2,1)S(1)}, u32[]{:S(2)}, u32[]{:S(2)}) collective-permute-start(bf16[8,64,384]{2,1,0:T(8,128)(2,1)S(1)} %get-tuple-element.69), channel_id=1, source_target_pairs={{0,2},{1,3},{2,0},{3,1},{4,6},{5,7},{6,4},{7,5},{8,16},{9,17},{10,... | collective-permute-start | bytes 1179656 | tf_op jit(solution)/shard_map/ppermute | solution.py:527
  91.5 15.1 %all-to-all-start.3 = ((bf16[8,2,64,384]{3,2,1,0:T(8,128)(2,1)}), bf16[8,2,64,384]{3,2,1,0:T(8,128)(2,1)S(1)}, u32[]{:S(2)}, u32[]{:S(2)}) async-start(bf16[8,2,64,384]{3,2,1,0:T(8,128)(2,1)} %shard_map.99), calls=%async_computation.3 | async-start | bytes 1572864 | tf_op jit(solution)/shard_map/all_to_all | solution.py:500

commit v7 on v6

--- a/solution.py
+++ b/solution.py
@@ -19,7 +19,7 @@
 FIRST_PACK_BYTES = 60 * 1024 * 1024
 
 FLOPS_PER_US = 1_150_000_000
-SECOND_HOP_WORK = 20
+PACK_VALUES_WORK = 40
 PICK_WORK = 20
 SUM_WORK = 20
 
@@ -387,10 +387,6 @@
         copy.wait()
 
 
-def pass_kernel(*refs):
-    pass
-
-
 def pick_kernel(places, in_ref, *out_refs):
     for place, ref in zip(places, out_refs):
         ref[...] = in_ref[:, place]
@@ -465,7 +461,7 @@
     def packed(count):
         return jax.ShapeDtypeStruct((peers, count, rows, width), BF16)
 
-    def pack(*arrays, limit=VMEM_BYTES):
+    def pack(*arrays, limit=VMEM_BYTES, work=0.5):
         count = len(arrays)
         return pl.pallas_call(
             pack_kernel,
@@ -479,22 +475,12 @@
                 pltpu.SemaphoreType.DMA((count,)),
             ],
             compiler_params=pltpu.CompilerParams(vmem_limit_bytes=limit),
-            cost_estimate=estimate(0.5),
+            cost_estimate=estimate(work),
         )(*arrays)
 
     def pick(landed, *places):
         kernel = functools.partial(pick_kernel, places)
         return call(kernel, (one,) * len(places), PICK_WORK, landed)
-
-    def later(work, *arrays):
-        return pl.pallas_call(
-            pass_kernel,
-            in_specs=[anywhere] * len(arrays),
-            out_specs=(anywhere,) * len(arrays),
-            out_shape=tuple(jax.ShapeDtypeStruct(x.shape, x.dtype) for x in arrays),
-            input_output_aliases={i: i for i in range(len(arrays))},
-            cost_estimate=estimate(work),
-        )(*arrays)
 
     def swap(array):
         return lax.all_to_all(array, plane, 0, 0, tiled=True)
@@ -532,27 +518,28 @@
         )
 
     v1_rows, v3_rows = send(value_rows, edge), send(value_rows, middle)
-    kqg = swap(pack(key_rows, query_rows, out_grad, limit=FIRST_PACK_BYTES))
-    values = pack(value_rows, v1_rows, v3_rows)
-    kqg, values = barrier(kqg, values)
-    (k0,) = pick(kqg, 0)
+    kq = swap(pack(key_rows, query_rows, limit=FIRST_PACK_BYTES))
+    values = pack(value_rows, v1_rows, v3_rows, out_grad, work=PACK_VALUES_WORK)
+    kq, values = barrier(kq, values)
+    (k0,) = pick(kq, 0)
     k1, k3 = send(k0, edge), send(k0, middle)
-    k1_on, k3_on = later(SECOND_HOP_WORK, k1, k3)
-    ka, kb = send(k3_on, edge), send(k1_on, middle)
+    ka, kb = send(k3, edge), send(k1, middle)
     for name, array in (("k0", k0), ("k1", k1), ("k3", k3), ("ka", ka), ("kb", kb)):
         found[name] = (array, None)
-    found.update(q=(kqg, 1), g=(kqg, 2))
+    found.update(q=(kq, 1))
+    values = swap(values)
+    v1, v3 = pick(values, 1, 2)
+    found.update(g=(values, 3), v0=(values, 0), v1=(values, 1), v3=(values, 2))
+    found.update(va=(send(v3, edge), None), vb=(send(v1, middle), None))
+    k0, v1 = barrier(k0, v1)
+    found["k0"] = (k0, None)
     e_near, ml = call(
         near_scores_kernel, (near_e, stat), 3.5, frame, block_mask,
         names=("q", "k0", "k1", "k3"),
     )
-    values, ml = barrier(swap(values), ml)
-    v1, v3 = pick(values, 1, 2)
-    found.update(v0=(values, 0), v1=(values, 1), v3=(values, 2))
-    found.update(va=(send(v3, edge), None), vb=(send(v1, middle), None))
 
     p_far, w, dv2, k2 = call(
-        far_scores_kernel, (far_e, stat, one, one), 2, frame, block_mask, ml,
+        far_scores_kernel, (far_e, stat, one, one), 10, frame, block_mask, ml,
         names=("q", "g", "ka", "kb"),
     )
     found["k2"] = (k2, None)

time: 109 us -> 109 us (level)
  waiting for transfers between devices: 47.3 us -> 51 us
  local copies, waits for them, and re-layouts: 4.32 us -> 0.8 us
  starting transfers between devices: 31.4 us -> 30 us
    all_to_all x4, waiting for transfers between devices: 11.8 us -> 22.7 us  [swap(): return lax.all_to_all(array, plane, 0, 0, tiled=True)]
    ppermute x16, waiting for transfers between devices: 35.5 us -> 28.3 us  [send(): return lax.ppermute(array, devices, pairs)]
    unnamed x32 -> x30, local copies, waits for them, and re-layouts: 4.32 us -> 0.8 us
    ppermute x16, starting transfers between devices: 14.4 us -> 13.3 us  [send(): return lax.ppermute(array, devices, pairs)]
  transfers between devices with their start and end apart: 20 -> 20, of which waited for: 17 -> 14; matrix products, arithmetic and copies ran while one was open for 1% -> 0% of each run, Pallas kernels for 19% -> 22%
where the time goes in v7:
time: 109 us; the launch traced here: 107 us
  waiting for transfers between devices  51 us (47%)
  starting transfers between devices  30 us (28%)
  Pallas kernels  24.4 us (22%)
    ppermute x16, waiting for transfers between devices, send(): return lax.ppermute(array, devices, pairs)  28.3 us
    all_to_all x4, waiting for transfers between devices, swap(): return lax.all_to_all(array, plane, 0, 0, tiled=True)  22.7 us
    pallas_call x14, Pallas kernels, call(): pl.pallas_call(body, in_specs=[smem if x.dtype == jnp.int32 else vmem for...  20.4 us
    all_to_all x4, starting transfers between devices, swap(): return lax.all_to_all(array, plane, 0, 0, tiled=True)  16.7 us
    ppermute x16, starting transfers between devices, send(): return lax.ppermute(array, devices, pairs)  13.3 us
    pallas_call x2, Pallas kernels, pack(): pl.pallas_call(pack_kernel, in_specs=[anywhere] * count, out_specs=anywhe...  3.97 us
  transfers between devices with their start and end apart: 20, of which 14 were waited for; matrix products, arithmetic and copies ran while one was open for 0% of the time, Pallas kernels for 22%

profile of v7, /device:TPU:10, one launch (start us, length us, event | category | flops | bytes accessed | tf_op | source)
XLA Modules:
  0.0 107.1 jit_solution(3470358106846947446)
XLA Ops:
  0.6 0.0 copy-start.4
  0.6 0.0 copy-start.5
  0.7 0.5 collective-permute-start
  1.2 2.7 %collective-permute-start.1 = (bf16[64,3072]{1,0:T(8,128)(2,1)}, bf16[64,3072]{1,0:T(8,128)(2,1)S(1)}, u32[]{:S(2)}, u32[]{:S(2)}) collective-permute-start(bf16[64,3072]{1,0:T(8,128)(2,1)} %refs_0_.3), channel_id=1, source_target_pairs={{0,2},{1,3},{2,0},{3,1},{4,6},{5,7},{6,4},{7,5},{8,16},{9,17},{10,... | collective-permute-start | bytes 1179656 | tf_op jit(solution)/shard_map/ppermute | solution.py:513
  3.9 2.0 %shard_map.84 = bf16[8,2,64,384]{3,2,1,0:T(8,128)(2,1)} custom-call(bf16[64,3072]{1,0:T(8,128)(2,1)} %refs_0_.2, bf16[64,3072]{1,0:T(8,128)(2,1)} %refs_1_.1), custom_call_target="tpu_custom_call" | custom-call | flops 575000000 | bytes 65536 | tf_op jit(solution)/shard_map/pallas_call | solution.py:466
  5.8 4.3 %all-to-all-start = ((bf16[8,2,64,384]{3,2,1,0:T(8,128)(2,1)}), bf16[8,2,64,384]{3,2,1,0:T(8,128)(2,1)S(1)}, u32[]{:S(2)}, u32[]{:S(2)}) async-start(bf16[8,2,64,384]{3,2,1,0:T(8,128)(2,1)} %shard_map.84), calls=%async_computation | async-start | bytes 1572864 | tf_op jit(solution)/shard_map/all_to_all | solution.py:486
  10.1 1.7 %collective-permute-done.refs_1_ = bf16[64,3072]{1,0:T(8,128)(2,1)S(1)} collective-permute-done((bf16[64,3072]{1,0:T(8,128)(2,1)}, bf16[64,3072]{1,0:T(8,128)(2,1)S(1)}, u32[]{:S(2)}, u32[]{:S(2)}) %collective-permute-start) | collective-permute-done | bytes 393248 | tf_op jit(solution)/shard_map/ppermute | solution.py:513
  11.8 1.2 %collective-permute-done.1.refs_2_ = bf16[64,3072]{1,0:T(8,128)(2,1)S(1)} collective-permute-done((bf16[64,3072]{1,0:T(8,128)(2,1)}, bf16[64,3072]{1,0:T(8,128)(2,1)S(1)}, u32[]{:S(2)}, u32[]{:S(2)}) %collective-permute-start.1) | collective-permute-done | bytes 393248 | tf_op jit(solution)/shard_map/ppermute | solution.py:513
  12.9 0.0 copy-done.4
  13.0 2.0 %shard_map.85 = bf16[8,4,64,384]{3,2,1,0:T(8,128)(2,1)} custom-call(bf16[64,3072]{1,0:T(8,128)(2,1)S(1)} %copy-done.4, bf16[64,3072]{1,0:T(8,128)(2,1)S(1)} %collective-permute-done.refs_1_, bf16[64,3072]{1,0:T(8,128)(2,1)S(1)} %collective-permute-done.1.refs_2_, bf16[64,3072]{1,0:T(8,128)(2,1)S(1)} %copy-done.5), custom_call_target="tpu_custom_call" | custom-call | flops 46000001024 | bytes 65536 | tf_op jit(solution)/shard_map/pallas_call | solution.py:466
  15.0 6.2 %all-to-all-done.refs_0_ = bf16[8,2,64,384]{3,2,1,0:T(8,128)(2,1)S(1)} async-done(((bf16[8,2,64,384]{3,2,1,0:T(8,128)(2,1)}), bf16[8,2,64,384]{3,2,1,0:T(8,128)(2,1)S(1)}, u32[]{:S(2)}, u32[]{:S(2)}) %all-to-all-start) | async-done | bytes 786464 | tf_op jit(solution)/shard_map/all_to_all | solution.py:486
  21.1 4.2 %all-to-all-start.1 = ((bf16[8,4,64,384]{3,2,1,0:T(8,128)(2,1)}), bf16[8,4,64,384]{3,2,1,0:T(8,128)(2,1)S(1)}, u32[]{:S(2)}, u32[]{:S(2)}) async-start(bf16[8,4,64,384]{3,2,1,0:T(8,128)(2,1)} %shard_map.85), calls=%async_computation.1 | async-start | bytes 3145728 | tf_op jit(solution)/shard_map/all_to_all | solution.py:486
  25.4 0.0 copy-start.6
  25.4 0.1 collective-permute-start.2
  25.5 0.1 collective-permute-start.4
  25.6 0.0 copy-start.12
  25.6 11.1 %collective-permute-done.2.refs_3_.refs_4_ = bf16[8,64,384]{2,1,0:T(8,128)(2,1)S(1)} collective-permute-done((bf16[8,64,384]{2,1,0:T(8,128)(2,1)S(1)}, bf16[8,64,384]{2,1,0:T(8,128)(2,1)S(1)}, u32[]{:S(2)}, u32[]{:S(2)}) %collective-permute-start.2) | collective-permute-done | bytes 393248 | tf_op jit(solution)/shard_map/ppermute | solution.py:513
  36.6 0.0 collective-permute-start.3
  36.6 0.1 collective-permute-done.4.refs_2_.refs_3_
  36.7 1.7 %collective-permute-start.5 = (bf16[8,64,384]{2,1,0:T(8,128)(2,1)S(1)}, bf16[8,64,384]{2,1,0:T(8,128)(2,1)}, u32[]{:S(2)}, u32[]{:S(2)}) collective-permute-start(bf16[8,64,384]{2,1,0:T(8,128)(2,1)S(1)} %collective-permute-done.4.refs_2_.refs_3_), channel_id=1, source_target_pairs={{0,2},{1,3},{2,0},{3,1},{4,6},{5,7},{6,4},{7,5},{8,16},{9,17},{10,... | collective-permute-start | bytes 1179656 | tf_op jit(solution)/shard_map/ppermute | solution.py:513
  38.4 6.4 %all-to-all-done.1.refs_0_.refs_1_ = bf16[8,4,64,384]{3,2,1,0:T(8,128)(2,1)S(1)} async-done(((bf16[8,4,64,384]{3,2,1,0:T(8,128)(2,1)}), bf16[8,4,64,384]{3,2,1,0:T(8,128)(2,1)S(1)}, u32[]{:S(2)}, u32[]{:S(2)}) %all-to-all-start.1) | async-done | bytes 1572896 | tf_op jit(solution)/shard_map/all_to_all | solution.py:486
  44.8 0.1 shard_map.87
  44.9 0.1 collective-permute-start.7
  45.0 0.1 collective-permute-start.6
  45.1 3.5 %shard_map.88 = (bf16[3,1536,512]{2,1,0:T(8,128)(2,1)S(1)}, f32[3,8,512]{2,1,0:T(8,128)S(1)}) custom-call(bf16[8,2,64,384]{3,2,1,0:T(8,128)(2,1)S(1)} %all-to-all-done.refs_0_, bf16[8,64,384]{2,1,0:T(8,128)(2,1)S(1)} %shard_map.86.refs_1_.refs_2_, bf16[8,64,384]{2,1,0:T(8,128)(2,1)S(1)} %collective-permute-done.4.refs_2_.refs_3_, ...), custom_call_target="tpu_custom_call" | custom-call | flops 4024999936 | bytes 65536 | tf_op jit(solution)/shard_map/pallas_call | solution.py:452
  48.6 0.0 collective-permute-done.3.refs_2_
  48.6 0.0 collective-permute-done.5.refs_3_
  48.6 2.8 %shard_map.89 = (bf16[3,512,512]{2,1,0:T(8,128)(2,1)S(1)}, f32[3,8,512]{2,1,0:T(8,128)S(1)}, bf16[8,64,384]{2,1,0:T(8,128)(2,1)S(1)}, bf16[8,64,384]{2,1,0:T(8,128)(2,1)S(1)}) custom-call(bf16[8,2,64,384]{3,2,1,0:T(8,128)(2,1)S(1)} %all-to-all-done.refs_0_, bf16[8,4,64,384]{3,2,1,0:T(8,128)(2,1)S(1)} %all-to-all-done.1.refs_0_.refs_1_, ...), custom_call_target="tpu_custom_call" | custom-call | flops 11500000256 | bytes 65536 | tf_op jit(solution)/shard_map/pallas_call | solution.py:452
  51.5 2.0 %collective-permute-start.12 = (bf16[8,64,384]{2,1,0:T(8,128)(2,1)S(1)}, bf16[8,64,384]{2,1,0:T(8,128)(2,1)S(1)}, u32[]{:S(2)}, u32[]{:S(2)}) collective-permute-start(bf16[8,64,384]{2,1,0:T(8,128)(2,1)S(1)} %get-tuple-element.66), channel_id=1, source_target_pairs={{0,2},{1,3},{2,0},{3,1},{4,6},{5,7},{6,4},{7,5},{8,16},{9,17},{10,... | collective-permute-start | bytes 1179656 | tf_op jit(solution)/shard_map/ppermute | solution.py:513
  53.5 0.1 collective-permute-start.13
  53.6 2.0 %shard_map.90 = (bf16[8,64,384]{2,1,0:T(8,128)(2,1)S(1)}, bf16[8,64,384]{2,1,0:T(8,128)(2,1)S(1)}, bf16[8,64,384]{2,1,0:T(8,128)(2,1)S(1)}, f32[3,128,512]{2,1,0:T(8,128)S(1)}) custom-call(bf16[8,4,64,384]{3,2,1,0:T(8,128)(2,1)S(1)} %all-to-all-done.1.refs_0_.refs_1_, bf16[3,1536,512]{2,1,0:T(8,128)(2,1)S(1)} %get-tuple-element.46.refs_1_.refs_5_, ...), custom_call_target="tpu_custom_call" | custom-call | flops 2300000000 | bytes 65536 | tf_op jit(solution)/shard_map/pallas_call | solution.py:452
  55.6 0.7 copy-done.13
  56.4 0.5 collective-permute-done.7.refs_4_
  56.9 0.0 collective-permute-done.6.refs_3_
  56.9 2.3 %shard_map.91 = (bf16[8,64,384]{2,1,0:T(8,128)(2,1)}, bf16[8,64,384]{2,1,0:T(8,128)(2,1)S(1)}, f32[3,8,512]{2,1,0:T(8,128)S(1)}, f32[3,128,512]{2,1,0:T(8,128)S(1)}) custom-call(bf16[8,2,64,384]{3,2,1,0:T(8,128)(2,1)S(1)} %all-to-all-done.refs_0_, bf16[8,4,64,384]{3,2,1,0:T(8,128)(2,1)S(1)} %all-to-all-done.1.refs_0_.refs_1_, ...), custom_call_target="tpu_custom_call" | custom-call | flops 2300000000 | bytes 65536 | tf_op jit(solution)/shard_map/pallas_call | solution.py:452
  59.2 2.1 %collective-permute-start.8 = (bf16[8,64,384]{2,1,0:T(8,128)(2,1)}, bf16[8,64,384]{2,1,0:T(8,128)(2,1)S(1)}, u32[]{:S(2)}, u32[]{:S(2)}) collective-permute-start(bf16[8,64,384]{2,1,0:T(8,128)(2,1)} %get-tuple-element.60), channel_id=1, source_target_pairs={{0,2},{1,3},{2,0},{3,1},{4,6},{5,7},{6,4},{7,5},{8,16},{9,17},{10,... | collective-permute-start | bytes 1179656 | tf_op jit(solution)/shard_map/ppermute | solution.py:513
  61.3 0.0 collective-permute-start.9
  61.3 0.0 copy-done.7
  61.3 3.4 %shard_map.92 = (bf16[8,64,384]{2,1,0:T(8,128)(2,1)S(1)}, bf16[8,64,384]{2,1,0:T(8,128)(2,1)S(1)}, bf16[8,64,384]{2,1,0:T(8,128)(2,1)S(1)}, bf16[8,64,384]{2,1,0:T(8,128)(2,1)S(1)}) custom-call(bf16[8,2,64,384]{3,2,1,0:T(8,128)(2,1)S(1)} %all-to-all-done.refs_0_, bf16[8,4,64,384]{3,2,1,0:T(8,128)(2,1)S(1)} %all-to-all-done.1.refs_0_.refs_1_, ...), custom_call_target="tpu_custom_call" | custom-call | flops 4600000000 | bytes 65536 | tf_op jit(solution)/shard_map/pallas_call | solution.py:452
  64.7 0.0 copy-start
  64.7 0.0 copy-start.2
  64.7 0.6 collective-permute-done.12.refs_2_
  65.3 0.2 collective-permute-done.13.refs_4_
  65.5 0.9 shard_map.96
  66.4 1.3 %collective-permute-start.14 = (bf16[8,64,384]{2,1,0:T(8,128)(2,1)}, bf16[8,64,384]{2,1,0:T(8,128)(2,1)S(1)}, u32[]{:S(2)}, u32[]{:S(2)}) collective-permute-start(bf16[8,64,384]{2,1,0:T(8,128)(2,1)} %get-tuple-element.68), channel_id=1, source_target_pairs={{0,8},{1,9},{2,10},{3,11},{4,12},{5,13},{6,14},{7,15},{8,0},{9,1},... | collective-permute-start | bytes 1179656 | tf_op jit(solution)/shard_map/ppermute | solution.py:513
  67.7 0.6 collective-permute-start.15
  68.3 1.0 shard_map.93
  69.3 4.2 %all-to-all-start.2 = ((bf16[8,2,64,384]{3,2,1,0:T(8,128)(2,1)}), bf16[8,2,64,384]{3,2,1,0:T(8,128)(2,1)S(1)}, u32[]{:S(2)}, u32[]{:S(2)}) async-start(bf16[8,2,64,384]{3,2,1,0:T(8,128)(2,1)} %shard_map.93), calls=%async_computation.2 | async-start | bytes 1572864 | tf_op jit(solution)/shard_map/all_to_all | solution.py:486
  73.5 0.2 collective-permute-done.8.refs_2_
  73.7 0.2 collective-permute-done.9.refs_4_
  73.9 0.2 shard_map.95
  74.1 0.1 collective-permute-start.10
  74.2 2.0 %collective-permute-start.11 = (bf16[8,64,384]{2,1,0:T(8,128)(2,1)S(1)}, bf16[8,64,384]{2,1,0:T(8,128)(2,1)S(1)}, u32[]{:S(2)}, u32[]{:S(2)}) collective-permute-start(bf16[8,64,384]{2,1,0:T(8,128)(2,1)S(1)} %get-tuple-element.63), channel_id=1, source_target_pairs={{0,2},{1,3},{2,0},{3,1},{4,6},{5,7},{6,4},{7,5},{8,16},{9,17},{10,... | collective-permute-start | bytes 1179656 | tf_op jit(solution)/shard_map/ppermute | solution.py:513
  76.2 6.2 %collective-permute-done.14.refs_2_ = bf16[8,64,384]{2,1,0:T(8,128)(2,1)S(1)} collective-permute-done((bf16[8,64,384]{2,1,0:T(8,128)(2,1)}, bf16[8,64,384]{2,1,0:T(8,128)(2,1)S(1)}, u32[]{:S(2)}, u32[]{:S(2)}) %collective-permute-start.14) | collective-permute-done | bytes 393248 | tf_op jit(solution)/shard_map/ppermute | solution.py:513
  82.3 0.0 collective-permute-done.15.refs_3_
  82.3 1.2 %shard_map.97.refs_4_ = bf16[8,64,384]{2,1,0:T(8,128)(2,1)S(1)} custom-call(s32[1]{0:T(128)} %bitcast.refs_4_.refs_5_.refs_0_, bf16[8,64,384]{2,1,0:T(8,128)(2,1)S(1)} %copy-done.14, bf16[8,64,384]{2,1,0:T(8,128)(2,1)S(1)} %collective-permute-done.14.refs_2_, bf16[8,64,384]{2,1,0:T(8,128)(2,1)} %collective-permute-done.15.refs_3_), custom_call_target="tpu_custom_call" | custom-call | flops 23000000512 | bytes 65536 | tf_op jit(solution)/shard_map/pallas_call | solution.py:452
  83.5 6.5 %collective-permute-done.10.refs_2_ = bf16[8,64,384]{2,1,0:T(8,128)(2,1)S(1)} collective-permute-done((bf16[8,64,384]{2,1,0:T(8,128)(2,1)S(1)}, bf16[8,64,384]{2,1,0:T(8,128)(2,1)S(1)}, u32[]{:S(2)}, u32[]{:S(2)}) %collective-permute-start.10) | collective-permute-done | bytes 393248 | tf_op jit(solution)/shard_map/ppermute | solution.py:513
  90.0 0.0 collective-permute-done.11.refs_3_
  90.0 1.1 %shard_map.98 = bf16[8,2,64,384]{3,2,1,0:T(8,128)(2,1)} custom-call(s32[1]{0:T(128)} %bitcast.refs_4_.refs_5_.refs_0_, bf16[8,64,384]{2,1,0:T(8,128)(2,1)S(1)} %get-tuple-element.58.refs_1_, bf16[8,64,384]{2,1,0:T(8,128)(2,1)S(1)} %collective-permute-done.10.refs_2_, bf16[8,64,384]{2,1,0:T(8,128)(2,1)S(1)} %collective-permute-done.11.refs_3_, ...), custom_call_target="tpu_custom_call" | custom-call | flops 575000000 | bytes 65536 | tf_op jit(solution)/shard_map/pallas_call | solution.py:452
  91.1 0.0 all-to-all-done.2.refs_0_
  91.1 4.0 %all-to-all-start.3 = ((bf16[8,2,64,384]{3,2,1,0:T(8,128)(2,1)}), bf16[8,2,64,384]{3,2,1,0:T(8,128)(2,1)S(1)}, u32[]{:S(2)}, u32[]{:S(2)}) async-start(bf16[8,2,64,384]{3,2,1,0:T(8,128)(2,1)} %shard_map.98), calls=%async_computation.3 | async-start | bytes 1572864 | tf_op jit(solution)/shard_map/all_to_all | solution.py:486
  95.2 0.9 shard_map.94
  96.1 10.1 %all-to-all-done.3.refs_0_ = bf16[8,2,64,384]{3,2,1,0:T(8,128)(2,1)S(1)} async-done(((bf16[8,2,64,384]{3,2,1,0:T(8,128)(2,1)}), bf16[8,2,64,384]{3,2,1,0:T(8,128)(2,1)S(1)}, u32[]{:S(2)}, u32[]{:S(2)}) %all-to-all-start.3) | async-done | bytes 786464 | tf_op jit(solution)/shard_map/all_to_all | solution.py:486
  106.2 0.9 shard_map.99
  (22 shorter events, 0.1 us)
Async XLA Ops:
  0.6 12.3 %copy-start.4 = (bf16[64,3072]{1,0:T(8,128)(2,1)S(1)}, bf16[64,3072]{1,0:T(8,128)(2,1)}, u32[]{:S(2)}) copy-start(bf16[64,3072]{1,0:T(8,128)(2,1)} %refs_0_.3) | copy-start | bytes 1179652
  0.6 12.3 %copy-start.5 = (bf16[64,3072]{1,0:T(8,128)(2,1)S(1)}, bf16[64,3072]{1,0:T(8,128)(2,1)}, u32[]{:S(2)}) copy-start(bf16[64,3072]{1,0:T(8,128)(2,1)} %refs_3_.1) | copy-start | bytes 1179652
  0.7 11.1 %collective-permute-start = (bf16[64,3072]{1,0:T(8,128)(2,1)}, bf16[64,3072]{1,0:T(8,128)(2,1)S(1)}, u32[]{:S(2)}, u32[]{:S(2)}) collective-permute-start(bf16[64,3072]{1,0:T(8,128)(2,1)} %refs_0_.3), channel_id=1, source_target_pairs={{0,8},{1,9},{2,10},{3,11},{4,12},{5,13},{6,14},{7,15},{8,0},{9,1},... | collective-permute-start | bytes 1179656 | tf_op jit(solution)/shard_map/ppermute | solution.py:513
  1.2 11.8 %collective-permute-start.1 = (bf16[64,3072]{1,0:T(8,128)(2,1)}, bf16[64,3072]{1,0:T(8,128)(2,1)S(1)}, u32[]{:S(2)}, u32[]{:S(2)}) collective-permute-start(bf16[64,3072]{1,0:T(8,128)(2,1)} %refs_0_.3), channel_id=1, source_target_pairs={{0,2},{1,3},{2,0},{3,1},{4,6},{5,7},{6,4},{7,5},{8,16},{9,17},{10,... | collective-permute-start | bytes 1179656 | tf_op jit(solution)/shard_map/ppermute | solution.py:513
  5.8 15.3 %all-to-all-start = ((bf16[8,2,64,384]{3,2,1,0:T(8,128)(2,1)}), bf16[8,2,64,384]{3,2,1,0:T(8,128)(2,1)S(1)}, u32[]{:S(2)}, u32[]{:S(2)}) async-start(bf16[8,2,64,384]{3,2,1,0:T(8,128)(2,1)} %shard_map.84), calls=%async_computation | async-start | bytes 1572864 | tf_op jit(solution)/shard_map/all_to_all | solution.py:486
  21.1 23.7 %all-to-all-start.1 = ((bf16[8,4,64,384]{3,2,1,0:T(8,128)(2,1)}), bf16[8,4,64,384]{3,2,1,0:T(8,128)(2,1)S(1)}, u32[]{:S(2)}, u32[]{:S(2)}) async-start(bf16[8,4,64,384]{3,2,1,0:T(8,128)(2,1)} %shard_map.85), calls=%async_computation.1 | async-start | bytes 3145728 | tf_op jit(solution)/shard_map/all_to_all | solution.py:486
  25.4 19.6 %copy-start.6 = (bf16[8,64,384]{2,1,0:T(8,128)(2,1)}, bf16[8,64,384]{2,1,0:T(8,128)(2,1)S(1)}, u32[]{:S(2)}) copy-start(bf16[8,64,384]{2,1,0:T(8,128)(2,1)S(1)} %shard_map.86.refs_1_.refs_2_) | copy-start | bytes 1179652
  25.4 11.2 %collective-permute-start.2 = (bf16[8,64,384]{2,1,0:T(8,128)(2,1)S(1)}, bf16[8,64,384]{2,1,0:T(8,128)(2,1)S(1)}, u32[]{:S(2)}, u32[]{:S(2)}) collective-permute-start(bf16[8,64,384]{2,1,0:T(8,128)(2,1)S(1)} %shard_map.86.refs_1_.refs_2_), channel_id=1, source_target_pairs={{0,2},{1,3},{2,0},{3,1},{4,6},{5,7},{6,4},{7,5},{8,16},{9,17},{10,... | collective-permute-start | bytes 1179656 | tf_op jit(solution)/shard_map/ppermute | solution.py:513
  25.5 11.2 %collective-permute-start.4 = (bf16[8,64,384]{2,1,0:T(8,128)(2,1)S(1)}, bf16[8,64,384]{2,1,0:T(8,128)(2,1)S(1)}, u32[]{:S(2)}, u32[]{:S(2)}) collective-permute-start(bf16[8,64,384]{2,1,0:T(8,128)(2,1)S(1)} %shard_map.86.refs_1_.refs_2_), channel_id=1, source_target_pairs={{0,8},{1,9},{2,10},{3,11},{4,12},{5,13},{6,14},{7,15},{8,0},{9,1},... | collective-permute-start | bytes 1179656 | tf_op jit(solution)/shard_map/ppermute | solution.py:513
  25.6 19.5 %copy-start.12 = (s32[2,4,4]{2,1,0:T(4,128)S(1)}, s32[2,4,4]{2,1,0:T(4,128)}, u32[]{:S(2)}) copy-start(s32[2,4,4]{2,1,0:T(4,128)} %refs_5_.3) | copy-start | bytes 388
  36.6 8.4 %copy-start.8 = (bf16[8,64,384]{2,1,0:T(8,128)(2,1)}, bf16[8,64,384]{2,1,0:T(8,128)(2,1)S(1)}, u32[]{:S(2)}) copy-start(bf16[8,64,384]{2,1,0:T(8,128)(2,1)S(1)} %collective-permute-done.2.refs_3_.refs_4_) | copy-start | bytes 1179652
  36.6 12.0 %collective-permute-start.3 = (bf16[8,64,384]{2,1,0:T(8,128)(2,1)S(1)}, bf16[8,64,384]{2,1,0:T(8,128)(2,1)}, u32[]{:S(2)}, u32[]{:S(2)}) collective-permute-start(bf16[8,64,384]{2,1,0:T(8,128)(2,1)S(1)} %collective-permute-done.2.refs_3_.refs_4_), channel_id=1, source_target_pairs={{0,8},{1,9},{2,10},{3,11},{4,12},{5,13},{6,14},{7,15},{8,0},{9,1},... | collective-permute-start | bytes 1179656 | tf_op jit(solution)/shard_map/ppermute | solution.py:513
  36.7 8.3 %copy-start.10 = (bf16[8,64,384]{2,1,0:T(8,128)(2,1)}, bf16[8,64,384]{2,1,0:T(8,128)(2,1)S(1)}, u32[]{:S(2)}) copy-start(bf16[8,64,384]{2,1,0:T(8,128)(2,1)S(1)} %collective-permute-done.4.refs_2_.refs_3_) | copy-start | bytes 1179652
  36.7 11.9 %collective-permute-start.5 = (bf16[8,64,384]{2,1,0:T(8,128)(2,1)S(1)}, bf16[8,64,384]{2,1,0:T(8,128)(2,1)}, u32[]{:S(2)}, u32[]{:S(2)}) collective-permute-start(bf16[8,64,384]{2,1,0:T(8,128)(2,1)S(1)} %collective-permute-done.4.refs_2_.refs_3_), channel_id=1, source_target_pairs={{0,2},{1,3},{2,0},{3,1},{4,6},{5,7},{6,4},{7,5},{8,16},{9,17},{10,... | collective-permute-start | bytes 1179656 | tf_op jit(solution)/shard_map/ppermute | solution.py:513
  44.9 12.0 %collective-permute-start.7 = (bf16[8,64,384]{2,1,0:T(8,128)(2,1)S(1)}, bf16[8,64,384]{2,1,0:T(8,128)(2,1)S(1)}, u32[]{:S(2)}, u32[]{:S(2)}) collective-permute-start(bf16[8,64,384]{2,1,0:T(8,128)(2,1)S(1)} %get-tuple-element.40), channel_id=1, source_target_pairs={{0,2},{1,3},{2,0},{3,1},{4,6},{5,7},{6,4},{7,5},{8,16},{9,17},{10,... | collective-permute-start | bytes 1179656 | tf_op jit(solution)/shard_map/ppermute | solution.py:513
  45.0 11.9 %collective-permute-start.6 = (bf16[8,64,384]{2,1,0:T(8,128)(2,1)S(1)}, bf16[8,64,384]{2,1,0:T(8,128)(2,1)S(1)}, u32[]{:S(2)}, u32[]{:S(2)}) collective-permute-start(bf16[8,64,384]{2,1,0:T(8,128)(2,1)S(1)} %get-tuple-element.44), channel_id=1, source_target_pairs={{0,8},{1,9},{2,10},{3,11},{4,12},{5,13},{6,14},{7,15},{8,0},{9,1},... | collective-permute-start | bytes 1179656 | tf_op jit(solution)/shard_map/ppermute | solution.py:513
  51.5 13.8 %collective-permute-start.12 = (bf16[8,64,384]{2,1,0:T(8,128)(2,1)S(1)}, bf16[8,64,384]{2,1,0:T(8,128)(2,1)S(1)}, u32[]{:S(2)}, u32[]{:S(2)}) collective-permute-start(bf16[8,64,384]{2,1,0:T(8,128)(2,1)S(1)} %get-tuple-element.66), channel_id=1, source_target_pairs={{0,2},{1,3},{2,0},{3,1},{4,6},{5,7},{6,4},{7,5},{8,16},{9,17},{10,... | collective-permute-start | bytes 1179656 | tf_op jit(solution)/shard_map/ppermute | solution.py:513
  53.5 12.0 %collective-permute-start.13 = (bf16[8,64,384]{2,1,0:T(8,128)(2,1)S(1)}, bf16[8,64,384]{2,1,0:T(8,128)(2,1)S(1)}, u32[]{:S(2)}, u32[]{:S(2)}) collective-permute-start(bf16[8,64,384]{2,1,0:T(8,128)(2,1)S(1)} %get-tuple-element.66), channel_id=1, source_target_pairs={{0,8},{1,9},{2,10},{3,11},{4,12},{5,13},{6,14},{7,15},{8,0},{9,1},... | collective-permute-start | bytes 1179656 | tf_op jit(solution)/shard_map/ppermute | solution.py:513
  55.6 0.7 copy-start.13
  56.9 4.4 %copy-start.7 = (bf16[8,64,384]{2,1,0:T(8,128)(2,1)S(1)}, bf16[8,64,384]{2,1,0:T(8,128)(2,1)}, u32[]{:S(2)}) copy-start(bf16[8,64,384]{2,1,0:T(8,128)(2,1)} %copy-done.6) | copy-start | bytes 1179652
  56.9 4.4 %copy-start.9 = (bf16[8,64,384]{2,1,0:T(8,128)(2,1)S(1)}, bf16[8,64,384]{2,1,0:T(8,128)(2,1)}, u32[]{:S(2)}) copy-start(bf16[8,64,384]{2,1,0:T(8,128)(2,1)} %copy-done.8) | copy-start | bytes 1179652
  56.9 4.4 %copy-start.11 = (bf16[8,64,384]{2,1,0:T(8,128)(2,1)S(1)}, bf16[8,64,384]{2,1,0:T(8,128)(2,1)}, u32[]{:S(2)}) copy-start(bf16[8,64,384]{2,1,0:T(8,128)(2,1)} %copy-done.10) | copy-start | bytes 1179652
  59.2 14.5 %collective-permute-start.8 = (bf16[8,64,384]{2,1,0:T(8,128)(2,1)}, bf16[8,64,384]{2,1,0:T(8,128)(2,1)S(1)}, u32[]{:S(2)}, u32[]{:S(2)}) collective-permute-start(bf16[8,64,384]{2,1,0:T(8,128)(2,1)} %get-tuple-element.60), channel_id=1, source_target_pairs={{0,2},{1,3},{2,0},{3,1},{4,6},{5,7},{6,4},{7,5},{8,16},{9,17},{10,... | collective-permute-start | bytes 1179656 | tf_op jit(solution)/shard_map/ppermute | solution.py:513
  61.3 12.6 %collective-permute-start.9 = (bf16[8,64,384]{2,1,0:T(8,128)(2,1)}, bf16[8,64,384]{2,1,0:T(8,128)(2,1)S(1)}, u32[]{:S(2)}, u32[]{:S(2)}) collective-permute-start(bf16[8,64,384]{2,1,0:T(8,128)(2,1)} %get-tuple-element.60), channel_id=1, source_target_pairs={{0,8},{1,9},{2,10},{3,11},{4,12},{5,13},{6,14},{7,15},{8,0},{9,1},... | collective-permute-start | bytes 1179656 | tf_op jit(solution)/shard_map/ppermute | solution.py:513
  64.7 1.7 %copy-start = (bf16[8,64,384]{2,1,0:T(8,128)(2,1)}, bf16[8,64,384]{2,1,0:T(8,128)(2,1)S(1)}, u32[]{:S(2)}) copy-start(bf16[8,64,384]{2,1,0:T(8,128)(2,1)S(1)} %get-tuple-element.59.refs_1_) | copy-start | bytes 1179652
  64.7 3.6 %copy-start.2 = (bf16[8,64,384]{2,1,0:T(8,128)(2,1)}, bf16[8,64,384]{2,1,0:T(8,128)(2,1)S(1)}, u32[]{:S(2)}) copy-start(bf16[8,64,384]{2,1,0:T(8,128)(2,1)S(1)} %get-tuple-element.61.refs_3_) | copy-start | bytes 1179652
  66.4 15.9 %collective-permute-start.14 = (bf16[8,64,384]{2,1,0:T(8,128)(2,1)}, bf16[8,64,384]{2,1,0:T(8,128)(2,1)S(1)}, u32[]{:S(2)}, u32[]{:S(2)}) collective-permute-start(bf16[8,64,384]{2,1,0:T(8,128)(2,1)} %get-tuple-element.68), channel_id=1, source_target_pairs={{0,8},{1,9},{2,10},{3,11},{4,12},{5,13},{6,14},{7,15},{8,0},{9,1},... | collective-permute-start | bytes 1179656 | tf_op jit(solution)/shard_map/ppermute | solution.py:513
  67.7 14.6 %collective-permute-start.15 = (bf16[8,64,384]{2,1,0:T(8,128)(2,1)S(1)}, bf16[8,64,384]{2,1,0:T(8,128)(2,1)}, u32[]{:S(2)}, u32[]{:S(2)}) collective-permute-start(bf16[8,64,384]{2,1,0:T(8,128)(2,1)S(1)} %get-tuple-element.69), channel_id=1, source_target_pairs={{0,2},{1,3},{2,0},{3,1},{4,6},{5,7},{6,4},{7,5},{8,16},{9,17},{10,... | collective-permute-start | bytes 1179656 | tf_op jit(solution)/shard_map/ppermute | solution.py:513
  68.3 5.6 %copy-start.1 = (bf16[8,64,384]{2,1,0:T(8,128)(2,1)S(1)}, bf16[8,64,384]{2,1,0:T(8,128)(2,1)}, u32[]{:S(2)}) copy-start(bf16[8,64,384]{2,1,0:T(8,128)(2,1)} %copy-done) | copy-start | bytes 1179652
  68.3 5.6 %copy-start.3 = (bf16[8,64,384]{2,1,0:T(8,128)(2,1)S(1)}, bf16[8,64,384]{2,1,0:T(8,128)(2,1)}, u32[]{:S(2)}) copy-start(bf16[8,64,384]{2,1,0:T(8,128)(2,1)} %copy-done.2) | copy-start | bytes 1179652
  69.3 21.8 %all-to-all-start.2 = ((bf16[8,2,64,384]{3,2,1,0:T(8,128)(2,1)}), bf16[8,2,64,384]{3,2,1,0:T(8,128)(2,1)S(1)}, u32[]{:S(2)}, u32[]{:S(2)}) async-start(bf16[8,2,64,384]{3,2,1,0:T(8,128)(2,1)} %shard_map.93), calls=%async_computation.2 | async-start | bytes 1572864 | tf_op jit(solution)/shard_map/all_to_all | solution.py:486
  73.5 8.8 %copy-start.14 = (bf16[8,64,384]{2,1,0:T(8,128)(2,1)S(1)}, bf16[8,64,384]{2,1,0:T(8,128)(2,1)}, u32[]{:S(2)}) copy-start(bf16[8,64,384]{2,1,0:T(8,128)(2,1)} %copy-done.13) | copy-start | bytes 1179652
  74.1 15.9 %collective-permute-start.10 = (bf16[8,64,384]{2,1,0:T(8,128)(2,1)S(1)}, bf16[8,64,384]{2,1,0:T(8,128)(2,1)S(1)}, u32[]{:S(2)}, u32[]{:S(2)}) collective-permute-start(bf16[8,64,384]{2,1,0:T(8,128)(2,1)S(1)} %get-tuple-element.62), channel_id=1, source_target_pairs={{0,8},{1,9},{2,10},{3,11},{4,12},{5,13},{6,14},{7,15},{8,0},{9,1},... | collective-permute-start | bytes 1179656 | tf_op jit(solution)/shard_map/ppermute | solution.py:513
  74.2 15.8 %collective-permute-start.11 = (bf16[8,64,384]{2,1,0:T(8,128)(2,1)S(1)}, bf16[8,64,384]{2,1,0:T(8,128)(2,1)S(1)}, u32[]{:S(2)}, u32[]{:S(2)}) collective-permute-start(bf16[8,64,384]{2,1,0:T(8,128)(2,1)S(1)} %get-tuple-element.63), channel_id=1, source_target_pairs={{0,2},{1,3},{2,0},{3,1},{4,6},{5,7},{6,4},{7,5},{8,16},{9,17},{10,... | collective-permute-start | bytes 1179656 | tf_op jit(solution)/shard_map/ppermute | solution.py:513
  91.1 15.1 %all-to-all-start.3 = ((bf16[8,2,64,384]{3,2,1,0:T(8,128)(2,1)}), bf16[8,2,64,384]{3,2,1,0:T(8,128)(2,1)S(1)}, u32[]{:S(2)}, u32[]{:S(2)}) async-start(bf16[8,2,64,384]{3,2,1,0:T(8,128)(2,1)} %shard_map.98), calls=%async_computation.3 | async-start | bytes 1572864 | tf_op jit(solution)/shard_map/all_to_all | solution.py:486

commit v8 on v6

--- a/solution.py
+++ b/solution.py
@@ -319,7 +319,10 @@
         dq_ref[head] = dot(keys.T, ds)
 
 
-def near_keys_kernel(rows, e_ref, w_ref, delta_ref, dq2_ref, dk0_ref, dk1_ref, dk3_ref, dq_ref):
+def near_keys_kernel(
+    rows, e_ref, w_ref, delta_ref, dq2_ref, att_ref, dk0_ref, dk1_ref, dk3_ref, pair_ref
+):
+    pair_ref[:, 0] = att_ref[...]
     for head in range(e_ref.shape[0]):
         queries = rows("q", head)
         grads = rows("g", head).T
@@ -331,7 +334,7 @@
             ds = (weights * (dot(rows(v_name, head), grads) - delta)).astype(BF16)
             put(dk_ref, head, (dot(ds, queries) * SCALE).astype(BF16))
             dq = dq + dot(rows(k_name, head).T, ds)
-        put(dq_ref, head, (dq * SCALE).astype(BF16).T)
+        put(pair_ref, head, (dq * SCALE).astype(BF16).T, 1)
 
 
 def add_both_kernel(frame_ref, first_ref, middle_ref, third_ref, edge_ref, first_out, third_out):
@@ -351,11 +354,6 @@
     inner = (frame_ref[0] == 1) | (frame_ref[0] == 2)
     total = own_ref[...].astype(F32) + edge_ref[...].astype(F32)
     out_ref[...] = (total + jnp.where(inner, middle_ref[...].astype(F32), 0.0)).astype(BF16)
-
-
-def pair_kernel(first_ref, second_ref, out_ref):
-    out_ref[:, 0] = first_ref[...]
-    out_ref[:, 1] = second_ref[...]
 
 
 def last_kernel(frame_ref, own_ref, edge_ref, middle_ref, second_ref, out_ref):
@@ -566,16 +564,16 @@
         names=("q", "g", "k2", "va", "vb"),
     )
     dk_edge, dk_middle = send(dk2, edge), send(dk2, middle)
-    dk0, dk1, dk3, dq = call(
-        near_keys_kernel, (one, one, one, one), 4, e_near, w, delta, dq2,
+    dk0, dk1, dk3, att_dq = call(
+        near_keys_kernel, (one, one, one, packed(2)), 4, e_near, w, delta, dq2, att,
         names=("q", "g", "k0", "k1", "k3", "v0", "v1", "v3"),
     )
-    dq, dv1, dv3 = barrier(dq, dv1, dv3)
+    att_dq, dv1, dv3 = barrier(att_dq, dv1, dv3)
     dv_first, dv_third = sums(dv1, dv3, dv_edge, dv_middle)
     dv_over = send(dv_first, edge), send(dv_third, middle)
     dk_first, dk_third = sums(dk1, dk3, dk_edge, dk_middle)
     dk_over = send(dk_first, edge), send(dk_third, middle)
-    attended, grad_query = leave(call(pair_kernel, packed(2), 0.5, att, dq))
+    attended, grad_query = leave(att_dq)
     dv = call(sum_kernel, one, SUM_WORK, frame, dv0, *dv_over)
     grad_keys, grad_values = leave(
         call(last_kernel, packed(2), 0.5, frame, dk0, *dk_over, dv)

time: 109 us -> 109 us (level)
  waiting for transfers between devices: 47.3 us -> 45.8 us
    ppermute x16, waiting for transfers between devices: 35.5 us -> 34 us  [send(): return lax.ppermute(array, devices, pairs)]
    pallas_call x14 -> x13, Pallas kernels: 19.8 us -> 19.8 us  [call(): pl.pallas_call(body, in_specs=[smem if x.dtype == jnp.int32 else vmem for...]
where the time goes in v8:
time: 109 us; the launch traced here: 107 us
  waiting for transfers between devices  45.8 us (42%)
  starting transfers between devices  32.2 us (30%)
  Pallas kernels  23.6 us (22%)
  local copies, waits for them, and re-layouts  5.05 us (5%)
    ppermute x16, waiting for transfers between devices, send(): return lax.ppermute(array, devices, pairs)  34 us
    pallas_call x13, Pallas kernels, call(): pl.pallas_call(body, in_specs=[smem if x.dtype == jnp.int32 else vmem for...  19.8 us
    all_to_all x4, starting transfers between devices, swap(): return lax.all_to_all(array, plane, 0, 0, tiled=True)  16.8 us
    ppermute x16, starting transfers between devices, send(): return lax.ppermute(array, devices, pairs)  15.4 us
    all_to_all x4, waiting for transfers between devices, swap(): return lax.all_to_all(array, plane, 0, 0, tiled=True)  11.8 us
    unnamed x32, local copies, waits for them, and re-layouts  5.05 us
    pallas_call x2, Pallas kernels, pack(): pl.pallas_call(pack_kernel, in_specs=[anywhere] * count, out_specs=anywhe...  3.85 us
  transfers between devices with their start and end apart: 20, of which 17 were waited for; matrix products, arithmetic and copies ran while one was open for 1% of the time, Pallas kernels for 19%

profile of v8, /device:TPU:10, one launch (start us, length us, event | category | flops | bytes accessed | tf_op | source)
XLA Modules:
  0.0 107.5 jit_solution(10691227469369531689)
XLA Ops:
  0.6 2.2 %shard_map.84 = bf16[8,3,64,384]{3,2,1,0:T(8,128)(2,1)} custom-call(bf16[64,3072]{1,0:T(8,128)(2,1)} %refs_0_.2, bf16[64,3072]{1,0:T(8,128)(2,1)} %refs_1_.1, bf16[64,3072]{1,0:T(8,128)(2,1)} %refs_2_.1), custom_call_target="tpu_custom_call" | custom-call | flops 575000000 | bytes 65536 | tf_op jit(solution)/shard_map/pallas_call | solution.py:468
  2.8 0.0 copy-start
  2.8 4.4 %all-to-all-start = ((bf16[8,3,64,384]{3,2,1,0:T(8,128)(2,1)}), bf16[8,3,64,384]{3,2,1,0:T(8,128)(2,1)S(1)}, u32[]{:S(2)}, u32[]{:S(2)}) async-start(bf16[8,3,64,384]{3,2,1,0:T(8,128)(2,1)} %shard_map.84), calls=%async_computation | async-start | bytes 2359296 | tf_op jit(solution)/shard_map/all_to_all | solution.py:498
  7.2 0.4 collective-permute-start
  7.7 2.7 %collective-permute-start.1 = (bf16[64,3072]{1,0:T(8,128)(2,1)S(1)}, bf16[64,3072]{1,0:T(8,128)(2,1)S(1)}, u32[]{:S(2)}, u32[]{:S(2)}) collective-permute-start(bf16[64,3072]{1,0:T(8,128)(2,1)S(1)} %copy-done), channel_id=1, source_target_pairs={{0,2},{1,3},{2,0},{3,1},{4,6},{5,7},{6,4},{7,5},{8,16},{9,17},{10,... | collective-permute-start | bytes 1179656 | tf_op jit(solution)/shard_map/ppermute | solution.py:525
  10.4 8.0 %collective-permute-done.refs_1_ = bf16[64,3072]{1,0:T(8,128)(2,1)S(1)} collective-permute-done((bf16[64,3072]{1,0:T(8,128)(2,1)S(1)}, bf16[64,3072]{1,0:T(8,128)(2,1)S(1)}, u32[]{:S(2)}, u32[]{:S(2)}) %collective-permute-start) | collective-permute-done | bytes 393248 | tf_op jit(solution)/shard_map/ppermute | solution.py:525
  18.4 1.1 %collective-permute-done.1.refs_2_ = bf16[64,3072]{1,0:T(8,128)(2,1)S(1)} collective-permute-done((bf16[64,3072]{1,0:T(8,128)(2,1)S(1)}, bf16[64,3072]{1,0:T(8,128)(2,1)S(1)}, u32[]{:S(2)}, u32[]{:S(2)}) %collective-permute-start.1) | collective-permute-done | bytes 393248 | tf_op jit(solution)/shard_map/ppermute | solution.py:525
  19.5 1.7 %shard_map.85 = bf16[8,3,64,384]{3,2,1,0:T(8,128)(2,1)} custom-call(bf16[64,3072]{1,0:T(8,128)(2,1)S(1)} %copy-done, bf16[64,3072]{1,0:T(8,128)(2,1)S(1)} %collective-permute-done.refs_1_, bf16[64,3072]{1,0:T(8,128)(2,1)S(1)} %collective-permute-done.1.refs_2_), custom_call_target="tpu_custom_call" | custom-call | flops 575000000 | bytes 65536 | tf_op jit(solution)/shard_map/pallas_call | solution.py:468
  21.2 1.3 %all-to-all-done.refs_0_ = bf16[8,3,64,384]{3,2,1,0:T(8,128)(2,1)S(1)} async-done(((bf16[8,3,64,384]{3,2,1,0:T(8,128)(2,1)}), bf16[8,3,64,384]{3,2,1,0:T(8,128)(2,1)S(1)}, u32[]{:S(2)}, u32[]{:S(2)}) %all-to-all-start) | async-done | bytes 1179680 | tf_op jit(solution)/shard_map/all_to_all | solution.py:498
  22.5 0.0 copy-start.5
  22.5 0.5 collective-permute-start.2
  23.0 2.7 %collective-permute-start.3 = (bf16[8,64,384]{2,1,0:T(8,128)(2,1)S(1)}, bf16[8,64,384]{2,1,0:T(8,128)(2,1)S(1)}, u32[]{:S(2)}, u32[]{:S(2)}) collective-permute-start(bf16[8,64,384]{2,1,0:T(8,128)(2,1)S(1)} %shard_map.86.refs_1_), channel_id=1, source_target_pairs={{0,2},{1,3},{2,0},{3,1},{4,6},{5,7},{6,4},{7,5},{8,16},{9,17},{10,... | collective-permute-start | bytes 1179656 | tf_op jit(solution)/shard_map/ppermute | solution.py:525
  25.7 4.2 %all-to-all-start.1 = ((bf16[8,3,64,384]{3,2,1,0:T(8,128)(2,1)}), bf16[8,3,64,384]{3,2,1,0:T(8,128)(2,1)S(1)}, u32[]{:S(2)}, u32[]{:S(2)}) async-start(bf16[8,3,64,384]{3,2,1,0:T(8,128)(2,1)} %shard_map.85), calls=%async_computation.1 | async-start | bytes 2359296 | tf_op jit(solution)/shard_map/all_to_all | solution.py:498
  29.9 3.8 %collective-permute-done.2.refs_2_ = bf16[8,64,384]{2,1,0:T(8,128)(2,1)S(1)} collective-permute-done((bf16[8,64,384]{2,1,0:T(8,128)(2,1)S(1)}, bf16[8,64,384]{2,1,0:T(8,128)(2,1)S(1)}, u32[]{:S(2)}, u32[]{:S(2)}) %collective-permute-start.2) | collective-permute-done | bytes 393248 | tf_op jit(solution)/shard_map/ppermute | solution.py:525
  33.7 0.7 copy.11.refs_0_
  34.5 0.4 collective-permute-done.3.refs_3_
  34.8 0.7 copy.12.refs_1_
  35.6 0.1 collective-permute-start.4
  35.7 2.7 %collective-permute-start.5 = (bf16[8,64,384]{2,1,0:T(8,128)(2,1)}, bf16[8,64,384]{2,1,0:T(8,128)(2,1)}, u32[]{:S(2)}, u32[]{:S(2)}) collective-permute-start(bf16[8,64,384]{2,1,0:T(8,128)(2,1)} %get-tuple-element.47), channel_id=1, source_target_pairs={{0,2},{1,3},{2,0},{3,1},{4,6},{5,7},{6,4},{7,5},{8,16},{9,17},{10,... | collective-permute-start | bytes 1179656 | tf_op jit(solution)/shard_map/ppermute | solution.py:525
  38.4 3.5 %shard_map.87 = (bf16[3,1536,512]{2,1,0:T(8,128)(2,1)S(1)}, f32[3,8,512]{2,1,0:T(8,128)S(1)}) custom-call(bf16[8,3,64,384]{3,2,1,0:T(8,128)(2,1)S(1)} %all-to-all-done.refs_0_, bf16[8,64,384]{2,1,0:T(8,128)(2,1)S(1)} %shard_map.86.refs_1_, bf16[8,64,384]{2,1,0:T(8,128)(2,1)S(1)} %collective-permute-done.2.refs_2_, ...), custom_call_target="tpu_custom_call" | custom-call | flops 4024999936 | bytes 65536 | tf_op jit(solution)/shard_map/pallas_call | solution.py:454
  41.9 2.1 %copy-done.8 = bf16[3,1536,512]{2,1,0:T(8,128)(2,1)} copy-done((bf16[3,1536,512]{2,1,0:T(8,128)(2,1)}, bf16[3,1536,512]{2,1,0:T(8,128)(2,1)S(1)}, u32[]{:S(2)}) %copy-start.8) | copy-done | bytes 4718616
  44.1 0.6 copy-done.11
  44.7 0.5 all-to-all-done.1.refs_0_.refs_1_.refs_4_
  45.2 0.1 shard_map.90
  45.2 0.1 collective-permute-start.6
  45.3 0.0 slice-start
  45.3 0.0 slice-start.1
  45.3 0.5 collective-permute-start.7
  45.8 0.4 collective-permute-done.4.refs_1_
  46.2 0.7 collective-permute-done.5.refs_2_
  47.0 2.8 %shard_map.89 = (bf16[3,512,512]{2,1,0:T(8,128)(2,1)S(1)}, f32[3,8,512]{2,1,0:T(8,128)S(1)}, bf16[8,64,384]{2,1,0:T(8,128)(2,1)S(1)}, bf16[8,64,384]{2,1,0:T(8,128)(2,1)S(1)}) custom-call(bf16[8,3,64,384]{3,2,1,0:T(8,128)(2,1)S(1)} %all-to-all-done.refs_0_, bf16[8,64,384]{2,1,0:T(8,128)(2,1)} %collective-permute-done.4.refs_1_, ...), custom_call_target="tpu_custom_call" | custom-call | flops 2300000000 | bytes 65536 | tf_op jit(solution)/shard_map/pallas_call | solution.py:454
  49.8 1.8 %collective-permute-start.12 = (bf16[8,64,384]{2,1,0:T(8,128)(2,1)S(1)}, bf16[8,64,384]{2,1,0:T(8,128)(2,1)S(1)}, u32[]{:S(2)}, u32[]{:S(2)}) collective-permute-start(bf16[8,64,384]{2,1,0:T(8,128)(2,1)S(1)} %get-tuple-element.72), channel_id=1, source_target_pairs={{0,2},{1,3},{2,0},{3,1},{4,6},{5,7},{6,4},{7,5},{8,16},{9,17},{10,... | collective-permute-start | bytes 1179656 | tf_op jit(solution)/shard_map/ppermute | solution.py:525
  51.6 0.0 collective-permute-start.13
  51.6 2.0 %shard_map.91 = (bf16[8,64,384]{2,1,0:T(8,128)(2,1)S(1)}, bf16[8,64,384]{2,1,0:T(8,128)(2,1)S(1)}, bf16[8,64,384]{2,1,0:T(8,128)(2,1)S(1)}, f32[3,128,512]{2,1,0:T(8,128)S(1)}) custom-call(bf16[8,3,64,384]{3,2,1,0:T(8,128)(2,1)S(1)} %all-to-all-done.refs_0_, bf16[8,3,64,384]{3,2,1,0:T(8,128)(2,1)S(1)} %all-to-all-done.1.refs_0_.refs_1_.refs_4_, ...), custom_call_target="tpu_custom_call" | custom-call | flops 2300000000 | bytes 65536 | tf_op jit(solution)/shard_map/pallas_call | solution.py:454
  53.6 0.0 copy-start.9
  53.6 0.7 copy-done.9
  54.4 2.8 %collective-permute-done.6.refs_2_ = bf16[8,64,384]{2,1,0:T(8,128)(2,1)S(1)} collective-permute-done((bf16[8,64,384]{2,1,0:T(8,128)(2,1)S(1)}, bf16[8,64,384]{2,1,0:T(8,128)(2,1)S(1)}, u32[]{:S(2)}, u32[]{:S(2)}) %collective-permute-start.6) | collective-permute-done | bytes 393248 | tf_op jit(solution)/shard_map/ppermute | solution.py:525
  57.2 0.1 collective-permute-done.7.refs_3_
  57.3 2.3 %shard_map.92 = (bf16[8,64,384]{2,1,0:T(8,128)(2,1)}, bf16[8,64,384]{2,1,0:T(8,128)(2,1)S(1)}, f32[3,8,512]{2,1,0:T(8,128)S(1)}, f32[3,128,512]{2,1,0:T(8,128)S(1)}) custom-call(bf16[8,3,64,384]{3,2,1,0:T(8,128)(2,1)S(1)} %all-to-all-done.refs_0_, bf16[8,64,384]{2,1,0:T(8,128)(2,1)S(1)} %get-tuple-element.50.refs_1_, ...), custom_call_target="tpu_custom_call" | custom-call | flops 2300000000 | bytes 65536 | tf_op jit(solution)/shard_map/pallas_call | solution.py:454
  59.7 0.4 collective-permute-start.8
  60.1 0.0 collective-permute-start.9
  60.1 4.3 %shard_map.93 = (bf16[8,64,384]{2,1,0:T(8,128)(2,1)S(1)}, bf16[8,64,384]{2,1,0:T(8,128)(2,1)S(1)}, bf16[8,64,384]{2,1,0:T(8,128)(2,1)S(1)}, bf16[8,2,64,384]{3,2,1,0:T(8,128)(2,1)}) custom-call(bf16[8,3,64,384]{3,2,1,0:T(8,128)(2,1)S(1)} %all-to-all-done.refs_0_, bf16[8,64,384]{2,1,0:T(8,128)(2,1)S(1)} %copy-done.6, ...), custom_call_target="tpu_custom_call" | custom-call | flops 4600000000 | bytes 65536 | tf_op jit(solution)/shard_map/pallas_call | solution.py:454
  64.4 1.4 %collective-permute-done.12.refs_2_ = bf16[8,64,384]{2,1,0:T(8,128)(2,1)S(1)} collective-permute-done((bf16[8,64,384]{2,1,0:T(8,128)(2,1)S(1)}, bf16[8,64,384]{2,1,0:T(8,128)(2,1)S(1)}, u32[]{:S(2)}, u32[]{:S(2)}) %collective-permute-start.12) | collective-permute-done | bytes 393248 | tf_op jit(solution)/shard_map/ppermute | solution.py:525
  65.8 0.0 collective-permute-done.13.refs_4_
  65.8 0.2 shard_map.96
  66.0 0.0 copy-start.2
  66.0 1.3 %collective-permute-start.14 = (bf16[8,64,384]{2,1,0:T(8,128)(2,1)S(1)}, bf16[8,64,384]{2,1,0:T(8,128)(2,1)S(1)}, u32[]{:S(2)}, u32[]{:S(2)}) collective-permute-start(bf16[8,64,384]{2,1,0:T(8,128)(2,1)S(1)} %get-tuple-element.74), channel_id=1, source_target_pairs={{0,8},{1,9},{2,10},{3,11},{4,12},{5,13},{6,14},{7,15},{8,0},{9,1},... | collective-permute-start | bytes 1179656 | tf_op jit(solution)/shard_map/ppermute | solution.py:525
  67.3 1.6 %collective-permute-start.15 = (bf16[8,64,384]{2,1,0:T(8,128)(2,1)S(1)}, bf16[8,64,384]{2,1,0:T(8,128)(2,1)S(1)}, u32[]{:S(2)}, u32[]{:S(2)}) collective-permute-start(bf16[8,64,384]{2,1,0:T(8,128)(2,1)S(1)} %get-tuple-element.75), channel_id=1, source_target_pairs={{0,2},{1,3},{2,0},{3,1},{4,6},{5,7},{6,4},{7,5},{8,16},{9,17},{10,... | collective-permute-start | bytes 1179656 | tf_op jit(solution)/shard_map/ppermute | solution.py:525
  68.9 4.2 %all-to-all-start.2 = ((bf16[8,2,64,384]{3,2,1,0:T(8,128)(2,1)}), bf16[8,2,64,384]{3,2,1,0:T(8,128)(2,1)S(1)}, u32[]{:S(2)}, u32[]{:S(2)}) async-start(bf16[8,2,64,384]{3,2,1,0:T(8,128)(2,1)} %get-tuple-element.61), calls=%async_computation.2 | async-start | bytes 1572864 | tf_op jit(solution)/shard_map/all_to_all | solution.py:498
  73.1 1.2 %collective-permute-done.8.refs_2_ = bf16[8,64,384]{2,1,0:T(8,128)(2,1)} collective-permute-done((bf16[8,64,384]{2,1,0:T(8,128)(2,1)}, bf16[8,64,384]{2,1,0:T(8,128)(2,1)}, u32[]{:S(2)}, u32[]{:S(2)}) %collective-permute-start.8) | collective-permute-done | bytes 393248 | tf_op jit(solution)/shard_map/ppermute | solution.py:525
  74.3 0.0 collective-permute-done.9.refs_4_
  74.3 1.3 %shard_map.95 = (bf16[8,64,384]{2,1,0:T(8,128)(2,1)S(1)}, bf16[8,64,384]{2,1,0:T(8,128)(2,1)S(1)}) custom-call(s32[1]{0:T(128)} %bitcast.refs_4_.refs_3_.refs_0_, bf16[8,64,384]{2,1,0:T(8,128)(2,1)S(1)} %copy-done.2, bf16[8,64,384]{2,1,0:T(8,128)(2,1)} %collective-permute-done.8.refs_2_, bf16[8,64,384]{2,1,0:T(8,128)(2,1)S(1)} %copy-done.4, ...), custom_call_target="tpu_custom_call" | custom-call | flops 230000000 | bytes 65536 | tf_op jit(solution)/shard_map/pallas_call | solution.py:454
  75.6 0.1 collective-permute-start.10
  75.7 0.5 collective-permute-start.11
  76.2 6.3 %collective-permute-done.14.refs_2_ = bf16[8,64,384]{2,1,0:T(8,128)(2,1)S(1)} collective-permute-done((bf16[8,64,384]{2,1,0:T(8,128)(2,1)S(1)}, bf16[8,64,384]{2,1,0:T(8,128)(2,1)S(1)}, u32[]{:S(2)}, u32[]{:S(2)}) %collective-permute-start.14) | collective-permute-done | bytes 393248 | tf_op jit(solution)/shard_map/ppermute | solution.py:525
  82.5 0.1 collective-permute-done.15.refs_3_
  82.6 0.2 shard_map.97.refs_4_
  82.8 7.5 %collective-permute-done.10.refs_2_ = bf16[8,64,384]{2,1,0:T(8,128)(2,1)S(1)} collective-permute-done((bf16[8,64,384]{2,1,0:T(8,128)(2,1)S(1)}, bf16[8,64,384]{2,1,0:T(8,128)(2,1)S(1)}, u32[]{:S(2)}, u32[]{:S(2)}) %collective-permute-start.10) | collective-permute-done | bytes 393248 | tf_op jit(solution)/shard_map/ppermute | solution.py:525
  90.3 0.1 collective-permute-done.11.refs_3_
  90.4 1.1 %shard_map.98 = bf16[8,2,64,384]{3,2,1,0:T(8,128)(2,1)} custom-call(s32[1]{0:T(128)} %bitcast.refs_4_.refs_3_.refs_0_, bf16[8,64,384]{2,1,0:T(8,128)(2,1)S(1)} %get-tuple-element.64.refs_1_, bf16[8,64,384]{2,1,0:T(8,128)(2,1)S(1)} %collective-permute-done.10.refs_2_, bf16[8,64,384]{2,1,0:T(8,128)(2,1)S(1)} %collective-permute-done.11.refs_3_, ...), custom_call_target="tpu_custom_call" | custom-call | flops 575000000 | bytes 65536 | tf_op jit(solution)/shard_map/pallas_call | solution.py:454
  91.5 4.0 %all-to-all-start.3 = ((bf16[8,2,64,384]{3,2,1,0:T(8,128)(2,1)}), bf16[8,2,64,384]{3,2,1,0:T(8,128)(2,1)S(1)}, u32[]{:S(2)}, u32[]{:S(2)}) async-start(bf16[8,2,64,384]{3,2,1,0:T(8,128)(2,1)} %shard_map.98), calls=%async_computation.3 | async-start | bytes 1572864 | tf_op jit(solution)/shard_map/all_to_all | solution.py:498
  95.5 0.9 shard_map.94
  96.5 10.1 %all-to-all-done.3.refs_0_ = bf16[8,2,64,384]{3,2,1,0:T(8,128)(2,1)S(1)} async-done(((bf16[8,2,64,384]{3,2,1,0:T(8,128)(2,1)}), bf16[8,2,64,384]{3,2,1,0:T(8,128)(2,1)S(1)}, u32[]{:S(2)}, u32[]{:S(2)}) %all-to-all-start.3) | async-done | bytes 786464 | tf_op jit(solution)/shard_map/all_to_all | solution.py:498
  106.5 0.9 shard_map.99
  (25 shorter events, 0.1 us)
Async XLA Ops:
  2.8 4.4 %copy-start = (bf16[64,3072]{1,0:T(8,128)(2,1)S(1)}, bf16[64,3072]{1,0:T(8,128)(2,1)}, u32[]{:S(2)}) copy-start(bf16[64,3072]{1,0:T(8,128)(2,1)} %refs_0_.3) | copy-start | bytes 1179652
  2.8 19.7 %all-to-all-start = ((bf16[8,3,64,384]{3,2,1,0:T(8,128)(2,1)}), bf16[8,3,64,384]{3,2,1,0:T(8,128)(2,1)S(1)}, u32[]{:S(2)}, u32[]{:S(2)}) async-start(bf16[8,3,64,384]{3,2,1,0:T(8,128)(2,1)} %shard_map.84), calls=%async_computation | async-start | bytes 2359296 | tf_op jit(solution)/shard_map/all_to_all | solution.py:498
  7.2 11.2 %collective-permute-start = (bf16[64,3072]{1,0:T(8,128)(2,1)S(1)}, bf16[64,3072]{1,0:T(8,128)(2,1)S(1)}, u32[]{:S(2)}, u32[]{:S(2)}) collective-permute-start(bf16[64,3072]{1,0:T(8,128)(2,1)S(1)} %copy-done), channel_id=1, source_target_pairs={{0,8},{1,9},{2,10},{3,11},{4,12},{5,13},{6,14},{7,15},{8,0},{9,1},... | collective-permute-start | bytes 1179656 | tf_op jit(solution)/shard_map/ppermute | solution.py:525
  7.7 11.8 %collective-permute-start.1 = (bf16[64,3072]{1,0:T(8,128)(2,1)S(1)}, bf16[64,3072]{1,0:T(8,128)(2,1)S(1)}, u32[]{:S(2)}, u32[]{:S(2)}) collective-permute-start(bf16[64,3072]{1,0:T(8,128)(2,1)S(1)} %copy-done), channel_id=1, source_target_pairs={{0,2},{1,3},{2,0},{3,1},{4,6},{5,7},{6,4},{7,5},{8,16},{9,17},{10,... | collective-permute-start | bytes 1179656 | tf_op jit(solution)/shard_map/ppermute | solution.py:525
  22.5 15.9 %copy-start.5 = (bf16[8,64,384]{2,1,0:T(8,128)(2,1)}, bf16[8,64,384]{2,1,0:T(8,128)(2,1)S(1)}, u32[]{:S(2)}) copy-start(bf16[8,64,384]{2,1,0:T(8,128)(2,1)S(1)} %shard_map.86.refs_1_) | copy-start | bytes 1179652
  22.5 11.2 %collective-permute-start.2 = (bf16[8,64,384]{2,1,0:T(8,128)(2,1)S(1)}, bf16[8,64,384]{2,1,0:T(8,128)(2,1)S(1)}, u32[]{:S(2)}, u32[]{:S(2)}) collective-permute-start(bf16[8,64,384]{2,1,0:T(8,128)(2,1)S(1)} %shard_map.86.refs_1_), channel_id=1, source_target_pairs={{0,8},{1,9},{2,10},{3,11},{4,12},{5,13},{6,14},{7,15},{8,0},{9,1},... | collective-permute-start | bytes 1179656 | tf_op jit(solution)/shard_map/ppermute | solution.py:525
  23.0 11.8 %collective-permute-start.3 = (bf16[8,64,384]{2,1,0:T(8,128)(2,1)S(1)}, bf16[8,64,384]{2,1,0:T(8,128)(2,1)S(1)}, u32[]{:S(2)}, u32[]{:S(2)}) collective-permute-start(bf16[8,64,384]{2,1,0:T(8,128)(2,1)S(1)} %shard_map.86.refs_1_), channel_id=1, source_target_pairs={{0,2},{1,3},{2,0},{3,1},{4,6},{5,7},{6,4},{7,5},{8,16},{9,17},{10,... | collective-permute-start | bytes 1179656 | tf_op jit(solution)/shard_map/ppermute | solution.py:525
  25.7 19.4 %all-to-all-start.1 = ((bf16[8,3,64,384]{3,2,1,0:T(8,128)(2,1)}), bf16[8,3,64,384]{3,2,1,0:T(8,128)(2,1)S(1)}, u32[]{:S(2)}, u32[]{:S(2)}) async-start(bf16[8,3,64,384]{3,2,1,0:T(8,128)(2,1)} %shard_map.85), calls=%async_computation.1 | async-start | bytes 2359296 | tf_op jit(solution)/shard_map/all_to_all | solution.py:498
  35.6 2.8 %copy-start.7 = (s32[2,4,4]{2,1,0:T(4,128)S(1)}, s32[2,4,4]{2,1,0:T(4,128)}, u32[]{:S(2)}) copy-start(s32[2,4,4]{2,1,0:T(4,128)} %refs_4_.1) | copy-start | bytes 388
  35.6 10.6 %collective-permute-start.4 = (bf16[8,64,384]{2,1,0:T(8,128)(2,1)}, bf16[8,64,384]{2,1,0:T(8,128)(2,1)}, u32[]{:S(2)}, u32[]{:S(2)}) collective-permute-start(bf16[8,64,384]{2,1,0:T(8,128)(2,1)} %get-tuple-element.46), channel_id=1, source_target_pairs={{0,8},{1,9},{2,10},{3,11},{4,12},{5,13},{6,14},{7,15},{8,0},{9,1},... | collective-permute-start | bytes 1179656 | tf_op jit(solution)/shard_map/ppermute | solution.py:525
  35.7 11.3 %collective-permute-start.5 = (bf16[8,64,384]{2,1,0:T(8,128)(2,1)}, bf16[8,64,384]{2,1,0:T(8,128)(2,1)}, u32[]{:S(2)}, u32[]{:S(2)}) collective-permute-start(bf16[8,64,384]{2,1,0:T(8,128)(2,1)} %get-tuple-element.47), channel_id=1, source_target_pairs={{0,2},{1,3},{2,0},{3,1},{4,6},{5,7},{6,4},{7,5},{8,16},{9,17},{10,... | collective-permute-start | bytes 1179656 | tf_op jit(solution)/shard_map/ppermute | solution.py:525
  41.9 2.2 %copy-start.8 = (bf16[3,1536,512]{2,1,0:T(8,128)(2,1)}, bf16[3,1536,512]{2,1,0:T(8,128)(2,1)S(1)}, u32[]{:S(2)}) copy-start(bf16[3,1536,512]{2,1,0:T(8,128)(2,1)S(1)} %get-tuple-element.45.refs_2_.refs_5_) | copy-start | bytes 14155780
  44.1 0.6 copy-start.11
  45.2 1.8 %copy-start.12 = (f32[3,8,512]{2,1,0:T(8,128)S(1)}, f32[3,8,512]{2,1,0:T(8,128)}, u32[]{:S(2)}) copy-start(f32[3,8,512]{2,1,0:T(8,128)} %copy-done.11) | copy-start | bytes 147460
  45.2 12.0 %collective-permute-start.6 = (bf16[8,64,384]{2,1,0:T(8,128)(2,1)S(1)}, bf16[8,64,384]{2,1,0:T(8,128)(2,1)S(1)}, u32[]{:S(2)}, u32[]{:S(2)}) collective-permute-start(bf16[8,64,384]{2,1,0:T(8,128)(2,1)S(1)} %get-tuple-element.51), channel_id=1, source_target_pairs={{0,8},{1,9},{2,10},{3,11},{4,12},{5,13},{6,14},{7,15},{8,0},{9,1},... | collective-permute-start | bytes 1179656 | tf_op jit(solution)/shard_map/ppermute | solution.py:525
  45.3 6.3 %slice-start = ((s8[4718592]{0:T(1024)(128)(4,1)}), s8[4194304]{0:T(1024)(128)(4,1)S(1)}, s32[]{:S(2)}) async-start(s8[4718592]{0:T(1024)(128)(4,1)} %bitcast.1), calls=%async_computation.4 | async-start | bytes 8388608
  45.3 6.3 %slice-start.1 = ((s8[4718592]{0:T(1024)(128)(4,1)}), s8[524288]{0:T(1024)(128)(4,1)S(1)}, s32[]{:S(2)}) async-start(s8[4718592]{0:T(1024)(128)(4,1)} %bitcast.1), calls=%async_computation.5 | async-start | bytes 1048576
  45.3 12.0 %collective-permute-start.7 = (bf16[8,64,384]{2,1,0:T(8,128)(2,1)S(1)}, bf16[8,64,384]{2,1,0:T(8,128)(2,1)S(1)}, u32[]{:S(2)}, u32[]{:S(2)}) collective-permute-start(bf16[8,64,384]{2,1,0:T(8,128)(2,1)S(1)} %get-tuple-element.52), channel_id=1, source_target_pairs={{0,2},{1,3},{2,0},{3,1},{4,6},{5,7},{6,4},{7,5},{8,16},{9,17},{10,... | collective-permute-start | bytes 1179656 | tf_op jit(solution)/shard_map/ppermute | solution.py:525
  49.8 16.0 %collective-permute-start.12 = (bf16[8,64,384]{2,1,0:T(8,128)(2,1)S(1)}, bf16[8,64,384]{2,1,0:T(8,128)(2,1)S(1)}, u32[]{:S(2)}, u32[]{:S(2)}) collective-permute-start(bf16[8,64,384]{2,1,0:T(8,128)(2,1)S(1)} %get-tuple-element.72), channel_id=1, source_target_pairs={{0,2},{1,3},{2,0},{3,1},{4,6},{5,7},{6,4},{7,5},{8,16},{9,17},{10,... | collective-permute-start | bytes 1179656 | tf_op jit(solution)/shard_map/ppermute | solution.py:525
  51.6 14.2 %collective-permute-start.13 = (bf16[8,64,384]{2,1,0:T(8,128)(2,1)S(1)}, bf16[8,64,384]{2,1,0:T(8,128)(2,1)S(1)}, u32[]{:S(2)}, u32[]{:S(2)}) collective-permute-start(bf16[8,64,384]{2,1,0:T(8,128)(2,1)S(1)} %get-tuple-element.72), channel_id=1, source_target_pairs={{0,8},{1,9},{2,10},{3,11},{4,12},{5,13},{6,14},{7,15},{8,0},{9,1},... | collective-permute-start | bytes 1179656 | tf_op jit(solution)/shard_map/ppermute | solution.py:525
  53.6 0.7 copy-start.9
  57.3 2.8 %copy-start.6 = (bf16[8,64,384]{2,1,0:T(8,128)(2,1)S(1)}, bf16[8,64,384]{2,1,0:T(8,128)(2,1)}, u32[]{:S(2)}) copy-start(bf16[8,64,384]{2,1,0:T(8,128)(2,1)} %copy-done.5) | copy-start | bytes 1179652
  59.7 14.6 %collective-permute-start.8 = (bf16[8,64,384]{2,1,0:T(8,128)(2,1)}, bf16[8,64,384]{2,1,0:T(8,128)(2,1)}, u32[]{:S(2)}, u32[]{:S(2)}) collective-permute-start(bf16[8,64,384]{2,1,0:T(8,128)(2,1)} %get-tuple-element.66), channel_id=1, source_target_pairs={{0,2},{1,3},{2,0},{3,1},{4,6},{5,7},{6,4},{7,5},{8,16},{9,17},{10,... | collective-permute-start | bytes 1179656 | tf_op jit(solution)/shard_map/ppermute | solution.py:525
  60.1 14.2 %collective-permute-start.9 = (bf16[8,64,384]{2,1,0:T(8,128)(2,1)}, bf16[8,64,384]{2,1,0:T(8,128)(2,1)}, u32[]{:S(2)}, u32[]{:S(2)}) collective-permute-start(bf16[8,64,384]{2,1,0:T(8,128)(2,1)} %get-tuple-element.66), channel_id=1, source_target_pairs={{0,8},{1,9},{2,10},{3,11},{4,12},{5,13},{6,14},{7,15},{8,0},{9,1},... | collective-permute-start | bytes 1179656 | tf_op jit(solution)/shard_map/ppermute | solution.py:525
  64.4 1.6 %copy-start.1 = (bf16[8,64,384]{2,1,0:T(8,128)(2,1)}, bf16[8,64,384]{2,1,0:T(8,128)(2,1)S(1)}, u32[]{:S(2)}) copy-start(bf16[8,64,384]{2,1,0:T(8,128)(2,1)S(1)} %get-tuple-element.65.refs_1_) | copy-start | bytes 1179652
  64.4 1.6 %copy-start.3 = (bf16[8,64,384]{2,1,0:T(8,128)(2,1)}, bf16[8,64,384]{2,1,0:T(8,128)(2,1)S(1)}, u32[]{:S(2)}) copy-start(bf16[8,64,384]{2,1,0:T(8,128)(2,1)S(1)} %get-tuple-element.67.refs_3_) | copy-start | bytes 1179652
  66.0 8.3 %copy-start.2 = (bf16[8,64,384]{2,1,0:T(8,128)(2,1)S(1)}, bf16[8,64,384]{2,1,0:T(8,128)(2,1)}, u32[]{:S(2)}) copy-start(bf16[8,64,384]{2,1,0:T(8,128)(2,1)} %copy-done.1) | copy-start | bytes 1179652
  66.0 16.5 %collective-permute-start.14 = (bf16[8,64,384]{2,1,0:T(8,128)(2,1)S(1)}, bf16[8,64,384]{2,1,0:T(8,128)(2,1)S(1)}, u32[]{:S(2)}, u32[]{:S(2)}) collective-permute-start(bf16[8,64,384]{2,1,0:T(8,128)(2,1)S(1)} %get-tuple-element.74), channel_id=1, source_target_pairs={{0,8},{1,9},{2,10},{3,11},{4,12},{5,13},{6,14},{7,15},{8,0},{9,1},... | collective-permute-start | bytes 1179656 | tf_op jit(solution)/shard_map/ppermute | solution.py:525
  67.3 7.0 %copy-start.4 = (bf16[8,64,384]{2,1,0:T(8,128)(2,1)S(1)}, bf16[8,64,384]{2,1,0:T(8,128)(2,1)}, u32[]{:S(2)}) copy-start(bf16[8,64,384]{2,1,0:T(8,128)(2,1)} %copy-done.3) | copy-start | bytes 1179652
  67.3 15.3 %collective-permute-start.15 = (bf16[8,64,384]{2,1,0:T(8,128)(2,1)S(1)}, bf16[8,64,384]{2,1,0:T(8,128)(2,1)S(1)}, u32[]{:S(2)}, u32[]{:S(2)}) collective-permute-start(bf16[8,64,384]{2,1,0:T(8,128)(2,1)S(1)} %get-tuple-element.75), channel_id=1, source_target_pairs={{0,2},{1,3},{2,0},{3,1},{4,6},{5,7},{6,4},{7,5},{8,16},{9,17},{10,... | collective-permute-start | bytes 1179656 | tf_op jit(solution)/shard_map/ppermute | solution.py:525
  68.9 22.6 %all-to-all-start.2 = ((bf16[8,2,64,384]{3,2,1,0:T(8,128)(2,1)}), bf16[8,2,64,384]{3,2,1,0:T(8,128)(2,1)S(1)}, u32[]{:S(2)}, u32[]{:S(2)}) async-start(bf16[8,2,64,384]{3,2,1,0:T(8,128)(2,1)} %get-tuple-element.61), calls=%async_computation.2 | async-start | bytes 1572864 | tf_op jit(solution)/shard_map/all_to_all | solution.py:498
  73.1 9.5 %copy-start.10 = (bf16[8,64,384]{2,1,0:T(8,128)(2,1)S(1)}, bf16[8,64,384]{2,1,0:T(8,128)(2,1)}, u32[]{:S(2)}) copy-start(bf16[8,64,384]{2,1,0:T(8,128)(2,1)} %copy-done.9) | copy-start | bytes 1179652
  75.6 14.7 %collective-permute-start.10 = (bf16[8,64,384]{2,1,0:T(8,128)(2,1)S(1)}, bf16[8,64,384]{2,1,0:T(8,128)(2,1)S(1)}, u32[]{:S(2)}, u32[]{:S(2)}) collective-permute-start(bf16[8,64,384]{2,1,0:T(8,128)(2,1)S(1)} %get-tuple-element.68), channel_id=1, source_target_pairs={{0,8},{1,9},{2,10},{3,11},{4,12},{5,13},{6,14},{7,15},{8,0},{9,1},... | collective-permute-start | bytes 1179656 | tf_op jit(solution)/shard_map/ppermute | solution.py:525
  75.7 14.7 %collective-permute-start.11 = (bf16[8,64,384]{2,1,0:T(8,128)(2,1)S(1)}, bf16[8,64,384]{2,1,0:T(8,128)(2,1)S(1)}, u32[]{:S(2)}, u32[]{:S(2)}) collective-permute-start(bf16[8,64,384]{2,1,0:T(8,128)(2,1)S(1)} %get-tuple-element.69), channel_id=1, source_target_pairs={{0,2},{1,3},{2,0},{3,1},{4,6},{5,7},{6,4},{7,5},{8,16},{9,17},{10,... | collective-permute-start | bytes 1179656 | tf_op jit(solution)/shard_map/ppermute | solution.py:525
  91.5 15.1 %all-to-all-start.3 = ((bf16[8,2,64,384]{3,2,1,0:T(8,128)(2,1)}), bf16[8,2,64,384]{3,2,1,0:T(8,128)(2,1)S(1)}, u32[]{:S(2)}, u32[]{:S(2)}) async-start(bf16[8,2,64,384]{3,2,1,0:T(8,128)(2,1)} %shard_map.98), calls=%async_computation.3 | async-start | bytes 1572864 | tf_op jit(solution)/shard_map/all_to_all | solution.py:498

commit v9 on v8

--- a/solution.py
+++ b/solution.py
@@ -544,7 +544,7 @@
         near_scores_kernel, (near_e, stat), 3.5, frame, block_mask,
         names=("q", "k0", "k1", "k3"),
     )
-    values, ml = barrier(swap(values), ml)
+    values = swap(values)
     v1, v3 = pick(values, 1, 2)
     found.update(v0=(values, 0), v1=(values, 1), v3=(values, 2))
     found.update(va=(send(v3, edge), None), vb=(send(v1, middle), None))

time: 109 us -> 109 us (level)
    unnamed x32 -> x30, local copies, waits for them, and re-layouts: 5.05 us -> 5.04 us
where the time goes in v9:
time: 109 us; the launch traced here: 107 us
  waiting for transfers between devices  45.6 us (42%)
  starting transfers between devices  32.3 us (30%)
  Pallas kernels  23.7 us (22%)
  local copies, waits for them, and re-layouts  5.04 us (5%)
    ppermute x16, waiting for transfers between devices, send(): return lax.ppermute(array, devices, pairs)  33.8 us
    pallas_call x13, Pallas kernels, call(): pl.pallas_call(body, in_specs=[smem if x.dtype == jnp.int32 else vmem for...  19.9 us
    all_to_all x4, starting transfers between devices, swap(): return lax.all_to_all(array, plane, 0, 0, tiled=True)  16.8 us
    ppermute x16, starting transfers between devices, send(): return lax.ppermute(array, devices, pairs)  15.4 us
    all_to_all x4, waiting for transfers between devices, swap(): return lax.all_to_all(array, plane, 0, 0, tiled=True)  11.8 us
    unnamed x30, local copies, waits for them, and re-layouts  5.04 us
    pallas_call x2, Pallas kernels, pack(): pl.pallas_call(pack_kernel, in_specs=[anywhere] * count, out_specs=anywhe...  3.79 us
  transfers between devices with their start and end apart: 20, of which 17 were waited for; matrix products, arithmetic and copies ran while one was open for 1% of the time, Pallas kernels for 19%

profile of v9, /device:TPU:10, one launch (start us, length us, event | category | flops | bytes accessed | tf_op | source)
XLA Modules:
  0.0 107.4 jit_solution(5266537024287374590)
XLA Ops:
  0.6 2.1 %shard_map.84 = bf16[8,3,64,384]{3,2,1,0:T(8,128)(2,1)} custom-call(bf16[64,3072]{1,0:T(8,128)(2,1)} %refs_0_.2, bf16[64,3072]{1,0:T(8,128)(2,1)} %refs_1_.1, bf16[64,3072]{1,0:T(8,128)(2,1)} %refs_2_.1), custom_call_target="tpu_custom_call" | custom-call | flops 575000000 | bytes 65536 | tf_op jit(solution)/shard_map/pallas_call | solution.py:468
  2.7 0.0 copy-start
  2.8 4.4 %all-to-all-start = ((bf16[8,3,64,384]{3,2,1,0:T(8,128)(2,1)}), bf16[8,3,64,384]{3,2,1,0:T(8,128)(2,1)S(1)}, u32[]{:S(2)}, u32[]{:S(2)}) async-start(bf16[8,3,64,384]{3,2,1,0:T(8,128)(2,1)} %shard_map.84), calls=%async_computation | async-start | bytes 2359296 | tf_op jit(solution)/shard_map/all_to_all | solution.py:498
  7.2 0.4 collective-permute-start
  7.6 2.7 %collective-permute-start.1 = (bf16[64,3072]{1,0:T(8,128)(2,1)S(1)}, bf16[64,3072]{1,0:T(8,128)(2,1)S(1)}, u32[]{:S(2)}, u32[]{:S(2)}) collective-permute-start(bf16[64,3072]{1,0:T(8,128)(2,1)S(1)} %copy-done), channel_id=1, source_target_pairs={{0,2},{1,3},{2,0},{3,1},{4,6},{5,7},{6,4},{7,5},{8,16},{9,17},{10,... | collective-permute-start | bytes 1179656 | tf_op jit(solution)/shard_map/ppermute | solution.py:525
  10.3 8.0 %collective-permute-done.refs_1_ = bf16[64,3072]{1,0:T(8,128)(2,1)S(1)} collective-permute-done((bf16[64,3072]{1,0:T(8,128)(2,1)S(1)}, bf16[64,3072]{1,0:T(8,128)(2,1)S(1)}, u32[]{:S(2)}, u32[]{:S(2)}) %collective-permute-start) | collective-permute-done | bytes 393248 | tf_op jit(solution)/shard_map/ppermute | solution.py:525
  18.3 1.1 %collective-permute-done.1.refs_2_ = bf16[64,3072]{1,0:T(8,128)(2,1)S(1)} collective-permute-done((bf16[64,3072]{1,0:T(8,128)(2,1)S(1)}, bf16[64,3072]{1,0:T(8,128)(2,1)S(1)}, u32[]{:S(2)}, u32[]{:S(2)}) %collective-permute-start.1) | collective-permute-done | bytes 393248 | tf_op jit(solution)/shard_map/ppermute | solution.py:525
  19.5 1.7 %shard_map.85 = bf16[8,3,64,384]{3,2,1,0:T(8,128)(2,1)} custom-call(bf16[64,3072]{1,0:T(8,128)(2,1)S(1)} %copy-done, bf16[64,3072]{1,0:T(8,128)(2,1)S(1)} %collective-permute-done.refs_1_, bf16[64,3072]{1,0:T(8,128)(2,1)S(1)} %collective-permute-done.1.refs_2_), custom_call_target="tpu_custom_call" | custom-call | flops 575000000 | bytes 65536 | tf_op jit(solution)/shard_map/pallas_call | solution.py:468
  21.1 1.3 %all-to-all-done.refs_0_ = bf16[8,3,64,384]{3,2,1,0:T(8,128)(2,1)S(1)} async-done(((bf16[8,3,64,384]{3,2,1,0:T(8,128)(2,1)}), bf16[8,3,64,384]{3,2,1,0:T(8,128)(2,1)S(1)}, u32[]{:S(2)}, u32[]{:S(2)}) %all-to-all-start) | async-done | bytes 1179680 | tf_op jit(solution)/shard_map/all_to_all | solution.py:498
  22.5 0.0 copy-start.5
  22.5 0.5 collective-permute-start.2
  23.0 2.7 %collective-permute-start.3 = (bf16[8,64,384]{2,1,0:T(8,128)(2,1)S(1)}, bf16[8,64,384]{2,1,0:T(8,128)(2,1)S(1)}, u32[]{:S(2)}, u32[]{:S(2)}) collective-permute-start(bf16[8,64,384]{2,1,0:T(8,128)(2,1)S(1)} %shard_map.86.refs_1_), channel_id=1, source_target_pairs={{0,2},{1,3},{2,0},{3,1},{4,6},{5,7},{6,4},{7,5},{8,16},{9,17},{10,... | collective-permute-start | bytes 1179656 | tf_op jit(solution)/shard_map/ppermute | solution.py:525
  25.7 4.2 %all-to-all-start.1 = ((bf16[8,3,64,384]{3,2,1,0:T(8,128)(2,1)}), bf16[8,3,64,384]{3,2,1,0:T(8,128)(2,1)S(1)}, u32[]{:S(2)}, u32[]{:S(2)}) async-start(bf16[8,3,64,384]{3,2,1,0:T(8,128)(2,1)} %shard_map.85), calls=%async_computation.1 | async-start | bytes 2359296 | tf_op jit(solution)/shard_map/all_to_all | solution.py:498
  29.9 3.8 %collective-permute-done.2.refs_2_ = bf16[8,64,384]{2,1,0:T(8,128)(2,1)S(1)} collective-permute-done((bf16[8,64,384]{2,1,0:T(8,128)(2,1)S(1)}, bf16[8,64,384]{2,1,0:T(8,128)(2,1)S(1)}, u32[]{:S(2)}, u32[]{:S(2)}) %collective-permute-start.2) | collective-permute-done | bytes 393248 | tf_op jit(solution)/shard_map/ppermute | solution.py:525
  33.7 0.7 copy.11.refs_0_
  34.4 0.4 collective-permute-done.3.refs_3_
  34.8 0.7 copy.12.refs_1_
  35.5 0.1 collective-permute-start.4
  35.6 2.7 %collective-permute-start.5 = (bf16[8,64,384]{2,1,0:T(8,128)(2,1)}, bf16[8,64,384]{2,1,0:T(8,128)(2,1)}, u32[]{:S(2)}, u32[]{:S(2)}) collective-permute-start(bf16[8,64,384]{2,1,0:T(8,128)(2,1)} %get-tuple-element.43), channel_id=1, source_target_pairs={{0,2},{1,3},{2,0},{3,1},{4,6},{5,7},{6,4},{7,5},{8,16},{9,17},{10,... | collective-permute-start | bytes 1179656 | tf_op jit(solution)/shard_map/ppermute | solution.py:525
  38.3 3.5 %shard_map.87 = (bf16[3,1536,512]{2,1,0:T(8,128)(2,1)S(1)}, f32[3,8,512]{2,1,0:T(8,128)S(1)}) custom-call(bf16[8,3,64,384]{3,2,1,0:T(8,128)(2,1)S(1)} %all-to-all-done.refs_0_, bf16[8,64,384]{2,1,0:T(8,128)(2,1)S(1)} %shard_map.86.refs_1_, bf16[8,64,384]{2,1,0:T(8,128)(2,1)S(1)} %collective-permute-done.2.refs_2_, ...), custom_call_target="tpu_custom_call" | custom-call | flops 4024999936 | bytes 65536 | tf_op jit(solution)/shard_map/pallas_call | solution.py:454
  41.9 2.1 %copy-done.8 = bf16[3,1536,512]{2,1,0:T(8,128)(2,1)} copy-done((bf16[3,1536,512]{2,1,0:T(8,128)(2,1)}, bf16[3,1536,512]{2,1,0:T(8,128)(2,1)S(1)}, u32[]{:S(2)}) %copy-start.8) | copy-done | bytes 4718616
  44.0 0.6 copy-done.12
  44.6 0.5 all-to-all-done.1.refs_0_.refs_1_.refs_4_
  45.1 0.1 shard_map.90
  45.2 0.1 collective-permute-start.6
  45.3 0.5 collective-permute-start.7
  45.8 0.4 collective-permute-done.4.refs_1_
  46.2 0.7 collective-permute-done.5.refs_2_
  46.9 3.0 %shard_map.89 = (bf16[3,512,512]{2,1,0:T(8,128)(2,1)S(1)}, f32[3,8,512]{2,1,0:T(8,128)S(1)}, bf16[8,64,384]{2,1,0:T(8,128)(2,1)S(1)}, bf16[8,64,384]{2,1,0:T(8,128)(2,1)S(1)}) custom-call(bf16[8,3,64,384]{3,2,1,0:T(8,128)(2,1)S(1)} %all-to-all-done.refs_0_, bf16[8,64,384]{2,1,0:T(8,128)(2,1)} %collective-permute-done.4.refs_1_, ...), custom_call_target="tpu_custom_call" | custom-call | flops 2300000000 | bytes 65536 | tf_op jit(solution)/shard_map/pallas_call | solution.py:454
  49.9 1.8 %collective-permute-start.12 = (bf16[8,64,384]{2,1,0:T(8,128)(2,1)S(1)}, bf16[8,64,384]{2,1,0:T(8,128)(2,1)S(1)}, u32[]{:S(2)}, u32[]{:S(2)}) collective-permute-start(bf16[8,64,384]{2,1,0:T(8,128)(2,1)S(1)} %get-tuple-element.68), channel_id=1, source_target_pairs={{0,2},{1,3},{2,0},{3,1},{4,6},{5,7},{6,4},{7,5},{8,16},{9,17},{10,... | collective-permute-start | bytes 1179656 | tf_op jit(solution)/shard_map/ppermute | solution.py:525
  51.7 0.0 collective-permute-start.13
  51.7 2.0 %shard_map.91 = (bf16[8,64,384]{2,1,0:T(8,128)(2,1)S(1)}, bf16[8,64,384]{2,1,0:T(8,128)(2,1)S(1)}, bf16[8,64,384]{2,1,0:T(8,128)(2,1)S(1)}, f32[3,128,512]{2,1,0:T(8,128)S(1)}) custom-call(bf16[8,3,64,384]{3,2,1,0:T(8,128)(2,1)S(1)} %all-to-all-done.refs_0_, bf16[8,3,64,384]{3,2,1,0:T(8,128)(2,1)S(1)} %all-to-all-done.1.refs_0_.refs_1_.refs_4_, ...), custom_call_target="tpu_custom_call" | custom-call | flops 2300000000 | bytes 65536 | tf_op jit(solution)/shard_map/pallas_call | solution.py:454
  53.7 0.0 copy-start.10
  53.7 0.7 copy-done.10
  54.5 2.7 %collective-permute-done.6.refs_2_ = bf16[8,64,384]{2,1,0:T(8,128)(2,1)S(1)} collective-permute-done((bf16[8,64,384]{2,1,0:T(8,128)(2,1)S(1)}, bf16[8,64,384]{2,1,0:T(8,128)(2,1)S(1)}, u32[]{:S(2)}, u32[]{:S(2)}) %collective-permute-start.6) | collective-permute-done | bytes 393248 | tf_op jit(solution)/shard_map/ppermute | solution.py:525
  57.2 0.1 collective-permute-done.7.refs_3_
  57.3 2.3 %shard_map.92 = (bf16[8,64,384]{2,1,0:T(8,128)(2,1)}, bf16[8,64,384]{2,1,0:T(8,128)(2,1)S(1)}, f32[3,8,512]{2,1,0:T(8,128)S(1)}, f32[3,128,512]{2,1,0:T(8,128)S(1)}) custom-call(bf16[8,3,64,384]{3,2,1,0:T(8,128)(2,1)S(1)} %all-to-all-done.refs_0_, bf16[8,64,384]{2,1,0:T(8,128)(2,1)S(1)} %get-tuple-element.46.refs_1_, ...), custom_call_target="tpu_custom_call" | custom-call | flops 2300000000 | bytes 65536 | tf_op jit(solution)/shard_map/pallas_call | solution.py:454
  59.6 0.4 collective-permute-start.8
  60.1 0.0 collective-permute-start.9
  60.1 4.3 %shard_map.93 = (bf16[8,64,384]{2,1,0:T(8,128)(2,1)S(1)}, bf16[8,64,384]{2,1,0:T(8,128)(2,1)S(1)}, bf16[8,64,384]{2,1,0:T(8,128)(2,1)S(1)}, bf16[8,2,64,384]{3,2,1,0:T(8,128)(2,1)}) custom-call(bf16[8,3,64,384]{3,2,1,0:T(8,128)(2,1)S(1)} %all-to-all-done.refs_0_, bf16[8,64,384]{2,1,0:T(8,128)(2,1)S(1)} %copy-done.6, ...), custom_call_target="tpu_custom_call" | custom-call | flops 4600000000 | bytes 65536 | tf_op jit(solution)/shard_map/pallas_call | solution.py:454
  64.3 1.3 %collective-permute-done.12.refs_2_ = bf16[8,64,384]{2,1,0:T(8,128)(2,1)S(1)} collective-permute-done((bf16[8,64,384]{2,1,0:T(8,128)(2,1)S(1)}, bf16[8,64,384]{2,1,0:T(8,128)(2,1)S(1)}, u32[]{:S(2)}, u32[]{:S(2)}) %collective-permute-start.12) | collective-permute-done | bytes 393248 | tf_op jit(solution)/shard_map/ppermute | solution.py:525
  65.7 0.0 collective-permute-done.13.refs_4_
  65.7 0.2 shard_map.96
  65.9 0.0 copy-start.2
  65.9 1.3 %collective-permute-start.14 = (bf16[8,64,384]{2,1,0:T(8,128)(2,1)S(1)}, bf16[8,64,384]{2,1,0:T(8,128)(2,1)S(1)}, u32[]{:S(2)}, u32[]{:S(2)}) collective-permute-start(bf16[8,64,384]{2,1,0:T(8,128)(2,1)S(1)} %get-tuple-element.70), channel_id=1, source_target_pairs={{0,8},{1,9},{2,10},{3,11},{4,12},{5,13},{6,14},{7,15},{8,0},{9,1},... | collective-permute-start | bytes 1179656 | tf_op jit(solution)/shard_map/ppermute | solution.py:525
  67.2 1.6 %collective-permute-start.15 = (bf16[8,64,384]{2,1,0:T(8,128)(2,1)S(1)}, bf16[8,64,384]{2,1,0:T(8,128)(2,1)S(1)}, u32[]{:S(2)}, u32[]{:S(2)}) collective-permute-start(bf16[8,64,384]{2,1,0:T(8,128)(2,1)S(1)} %get-tuple-element.71), channel_id=1, source_target_pairs={{0,2},{1,3},{2,0},{3,1},{4,6},{5,7},{6,4},{7,5},{8,16},{9,17},{10,... | collective-permute-start | bytes 1179656 | tf_op jit(solution)/shard_map/ppermute | solution.py:525
  68.8 4.2 %all-to-all-start.2 = ((bf16[8,2,64,384]{3,2,1,0:T(8,128)(2,1)}), bf16[8,2,64,384]{3,2,1,0:T(8,128)(2,1)S(1)}, u32[]{:S(2)}, u32[]{:S(2)}) async-start(bf16[8,2,64,384]{3,2,1,0:T(8,128)(2,1)} %get-tuple-element.57), calls=%async_computation.2 | async-start | bytes 1572864 | tf_op jit(solution)/shard_map/all_to_all | solution.py:498
  73.0 1.2 %collective-permute-done.8.refs_2_ = bf16[8,64,384]{2,1,0:T(8,128)(2,1)} collective-permute-done((bf16[8,64,384]{2,1,0:T(8,128)(2,1)}, bf16[8,64,384]{2,1,0:T(8,128)(2,1)}, u32[]{:S(2)}, u32[]{:S(2)}) %collective-permute-start.8) | collective-permute-done | bytes 393248 | tf_op jit(solution)/shard_map/ppermute | solution.py:525
  74.2 0.0 collective-permute-done.9.refs_4_
  74.2 0.0 copy-done.4
  74.2 1.3 %shard_map.95 = (bf16[8,64,384]{2,1,0:T(8,128)(2,1)S(1)}, bf16[8,64,384]{2,1,0:T(8,128)(2,1)S(1)}) custom-call(s32[1]{0:T(128)} %bitcast.refs_4_.refs_3_.refs_0_, bf16[8,64,384]{2,1,0:T(8,128)(2,1)S(1)} %copy-done.2, bf16[8,64,384]{2,1,0:T(8,128)(2,1)} %collective-permute-done.8.refs_2_, bf16[8,64,384]{2,1,0:T(8,128)(2,1)S(1)} %copy-done.4, ...), custom_call_target="tpu_custom_call" | custom-call | flops 230000000 | bytes 65536 | tf_op jit(solution)/shard_map/pallas_call | solution.py:454
  75.6 0.1 collective-permute-start.10
  75.6 0.5 collective-permute-start.11
  76.1 6.3 %collective-permute-done.14.refs_2_ = bf16[8,64,384]{2,1,0:T(8,128)(2,1)S(1)} collective-permute-done((bf16[8,64,384]{2,1,0:T(8,128)(2,1)S(1)}, bf16[8,64,384]{2,1,0:T(8,128)(2,1)S(1)}, u32[]{:S(2)}, u32[]{:S(2)}) %collective-permute-start.14) | collective-permute-done | bytes 393248 | tf_op jit(solution)/shard_map/ppermute | solution.py:525
  82.5 0.1 collective-permute-done.15.refs_3_
  82.6 0.2 shard_map.97.refs_4_
  82.7 7.5 %collective-permute-done.10.refs_2_ = bf16[8,64,384]{2,1,0:T(8,128)(2,1)S(1)} collective-permute-done((bf16[8,64,384]{2,1,0:T(8,128)(2,1)S(1)}, bf16[8,64,384]{2,1,0:T(8,128)(2,1)S(1)}, u32[]{:S(2)}, u32[]{:S(2)}) %collective-permute-start.10) | collective-permute-done | bytes 393248 | tf_op jit(solution)/shard_map/ppermute | solution.py:525
  90.2 0.1 collective-permute-done.11.refs_3_
  90.3 1.1 %shard_map.98 = bf16[8,2,64,384]{3,2,1,0:T(8,128)(2,1)} custom-call(s32[1]{0:T(128)} %bitcast.refs_4_.refs_3_.refs_0_, bf16[8,64,384]{2,1,0:T(8,128)(2,1)S(1)} %get-tuple-element.60.refs_1_, bf16[8,64,384]{2,1,0:T(8,128)(2,1)S(1)} %collective-permute-done.10.refs_2_, bf16[8,64,384]{2,1,0:T(8,128)(2,1)S(1)} %collective-permute-done.11.refs_3_, ...), custom_call_target="tpu_custom_call" | custom-call | flops 575000000 | bytes 65536 | tf_op jit(solution)/shard_map/pallas_call | solution.py:454
  91.4 0.0 all-to-all-done.2.refs_0_
  91.4 4.0 %all-to-all-start.3 = ((bf16[8,2,64,384]{3,2,1,0:T(8,128)(2,1)}), bf16[8,2,64,384]{3,2,1,0:T(8,128)(2,1)S(1)}, u32[]{:S(2)}, u32[]{:S(2)}) async-start(bf16[8,2,64,384]{3,2,1,0:T(8,128)(2,1)} %shard_map.98), calls=%async_computation.3 | async-start | bytes 1572864 | tf_op jit(solution)/shard_map/all_to_all | solution.py:498
  95.5 0.9 shard_map.94
  96.4 10.1 %all-to-all-done.3.refs_0_ = bf16[8,2,64,384]{3,2,1,0:T(8,128)(2,1)S(1)} async-done(((bf16[8,2,64,384]{3,2,1,0:T(8,128)(2,1)}), bf16[8,2,64,384]{3,2,1,0:T(8,128)(2,1)S(1)}, u32[]{:S(2)}, u32[]{:S(2)}) %all-to-all-start.3) | async-done | bytes 786464 | tf_op jit(solution)/shard_map/all_to_all | solution.py:498
  106.5 0.9 shard_map.99
  (22 shorter events, 0.1 us)
Async XLA Ops:
  2.7 4.4 %copy-start = (bf16[64,3072]{1,0:T(8,128)(2,1)S(1)}, bf16[64,3072]{1,0:T(8,128)(2,1)}, u32[]{:S(2)}) copy-start(bf16[64,3072]{1,0:T(8,128)(2,1)} %refs_0_.3) | copy-start | bytes 1179652
  2.8 19.7 %all-to-all-start = ((bf16[8,3,64,384]{3,2,1,0:T(8,128)(2,1)}), bf16[8,3,64,384]{3,2,1,0:T(8,128)(2,1)S(1)}, u32[]{:S(2)}, u32[]{:S(2)}) async-start(bf16[8,3,64,384]{3,2,1,0:T(8,128)(2,1)} %shard_map.84), calls=%async_computation | async-start | bytes 2359296 | tf_op jit(solution)/shard_map/all_to_all | solution.py:498
  7.2 11.2 %collective-permute-start = (bf16[64,3072]{1,0:T(8,128)(2,1)S(1)}, bf16[64,3072]{1,0:T(8,128)(2,1)S(1)}, u32[]{:S(2)}, u32[]{:S(2)}) collective-permute-start(bf16[64,3072]{1,0:T(8,128)(2,1)S(1)} %copy-done), channel_id=1, source_target_pairs={{0,8},{1,9},{2,10},{3,11},{4,12},{5,13},{6,14},{7,15},{8,0},{9,1},... | collective-permute-start | bytes 1179656 | tf_op jit(solution)/shard_map/ppermute | solution.py:525
  7.6 11.8 %collective-permute-start.1 = (bf16[64,3072]{1,0:T(8,128)(2,1)S(1)}, bf16[64,3072]{1,0:T(8,128)(2,1)S(1)}, u32[]{:S(2)}, u32[]{:S(2)}) collective-permute-start(bf16[64,3072]{1,0:T(8,128)(2,1)S(1)} %copy-done), channel_id=1, source_target_pairs={{0,2},{1,3},{2,0},{3,1},{4,6},{5,7},{6,4},{7,5},{8,16},{9,17},{10,... | collective-permute-start | bytes 1179656 | tf_op jit(solution)/shard_map/ppermute | solution.py:525
  22.5 15.9 %copy-start.5 = (bf16[8,64,384]{2,1,0:T(8,128)(2,1)}, bf16[8,64,384]{2,1,0:T(8,128)(2,1)S(1)}, u32[]{:S(2)}) copy-start(bf16[8,64,384]{2,1,0:T(8,128)(2,1)S(1)} %shard_map.86.refs_1_) | copy-start | bytes 1179652
  22.5 11.2 %collective-permute-start.2 = (bf16[8,64,384]{2,1,0:T(8,128)(2,1)S(1)}, bf16[8,64,384]{2,1,0:T(8,128)(2,1)S(1)}, u32[]{:S(2)}, u32[]{:S(2)}) collective-permute-start(bf16[8,64,384]{2,1,0:T(8,128)(2,1)S(1)} %shard_map.86.refs_1_), channel_id=1, source_target_pairs={{0,8},{1,9},{2,10},{3,11},{4,12},{5,13},{6,14},{7,15},{8,0},{9,1},... | collective-permute-start | bytes 1179656 | tf_op jit(solution)/shard_map/ppermute | solution.py:525
  23.0 11.8 %collective-permute-start.3 = (bf16[8,64,384]{2,1,0:T(8,128)(2,1)S(1)}, bf16[8,64,384]{2,1,0:T(8,128)(2,1)S(1)}, u32[]{:S(2)}, u32[]{:S(2)}) collective-permute-start(bf16[8,64,384]{2,1,0:T(8,128)(2,1)S(1)} %shard_map.86.refs_1_), channel_id=1, source_target_pairs={{0,2},{1,3},{2,0},{3,1},{4,6},{5,7},{6,4},{7,5},{8,16},{9,17},{10,... | collective-permute-start | bytes 1179656 | tf_op jit(solution)/shard_map/ppermute | solution.py:525
  25.7 19.4 %all-to-all-start.1 = ((bf16[8,3,64,384]{3,2,1,0:T(8,128)(2,1)}), bf16[8,3,64,384]{3,2,1,0:T(8,128)(2,1)S(1)}, u32[]{:S(2)}, u32[]{:S(2)}) async-start(bf16[8,3,64,384]{3,2,1,0:T(8,128)(2,1)} %shard_map.85), calls=%async_computation.1 | async-start | bytes 2359296 | tf_op jit(solution)/shard_map/all_to_all | solution.py:498
  35.5 2.8 %copy-start.7 = (s32[2,4,4]{2,1,0:T(4,128)S(1)}, s32[2,4,4]{2,1,0:T(4,128)}, u32[]{:S(2)}) copy-start(s32[2,4,4]{2,1,0:T(4,128)} %refs_4_.1) | copy-start | bytes 388
  35.5 10.6 %collective-permute-start.4 = (bf16[8,64,384]{2,1,0:T(8,128)(2,1)}, bf16[8,64,384]{2,1,0:T(8,128)(2,1)}, u32[]{:S(2)}, u32[]{:S(2)}) collective-permute-start(bf16[8,64,384]{2,1,0:T(8,128)(2,1)} %get-tuple-element.42), channel_id=1, source_target_pairs={{0,8},{1,9},{2,10},{3,11},{4,12},{5,13},{6,14},{7,15},{8,0},{9,1},... | collective-permute-start | bytes 1179656 | tf_op jit(solution)/shard_map/ppermute | solution.py:525
  35.6 11.3 %collective-permute-start.5 = (bf16[8,64,384]{2,1,0:T(8,128)(2,1)}, bf16[8,64,384]{2,1,0:T(8,128)(2,1)}, u32[]{:S(2)}, u32[]{:S(2)}) collective-permute-start(bf16[8,64,384]{2,1,0:T(8,128)(2,1)} %get-tuple-element.43), channel_id=1, source_target_pairs={{0,2},{1,3},{2,0},{3,1},{4,6},{5,7},{6,4},{7,5},{8,16},{9,17},{10,... | collective-permute-start | bytes 1179656 | tf_op jit(solution)/shard_map/ppermute | solution.py:525
  41.8 2.1 %copy-start.8 = (bf16[3,1536,512]{2,1,0:T(8,128)(2,1)}, bf16[3,1536,512]{2,1,0:T(8,128)(2,1)S(1)}, u32[]{:S(2)}) copy-start(bf16[3,1536,512]{2,1,0:T(8,128)(2,1)S(1)} %get-tuple-element.41.refs_2_.refs_5_) | copy-start | bytes 14155780
  44.0 0.6 copy-start.12
  45.1 1.8 %copy-start.13 = (f32[3,8,512]{2,1,0:T(8,128)S(1)}, f32[3,8,512]{2,1,0:T(8,128)}, u32[]{:S(2)}) copy-start(f32[3,8,512]{2,1,0:T(8,128)} %copy-done.12) | copy-start | bytes 147460
  45.2 12.0 %collective-permute-start.6 = (bf16[8,64,384]{2,1,0:T(8,128)(2,1)S(1)}, bf16[8,64,384]{2,1,0:T(8,128)(2,1)S(1)}, u32[]{:S(2)}, u32[]{:S(2)}) collective-permute-start(bf16[8,64,384]{2,1,0:T(8,128)(2,1)S(1)} %get-tuple-element.47), channel_id=1, source_target_pairs={{0,8},{1,9},{2,10},{3,11},{4,12},{5,13},{6,14},{7,15},{8,0},{9,1},... | collective-permute-start | bytes 1179656 | tf_op jit(solution)/shard_map/ppermute | solution.py:525
  45.3 12.0 %collective-permute-start.7 = (bf16[8,64,384]{2,1,0:T(8,128)(2,1)S(1)}, bf16[8,64,384]{2,1,0:T(8,128)(2,1)S(1)}, u32[]{:S(2)}, u32[]{:S(2)}) collective-permute-start(bf16[8,64,384]{2,1,0:T(8,128)(2,1)S(1)} %get-tuple-element.48), channel_id=1, source_target_pairs={{0,2},{1,3},{2,0},{3,1},{4,6},{5,7},{6,4},{7,5},{8,16},{9,17},{10,... | collective-permute-start | bytes 1179656 | tf_op jit(solution)/shard_map/ppermute | solution.py:525
  46.9 4.8 %copy-start.9 = (bf16[3,1536,512]{2,1,0:T(8,128)(2,1)S(1)}, bf16[3,1536,512]{2,1,0:T(8,128)(2,1)}, u32[]{:S(2)}) copy-start(bf16[3,1536,512]{2,1,0:T(8,128)(2,1)} %copy-done.8) | copy-start | bytes 14155780
  49.9 15.8 %collective-permute-start.12 = (bf16[8,64,384]{2,1,0:T(8,128)(2,1)S(1)}, bf16[8,64,384]{2,1,0:T(8,128)(2,1)S(1)}, u32[]{:S(2)}, u32[]{:S(2)}) collective-permute-start(bf16[8,64,384]{2,1,0:T(8,128)(2,1)S(1)} %get-tuple-element.68), channel_id=1, source_target_pairs={{0,2},{1,3},{2,0},{3,1},{4,6},{5,7},{6,4},{7,5},{8,16},{9,17},{10,... | collective-permute-start | bytes 1179656 | tf_op jit(solution)/shard_map/ppermute | solution.py:525
  51.7 14.0 %collective-permute-start.13 = (bf16[8,64,384]{2,1,0:T(8,128)(2,1)S(1)}, bf16[8,64,384]{2,1,0:T(8,128)(2,1)S(1)}, u32[]{:S(2)}, u32[]{:S(2)}) collective-permute-start(bf16[8,64,384]{2,1,0:T(8,128)(2,1)S(1)} %get-tuple-element.68), channel_id=1, source_target_pairs={{0,8},{1,9},{2,10},{3,11},{4,12},{5,13},{6,14},{7,15},{8,0},{9,1},... | collective-permute-start | bytes 1179656 | tf_op jit(solution)/shard_map/ppermute | solution.py:525
  53.7 0.7 copy-start.10
  57.3 2.8 %copy-start.6 = (bf16[8,64,384]{2,1,0:T(8,128)(2,1)S(1)}, bf16[8,64,384]{2,1,0:T(8,128)(2,1)}, u32[]{:S(2)}) copy-start(bf16[8,64,384]{2,1,0:T(8,128)(2,1)} %copy-done.5) | copy-start | bytes 1179652
  59.6 14.6 %collective-permute-start.8 = (bf16[8,64,384]{2,1,0:T(8,128)(2,1)}, bf16[8,64,384]{2,1,0:T(8,128)(2,1)}, u32[]{:S(2)}, u32[]{:S(2)}) collective-permute-start(bf16[8,64,384]{2,1,0:T(8,128)(2,1)} %get-tuple-element.62), channel_id=1, source_target_pairs={{0,2},{1,3},{2,0},{3,1},{4,6},{5,7},{6,4},{7,5},{8,16},{9,17},{10,... | collective-permute-start | bytes 1179656 | tf_op jit(solution)/shard_map/ppermute | solution.py:525
  60.1 14.2 %collective-permute-start.9 = (bf16[8,64,384]{2,1,0:T(8,128)(2,1)}, bf16[8,64,384]{2,1,0:T(8,128)(2,1)}, u32[]{:S(2)}, u32[]{:S(2)}) collective-permute-start(bf16[8,64,384]{2,1,0:T(8,128)(2,1)} %get-tuple-element.62), channel_id=1, source_target_pairs={{0,8},{1,9},{2,10},{3,11},{4,12},{5,13},{6,14},{7,15},{8,0},{9,1},... | collective-permute-start | bytes 1179656 | tf_op jit(solution)/shard_map/ppermute | solution.py:525
  64.3 1.6 %copy-start.1 = (bf16[8,64,384]{2,1,0:T(8,128)(2,1)}, bf16[8,64,384]{2,1,0:T(8,128)(2,1)S(1)}, u32[]{:S(2)}) copy-start(bf16[8,64,384]{2,1,0:T(8,128)(2,1)S(1)} %get-tuple-element.61.refs_1_) | copy-start | bytes 1179652
  64.3 1.6 %copy-start.3 = (bf16[8,64,384]{2,1,0:T(8,128)(2,1)}, bf16[8,64,384]{2,1,0:T(8,128)(2,1)S(1)}, u32[]{:S(2)}) copy-start(bf16[8,64,384]{2,1,0:T(8,128)(2,1)S(1)} %get-tuple-element.63.refs_3_) | copy-start | bytes 1179652
  65.9 8.3 %copy-start.2 = (bf16[8,64,384]{2,1,0:T(8,128)(2,1)S(1)}, bf16[8,64,384]{2,1,0:T(8,128)(2,1)}, u32[]{:S(2)}) copy-start(bf16[8,64,384]{2,1,0:T(8,128)(2,1)} %copy-done.1) | copy-start | bytes 1179652
  65.9 16.5 %collective-permute-start.14 = (bf16[8,64,384]{2,1,0:T(8,128)(2,1)S(1)}, bf16[8,64,384]{2,1,0:T(8,128)(2,1)S(1)}, u32[]{:S(2)}, u32[]{:S(2)}) collective-permute-start(bf16[8,64,384]{2,1,0:T(8,128)(2,1)S(1)} %get-tuple-element.70), channel_id=1, source_target_pairs={{0,8},{1,9},{2,10},{3,11},{4,12},{5,13},{6,14},{7,15},{8,0},{9,1},... | collective-permute-start | bytes 1179656 | tf_op jit(solution)/shard_map/ppermute | solution.py:525
  67.2 7.0 %copy-start.4 = (bf16[8,64,384]{2,1,0:T(8,128)(2,1)S(1)}, bf16[8,64,384]{2,1,0:T(8,128)(2,1)}, u32[]{:S(2)}) copy-start(bf16[8,64,384]{2,1,0:T(8,128)(2,1)} %copy-done.3) | copy-start | bytes 1179652
  67.2 15.3 %collective-permute-start.15 = (bf16[8,64,384]{2,1,0:T(8,128)(2,1)S(1)}, bf16[8,64,384]{2,1,0:T(8,128)(2,1)S(1)}, u32[]{:S(2)}, u32[]{:S(2)}) collective-permute-start(bf16[8,64,384]{2,1,0:T(8,128)(2,1)S(1)} %get-tuple-element.71), channel_id=1, source_target_pairs={{0,2},{1,3},{2,0},{3,1},{4,6},{5,7},{6,4},{7,5},{8,16},{9,17},{10,... | collective-permute-start | bytes 1179656 | tf_op jit(solution)/shard_map/ppermute | solution.py:525
  68.8 22.6 %all-to-all-start.2 = ((bf16[8,2,64,384]{3,2,1,0:T(8,128)(2,1)}), bf16[8,2,64,384]{3,2,1,0:T(8,128)(2,1)S(1)}, u32[]{:S(2)}, u32[]{:S(2)}) async-start(bf16[8,2,64,384]{3,2,1,0:T(8,128)(2,1)} %get-tuple-element.57), calls=%async_computation.2 | async-start | bytes 1572864 | tf_op jit(solution)/shard_map/all_to_all | solution.py:498
  73.0 9.5 %copy-start.11 = (bf16[8,64,384]{2,1,0:T(8,128)(2,1)S(1)}, bf16[8,64,384]{2,1,0:T(8,128)(2,1)}, u32[]{:S(2)}) copy-start(bf16[8,64,384]{2,1,0:T(8,128)(2,1)} %copy-done.10) | copy-start | bytes 1179652
  75.6 14.7 %collective-permute-start.10 = (bf16[8,64,384]{2,1,0:T(8,128)(2,1)S(1)}, bf16[8,64,384]{2,1,0:T(8,128)(2,1)S(1)}, u32[]{:S(2)}, u32[]{:S(2)}) collective-permute-start(bf16[8,64,384]{2,1,0:T(8,128)(2,1)S(1)} %get-tuple-element.64), channel_id=1, source_target_pairs={{0,8},{1,9},{2,10},{3,11},{4,12},{5,13},{6,14},{7,15},{8,0},{9,1},... | collective-permute-start | bytes 1179656 | tf_op jit(solution)/shard_map/ppermute | solution.py:525
  75.6 14.7 %collective-permute-start.11 = (bf16[8,64,384]{2,1,0:T(8,128)(2,1)S(1)}, bf16[8,64,384]{2,1,0:T(8,128)(2,1)S(1)}, u32[]{:S(2)}, u32[]{:S(2)}) collective-permute-start(bf16[8,64,384]{2,1,0:T(8,128)(2,1)S(1)} %get-tuple-element.65), channel_id=1, source_target_pairs={{0,2},{1,3},{2,0},{3,1},{4,6},{5,7},{6,4},{7,5},{8,16},{9,17},{10,... | collective-permute-start | bytes 1179656 | tf_op jit(solution)/shard_map/ppermute | solution.py:525
  91.4 15.1 %all-to-all-start.3 = ((bf16[8,2,64,384]{3,2,1,0:T(8,128)(2,1)}), bf16[8,2,64,384]{3,2,1,0:T(8,128)(2,1)S(1)}, u32[]{:S(2)}, u32[]{:S(2)}) async-start(bf16[8,2,64,384]{3,2,1,0:T(8,128)(2,1)} %shard_map.98), calls=%async_computation.3 | async-start | bytes 1572864 | tf_op jit(solution)/shard_map/all_to_all | solution.py:498
